TPU v7x, 32 devices: a whole 2x2x4 slice. The times are simulated.
32 devices in a mesh: seq: 16 (over z, y, x), tp: 2 (over core).
Axes of the slice: x: 2, y: 2, z: 4, core: 2. Of those that a mesh axis runs over, the one named last changes fastest.
Arguments:
- prev_hidden: bfloat16 [256, 7168], P('seq', 'tp'), may hold values from -12 to 12
- token_embed: bfloat16 [256, 7168], P('seq', 'tp'), may hold values from -6 to 6
- gain_hidden: float32 [7168], P('tp'), may hold values from 0.25 to 1.75
- gain_embed: float32 [7168], P('tp'), may hold values from 0.25 to 1.75
- gain_final: float32 [7168], P('seq'), may hold values from 0.25 to 1.75
- proj_hidden: bfloat16 [7168, 7168], P('tp', 'seq'), as said below
- proj_embed: bfloat16 [7168, 7168], P('tp', 'seq'), may hold values from -0.046875 to 0.046875
- head: bfloat16 [65536, 7168], P(('seq', 'tp')), as said below
- target_ids: int32 [256], P('seq'), may hold values from 0 to 65535
- valid: int32 [256], P('seq'), may hold values 0 or 1
- rest_count: int32 [1], replicated, may hold values from 1024 to 3839
Outputs:
- grad_prev_hidden: bfloat16 [256, 7168], P('seq', 'tp')
- grad_token_embed: bfloat16 [256, 7168], P('seq', 'tp')
- grad_proj_hidden: bfloat16 [7168, 7168], P('tp', 'seq')
- grad_proj_embed: bfloat16 [7168, 7168], P('tp', 'seq')
- grad_head: bfloat16 [65536, 7168], P(('seq', 'tp'))
Inputs may be any that keep to these rules, and one draw needn't show every extreme that they name: `proj_hidden`: weights of the order of one over the square root of 14336. `head`: weights of the order of one over the square root of 796.
All inputs are finite; a program needn't handle non-finite values. No bound on the sum of `valid` on one device may be relied on, other than what follows from the above.
Results may differ from a plain program's by a relative error of at most 0.0071.
Values may be sent and summed in bfloat16 or wider, within the bound.
No kernel may reach another device: no remote copies, remote signals or barrier semaphores. Data moves between devices by JAX's collectives and lax.ppermute only.
A program may use at most 192 MiB of HBM per device.

v0:
```python
import jax
import jax.numpy as jnp
from jax import lax
from jax.sharding import PartitionSpec as P

D = 7168


loss_scale = 4096.0
epsilon = 1e-06


def from_behind(array, axis, by):
    count = lax.axis_size(axis)
    pairs = [(i, i + by) for i in range(count) if 0 <= i + by < count]
    return lax.ppermute(array, axis, pairs)


def contract_first(left, right):
    return lax.dot_general(
        left, right, (((0,), (0,)), ((), ())), preferred_element_type=jnp.float32
    )


def contract_last(left, right):
    return lax.dot_general(
        left, right, (((1,), (1,)), ((), ())), preferred_element_type=jnp.float32
    )


def shards(
    prev_hidden,
    token_embed,
    gain_hidden,
    gain_embed,
    gain_final,
    proj_hidden,
    proj_embed,
    head,
    target_ids,
    valid,
    rest_count,
):
    ids_all, valid_all = (
        lax.all_gather(target_ids, "seq", axis=0, tiled=True),
        lax.all_gather(valid, "seq", axis=0, tiled=True),
    )
    next_row = from_behind(token_embed[:1], "seq", -1)
    prev_f = prev_hidden.astype(jnp.float32)
    shifted = jnp.concatenate([token_embed[1:], next_row], axis=0).astype(jnp.float32)
    sum_prev, sum_embed = lax.psum(
        (jnp.sum(prev_f * prev_f, axis=-1), jnp.sum(shifted * shifted, axis=-1)), "tp"
    )
    scale_prev = lax.rsqrt(sum_prev / D + epsilon)[:, None]
    scale_embed = lax.rsqrt(sum_embed / D + epsilon)[:, None]
    normed_prev = (prev_f * scale_prev * gain_hidden).astype(jnp.bfloat16)
    normed_embed = (shifted * scale_embed * gain_embed).astype(jnp.bfloat16)
    prev_all, embed_all = (
        lax.all_gather(normed_prev, "seq", axis=0, tiled=True),
        lax.all_gather(normed_embed, "seq", axis=0, tiled=True),
    )
    partial_value = jnp.dot(prev_all, proj_hidden, preferred_element_type=jnp.float32) + jnp.dot(
        embed_all, proj_embed, preferred_element_type=jnp.float32
    )
    mixed_f = lax.psum(partial_value, "tp").astype(jnp.bfloat16).astype(jnp.float32)
    sum_mixed = lax.psum(jnp.sum(mixed_f * mixed_f, axis=-1), "seq")
    scale_final = lax.rsqrt(sum_mixed / D + epsilon)[:, None]
    final = (mixed_f * scale_final * gain_final).astype(jnp.bfloat16)
    final_all = lax.all_gather(final, "seq", axis=1, tiled=True)
    logits = contract_last(final_all, head)
    vocab_rows = head.shape[0]
    vocab_start = lax.axis_index(("seq", "tp")) * vocab_rows
    columns = lax.broadcasted_iota(jnp.int32, (1, vocab_rows), 1) + vocab_start
    onehot = (columns == ids_all[:, None]).astype(jnp.float32)
    local_top = jnp.max(logits, axis=-1)
    row_top = lax.pmax(local_top, ("seq", "tp"))
    expd = jnp.exp(logits - row_top[:, None])
    row_total = lax.psum(jnp.sum(expd, axis=-1), ("seq", "tp"))
    probs = expd / row_total[:, None]
    count = jnp.sum(valid_all).astype(jnp.float32) + rest_count[0].astype(jnp.float32)
    coef = loss_scale * valid_all.astype(jnp.float32) / count
    dlogits = (coef[:, None] * (probs - onehot)).astype(jnp.bfloat16)
    grad_head = contract_first(dlogits, final_all).astype(jnp.bfloat16)
    dfinal_part = jnp.dot(dlogits, head, preferred_element_type=jnp.float32)
    by_seq = lax.psum_scatter(dfinal_part, "seq", scatter_dimension=1, tiled=True)
    dfinal = lax.psum(by_seq, "tp")
    grad_final = dfinal * gain_final
    total_dot = lax.psum(jnp.sum(grad_final * mixed_f, axis=-1), "seq")
    dmixed = (
        scale_final * grad_final - mixed_f * scale_final**3 * (total_dot / D)[:, None]
    ).astype(jnp.bfloat16)
    grad_proj_hidden = contract_first(prev_all, dmixed).astype(jnp.bfloat16)
    grad_proj_embed = contract_first(embed_all, dmixed).astype(jnp.bfloat16)
    both_grads = lax.psum_scatter(
        jnp.concatenate(
            [contract_last(dmixed, proj_hidden), contract_last(dmixed, proj_embed)], axis=1
        ),
        "seq",
        scatter_dimension=0,
        tiled=True,
    )
    width_tp = proj_hidden.shape[0]
    grad_prev = both_grads[:, :width_tp] * gain_hidden
    grad_embed = both_grads[:, width_tp:] * gain_embed
    dot_prev, dot_embed = lax.psum(
        (jnp.sum(grad_prev * prev_f, axis=-1), jnp.sum(grad_embed * shifted, axis=-1)), "tp"
    )
    grad_prev_hidden = (
        scale_prev * grad_prev - prev_f * scale_prev**3 * (dot_prev / D)[:, None]
    ).astype(jnp.bfloat16)
    dshifted = scale_embed * grad_embed - shifted * scale_embed**3 * (dot_embed / D)[:, None]
    incoming = from_behind(dshifted[-1:], "seq", 1)
    grad_token_embed = jnp.concatenate([incoming, dshifted[:-1]], axis=0).astype(jnp.bfloat16)
    return (grad_prev_hidden, grad_token_embed, grad_proj_hidden, grad_proj_embed, grad_head)


def solution(mesh):
    return jax.shard_map(
        shards,
        mesh=mesh,
        in_specs=(
            P("seq", "tp"),
            P("seq", "tp"),
            P("tp"),
            P("tp"),
            P("seq"),
            P("tp", "seq"),
            P("tp", "seq"),
            P(("seq", "tp"), None),
            P("seq"),
            P("seq"),
            P(),
        ),
        out_specs=(
            P("seq", "tp"),
            P("seq", "tp"),
            P("tp", "seq"),
            P("tp", "seq"),
            P(("seq", "tp"), None),
        ),
        check_vma=False,
    )
```

profile of v0, /device:TPU:0, one launch (start us, length us, event | category | flops | bytes accessed | tf_op | source)
XLA Modules:
  0.0 783.7 jit_solution(12881973529256108308)
XLA Ops:
  7.2 0.0 all-gather.4.cloned.1.call-start
  7.2 1.0 slice.20
  8.2 1.3 collective-permute-start
  9.5 1.0 fusion.8
  10.6 0.9 slice.19
  11.5 3.3 collective-permute-done
  14.7 0.2 fusion.15
  14.9 2.5 all-reduce.4
  17.4 0.6 multiply_multiply_fusion.1
  18.0 1.6 fusion.10
  19.6 0.0 all-gather.4.cloned.1.call-update
  19.6 0.0 all-gather.6.cloned.1.call-start
  19.7 1.5 fusion.17
  21.1 0.0 all-gather.6.cloned.1.call-update
  21.2 0.0 all-gather.8.cloned.1.call-start
  21.2 60.3 %all-gather.4.cloned.1.call-done = bf16[256,3584]{1,0:T(8,128)(2,1)} async-done(((bf16[16,3584]{1,0:T(8,128)(2,1)}), bf16[256,3584]{1,0:T(8,128)(2,1)}) %all-gather.4.cloned.1.call-update) | async-done | bytes 1835024 | tf_op jit(solution)/shard_map/all_gather | solution.py:59
  81.5 4.3 fusion.23
  85.8 57.0 %all-gather.6.cloned.1.call-done = bf16[256,3584]{1,0:T(8,128)(2,1)} async-done(((bf16[16,3584]{1,0:T(8,128)(2,1)}), bf16[256,3584]{1,0:T(8,128)(2,1)}) %all-gather.6.cloned.1.call-update) | async-done | bytes 1835024 | tf_op jit(solution)/shard_map/all_gather | solution.py:60
  142.8 3.4 convolution_add_fusion
  146.2 5.4 all-reduce.9
  151.6 0.6 fusion.1
  152.3 40.3 %psum.66 = f32[256]{0:T(256)} all-reduce(f32[256]{0:T(256)} %fusion.1), channel_id=1, replica_groups=mesh['seq'=16,'tp'=2] {'seq'}, use_global_device_ids=true, to_apply=%region_6.0 | all-reduce | flops 256 | bytes 2048 | tf_op jit(solution)/shard_map/psum | solution.py:66
  192.6 1.3 multiply_multiply_fusion
  193.8 0.6 copy-done.6
  194.4 1.5 fusion.3
  195.9 0.0 all-gather.8.cloned.1.call-update
  195.9 0.0 reduce-scatter.3.cloned.1.call-start
  196.6 1.2 dynamic-slice
  198.5 0.6 broadcast.39.clone
  199.1 1.3 dynamic-update-slice
  200.4 0.6 broadcast.39.clone.1
  201.0 1.3 dynamic-update-slice.1
  202.3 9.3 %all-reduce.2 = (s32[256]{0:T(256)}, s32[256]{0:T(256)}) all-reduce(s32[256]{0:T(256)} %dynamic-update-slice, s32[256]{0:T(256)} %dynamic-update-slice.1), channel_id=1, replica_groups=mesh['seq'=16,'tp'=2] {'seq'}, use_global_device_ids=true, to_apply=%add | all-reduce | flops 512 | bytes 4096
  211.6 1.3 reduce_sum.75
  213.5 0.6 iota_add_fusion
  214.1 1.3 multiply_divide_fusion
  215.4 48.6 %all-gather.8.cloned.1.call-done = bf16[256,7168]{0,1:T(8,128)(2,1)} async-done(((bf16[256,448]{0,1:T(8,128)(2,1)}), bf16[256,7168]{0,1:T(8,128)(2,1)}) %all-gather.8.cloned.1.call-update) | async-done | bytes 3670032 | tf_op jit(solution)/shard_map/all_gather | solution.py:69
  264.0 16.2 %fusion.22 = (f32[256]{0:T(256)}, f32[256,2048]{1,0:T(8,128)}) fusion(bf16[256,7168]{0,1:T(8,128)(2,1)} %all-gather.8.cloned.1.call-done, bf16[2048,7168]{1,0:T(8,128)(2,1)} %param.18), kind=kOutput, calls=%fused_computation.57 | convolution fusion | flops 7516717056 | bytes 35128320 | tf_op jit(solution)/shard_map/dot_general | solution.py:26
  280.2 39.5 %pmax.7 = f32[256]{0:T(256)} all-reduce(f32[256]{0:T(256)} %get-tuple-element.19), channel_id=1, replica_groups=mesh['seq'=16,'tp'=2] {'seq','tp'}, use_global_device_ids=true, to_apply=%region_9.0 | all-reduce | flops 256 | bytes 2048 | tf_op jit(solution)/shard_map/pmax | solution.py:76
  319.7 2.6 fusion
  322.3 40.6 %psum.67 = f32[256]{0:T(256)} all-reduce(f32[256]{0:T(256)} %fusion), channel_id=1, replica_groups=mesh['seq'=16,'tp'=2] {'seq','tp'}, use_global_device_ids=true, to_apply=%region_11.0 | all-reduce | flops 256 | bytes 2048 | tf_op jit(solution)/shard_map/psum | solution.py:78
  362.9 19.0 %fusion.21 = f32[256,7168]{0,1:T(8,128)} fusion(bf16[2048,7168]{1,0:T(8,128)(2,1)} %param.18, f32[256,2048]{1,0:T(8,128)} %get-tuple-element.20, s32[2048]{0:T(1024)} %iota_add_fusion, f32[256]{0:T(256)} %psum.67, f32[256]{0:T(256)} %pmax.7, f32[256]{0:T(256)} %multiply_divide_fusion, s32[256]{0:T(256)} %get-tuple-element.8), kind=kOutput, calls=%fused_computation.56 | convolution fusion | flops 7519862784 | bytes 38809600 | tf_op jit(solution)/shard_map/dot_general | solution.py:84
  381.9 0.0 all-reduce.8.cloned.1.call-start
  382.0 156.5 %reduce-scatter.3.cloned.1.call-done = f32[256,448]{0,1:T(8,128)} async-done(((f32[256,7168]{0,1:T(8,128)}), f32[256,448]{0,1:T(8,128)}) %reduce-scatter.3.cloned.1.call-update) | async-done | bytes 458768 | tf_op jit(solution)/shard_map/reduce_scatter | solution.py:85
  538.5 0.0 all-reduce.8.cloned.1.call-update
  538.5 0.0 reduce-scatter.5.cloned.1.call-start
  538.6 23.1 %all-reduce.8.cloned.1.call-done = f32[256,448]{0,1:T(8,128)} async-done(((f32[256,448]{0,1:T(8,128)}), f32[256,448]{0,1:T(8,128)}) %all-reduce.8.cloned.1.call-update) | async-done | bytes 458768 | tf_op jit(solution)/shard_map/psum | solution.py:86
  561.7 1.7 fusion.7
  563.4 42.3 %psum.69 = f32[256]{0:T(256)S(1)} all-reduce(f32[256]{0:T(256)} %fusion.7), channel_id=1, replica_groups=mesh['seq'=16,'tp'=2] {'seq'}, use_global_device_ids=true, to_apply=%region_15.0 | all-reduce | flops 256 | bytes 2048 | tf_op jit(solution)/shard_map/psum | solution.py:88
  605.7 1.2 fusion.6
  607.0 1.1 fusion.25
  608.1 0.8 copy-done.1
  608.9 1.1 fusion.24
  610.0 3.5 pad_maximum_fusion
  613.5 16.2 %convolution_convert_fusion = bf16[2048,7168]{1,0:T(8,128)(2,1)} fusion(bf16[256,7168]{0,1:T(8,128)(2,1)} %all-gather.8.cloned.1.call-done, f32[256,2048]{1,0:T(8,128)} %get-tuple-element.20, s32[2048]{0:T(1024)} %iota_add_fusion, f32[256]{0:T(256)} %psum.67, f32[256]{0:T(256)} %pmax.7, f32[256]{0:T(256)} %multiply_divide_fusion, s32[256]{0:T(256)} %get-tuple-element.8), kind=kOutput, calls=%fused_computation | convolution fusion | flops 7534542848 | bytes 35139584 | tf_op jit(solution)/shard_map/dot_general | solution.py:20
  629.8 2.7 convolution_convert_fusion.2
  632.4 2.7 convolution_convert_fusion.1
  635.1 131.2 %reduce-scatter.5.cloned.1.call-done = f32[16,7168]{1,0:T(8,128)} async-done(((f32[256,7168]{1,0:T(8,128)}), f32[16,7168]{1,0:T(8,128)}) %reduce-scatter.5.cloned.1.call-update) | async-done | bytes 458768 | tf_op jit(solution)/shard_map/reduce_scatter | solution.py:94
  766.3 1.4 fusion.20
  767.7 2.5 all-reduce.3
  770.1 1.1 fusion.19
  771.2 3.1 collective-permute-start.1
  774.3 1.8 fusion.13
  776.1 0.7 pad_maximum_fusion.2
  (23 shorter events, 0.1 us)
Async XLA Ops:
  7.2 135.6 %copy-start = (bf16[3584,448]{0,1:T(8,128)(2,1)S(1)}, bf16[3584,448]{0,1:T(8,128)(2,1)}, u32[]{:S(2)}) copy-start(bf16[3584,448]{0,1:T(8,128)(2,1)} %param.17) | copy-start | bytes 9633796
  7.2 74.3 %all-gather.4.cloned.1.call-start = ((), (), s32[]{:S(2)}) async-start(), calls=%async_computation.2 | async-start | bytes 1949696 | tf_op jit(solution)/shard_map/all_gather | solution.py:59
  8.2 6.5 collective-permute-start
  14.7 71.0 %copy-start.5 = (bf16[1,3584]{1,0:T(2,128)(2,1)}, bf16[1,3584]{1,0:T(2,128)(2,1)S(1)}, u32[]{:S(2)}) copy-start(bf16[1,3584]{1,0:T(2,128)(2,1)S(1)} %collective-permute-done) | copy-start | bytes 21508
  18.0 67.8 %copy-start.7 = (f32[16]{0:T(128)}, f32[16]{0:T(128)S(1)}, u32[]{:S(2)}) copy-start(f32[16]{0:T(128)S(1)} %get-tuple-element.21) | copy-start | bytes 196
  18.0 67.8 %copy-start.8 = (f32[16]{0:T(128)}, f32[16]{0:T(128)S(1)}, u32[]{:S(2)}) copy-start(f32[16]{0:T(128)S(1)} %get-tuple-element.16) | copy-start | bytes 196
  19.6 123.2 %all-gather.6.cloned.1.call-start = ((), (), s32[]{:S(2)}) async-start(), calls=%async_computation.3 | async-start | bytes 1949696 | tf_op jit(solution)/shard_map/all_gather | solution.py:60
  21.2 242.8 %all-gather.8.cloned.1.call-start = ((), (), s32[]{:S(2)}) async-start(), calls=%async_computation.4 | async-start | bytes 3899392 | tf_op jit(solution)/shard_map/all_gather | solution.py:69
  151.6 410.1 %copy-start.2 = (bf16[256,448]{0,1:T(8,128)(2,1)}, bf16[256,448]{0,1:T(8,128)(2,1)S(1)}, u32[]{:S(2)}) copy-start(bf16[256,448]{0,1:T(8,128)(2,1)S(1)} %all-reduce.9) | copy-start | bytes 688132
  193.8 0.6 copy-start.6
  195.9 342.6 %reduce-scatter.3.cloned.1.call-start = ((), (), s32[]{:S(2)}) async-start(), calls=%async_computation.5 | async-start | bytes 7798784 | tf_op jit(solution)/shard_map/reduce_scatter | solution.py:85
  381.9 179.8 %all-reduce.8.cloned.1.call-start = ((), (), s32[]{:S(2)}) async-start(), calls=%async_computation.6 | async-start | bytes 917504 | tf_op jit(solution)/shard_map/psum | solution.py:86
  538.5 227.8 %reduce-scatter.5.cloned.1.call-start = ((), (), s32[]{:S(2)}) async-start(), calls=%async_computation.7 | async-start | bytes 7798784 | tf_op jit(solution)/shard_map/reduce_scatter | solution.py:94
  607.0 1.9 copy-start.1
  613.5 16.2 %copy-start.3 = (bf16[256,3584]{1,0:T(8,128)(2,1)S(1)}, bf16[256,3584]{1,0:T(8,128)(2,1)}, u32[]{:S(2)}) copy-start(bf16[256,3584]{1,0:T(8,128)(2,1)} %all-gather.4.cloned.1.call-done) | copy-start | bytes 5505028
  629.7 2.7 copy-start.4
  771.2 4.9 collective-permute-start.1
Sparse Core Ops, SparseCore 0:
  19.8 61.7 all-gather.3
  84.8 57.9 all-gather.5
  196.0 67.9 all-gather.7
  382.0 156.4 reduce-scatter.2
  540.7 20.9 all-reduce.7
  613.6 152.6 reduce-scatter.4
where the time goes:
time: 786 us; the launch traced here: 784 us
  waiting for transfers between devices  480 us (61%)
  blocking collectives  182 us (23%)
  matrix products  66.7 us (8%)
  other arithmetic  25.4 us (3%)
  between operations  16.2 us (2%)
  local copies, waits for them, and re-layouts  8.34 us (1%)
    reduce_scatter x1, waiting for transfers between devices, shards(): lax.psum_scatter(dfinal_part, 'seq', scatter_dimension=1, tiled=True)  157 us
    reduce_scatter x1, waiting for transfers between devices, shards(): lax.psum_scatter(jnp.concatenate([contract_last(dmixed, proj_hidden), con...  131 us
    all_gather x1, waiting for transfers between devices, shards(): lax.all_gather(normed_prev, 'seq', axis=0, tiled=True)  60.3 us
    all_gather x1, waiting for transfers between devices, shards(): lax.all_gather(normed_embed, 'seq', axis=0, tiled=True)  57 us
    all_gather x1, waiting for transfers between devices, shards(): final_all = lax.all_gather(final, 'seq', axis=1, tiled=True)  48.6 us
    psum x1, blocking collectives, shards(): total_dot = lax.psum(jnp.sum(grad_final * mixed_f, axis=-1), 'seq')  42.3 us
    psum x1, blocking collectives, shards(): row_total = lax.psum(jnp.sum(expd, axis=-1), ('seq', 'tp'))  40.6 us
    psum x1, blocking collectives, shards(): sum_mixed = lax.psum(jnp.sum(mixed_f * mixed_f, axis=-1), 'seq')  40.3 us
  transfers between devices with their start and end apart: 8, of which 7 were waited for; matrix products, arithmetic and copies ran while one was open for 5% of the time, Pallas kernels for 0%

commit v1 on v0

v1 whole, which is shorter than its diff:
```python
import functools

import jax
import jax.numpy as jnp
from jax import lax
from jax.experimental import pallas as pl
from jax.experimental.pallas import tpu as pltpu
from jax.sharding import PartitionSpec as P

D = 7168


loss_scale = 4096.0
epsilon = 1e-06

f32 = jnp.float32
bf16 = jnp.bfloat16
i32 = jnp.int32


def from_partner(array, axis, mask):
    size = lax.axis_size(axis)
    return lax.ppermute(array, axis, [(i, i ^ mask) for i in range(size)])


def plane_and_line():
    size = lax.axis_size("seq")
    plane = min(4, size)
    return list(range(plane)), list(range(0, size, plane))


def fetch(array, masks):
    return jnp.stack([array if mask == 0 else from_partner(array, "seq", mask) for mask in masks])


def gather_line_first(array):
    plane, line = plane_and_line()
    return fetch(fetch(array, line), plane)


def gather_plane_first(array):
    plane, line = plane_and_line()
    return fetch(fetch(array, plane), line)


def scatter_two(first, second, beside=None):
    plane, line = plane_and_line()
    done = None
    sent_one = [first[i].astype(bf16) for i in range(1, len(plane))]
    sent_two = [second[i].astype(bf16) for i in range(1, len(line))]
    if beside is not None:
        work, argument = beside
        argument, sent_one, sent_two = lax.optimization_barrier((argument, sent_one, sent_two))
    came_one = [from_partner(block, "seq", mask) for block, mask in zip(sent_one, plane[1:])]
    came_two = [from_partner(block, "seq", mask) for block, mask in zip(sent_two, line[1:])]
    if beside is not None:
        done, came_one, came_two = lax.optimization_barrier((work(argument), came_one, came_two))
    half_one, half_two = first[0].astype(f32), second[0].astype(f32)
    for block in came_one:
        half_one = half_one + block.astype(f32)
    for block in came_two:
        half_two = half_two + block.astype(f32)
    sent_one = [half_one[i].astype(bf16) for i in range(1, len(line))]
    sent_two = [half_two[i].astype(bf16) for i in range(1, len(plane))]
    came_one = [from_partner(block, "seq", mask) for block, mask in zip(sent_one, line[1:])]
    came_two = [from_partner(block, "seq", mask) for block, mask in zip(sent_two, plane[1:])]
    one, two = half_one[0], half_two[0]
    for block in came_one:
        one = one + block.astype(f32)
    for block in came_two:
        two = two + block.astype(f32)
    return one, two, done


def tp_masks():
    return range(1, lax.axis_size("tp"))


def over_cores(array):
    return jnp.concatenate([array] + [from_partner(array, "tp", mask) for mask in tp_masks()], axis=-1)


def lanes_by_index(array):
    count = lax.axis_size("tp")
    pieces = jnp.split(array, count, axis=-1)
    me = lax.axis_index("tp")
    step = 1
    while step < count:
        flipped = [pieces[i ^ step] for i in range(count)]
        pieces = [jnp.where(me & step == 0, a, b) for a, b in zip(pieces, flipped)]
        step *= 2
    return jnp.concatenate(pieces, axis=-1)


def merged(group):
    tops, totals, weighted, targets = (jnp.stack([one[i] for one in group]) for i in range(4))
    top = jnp.max(tops, axis=0)
    shares = jnp.exp(tops - top)
    return jnp.stack(
        [
            top,
            jnp.sum(shares * totals, axis=0),
            jnp.sum(shares * weighted, axis=0),
            jnp.sum(targets, axis=0),
        ]
    )


def in_parts(values):
    high = lax.reduce_precision(values, 8, 7)
    middle = lax.reduce_precision(values - high, 8, 7)
    return high, middle, values - high - middle


def dot(left, right, on_left, on_right, precision=None):
    return lax.dot_general(
        left,
        right,
        (((on_left,), (on_right,)), ((), ())),
        precision=precision,
        preferred_element_type=f32,
    )


def logits_kernel(
    where, ids, scale, own_a, own_b, other_a, other_b, head, out, stats, all_features, *, line
):
    step = pl.program_id(0)
    tile = head.shape[0]
    blocks, rows_a, lanes = own_a.shape
    features = all_features.shape[0] // blocks
    rows_b = features - rows_a

    @pl.when(step == 0)
    def _():
        plane = blocks // line
        for device in range(blocks):
            relative = where[0] ^ device
            low, high = relative % plane, relative // plane
            at_a, at_b = low * line + high, high * plane + low
            start = device * features
            for side, (a, b) in enumerate(((own_a, own_b), (other_a, other_b))):
                columns = slice(side * lanes, (side + 1) * lanes)
                all_features[start : start + rows_a, columns] = a[at_a]
                all_features[start + rows_a : start + features, columns] = b[at_b][:rows_b]
        stats[...] = jnp.zeros_like(stats)
        stats[0:1, :] = jnp.full((1, stats.shape[1]), -jnp.inf, f32)

    logits = jnp.dot(head[...], all_features[...], preferred_element_type=f32) * scale[...]
    out[...] = logits
    entries = lax.broadcasted_iota(i32, logits.shape, 0) + (where[1] + step * tile)
    before = stats[0:1, :]
    top = jnp.maximum(before, jnp.max(logits, axis=0, keepdims=True))
    shrink = jnp.exp(before - top)
    expd = jnp.exp(logits - top)
    stats[0:1, :] = top
    stats[1:2, :] = stats[1:2, :] * shrink + jnp.sum(expd, axis=0, keepdims=True)
    stats[2:3, :] = stats[2:3, :] * shrink + jnp.sum(expd * logits, axis=0, keepdims=True)
    stats[3:4, :] = stats[3:4, :] + jnp.sum(
        jnp.where(entries == ids[...], logits, 0.0), axis=0, keepdims=True
    )


def head_logits(where, ids, scale, own_a, own_b, other_a, other_b, head, line):
    vocab, tokens = head.shape[0], ids.shape[1]
    tile = 512
    whole = lambda array: pl.BlockSpec(array.shape, lambda i, w: (0,) * array.ndim)
    return pl.pallas_call(
        functools.partial(logits_kernel, line=line),
        grid_spec=pltpu.PrefetchScalarGridSpec(
            num_scalar_prefetch=1,
            grid=(vocab // tile,),
            in_specs=[
                whole(ids),
                whole(scale),
                whole(own_a),
                whole(own_b),
                whole(other_a),
                whole(other_b),
                pl.BlockSpec((tile, D), lambda i, w: (i, 0)),
            ],
            out_specs=[
                pl.BlockSpec((tile, tokens), lambda i, w: (i, 0)),
                pl.BlockSpec((8, tokens), lambda i, w: (0, 0)),
                pl.BlockSpec((D, tokens), lambda i, w: (0, 0)),
            ],
        ),
        out_shape=[
            jax.ShapeDtypeStruct((vocab, tokens), f32),
            jax.ShapeDtypeStruct((8, tokens), f32),
            jax.ShapeDtypeStruct((D, tokens), bf16),
        ],
        compiler_params=pltpu.CompilerParams(vmem_limit_bytes=44 << 20),
        cost_estimate=pl.CostEstimate(
            flops=2 * vocab * D * tokens,
            bytes_accessed=2 * vocab * D + 4 * D * tokens,
            transcendentals=vocab * tokens,
        ),
    )(where, ids, scale, own_a, own_b, other_a, other_b, head)


def dfinal_kernel(where, ids, rows, logits, head, kept, sent, scaled, turned):
    step = pl.program_id(0)
    vocab, tokens = logits.shape
    lanes = kept.shape[3]

    @pl.when(step == 0)
    def _():
        top, share, coef, scale = (rows[i : i + 1, :] for i in range(4))
        tile = 256
        for start in range(0, vocab, tile):
            probs = jnp.exp(logits[start : start + tile, :] - top) * share
            entries = lax.broadcasted_iota(i32, probs.shape, 0) + (where[1] + start)
            dlogits = coef * (probs - (entries == ids[...]).astype(f32))
            scaled[start : start + tile, :] = (dlogits * scale).astype(bf16)
            turned[:, start : start + tile] = dlogits.T.astype(bf16)

    product = jnp.dot(turned[...], head[...], preferred_element_type=f32).T
    half = product.shape[0] // 2
    flip = where[0] & 1
    for piece in range(2):
        block = product[piece * half : (piece + 1) * half]
        kept[0, piece ^ flip] = block[:, :lanes]
        sent[0, piece ^ flip] = block[:, lanes:].astype(bf16)


def head_back(where, ids, rows, logits, head, blocks):
    vocab, tokens = logits.shape
    features = D // blocks
    lanes = tokens // 2
    pairs = blocks // 2
    whole = lambda array: pl.BlockSpec(array.shape, lambda i, w: (0,) * array.ndim)
    place = lambda i, w: (i ^ (w[0] >> 1), 0, 0, 0)
    return pl.pallas_call(
        dfinal_kernel,
        grid_spec=pltpu.PrefetchScalarGridSpec(
            num_scalar_prefetch=1,
            grid=(pairs,),
            in_specs=[
                whole(ids),
                whole(rows),
                whole(logits),
                pl.BlockSpec((vocab, 2 * features), lambda i, w: (0, i)),
            ],
            out_specs=[
                pl.BlockSpec((1, 2, features, lanes), place),
                pl.BlockSpec((1, 2, features, lanes), place),
                pl.BlockSpec((vocab, tokens), lambda i, w: (0, 0)),
            ],
            scratch_shapes=[pltpu.VMEM((tokens, vocab), bf16)],
        ),
        out_shape=[
            jax.ShapeDtypeStruct((pairs, 2, features, lanes), f32),
            jax.ShapeDtypeStruct((pairs, 2, features, lanes), bf16),
            jax.ShapeDtypeStruct((vocab, tokens), bf16),
        ],
        compiler_params=pltpu.CompilerParams(vmem_limit_bytes=32 << 20),
        cost_estimate=pl.CostEstimate(
            flops=2 * vocab * D * tokens,
            bytes_accessed=2 * vocab * D + 4 * D * tokens,
            transcendentals=vocab * tokens,
        ),
    )(where, ids, rows, logits, head)


def plain_logits(where, ids, scale, pieces_a, pieces_b, head, line):
    rows_a = pieces_a[0].shape[1]
    blocks, _, lanes = pieces_a[0].shape
    features = D // blocks
    plane = blocks // line
    sides = []
    for a, b in zip(pieces_a, pieces_b):
        a = a.reshape(plane, line, rows_a, lanes).swapaxes(0, 1).reshape(blocks, rows_a, lanes)
        both = jnp.concatenate([a, b[:, : features - rows_a]], axis=1)
        sides.append(both[where[0] ^ jnp.arange(blocks)].reshape(D, lanes))
    all_features = jnp.concatenate(sides, axis=1)
    logits = dot(head, all_features, 1, 0) * scale
    top = jnp.max(logits, axis=0)
    expd = jnp.exp(logits - top)
    onehot = (jnp.arange(head.shape[0])[:, None] + where[1]) == ids
    stats = [
        top,
        jnp.sum(expd, axis=0),
        jnp.sum(expd * logits, axis=0),
        jnp.sum(jnp.where(onehot, logits, 0.0), axis=0),
    ]
    return logits, jnp.stack(stats), all_features


def plain_back(where, ids, rows, logits, head, blocks):
    top, share, coef, scale = rows[0], rows[1], rows[2], rows[3]
    lanes = logits.shape[1] // lax.axis_size("tp")
    onehot = (jnp.arange(head.shape[0])[:, None] + where[1]) == ids
    dlogits = coef * (jnp.exp(logits - top) * share - onehot.astype(f32))
    product = dot(head, dlogits.astype(bf16), 0, 0).reshape(blocks, D // blocks, -1)
    product = product[where[0] ^ jnp.arange(blocks)]
    return product[..., :lanes], product[..., lanes:].astype(bf16), (dlogits * scale).astype(bf16)


def shards(
    prev_hidden,
    token_embed,
    gain_hidden,
    gain_embed,
    gain_final,
    proj_hidden,
    proj_embed,
    head,
    target_ids,
    valid,
    rest_count,
):
    blocks, cores = lax.axis_size("seq"), lax.axis_size("tp")
    plane, line = (len(masks) for masks in plane_and_line())
    me = lax.axis_index("seq")
    rows, width = prev_hidden.shape
    features = proj_hidden.shape[1]
    tokens = rows * blocks
    lanes = tokens // cores

    prev_f = prev_hidden.astype(f32)
    embed_f = token_embed.astype(f32)
    sums = lax.psum(
        jnp.stack([jnp.sum(prev_f * prev_f, axis=-1), jnp.sum(embed_f * embed_f, axis=-1)]), "tp"
    )
    scales = lax.rsqrt(sums / D + epsilon)
    scale_prev, scale_embed = scales[0][:, None], scales[1][:, None]
    normed_prev = (prev_f * scale_prev * gain_hidden).astype(bf16)
    normed_embed = (embed_f * scale_embed * gain_embed).astype(bf16)
    facts = jnp.stack([target_ids // 256, target_ids % 256, valid], axis=1).astype(bf16)
    facts = jnp.pad(facts, ((0, 0), (0, 125)))

    cut = round((2 * width + 128) / 192) * 128 - width
    rest = width - cut
    first = gather_line_first(jnp.concatenate([normed_prev, normed_embed[:, :cut]], axis=1))
    second = gather_plane_first(jnp.concatenate([normed_embed[:, cut:], facts], axis=1))
    first = first.reshape(tokens, width + cut)
    second = second.swapaxes(0, 1).reshape(tokens, rest + 128)

    row = lax.broadcasted_iota(i32, (tokens, 1), 0)
    place = row // rows
    partner = (place % line) * plane + place // line
    position = (me ^ partner) * rows + row % rows
    column = lax.broadcasted_iota(i32, (1, tokens), 1)
    order_prev = (position == column).astype(f32)
    order_embed = (position - 1 == column).astype(f32)

    from_prev = dot(proj_hidden, first[:, :width], 0, 1)
    from_embed = dot(proj_embed[:cut], first[:, width:], 0, 1) + dot(
        proj_embed[cut:], second[:, :rest], 0, 1
    )
    partial_value = dot(
        jnp.concatenate([from_prev, from_embed], axis=1),
        jnp.concatenate([order_prev, order_embed], axis=0),
        1,
        0,
        lax.Precision.HIGHEST,
    )
    facts_all = dot(second[:, rest:], order_prev.astype(bf16), 0, 0)
    ids_all = (facts_all[0:1] * 256 + facts_all[1:2]).astype(i32)
    valid_all = facts_all[2]
    core = lax.axis_index("tp")
    cut_of = lambda mask: lax.dynamic_slice_in_dim(partial_value, (core ^ mask) * lanes, lanes, 1)
    mixed_f = cut_of(0)
    for mask in tp_masks():
        mixed_f = mixed_f + from_partner(cut_of(mask), "tp", mask)
    mixed_f = mixed_f.astype(bf16).astype(f32)
    scaled = (mixed_f * gain_final[:, None]).astype(bf16)
    square_parts = jnp.stack(in_parts(jnp.sum(mixed_f * mixed_f, axis=0))).astype(bf16)
    square_parts = jnp.pad(square_parts, ((0, 13), (0, 0)))
    rows_a = features - round(0.32 * features / 16) * 16
    own_a = gather_line_first(scaled[:rows_a]).reshape(blocks, rows_a, lanes)
    own_b = gather_plane_first(jnp.concatenate([scaled[rows_a:], square_parts], axis=0))
    own_b = own_b.reshape(blocks, features - rows_a + 16, lanes)
    pieces_a = [own_a] + [from_partner(own_a, "tp", mask) for mask in tp_masks()]
    pieces_b = [own_b] + [from_partner(own_b, "tp", mask) for mask in tp_masks()]
    squares = [
        jnp.sum(b[:, features - rows_a : features - rows_a + 3].astype(f32), axis=(0, 1))
        for b in pieces_b
    ]
    scale_own = lax.rsqrt(squares[0] / D + epsilon)
    scale_final = lax.rsqrt(jnp.concatenate(squares) / D + epsilon)

    vocab_rows = head.shape[0]
    where = jnp.stack([me, lax.axis_index(("seq", "tp")) * vocab_rows]).astype(i32)
    ids = lanes_by_index(ids_all)
    valid_here = lanes_by_index(valid_all)
    fits = cores == 2 and lanes % 128 == 0 and vocab_rows % 512 == 0 and 2 * features % 128 == 0
    if fits:
        pieces = (pieces_a[0], pieces_b[0], pieces_a[1], pieces_b[1])
        logits, stats, scaled_all = head_logits(
            where, ids, scale_final[None, :], *pieces, head, line
        )
    else:
        logits, stats, scaled_all = plain_logits(
            where, ids, scale_final, pieces_a, pieces_b, head, line
        )
    stats = stats[:4]
    for masks in plane_and_line():
        stats = merged([stats] + [from_partner(stats, "seq", mask) for mask in masks[1:]])
    stats = lanes_by_index(stats)
    stats = merged([stats] + [from_partner(stats, "tp", mask) for mask in tp_masks()])
    row_top, row_total, row_weighted, target_logit = lanes_by_index(stats)
    count = jnp.sum(valid_all) + rest_count[0].astype(f32)
    coef = loss_scale * valid_here / count
    row_values = jnp.stack([row_top, 1.0 / row_total, coef, scale_final])
    row_values = jnp.pad(row_values, ((0, 4), (0, 0)))
    back = head_back if fits else plain_back
    kept, sent, dlogits_scaled = back(where, ids, row_values, logits, head, blocks)
    dfinal = kept.reshape(blocks, features, lanes)
    for mask in tp_masks():
        piece = sent[..., (mask - 1) * lanes : mask * lanes]
        dfinal = dfinal + from_partner(piece, "tp", mask).astype(f32).reshape(dfinal.shape)
    dfinal = dfinal.reshape(line, plane, features, lanes)
    one, two, _ = scatter_two(dfinal[:, :, :rows_a].swapaxes(0, 1), dfinal[:, :, rows_a:])
    dfinal = jnp.concatenate([one, two], axis=0)

    total_dot = (coef * (row_weighted / row_total - target_logit))[:lanes] / scale_own
    dmixed = (
        scale_own * (dfinal * gain_final[:, None]) - mixed_f * (scale_own**3 * (total_dot / D))
    ).astype(bf16)
    dmixed = lanes_by_index(over_cores(dmixed))
    dmixed_prev = dot(dmixed, order_prev.astype(bf16), 1, 1).astype(bf16)
    dmixed_embed = dot(dmixed, order_embed.astype(bf16), 1, 1).astype(bf16)
    back_prev = dot(dmixed_prev, proj_hidden, 0, 1)
    back_embed = dot(dmixed_embed, proj_embed, 0, 1)
    one = jnp.concatenate([back_prev, back_embed[:, :cut]], axis=1)
    two = back_embed[:, cut:]
    one, two, done = scatter_two(
        one.reshape(plane, line, rows, width + cut),
        two.reshape(plane, line, rows, rest).swapaxes(0, 1),
        (
            lambda given: (
                dot(given[0], scaled_all, 1, 1).astype(bf16),
                dot(first[:, :width], given[1], 0, 1).astype(bf16),
                dot(
                    jnp.concatenate([first[:, width:], second[:, :rest]], axis=1), given[2], 0, 1
                ).astype(bf16),
            ),
            (dlogits_scaled, dmixed_prev, dmixed_embed),
        ),
    )
    grad_head, grad_proj_hidden, grad_proj_embed = done
    grad_prev = one[:, :width] * gain_hidden
    grad_embed = jnp.concatenate([one[:, width:], two], axis=1) * gain_embed
    dots = lax.psum(
        jnp.stack([jnp.sum(grad_prev * prev_f, axis=-1), jnp.sum(grad_embed * embed_f, axis=-1)]),
        "tp",
    )
    grad_prev_hidden = (
        scale_prev * grad_prev - prev_f * (scale_prev**3 * (dots[0] / D)[:, None])
    ).astype(bf16)
    grad_token_embed = (
        scale_embed * grad_embed - embed_f * (scale_embed**3 * (dots[1] / D)[:, None])
    ).astype(bf16)
    return (grad_prev_hidden, grad_token_embed, grad_proj_hidden, grad_proj_embed, grad_head)


def solution(mesh):
    return jax.shard_map(
        shards,
        mesh=mesh,
        in_specs=(
            P("seq", "tp"),
            P("seq", "tp"),
            P("tp"),
            P("tp"),
            P("seq"),
            P("tp", "seq"),
            P("tp", "seq"),
            P(("seq", "tp"), None),
            P("seq"),
            P("seq"),
            P(),
        ),
        out_specs=(
            P("seq", "tp"),
            P("seq", "tp"),
            P("tp", "seq"),
            P("tp", "seq"),
            P(("seq", "tp"), None),
        ),
        check_vma=False,
    )
```

time: 786 us -> 294 us (0.37)
  waiting for transfers between devices: 480 us -> 98.1 us
  blocking collectives: 182 us -> 5.71 us
  starting transfers between devices: 4.63 us -> 83.3 us
  matrix products: 66.7 us -> 30.7 us
  Pallas kernels: 0 us -> 31.5 us
  between operations: 16.2 us -> 2.77 us
    reduce_scatter x2 -> x0, waiting for transfers between devices: 288 us -> none  [the longest x1 157 us: shards(): lax.psum_scatter(dfinal_part, 'seq', scatter_dimension=1, tiled=True)]
    all_gather x3 -> x0, waiting for transfers between devices: 166 us -> none  [the longest x1 60.3 us: shards(): lax.all_gather(normed_prev, 'seq', axis=0, tiled=True)]
    psum x6 -> x2, blocking collectives: 134 us -> 5.71 us  [the longest x1 3.13 us: shards(): lax.psum(jnp.stack([jnp.sum(grad_prev * prev_f, axis=-1), jnp.sum(grad_em...]
    ppermute x2 -> x60, waiting for transfers between devices: 3.26 us -> 98.1 us  [from_partner(): return lax.ppermute(array, axis, [(i, i ^ mask) for i in range(size)])]
    ppermute x2 -> x60, starting transfers between devices: 4.39 us -> 83.3 us  [from_partner(): return lax.ppermute(array, axis, [(i, i ^ mask) for i in range(size)])]
    pmax x1 -> x0, blocking collectives: 39.5 us -> none  [shards(): row_top = lax.pmax(local_top, ('seq', 'tp'))]
    dot_general x9 -> x12, matrix products: 66.7 us -> 30.7 us  [dot(): lax.dot_general(left, right, (((on_left,), (on_right,)), ((), ())), preci...]
    pallas_call x0 -> x2, Pallas kernels: none -> 31.5 us  [the longest x1 16.8 us: head_back(): pl.pallas_call(dfinal_kernel, grid_spec=pltpu.PrefetchScalarGridSpec(num_...]
  transfers between devices with their start and end apart: 8 -> 60, of which waited for: 7 -> 31; matrix products, arithmetic and copies ran while one was open for 5% -> 13% of each run, Pallas kernels for 0% -> 0%
where the time goes in v1:
time: 294 us; the launch traced here: 293 us
  waiting for transfers between devices  98.1 us (33%)
  starting transfers between devices  83.3 us (28%)
  Pallas kernels  31.5 us (11%)
  matrix products  30.7 us (10%)
  other arithmetic  25.9 us (9%)
  local copies, waits for them, and re-layouts  15 us (5%)
  blocking collectives  5.71 us (2%)
    ppermute x60, waiting for transfers between devices, from_partner(): return lax.ppermute(array, axis, [(i, i ^ mask) for i in range(size)])  98.1 us
    ppermute x60, starting transfers between devices, from_partner(): return lax.ppermute(array, axis, [(i, i ^ mask) for i in range(size)])  83.3 us
    dot_general x12, matrix products, dot(): lax.dot_general(left, right, (((on_left,), (on_right,)), ((), ())), preci...  30.7 us
    pallas_call x1, Pallas kernels, head_back(): pl.pallas_call(dfinal_kernel, grid_spec=pltpu.PrefetchScalarGridSpec(num_...  16.8 us
    pallas_call x1, Pallas kernels, head_logits(): pl.pallas_call(functools.partial(logits_kernel, line=line), grid_spec=plt...  14.6 us
    another operation x11, other arithmetic, fetch(): jnp.stack([array if mask == 0 else from_partner(array, 'seq', mask) for m...  7.89 us
    unnamed x63, local copies, waits for them, and re-layouts  6.93 us
  transfers between devices with their start and end apart: 60, of which 31 were waited for; matrix products, arithmetic and copies ran while one was open for 13% of the time, Pallas kernels for 0%

profile of v1, /device:TPU:0, one launch (start us, length us, event | category | flops | bytes accessed | tf_op | source)
XLA Modules:
  0.0 292.9 jit_solution(13354992593084739904)
XLA Ops:
  2.9 2.6 psum.14
  8.1 2.9 collective-permute-start.7
  13.2 3.1 %collective-permute-start.1 = (bf16[16,4864]{1,0:T(8,128)(2,1)}, bf16[16,4864]{1,0:T(8,128)(2,1)}, u32[]{:S(2)}, u32[]{:S(2)}) collective-permute-start(bf16[16,4864]{1,0:T(8,128)(2,1)} %get-tuple-element.103), channel_id=1, source_target_pairs={{0,16},{2,18},{4,20},{6,22},{8,24},{10,26},{12,28},{14,30},{16,0},... | collective-permute-start | bytes 466952 | tf_op jit(solution)/shard_map/ppermute | solution.py:23
  16.3 1.6 collective-permute-start
  20.5 2.0 collective-permute-start.10
  22.5 2.5 collective-permute-start.9
  25.0 8.1 %collective-permute-done.1 = bf16[16,4864]{1,0:T(8,128)(2,1)} collective-permute-done((bf16[16,4864]{1,0:T(8,128)(2,1)}, bf16[16,4864]{1,0:T(8,128)(2,1)}, u32[]{:S(2)}, u32[]{:S(2)}) %collective-permute-start.1) | collective-permute-done | bytes 155680 | tf_op jit(solution)/shard_map/ppermute | solution.py:23
  33.1 2.5 collective-permute-start.11
  36.7 1.6 collective-permute-start.4
  39.8 11.4 %collective-permute-done.10 = bf16[4,16,2432]{2,1,0:T(8,128)(2,1)S(1)} collective-permute-done((bf16[4,16,2432]{2,1,0:T(8,128)(2,1)S(1)}, bf16[4,16,2432]{2,1,0:T(8,128)(2,1)S(1)}, u32[]{:S(2)}, u32[]{:S(2)}) %collective-permute-start.10) | collective-permute-done | bytes 311328 | tf_op jit(solution)/shard_map/ppermute | solution.py:23
  51.2 2.5 collective-permute-start.5
  54.9 10.8 %collective-permute-done.5 = bf16[4,16,4864]{2,1,0:T(8,128)(2,1)S(1)} collective-permute-done((bf16[4,16,4864]{2,1,0:T(8,128)(2,1)S(1)}, bf16[4,16,4864]{2,1,0:T(8,128)(2,1)S(1)}, u32[]{:S(2)}, u32[]{:S(2)}) %collective-permute-start.5) | collective-permute-done | bytes 622624 | tf_op jit(solution)/shard_map/ppermute | solution.py:23
  67.8 1.8 fusion.15
  71.1 1.7 collective-permute-done.12
  73.9 5.4 %collective-permute-start.21 = (bf16[304,128]{1,0:T(8,128)(2,1)S(1)}, bf16[304,128]{1,0:T(8,128)(2,1)S(1)}, u32[]{:S(2)}, u32[]{:S(2)}) collective-permute-start(bf16[304,128]{1,0:T(8,128)(2,1)S(1)} %get-tuple-element.112), channel_id=1, source_target_pairs={{0,16},{2,18},{4,20},{6,22},{8,24},{10,26},{12,28},{14,30},{16,0},... | collective-permute-start | bytes 233480 | tf_op jit(solution)/shard_map/ppermute | solution.py:23
  79.3 1.5 collective-permute-start.22
  80.9 3.3 %collective-permute-done.21 = bf16[304,128]{1,0:T(8,128)(2,1)S(1)} collective-permute-done((bf16[304,128]{1,0:T(8,128)(2,1)S(1)}, bf16[304,128]{1,0:T(8,128)(2,1)S(1)}, u32[]{:S(2)}, u32[]{:S(2)}) %collective-permute-start.21) | collective-permute-done | bytes 77856 | tf_op jit(solution)/shard_map/ppermute | solution.py:23
  84.2 2.1 collective-permute-done.20
  87.1 1.5 collective-permute-start.24
  91.2 1.5 collective-permute-start.14
  92.8 1.5 collective-permute-start.13
  94.3 4.3 %collective-permute-done.14 = bf16[160,128]{1,0:T(8,128)(2,1)} collective-permute-done((bf16[160,128]{1,0:T(8,128)(2,1)}, bf16[160,128]{1,0:T(8,128)(2,1)}, u32[]{:S(2)}, u32[]{:S(2)}) %collective-permute-start.14) | collective-permute-done | bytes 40992 | tf_op jit(solution)/shard_map/ppermute | solution.py:23
  98.6 2.4 collective-permute-start.15
  101.1 4.4 %collective-permute-done.13 = bf16[160,128]{1,0:T(8,128)(2,1)} collective-permute-done((bf16[160,128]{1,0:T(8,128)(2,1)}, bf16[160,128]{1,0:T(8,128)(2,1)}, u32[]{:S(2)}, u32[]{:S(2)}) %collective-permute-start.13) | collective-permute-done | bytes 40992 | tf_op jit(solution)/shard_map/ppermute | solution.py:23
  106.7 2.3 collective-permute-start.17
  109.6 1.6 collective-permute-start.18
  113.7 4.8 %collective-permute-done.17 = bf16[4,160,128]{2,1,0:T(8,128)(2,1)S(1)} collective-permute-done((bf16[4,160,128]{2,1,0:T(8,128)(2,1)S(1)}, bf16[4,160,128]{2,1,0:T(8,128)(2,1)S(1)}, u32[]{:S(2)}, u32[]{:S(2)}) %collective-permute-start.17) | collective-permute-done | bytes 163872 | tf_op jit(solution)/shard_map/ppermute | solution.py:23
  118.4 1.8 collective-permute-done.18
  122.5 14.6 %shard_map.146 = (f32[2048,256]{1,0:T(8,128)S(1)}, f32[8,256]{1,0:T(8,128)S(1)}, bf16[7168,256]{1,0:T(8,128)(2,1)S(1)}) custom-call(s32[2]{0:T(128)S(1)} %pad_add_fusion.1.where, s32[1,256]{1,0:T(1,128)S(1)} %pad_add_fusion.ids, f32[1,256]{1,0:T(1,128)S(1)} %fusion.107.scale, bf16[16,304,128]{2,1,0:T(8,128)(2,1)S(1)} %bitcast.237, ...), custom_call_target="tpu_custom_call" | custom-call | flops 7516192768 | bytes 36700160 | tf_op jit(solution)/shard_map/pallas_call | solution.py:168
  137.2 1.8 copy-done.1
  140.3 2.4 collective-permute-start.29
  144.8 1.5 collective-permute-done.28
  147.0 2.7 collective-permute-start.32
  149.7 1.9 collective-permute-start.31
  152.4 1.8 collective-permute-done.31
  156.7 1.6 copy-done.3
  158.3 16.8 %shard_map.147 = (f32[8,2,448,128]{3,2,1,0:T(8,128)S(1)}, bf16[8,2,448,128]{3,2,1,0:T(8,128)(2,1)S(1)}, bf16[2048,256]{1,0:T(8,128)(2,1)S(1)}) custom-call(s32[2]{0:T(128)S(1)} %pad_add_fusion.1.where, s32[1,256]{1,0:T(1,128)S(1)} %pad_add_fusion.ids, f32[8,256]{1,0:T(8,128)S(1)} %select_maximum_fusion.rows, f32[2048,256]{1,0:T(8,128)S(1)} %copy-done.3, ...), custom_call_target="tpu_custom_call" | custom-call | flops 7516192768 | bytes 36700160 | tf_op jit(solution)/shard_map/pallas_call | solution.py:234
  175.4 3.6 %collective-permute-done.34 = bf16[8,2,448,128]{3,2,1,0:T(8,128)(2,1)S(1)} collective-permute-done((bf16[8,2,448,128]{3,2,1,0:T(8,128)(2,1)S(1)}, bf16[8,2,448,128]{3,2,1,0:T(8,128)(2,1)S(1)}, u32[]{:S(2)}, u32[]{:S(2)}) %collective-permute-start.34) | collective-permute-done | bytes 1835040 | tf_op jit(solution)/shard_map/ppermute | solution.py:23
  180.5 2.1 collective-permute-start.43
  184.3 2.4 collective-permute-start.37
  187.9 2.6 collective-permute-done.43
  190.5 6.2 %collective-permute-done.42 = bf16[4,144,128]{2,1,0:T(8,128)(2,1)S(1)} collective-permute-done((bf16[4,144,128]{2,1,0:T(8,128)(2,1)S(1)}, bf16[4,144,128]{2,1,0:T(8,128)(2,1)S(1)}, u32[]{:S(2)}, u32[]{:S(2)}) %collective-permute-start.42) | collective-permute-done | bytes 147488 | tf_op jit(solution)/shard_map/ppermute | solution.py:23
  197.4 2.4 collective-permute-start.46
  200.5 2.1 collective-permute-done.36
  204.2 2.1 collective-permute-start.40
  207.4 3.0 %collective-permute-done.40 = bf16[304,128]{1,0:T(8,128)(2,1)S(1)} collective-permute-done((bf16[304,128]{1,0:T(8,128)(2,1)S(1)}, bf16[304,128]{1,0:T(8,128)(2,1)S(1)}, u32[]{:S(2)}, u32[]{:S(2)}) %collective-permute-start.40) | collective-permute-done | bytes 77856 | tf_op jit(solution)/shard_map/ppermute | solution.py:23
  210.4 1.7 collective-permute-done.39
  217.0 1.6 copy.36
  223.6 2.7 collective-permute-start.52
  227.3 2.4 collective-permute-start.50
  229.7 15.3 %convolution_convert_fusion = bf16[2048,7168]{1,0:T(8,128)(2,1)} fusion(bf16[2048,256]{1,0:T(8,128)(2,1)S(1)} %get-tuple-element.34, bf16[7168,256]{1,0:T(8,128)(2,1)} %copy-done.1), kind=kOutput, calls=%fused_computation | convolution fusion | flops 7530872832 | bytes 34078720 | tf_op jit(solution)/shard_map/dot_general | solution.py:116
  245.0 4.4 %convolution_convert_fusion.2 = bf16[3584,448]{0,1:T(8,128)(2,1)} fusion(bf16[448,256]{1,0:T(8,128)(2,1)} %copy-done.13, bf16[256,4864]{1,0:T(8,128)(2,1)} %bitcast.250), kind=kOutput, calls=%fused_computation.4 | convolution fusion | flops 823689216 | bytes 5275648 | tf_op jit(solution)/shard_map/dot_general | solution.py:116
  249.4 1.7 collective-permute-start.53
  251.2 2.7 convolution_convert_fusion.1
  253.9 5.3 %collective-permute-done.53 = bf16[4,16,2304]{2,1,0:T(8,128)(2,1)S(1)} collective-permute-done((bf16[4,16,2304]{2,1,0:T(8,128)(2,1)S(1)}, bf16[4,16,2304]{2,1,0:T(8,128)(2,1)S(1)}, u32[]{:S(2)}, u32[]{:S(2)}) %collective-permute-start.53) | collective-permute-done | bytes 294944 | tf_op jit(solution)/shard_map/ppermute | solution.py:23
  264.2 1.8 fusion.132
  266.0 4.8 %collective-permute-start.54 = (bf16[16,4864]{1,0:T(8,128)(2,1)S(1)}, bf16[16,4864]{1,0:T(8,128)(2,1)S(1)}, u32[]{:S(2)}, u32[]{:S(2)}) collective-permute-start(bf16[16,4864]{1,0:T(8,128)(2,1)S(1)} %get-tuple-element.83), channel_id=1, source_target_pairs={{0,8},{2,10},{4,12},{6,14},{8,0},{10,2},{12,4},{14,6},{16,24},{18,... | collective-permute-start | bytes 466952 | tf_op jit(solution)/shard_map/ppermute | solution.py:23
  270.8 1.8 collective-permute-start.56
  272.6 3.6 %collective-permute-done.54 = bf16[16,4864]{1,0:T(8,128)(2,1)S(1)} collective-permute-done((bf16[16,4864]{1,0:T(8,128)(2,1)S(1)}, bf16[16,4864]{1,0:T(8,128)(2,1)S(1)}, u32[]{:S(2)}, u32[]{:S(2)}) %collective-permute-start.54) | collective-permute-done | bytes 155680 | tf_op jit(solution)/shard_map/ppermute | solution.py:23
  276.2 2.9 collective-permute-done.56
  279.1 5.0 %collective-permute-done.55 = bf16[16,4864]{1,0:T(8,128)(2,1)S(1)} collective-permute-done((bf16[16,4864]{1,0:T(8,128)(2,1)S(1)}, bf16[16,4864]{1,0:T(8,128)(2,1)S(1)}, u32[]{:S(2)}, u32[]{:S(2)}) %collective-permute-start.55) | collective-permute-done | bytes 155680 | tf_op jit(solution)/shard_map/ppermute | solution.py:23
  285.6 3.1 %psum.15 = f32[2,16]{1,0:T(2,128)} all-reduce(f32[2,16]{1,0:T(2,128)} %pad_maximum_fusion.22), channel_id=1, replica_groups=mesh['seq'=16,'tp'=2] {'tp'}, use_global_device_ids=true, to_apply=%region_15.16 | all-reduce | flops 32 | bytes 256 | tf_op jit(solution)/shard_map/psum | solution.py:446
  289.5 1.6 fusion.45
  291.1 1.8 fusion.51
  (230 shorter events, 60.9 us)
Async XLA Ops:
  0.6 66.0 %copy-start = (bf16[3584,448]{0,1:T(8,128)(2,1)S(1)}, bf16[3584,448]{0,1:T(8,128)(2,1)}, u32[]{:S(2)}) copy-start(bf16[3584,448]{0,1:T(8,128)(2,1)} %param.16) | copy-start | bytes 9633796
  8.1 11.2 %collective-permute-start.7 = (bf16[16,2432]{1,0:T(8,128)(2,1)}, bf16[16,2432]{1,0:T(8,128)(2,1)}, u32[]{:S(2)}, u32[]{:S(2)}) collective-permute-start(bf16[16,2432]{1,0:T(8,128)(2,1)} %get-tuple-element.114), channel_id=1, source_target_pairs={{0,4},{2,6},{4,0},{6,2},{8,12},{10,14},{12,8},{14,10},{16,20},{18,... | collective-permute-start | bytes 233480 | tf_op jit(solution)/shard_map/ppermute | solution.py:23
  11.0 8.4 %collective-permute-start.6 = (bf16[16,2432]{1,0:T(8,128)(2,1)}, bf16[16,2432]{1,0:T(8,128)(2,1)}, u32[]{:S(2)}, u32[]{:S(2)}) collective-permute-start(bf16[16,2432]{1,0:T(8,128)(2,1)} %get-tuple-element.114), channel_id=1, source_target_pairs={{0,2},{2,0},{4,6},{6,4},{8,10},{10,8},{12,14},{14,12},{16,18},{18,... | collective-permute-start | bytes 233480 | tf_op jit(solution)/shard_map/ppermute | solution.py:23
  12.4 6.9 %collective-permute-start.8 = (bf16[16,2432]{1,0:T(8,128)(2,1)}, bf16[16,2432]{1,0:T(8,128)(2,1)}, u32[]{:S(2)}, u32[]{:S(2)}) collective-permute-start(bf16[16,2432]{1,0:T(8,128)(2,1)} %get-tuple-element.114), channel_id=1, source_target_pairs={{0,6},{2,4},{4,2},{6,0},{8,14},{10,12},{12,10},{14,8},{16,22},{18,... | collective-permute-start | bytes 233480 | tf_op jit(solution)/shard_map/ppermute | solution.py:23
  13.2 19.9 %collective-permute-start.1 = (bf16[16,4864]{1,0:T(8,128)(2,1)}, bf16[16,4864]{1,0:T(8,128)(2,1)}, u32[]{:S(2)}, u32[]{:S(2)}) collective-permute-start(bf16[16,4864]{1,0:T(8,128)(2,1)} %get-tuple-element.103), channel_id=1, source_target_pairs={{0,16},{2,18},{4,20},{6,22},{8,24},{10,26},{12,28},{14,30},{16,0},... | collective-permute-start | bytes 466952 | tf_op jit(solution)/shard_map/ppermute | solution.py:23
  16.3 19.3 %collective-permute-start = (bf16[16,4864]{1,0:T(8,128)(2,1)}, bf16[16,4864]{1,0:T(8,128)(2,1)}, u32[]{:S(2)}, u32[]{:S(2)}) collective-permute-start(bf16[16,4864]{1,0:T(8,128)(2,1)} %get-tuple-element.103), channel_id=1, source_target_pairs={{0,8},{2,10},{4,12},{6,14},{8,0},{10,2},{12,4},{14,6},{16,24},{18,... | collective-permute-start | bytes 466952 | tf_op jit(solution)/shard_map/ppermute | solution.py:23
  19.3 16.2 %collective-permute-start.2 = (bf16[16,4864]{1,0:T(8,128)(2,1)}, bf16[16,4864]{1,0:T(8,128)(2,1)S(1)}, u32[]{:S(2)}, u32[]{:S(2)}) collective-permute-start(bf16[16,4864]{1,0:T(8,128)(2,1)} %get-tuple-element.103), channel_id=1, source_target_pairs={{0,24},{2,26},{4,28},{6,30},{8,16},{10,18},{12,20},{14,22},{16,8},... | collective-permute-start | bytes 466952 | tf_op jit(solution)/shard_map/ppermute | solution.py:23
  19.3 34.5 %copy-start.5 = (bf16[3584,448]{0,1:T(8,128)(2,1)S(1)}, bf16[3584,448]{0,1:T(8,128)(2,1)}, u32[]{:S(2)}) copy-start(bf16[3584,448]{0,1:T(8,128)(2,1)} %param.17) | copy-start | bytes 9633796
  20.5 30.7 %collective-permute-start.10 = (bf16[4,16,2432]{2,1,0:T(8,128)(2,1)S(1)}, bf16[4,16,2432]{2,1,0:T(8,128)(2,1)S(1)}, u32[]{:S(2)}, u32[]{:S(2)}) collective-permute-start(bf16[4,16,2432]{2,1,0:T(8,128)(2,1)S(1)} %get-tuple-element.94), channel_id=1, source_target_pairs={{0,16},{2,18},{4,20},{6,22},{8,24},{10,26},{12,28},{14,30},{16,0},... | collective-permute-start | bytes 933896 | tf_op jit(solution)/shard_map/ppermute | solution.py:23
  22.5 31.2 %collective-permute-start.9 = (bf16[4,16,2432]{2,1,0:T(8,128)(2,1)S(1)}, bf16[4,16,2432]{2,1,0:T(8,128)(2,1)S(1)}, u32[]{:S(2)}, u32[]{:S(2)}) collective-permute-start(bf16[4,16,2432]{2,1,0:T(8,128)(2,1)S(1)} %get-tuple-element.94), channel_id=1, source_target_pairs={{0,8},{2,10},{4,12},{6,14},{8,0},{10,2},{12,4},{14,6},{16,24},{18,... | collective-permute-start | bytes 933896 | tf_op jit(solution)/shard_map/ppermute | solution.py:23
  33.1 20.6 %collective-permute-start.11 = (bf16[4,16,2432]{2,1,0:T(8,128)(2,1)S(1)}, bf16[4,16,2432]{2,1,0:T(8,128)(2,1)S(1)}, u32[]{:S(2)}, u32[]{:S(2)}) collective-permute-start(bf16[4,16,2432]{2,1,0:T(8,128)(2,1)S(1)} %get-tuple-element.94), channel_id=1, source_target_pairs={{0,24},{2,26},{4,28},{6,30},{8,16},{10,18},{12,20},{14,22},{16,8},... | collective-permute-start | bytes 933896 | tf_op jit(solution)/shard_map/ppermute | solution.py:23
  36.7 18.2 %collective-permute-start.4 = (bf16[4,16,4864]{2,1,0:T(8,128)(2,1)S(1)}, bf16[4,16,4864]{2,1,0:T(8,128)(2,1)S(1)}, u32[]{:S(2)}, u32[]{:S(2)}) collective-permute-start(bf16[4,16,4864]{2,1,0:T(8,128)(2,1)S(1)} %get-tuple-element.87), channel_id=1, source_target_pairs={{0,4},{2,6},{4,0},{6,2},{8,12},{10,14},{12,8},{14,10},{16,20},{18,... | collective-permute-start | bytes 1867784 | tf_op jit(solution)/shard_map/ppermute | solution.py:23
  38.3 16.6 %collective-permute-start.3 = (bf16[4,16,4864]{2,1,0:T(8,128)(2,1)S(1)}, bf16[4,16,4864]{2,1,0:T(8,128)(2,1)S(1)}, u32[]{:S(2)}, u32[]{:S(2)}) collective-permute-start(bf16[4,16,4864]{2,1,0:T(8,128)(2,1)S(1)} %get-tuple-element.87), channel_id=1, source_target_pairs={{0,2},{2,0},{4,6},{6,4},{8,10},{10,8},{12,14},{14,12},{16,18},{18,... | collective-permute-start | bytes 1867784 | tf_op jit(solution)/shard_map/ppermute | solution.py:23
  51.2 14.5 %collective-permute-start.5 = (bf16[4,16,4864]{2,1,0:T(8,128)(2,1)S(1)}, bf16[4,16,4864]{2,1,0:T(8,128)(2,1)S(1)}, u32[]{:S(2)}, u32[]{:S(2)}) collective-permute-start(bf16[4,16,4864]{2,1,0:T(8,128)(2,1)S(1)} %get-tuple-element.87), channel_id=1, source_target_pairs={{0,6},{2,4},{4,2},{6,0},{8,14},{10,12},{12,10},{14,8},{16,22},{18,... | collective-permute-start | bytes 1867784 | tf_op jit(solution)/shard_map/ppermute | solution.py:23
  71.1 1.7 collective-permute-start.12
  73.9 10.3 %collective-permute-start.21 = (bf16[304,128]{1,0:T(8,128)(2,1)S(1)}, bf16[304,128]{1,0:T(8,128)(2,1)S(1)}, u32[]{:S(2)}, u32[]{:S(2)}) collective-permute-start(bf16[304,128]{1,0:T(8,128)(2,1)S(1)} %get-tuple-element.112), channel_id=1, source_target_pairs={{0,16},{2,18},{4,20},{6,22},{8,24},{10,26},{12,28},{14,30},{16,0},... | collective-permute-start | bytes 233480 | tf_op jit(solution)/shard_map/ppermute | solution.py:23
  79.3 7.1 %collective-permute-start.20 = (bf16[304,128]{1,0:T(8,128)(2,1)S(1)}, bf16[304,128]{1,0:T(8,128)(2,1)S(1)}, u32[]{:S(2)}, u32[]{:S(2)}) collective-permute-start(bf16[304,128]{1,0:T(8,128)(2,1)S(1)} %get-tuple-element.112), channel_id=1, source_target_pairs={{0,8},{2,10},{4,12},{6,14},{8,0},{10,2},{12,4},{14,6},{16,24},{18,... | collective-permute-start | bytes 233480 | tf_op jit(solution)/shard_map/ppermute | solution.py:23
  79.3 7.1 %collective-permute-start.22 = (bf16[304,128]{1,0:T(8,128)(2,1)S(1)}, bf16[304,128]{1,0:T(8,128)(2,1)S(1)}, u32[]{:S(2)}, u32[]{:S(2)}) collective-permute-start(bf16[304,128]{1,0:T(8,128)(2,1)S(1)} %get-tuple-element.112), channel_id=1, source_target_pairs={{0,24},{2,26},{4,28},{6,30},{8,16},{10,18},{12,20},{14,22},{16,8},... | collective-permute-start | bytes 233480 | tf_op jit(solution)/shard_map/ppermute | solution.py:23
  87.1 22.5 %collective-permute-start.24 = (bf16[4,304,128]{2,1,0:T(8,128)(2,1)}, bf16[4,304,128]{2,1,0:T(8,128)(2,1)}, u32[]{:S(2)}, u32[]{:S(2)}) collective-permute-start(bf16[4,304,128]{2,1,0:T(8,128)(2,1)} %get-tuple-element.92), channel_id=1, source_target_pairs={{0,4},{2,6},{4,0},{6,2},{8,12},{10,14},{12,8},{14,10},{16,20},{18,... | collective-permute-start | bytes 933896 | tf_op jit(solution)/shard_map/ppermute | solution.py:23
  88.6 22.5 %collective-permute-start.23 = (bf16[4,304,128]{2,1,0:T(8,128)(2,1)}, bf16[4,304,128]{2,1,0:T(8,128)(2,1)}, u32[]{:S(2)}, u32[]{:S(2)}) collective-permute-start(bf16[4,304,128]{2,1,0:T(8,128)(2,1)} %get-tuple-element.92), channel_id=1, source_target_pairs={{0,2},{2,0},{4,6},{6,4},{8,10},{10,8},{12,14},{14,12},{16,18},{18,... | collective-permute-start | bytes 933896 | tf_op jit(solution)/shard_map/ppermute | solution.py:23
  90.1 21.1 %collective-permute-start.25 = (bf16[4,304,128]{2,1,0:T(8,128)(2,1)}, bf16[4,304,128]{2,1,0:T(8,128)(2,1)}, u32[]{:S(2)}, u32[]{:S(2)}) collective-permute-start(bf16[4,304,128]{2,1,0:T(8,128)(2,1)} %get-tuple-element.92), channel_id=1, source_target_pairs={{0,6},{2,4},{4,2},{6,0},{8,14},{10,12},{12,10},{14,8},{16,22},{18,... | collective-permute-start | bytes 933896 | tf_op jit(solution)/shard_map/ppermute | solution.py:23
  91.2 7.3 %collective-permute-start.14 = (bf16[160,128]{1,0:T(8,128)(2,1)}, bf16[160,128]{1,0:T(8,128)(2,1)}, u32[]{:S(2)}, u32[]{:S(2)}) collective-permute-start(bf16[160,128]{1,0:T(8,128)(2,1)} %get-tuple-element.116), channel_id=1, source_target_pairs={{0,4},{2,6},{4,0},{6,2},{8,12},{10,14},{12,8},{14,10},{16,20},{18,... | collective-permute-start | bytes 122888 | tf_op jit(solution)/shard_map/ppermute | solution.py:23
  92.8 12.7 %collective-permute-start.13 = (bf16[160,128]{1,0:T(8,128)(2,1)}, bf16[160,128]{1,0:T(8,128)(2,1)}, u32[]{:S(2)}, u32[]{:S(2)}) collective-permute-start(bf16[160,128]{1,0:T(8,128)(2,1)} %get-tuple-element.116), channel_id=1, source_target_pairs={{0,2},{2,0},{4,6},{6,4},{8,10},{10,8},{12,14},{14,12},{16,18},{18,... | collective-permute-start | bytes 122888 | tf_op jit(solution)/shard_map/ppermute | solution.py:23
  98.6 7.3 %collective-permute-start.15 = (bf16[160,128]{1,0:T(8,128)(2,1)}, bf16[160,128]{1,0:T(8,128)(2,1)}, u32[]{:S(2)}, u32[]{:S(2)}) collective-permute-start(bf16[160,128]{1,0:T(8,128)(2,1)} %get-tuple-element.116), channel_id=1, source_target_pairs={{0,6},{2,4},{4,2},{6,0},{8,14},{10,12},{12,10},{14,8},{16,22},{18,... | collective-permute-start | bytes 122888 | tf_op jit(solution)/shard_map/ppermute | solution.py:23
  106.7 11.7 %collective-permute-start.17 = (bf16[4,160,128]{2,1,0:T(8,128)(2,1)S(1)}, bf16[4,160,128]{2,1,0:T(8,128)(2,1)S(1)}, u32[]{:S(2)}, u32[]{:S(2)}) collective-permute-start(bf16[4,160,128]{2,1,0:T(8,128)(2,1)S(1)} %get-tuple-element.101), channel_id=1, source_target_pairs={{0,16},{2,18},{4,20},{6,22},{8,24},{10,26},{12,28},{14,30},{16,0},... | collective-permute-start | bytes 491528 | tf_op jit(solution)/shard_map/ppermute | solution.py:23
  109.0 9.4 %collective-permute-start.16 = (bf16[4,160,128]{2,1,0:T(8,128)(2,1)S(1)}, bf16[4,160,128]{2,1,0:T(8,128)(2,1)S(1)}, u32[]{:S(2)}, u32[]{:S(2)}) collective-permute-start(bf16[4,160,128]{2,1,0:T(8,128)(2,1)S(1)} %get-tuple-element.101), channel_id=1, source_target_pairs={{0,8},{2,10},{4,12},{6,14},{8,0},{10,2},{12,4},{14,6},{16,24},{18,... | collective-permute-start | bytes 491528 | tf_op jit(solution)/shard_map/ppermute | solution.py:23
  109.6 10.6 %collective-permute-start.18 = (bf16[4,160,128]{2,1,0:T(8,128)(2,1)S(1)}, bf16[4,160,128]{2,1,0:T(8,128)(2,1)S(1)}, u32[]{:S(2)}, u32[]{:S(2)}) collective-permute-start(bf16[4,160,128]{2,1,0:T(8,128)(2,1)S(1)} %get-tuple-element.101), channel_id=1, source_target_pairs={{0,24},{2,26},{4,28},{6,30},{8,16},{10,18},{12,20},{14,22},{16,8},... | collective-permute-start | bytes 491528 | tf_op jit(solution)/shard_map/ppermute | solution.py:23
  112.5 10.0 %collective-permute-start.26 = (bf16[16,304,128]{2,1,0:T(8,128)(2,1)S(1)}, bf16[16,304,128]{2,1,0:T(8,128)(2,1)S(1)}, u32[]{:S(2)}, u32[]{:S(2)}) collective-permute-start(bf16[16,304,128]{2,1,0:T(8,128)(2,1)S(1)} %bitcast.236), channel_id=1, source_target_pairs={{0,1},{1,0},{2,3},{3,2},{4,5},{5,4},{6,7},{7,6},{8,9},{9,8},{10,11... | collective-permute-start | bytes 3735560 | tf_op jit(solution)/shard_map/ppermute | solution.py:23
  120.3 2.2 collective-permute-start.19
  140.3 4.5 %collective-permute-start.29 = (f32[4,256]{1,0:T(4,128)S(1)}, f32[4,256]{1,0:T(4,128)S(1)}, u32[]{:S(2)}, u32[]{:S(2)}) collective-permute-start(f32[4,256]{1,0:T(4,128)S(1)} %slice.343), channel_id=1, source_target_pairs={{0,6},{2,4},{4,2},{6,0},{8,14},{10,12},{12,10},{14,8},{16,22},{18,... | collective-permute-start | bytes 12296 | tf_op jit(solution)/shard_map/ppermute | solution.py:23
  142.8 3.6 %collective-permute-start.28 = (f32[4,256]{1,0:T(4,128)S(1)}, f32[4,256]{1,0:T(4,128)S(1)}, u32[]{:S(2)}, u32[]{:S(2)}) collective-permute-start(f32[4,256]{1,0:T(4,128)S(1)} %slice.343), channel_id=1, source_target_pairs={{0,4},{2,6},{4,0},{6,2},{8,12},{10,14},{12,8},{14,10},{16,20},{18,... | collective-permute-start | bytes 12296 | tf_op jit(solution)/shard_map/ppermute | solution.py:23
  143.3 3.6 %collective-permute-start.27 = (f32[4,256]{1,0:T(4,128)S(1)}, f32[4,256]{1,0:T(4,128)S(1)}, u32[]{:S(2)}, u32[]{:S(2)}) collective-permute-start(f32[4,256]{1,0:T(4,128)S(1)} %slice.343), channel_id=1, source_target_pairs={{0,2},{2,0},{4,6},{6,4},{8,10},{10,8},{12,14},{14,12},{16,18},{18,... | collective-permute-start | bytes 12296 | tf_op jit(solution)/shard_map/ppermute | solution.py:23
  147.0 5.5 %collective-permute-start.32 = (f32[4,256]{1,0:T(4,128)S(1)}, f32[4,256]{1,0:T(4,128)S(1)}, u32[]{:S(2)}, u32[]{:S(2)}) collective-permute-start(f32[4,256]{1,0:T(4,128)S(1)} %fusion.75), channel_id=1, source_target_pairs={{0,24},{2,26},{4,28},{6,30},{8,16},{10,18},{12,20},{14,22},{16,8},... | collective-permute-start | bytes 12296 | tf_op jit(solution)/shard_map/ppermute | solution.py:23
  149.7 4.5 %collective-permute-start.31 = (f32[4,256]{1,0:T(4,128)S(1)}, f32[4,256]{1,0:T(4,128)S(1)}, u32[]{:S(2)}, u32[]{:S(2)}) collective-permute-start(f32[4,256]{1,0:T(4,128)S(1)} %fusion.75), channel_id=1, source_target_pairs={{0,16},{2,18},{4,20},{6,22},{8,24},{10,26},{12,28},{14,30},{16,0},... | collective-permute-start | bytes 12296 | tf_op jit(solution)/shard_map/ppermute | solution.py:23
  151.6 3.6 %collective-permute-start.30 = (f32[4,256]{1,0:T(4,128)S(1)}, f32[4,256]{1,0:T(4,128)S(1)}, u32[]{:S(2)}, u32[]{:S(2)}) collective-permute-start(f32[4,256]{1,0:T(4,128)S(1)} %fusion.75), channel_id=1, source_target_pairs={{0,8},{2,10},{4,12},{6,14},{8,0},{10,2},{12,4},{14,6},{16,24},{18,... | collective-permute-start | bytes 12296 | tf_op jit(solution)/shard_map/ppermute | solution.py:23
  155.3 1.2 collective-permute-start.33
  175.1 3.9 %collective-permute-start.34 = (bf16[8,2,448,128]{3,2,1,0:T(8,128)(2,1)S(1)}, bf16[8,2,448,128]{3,2,1,0:T(8,128)(2,1)S(1)}, u32[]{:S(2)}, u32[]{:S(2)}) collective-permute-start(bf16[8,2,448,128]{3,2,1,0:T(8,128)(2,1)S(1)} %get-tuple-element.32), channel_id=1, source_target_pairs={{0,1},{1,0},{2,3},{3,2},{4,5},{5,4},{6,7},{7,6},{8,9},{9,8},{10,11... | collective-permute-start | bytes 5505032 | tf_op jit(solution)/shard_map/ppermute | solution.py:23
  180.1 6.7 %collective-permute-start.41 = (bf16[4,144,128]{2,1,0:T(8,128)(2,1)S(1)}, bf16[4,144,128]{2,1,0:T(8,128)(2,1)S(1)}, u32[]{:S(2)}, u32[]{:S(2)}) collective-permute-start(bf16[4,144,128]{2,1,0:T(8,128)(2,1)S(1)} %get-tuple-element.74), channel_id=1, source_target_pairs={{0,8},{2,10},{4,12},{6,14},{8,0},{10,2},{12,4},{14,6},{16,24},{18,... | collective-permute-start | bytes 442376 | tf_op jit(solution)/shard_map/ppermute | solution.py:23
  180.5 10.0 %collective-permute-start.43 = (bf16[4,144,128]{2,1,0:T(8,128)(2,1)S(1)}, bf16[4,144,128]{2,1,0:T(8,128)(2,1)S(1)}, u32[]{:S(2)}, u32[]{:S(2)}) collective-permute-start(bf16[4,144,128]{2,1,0:T(8,128)(2,1)S(1)} %get-tuple-element.75), channel_id=1, source_target_pairs={{0,24},{2,26},{4,28},{6,30},{8,16},{10,18},{12,20},{14,22},{16,8},... | collective-permute-start | bytes 442376 | tf_op jit(solution)/shard_map/ppermute | solution.py:23
  182.6 14.1 %collective-permute-start.42 = (bf16[4,144,128]{2,1,0:T(8,128)(2,1)S(1)}, bf16[4,144,128]{2,1,0:T(8,128)(2,1)S(1)}, u32[]{:S(2)}, u32[]{:S(2)}) collective-permute-start(bf16[4,144,128]{2,1,0:T(8,128)(2,1)S(1)} %get-tuple-element.76), channel_id=1, source_target_pairs={{0,16},{2,18},{4,20},{6,22},{8,24},{10,26},{12,28},{14,30},{16,0},... | collective-permute-start | bytes 442376 | tf_op jit(solution)/shard_map/ppermute | solution.py:23
  183.7 16.2 %collective-permute-start.35 = (bf16[4,304,128]{2,1,0:T(8,128)(2,1)S(1)}, bf16[4,304,128]{2,1,0:T(8,128)(2,1)S(1)}, u32[]{:S(2)}, u32[]{:S(2)}) collective-permute-start(bf16[4,304,128]{2,1,0:T(8,128)(2,1)S(1)} %get-tuple-element.77), channel_id=1, source_target_pairs={{0,2},{2,0},{4,6},{6,4},{8,10},{10,8},{12,14},{14,12},{16,18},{18,... | collective-permute-start | bytes 933896 | tf_op jit(solution)/shard_map/ppermute | solution.py:23
  184.3 16.2 %collective-permute-start.37 = (bf16[4,304,128]{2,1,0:T(8,128)(2,1)S(1)}, bf16[4,304,128]{2,1,0:T(8,128)(2,1)S(1)}, u32[]{:S(2)}, u32[]{:S(2)}) collective-permute-start(bf16[4,304,128]{2,1,0:T(8,128)(2,1)S(1)} %get-tuple-element.78), channel_id=1, source_target_pairs={{0,6},{2,4},{4,2},{6,0},{8,14},{10,12},{12,10},{14,8},{16,22},{18,... | collective-permute-start | bytes 933896 | tf_op jit(solution)/shard_map/ppermute | solution.py:23
  186.7 25.3 %copy-start.20 = (bf16[448,128]{1,0:T(8,128)(2,1)S(1)}, bf16[448,128]{1,0:T(8,128)(2,1)}, u32[]{:S(2)}) copy-start(bf16[448,128]{1,0:T(8,128)(2,1)} %copy-done.19) | copy-start | bytes 344068
  186.7 15.9 %collective-permute-start.36 = (bf16[4,304,128]{2,1,0:T(8,128)(2,1)S(1)}, bf16[4,304,128]{2,1,0:T(8,128)(2,1)S(1)}, u32[]{:S(2)}, u32[]{:S(2)}) collective-permute-start(bf16[4,304,128]{2,1,0:T(8,128)(2,1)S(1)} %get-tuple-element.79), channel_id=1, source_target_pairs={{0,4},{2,6},{4,0},{6,2},{8,12},{10,14},{12,8},{14,10},{16,20},{18,... | collective-permute-start | bytes 933896 | tf_op jit(solution)/shard_map/ppermute | solution.py:23
  196.8 9.4 %collective-permute-start.44 = (bf16[144,128]{1,0:T(8,128)(2,1)S(1)}, bf16[144,128]{1,0:T(8,128)(2,1)S(1)}, u32[]{:S(2)}, u32[]{:S(2)}) collective-permute-start(bf16[144,128]{1,0:T(8,128)(2,1)S(1)} %get-tuple-element.104), channel_id=1, source_target_pairs={{0,2},{2,0},{4,6},{6,4},{8,10},{10,8},{12,14},{14,12},{16,18},{18,... | collective-permute-start | bytes 110600 | tf_op jit(solution)/shard_map/ppermute | solution.py:23
  197.4 9.0 %collective-permute-start.46 = (bf16[144,128]{1,0:T(8,128)(2,1)S(1)}, bf16[144,128]{1,0:T(8,128)(2,1)S(1)}, u32[]{:S(2)}, u32[]{:S(2)}) collective-permute-start(bf16[144,128]{1,0:T(8,128)(2,1)S(1)} %get-tuple-element.105), channel_id=1, source_target_pairs={{0,6},{2,4},{4,2},{6,0},{8,14},{10,12},{12,10},{14,8},{16,22},{18,... | collective-permute-start | bytes 110600 | tf_op jit(solution)/shard_map/ppermute | solution.py:23
  199.9 6.5 %collective-permute-start.45 = (bf16[144,128]{1,0:T(8,128)(2,1)S(1)}, bf16[144,128]{1,0:T(8,128)(2,1)S(1)}, u32[]{:S(2)}, u32[]{:S(2)}) collective-permute-start(bf16[144,128]{1,0:T(8,128)(2,1)S(1)} %get-tuple-element.106), channel_id=1, source_target_pairs={{0,4},{2,6},{4,0},{6,2},{8,12},{10,14},{12,8},{14,10},{16,20},{18,... | collective-permute-start | bytes 110600 | tf_op jit(solution)/shard_map/ppermute | solution.py:23
  202.8 4.6 %collective-permute-start.38 = (bf16[304,128]{1,0:T(8,128)(2,1)S(1)}, bf16[304,128]{1,0:T(8,128)(2,1)S(1)}, u32[]{:S(2)}, u32[]{:S(2)}) collective-permute-start(bf16[304,128]{1,0:T(8,128)(2,1)S(1)} %get-tuple-element.88), channel_id=1, source_target_pairs={{0,8},{2,10},{4,12},{6,14},{8,0},{10,2},{12,4},{14,6},{16,24},{18,... | collective-permute-start | bytes 233480 | tf_op jit(solution)/shard_map/ppermute | solution.py:23
  204.2 6.2 %collective-permute-start.40 = (bf16[304,128]{1,0:T(8,128)(2,1)S(1)}, bf16[304,128]{1,0:T(8,128)(2,1)S(1)}, u32[]{:S(2)}, u32[]{:S(2)}) collective-permute-start(bf16[304,128]{1,0:T(8,128)(2,1)S(1)} %get-tuple-element.89), channel_id=1, source_target_pairs={{0,24},{2,26},{4,28},{6,30},{8,16},{10,18},{12,20},{14,22},{16,8},... | collective-permute-start | bytes 233480 | tf_op jit(solution)/shard_map/ppermute | solution.py:23
  206.2 5.8 %collective-permute-start.39 = (bf16[304,128]{1,0:T(8,128)(2,1)S(1)}, bf16[304,128]{1,0:T(8,128)(2,1)S(1)}, u32[]{:S(2)}, u32[]{:S(2)}) collective-permute-start(bf16[304,128]{1,0:T(8,128)(2,1)S(1)} %get-tuple-element.90), channel_id=1, source_target_pairs={{0,16},{2,18},{4,20},{6,22},{8,24},{10,26},{12,28},{14,30},{16,0},... | collective-permute-start | bytes 233480 | tf_op jit(solution)/shard_map/ppermute | solution.py:23
  212.2 2.5 collective-permute-start.47
  223.6 25.9 %collective-permute-start.51 = (bf16[4,16,2304]{2,1,0:T(8,128)(2,1)}, bf16[4,16,2304]{2,1,0:T(8,128)(2,1)}, u32[]{:S(2)}, u32[]{:S(2)}) collective-permute-start(bf16[4,16,2304]{2,1,0:T(8,128)(2,1)} %get-tuple-element.41), channel_id=1, source_target_pairs={{0,8},{2,10},{4,12},{6,14},{8,0},{10,2},{12,4},{14,6},{16,24},{18,... | collective-permute-start | bytes 884744 | tf_op jit(solution)/shard_map/ppermute | solution.py:23
  223.6 30.3 %collective-permute-start.52 = (bf16[4,16,2304]{2,1,0:T(8,128)(2,1)}, bf16[4,16,2304]{2,1,0:T(8,128)(2,1)}, u32[]{:S(2)}, u32[]{:S(2)}) collective-permute-start(bf16[4,16,2304]{2,1,0:T(8,128)(2,1)} %get-tuple-element.42), channel_id=1, source_target_pairs={{0,16},{2,18},{4,20},{6,22},{8,24},{10,26},{12,28},{14,30},{16,0},... | collective-permute-start | bytes 884744 | tf_op jit(solution)/shard_map/ppermute | solution.py:23
  226.2 33.0 %collective-permute-start.48 = (bf16[4,16,4864]{2,1,0:T(8,128)(2,1)}, bf16[4,16,4864]{2,1,0:T(8,128)(2,1)}, u32[]{:S(2)}, u32[]{:S(2)}) collective-permute-start(bf16[4,16,4864]{2,1,0:T(8,128)(2,1)} %bitcast.87), channel_id=1, source_target_pairs={{0,2},{2,0},{4,6},{6,4},{8,10},{10,8},{12,14},{14,12},{16,18},{18,... | collective-permute-start | bytes 1867784 | tf_op jit(solution)/shard_map/ppermute | solution.py:23
  226.8 32.4 %collective-permute-start.49 = (bf16[4,16,4864]{2,1,0:T(8,128)(2,1)}, bf16[4,16,4864]{2,1,0:T(8,128)(2,1)}, u32[]{:S(2)}, u32[]{:S(2)}) collective-permute-start(bf16[4,16,4864]{2,1,0:T(8,128)(2,1)} %bitcast.88), channel_id=1, source_target_pairs={{0,4},{2,6},{4,0},{6,2},{8,12},{10,14},{12,8},{14,10},{16,20},{18,... | collective-permute-start | bytes 1867784 | tf_op jit(solution)/shard_map/ppermute | solution.py:23
  227.3 31.9 %collective-permute-start.50 = (bf16[4,16,4864]{2,1,0:T(8,128)(2,1)}, bf16[4,16,4864]{2,1,0:T(8,128)(2,1)}, u32[]{:S(2)}, u32[]{:S(2)}) collective-permute-start(bf16[4,16,4864]{2,1,0:T(8,128)(2,1)} %bitcast.89), channel_id=1, source_target_pairs={{0,6},{2,4},{4,2},{6,0},{8,14},{10,12},{12,10},{14,8},{16,22},{18,... | collective-permute-start | bytes 1867784 | tf_op jit(solution)/shard_map/ppermute | solution.py:23
  249.4 9.8 %collective-permute-start.53 = (bf16[4,16,2304]{2,1,0:T(8,128)(2,1)S(1)}, bf16[4,16,2304]{2,1,0:T(8,128)(2,1)S(1)}, u32[]{:S(2)}, u32[]{:S(2)}) collective-permute-start(bf16[4,16,2304]{2,1,0:T(8,128)(2,1)S(1)} %copy-done.22), channel_id=1, source_target_pairs={{0,24},{2,26},{4,28},{6,30},{8,16},{10,18},{12,20},{14,22},{16,8},... | collective-permute-start | bytes 884744 | tf_op jit(solution)/shard_map/ppermute | solution.py:23
  260.6 11.9 %collective-permute-start.57 = (bf16[16,2304]{1,0:T(8,128)(2,1)S(1)}, bf16[16,2304]{1,0:T(8,128)(2,1)S(1)}, u32[]{:S(2)}, u32[]{:S(2)}) collective-permute-start(bf16[16,2304]{1,0:T(8,128)(2,1)S(1)} %get-tuple-element.95), channel_id=1, source_target_pairs={{0,2},{2,0},{4,6},{6,4},{8,10},{10,8},{12,14},{14,12},{16,18},{18,... | collective-permute-start | bytes 221192 | tf_op jit(solution)/shard_map/ppermute | solution.py:23
  261.2 11.3 %collective-permute-start.59 = (bf16[16,2304]{1,0:T(8,128)(2,1)S(1)}, bf16[16,2304]{1,0:T(8,128)(2,1)S(1)}, u32[]{:S(2)}, u32[]{:S(2)}) collective-permute-start(bf16[16,2304]{1,0:T(8,128)(2,1)S(1)} %get-tuple-element.96), channel_id=1, source_target_pairs={{0,6},{2,4},{4,2},{6,0},{8,14},{10,12},{12,10},{14,8},{16,22},{18,... | collective-permute-start | bytes 221192 | tf_op jit(solution)/shard_map/ppermute | solution.py:23
  262.7 9.9 %collective-permute-start.58 = (bf16[16,2304]{1,0:T(8,128)(2,1)S(1)}, bf16[16,2304]{1,0:T(8,128)(2,1)S(1)}, u32[]{:S(2)}, u32[]{:S(2)}) collective-permute-start(bf16[16,2304]{1,0:T(8,128)(2,1)S(1)} %get-tuple-element.97), channel_id=1, source_target_pairs={{0,4},{2,6},{4,0},{6,2},{8,12},{10,14},{12,8},{14,10},{16,20},{18,... | collective-permute-start | bytes 221192 | tf_op jit(solution)/shard_map/ppermute | solution.py:23
  266.0 18.4 %copy-start.16 = (bf16[16,3584]{1,0:T(8,128)(2,1)S(1)}, bf16[16,3584]{1,0:T(8,128)(2,1)}, u32[]{:S(2)}) copy-start(bf16[16,3584]{1,0:T(8,128)(2,1)} %param.12) | copy-start | bytes 344068
  266.0 10.2 %collective-permute-start.54 = (bf16[16,4864]{1,0:T(8,128)(2,1)S(1)}, bf16[16,4864]{1,0:T(8,128)(2,1)S(1)}, u32[]{:S(2)}, u32[]{:S(2)}) collective-permute-start(bf16[16,4864]{1,0:T(8,128)(2,1)S(1)} %get-tuple-element.83), channel_id=1, source_target_pairs={{0,8},{2,10},{4,12},{6,14},{8,0},{10,2},{12,4},{14,6},{16,24},{18,... | collective-permute-start | bytes 466952 | tf_op jit(solution)/shard_map/ppermute | solution.py:23
  270.8 8.3 %collective-permute-start.56 = (bf16[16,4864]{1,0:T(8,128)(2,1)S(1)}, bf16[16,4864]{1,0:T(8,128)(2,1)S(1)}, u32[]{:S(2)}, u32[]{:S(2)}) collective-permute-start(bf16[16,4864]{1,0:T(8,128)(2,1)S(1)} %get-tuple-element.84), channel_id=1, source_target_pairs={{0,24},{2,26},{4,28},{6,30},{8,16},{10,18},{12,20},{14,22},{16,8},... | collective-permute-start | bytes 466952 | tf_op jit(solution)/shard_map/ppermute | solution.py:23
  272.6 11.6 %collective-permute-start.55 = (bf16[16,4864]{1,0:T(8,128)(2,1)S(1)}, bf16[16,4864]{1,0:T(8,128)(2,1)S(1)}, u32[]{:S(2)}, u32[]{:S(2)}) collective-permute-start(bf16[16,4864]{1,0:T(8,128)(2,1)S(1)} %get-tuple-element.85), channel_id=1, source_target_pairs={{0,16},{2,18},{4,20},{6,22},{8,24},{10,26},{12,28},{14,30},{16,0},... | collective-permute-start | bytes 466952 | tf_op jit(solution)/shard_map/ppermute | solution.py:23
  (27 other events, 173.7 us)

commit v2 on v1

v2 whole, which is shorter than its diff:
```python
import jax
import jax.numpy as jnp
from jax import lax
from jax.experimental import pallas as pl
from jax.experimental.pallas import tpu as pltpu
from jax.sharding import PartitionSpec as P

D = 7168


loss_scale = 4096.0
epsilon = 1e-06

f32 = jnp.float32
bf16 = jnp.bfloat16
i32 = jnp.int32


def from_partner(array, axis, mask):
    size = lax.axis_size(axis)
    return lax.ppermute(array, axis, [(i, i ^ mask) for i in range(size)])


def bits_of(axis):
    return lax.axis_size(axis).bit_length() - 1


def gather(array, order):
    count, shape = len(order), array.shape
    for bit in order:
        array = jnp.stack([array, from_partner(array, "seq", 1 << bit)])
    dims = [count - 1 - order.index(bit) for bit in reversed(range(count))]
    array = array.transpose(dims + list(range(count, array.ndim)))
    return array.reshape((1 << count,) + shape)


def scatter(arrays, orders, beside=()):
    count = bits_of("seq")
    arrays = [array.reshape((2,) * count + array.shape[1:]) for array in arrays]
    left = [list(reversed(range(count))) for _ in arrays]
    results = []
    for step in range(count):
        for k, order in enumerate(orders):
            bit = order[step]
            dim = left[k].index(bit)
            left[k].remove(bit)
            sent = lax.index_in_dim(arrays[k], 1, dim, keepdims=False).astype(bf16)
            tied = k == 0 and step < len(beside)
            if tied:
                work, argument = beside[step]
                sent, argument = lax.optimization_barrier((sent, argument))
            came = from_partner(sent, "seq", 1 << bit)
            if tied:
                result, mark = work(argument, results)
                came, mark = lax.optimization_barrier((came, mark))
                results.append(result)
            kept = lax.index_in_dim(arrays[k], 0, dim, keepdims=False).astype(f32)
            arrays[k] = kept + came.astype(f32)
    return arrays, results


def orders_of():
    down = list(reversed(range(bits_of("seq"))))
    return [down, down[:-2] + [0, 1], [0, 1] + down[:-2]]


def cut_in_three(size, unit):
    third = round(0.25 * size / unit) * unit
    first = (size - third + unit) // (2 * unit) * unit
    return first, size - third


def tp_masks():
    return range(1, lax.axis_size("tp"))


def over_cores(array):
    return jnp.concatenate([array] + [from_partner(array, "tp", mask) for mask in tp_masks()], axis=-1)


def lanes_by_index(array):
    count = lax.axis_size("tp")
    pieces = jnp.split(array, count, axis=-1)
    me = lax.axis_index("tp")
    step = 1
    while step < count:
        flipped = [pieces[i ^ step] for i in range(count)]
        pieces = [jnp.where(me & step == 0, a, b) for a, b in zip(pieces, flipped)]
        step *= 2
    return jnp.concatenate(pieces, axis=-1)


def merged(group):
    tops, totals, weighted, targets = (jnp.stack([one[i] for one in group]) for i in range(4))
    top = jnp.max(tops, axis=0)
    shares = jnp.exp(tops - top)
    return jnp.stack(
        [
            top,
            jnp.sum(shares * totals, axis=0),
            jnp.sum(shares * weighted, axis=0),
            jnp.sum(targets, axis=0),
        ]
    )


def in_parts(values):
    high = lax.reduce_precision(values, 8, 7)
    middle = lax.reduce_precision(values - high, 8, 7)
    return high, middle, values - high - middle


def dot(left, right, on_left, on_right, precision=None):
    return lax.dot_general(
        left,
        right,
        (((on_left,), (on_right,)), ((), ())),
        precision=precision,
        preferred_element_type=f32,
    )


def logits_kernel(where, ids, scale, gain, *refs):
    *pieces, head, out, stats, all_features = refs
    step = pl.program_id(0)
    tile = head.shape[0]
    blocks, _, lanes = pieces[0].shape
    features = all_features.shape[0] // blocks

    @pl.when(step == 0)
    def _():
        for device in range(blocks):
            for side in range(2):
                start = device * features
                columns = slice(side * lanes, (side + 1) * lanes)
                for piece in pieces[3 * side : 3 * side + 3]:
                    rows = min(piece.shape[1], (device + 1) * features - start)
                    all_features[start : start + rows, columns] = piece[where[0] ^ device][:rows]
                    start += rows
        columns_of_gain = gain[...].T
        for k in range(gain.shape[0]):
            part = slice(128 * k, 128 * (k + 1))
            values = all_features[part, :].astype(f32) * scale[...] * columns_of_gain[:, k : k + 1]
            all_features[part, :] = values.astype(bf16)
        stats[...] = jnp.zeros_like(stats)
        stats[0:1, :] = jnp.full((1, stats.shape[1]), -jnp.inf, f32)

    logits = jnp.dot(head[...], all_features[...], preferred_element_type=f32)
    out[...] = logits
    entries = lax.broadcasted_iota(i32, logits.shape, 0) + (where[1] + step * tile)
    before = stats[0:1, :]
    top = jnp.maximum(before, jnp.max(logits, axis=0, keepdims=True))
    shrink = jnp.exp(before - top)
    expd = jnp.exp(logits - top)
    stats[0:1, :] = top
    stats[1:2, :] = stats[1:2, :] * shrink + jnp.sum(expd, axis=0, keepdims=True)
    stats[2:3, :] = stats[2:3, :] * shrink + jnp.sum(expd * logits, axis=0, keepdims=True)
    stats[3:4, :] = stats[3:4, :] + jnp.sum(
        jnp.where(entries == ids[...], logits, 0.0), axis=0, keepdims=True
    )


def head_logits(where, ids, scale, gain, pieces, head):
    vocab, tokens = head.shape[0], ids.shape[1]
    tile = 512
    gain = gain.reshape(-1, 128)
    whole = lambda array: pl.BlockSpec(array.shape, lambda i, w: (0,) * array.ndim)
    return pl.pallas_call(
        logits_kernel,
        grid_spec=pltpu.PrefetchScalarGridSpec(
            num_scalar_prefetch=1,
            grid=(vocab // tile,),
            in_specs=[
                whole(ids),
                whole(scale),
                whole(gain),
                *[whole(piece) for piece in pieces],
                pl.BlockSpec((tile, D), lambda i, w: (i, 0)),
            ],
            out_specs=[
                pl.BlockSpec((tile, tokens), lambda i, w: (i, 0)),
                pl.BlockSpec((8, tokens), lambda i, w: (0, 0)),
                pl.BlockSpec((D, tokens), lambda i, w: (0, 0)),
            ],
        ),
        out_shape=[
            jax.ShapeDtypeStruct((vocab, tokens), f32),
            jax.ShapeDtypeStruct((8, tokens), f32),
            jax.ShapeDtypeStruct((D, tokens), bf16),
        ],
        compiler_params=pltpu.CompilerParams(vmem_limit_bytes=44 << 20),
        cost_estimate=pl.CostEstimate(
            flops=2 * vocab * D * tokens,
            bytes_accessed=2 * vocab * D + 4 * D * tokens,
            transcendentals=vocab * tokens,
        ),
    )(where, ids, scale, gain, *pieces, head)


def dfinal_kernel(where, ids, rows, logits, head, kept, sent, plain, turned):
    step = pl.program_id(0)
    vocab, tokens = logits.shape
    lanes = kept.shape[3]

    @pl.when(step == 0)
    def _():
        top, share, coef = (rows[i : i + 1, :] for i in range(3))
        tile = 256
        for start in range(0, vocab, tile):
            probs = jnp.exp(logits[start : start + tile, :] - top) * share
            entries = lax.broadcasted_iota(i32, probs.shape, 0) + (where[1] + start)
            dlogits = coef * (probs - (entries == ids[...]).astype(f32))
            plain[start : start + tile, :] = dlogits.astype(bf16)
            turned[:, start : start + tile] = dlogits.T.astype(bf16)

    product = jnp.dot(turned[...], head[...], preferred_element_type=f32).T
    half = product.shape[0] // 2
    flip = where[0] & 1
    for piece in range(2):
        block = product[piece * half : (piece + 1) * half]
        kept[0, piece ^ flip] = block[:, :lanes]
        sent[0, piece ^ flip] = block[:, lanes:].astype(bf16)


def head_back(where, ids, rows, logits, head, blocks):
    vocab, tokens = logits.shape
    features = D // blocks
    lanes = tokens // 2
    pairs = blocks // 2
    whole = lambda array: pl.BlockSpec(array.shape, lambda i, w: (0,) * array.ndim)
    place = lambda i, w: (i ^ (w[0] >> 1), 0, 0, 0)
    return pl.pallas_call(
        dfinal_kernel,
        grid_spec=pltpu.PrefetchScalarGridSpec(
            num_scalar_prefetch=1,
            grid=(pairs,),
            in_specs=[
                whole(ids),
                whole(rows),
                whole(logits),
                pl.BlockSpec((vocab, 2 * features), lambda i, w: (0, i)),
            ],
            out_specs=[
                pl.BlockSpec((1, 2, features, lanes), place),
                pl.BlockSpec((1, 2, features, lanes), place),
                pl.BlockSpec((vocab, tokens), lambda i, w: (0, 0)),
            ],
            scratch_shapes=[pltpu.VMEM((tokens, vocab), bf16)],
        ),
        out_shape=[
            jax.ShapeDtypeStruct((pairs, 2, features, lanes), f32),
            jax.ShapeDtypeStruct((pairs, 2, features, lanes), bf16),
            jax.ShapeDtypeStruct((vocab, tokens), bf16),
        ],
        compiler_params=pltpu.CompilerParams(vmem_limit_bytes=32 << 20),
        cost_estimate=pl.CostEstimate(
            flops=2 * vocab * D * tokens,
            bytes_accessed=2 * vocab * D + 4 * D * tokens,
            transcendentals=vocab * tokens,
        ),
    )(where, ids, rows, logits, head)


def grad_head_kernel(left, features, *refs):
    out, mark = refs[-2:]
    out[...] = lax.dot_general(
        left[...], features[...], (((1,), (1,)), ((), ())), preferred_element_type=f32
    ).astype(bf16)
    mark[...] = jnp.zeros_like(mark)


def grad_head_rows(left, features, index, count, before):
    vocab, tokens = left.shape
    rows, tile = vocab // count, 1024
    given = () if before is None else (before,)
    return pl.pallas_call(
        grad_head_kernel,
        grid=(D // tile,),
        in_specs=[
            pl.BlockSpec((rows, tokens), lambda i: (index, 0)),
            pl.BlockSpec((tile, tokens), lambda i: (i, 0)),
            *[pl.BlockSpec(memory_space=pl.ANY) for _ in given],
        ],
        out_specs=[
            pl.BlockSpec((rows, tile), lambda i: (index, i)),
            pl.BlockSpec((8, 128), lambda i: (0, 0)),
        ],
        out_shape=[
            jax.ShapeDtypeStruct((vocab, D), bf16),
            jax.ShapeDtypeStruct((8, 128), f32),
        ],
        input_output_aliases={2: 0} if given else {},
        compiler_params=pltpu.CompilerParams(vmem_limit_bytes=20 << 20),
        cost_estimate=pl.CostEstimate(
            flops=2 * rows * D * tokens, bytes_accessed=2 * rows * D + 2 * D * tokens, transcendentals=0
        ),
    )(left, features, *given)


def plain_logits(where, ids, scale, gain, pieces, head):
    blocks, _, lanes = pieces[0].shape
    features = D // blocks
    sides = []
    for i in range(0, len(pieces), 3):
        side = jnp.concatenate(pieces[i : i + 3], axis=1)[:, :features]
        sides.append(side[where[0] ^ jnp.arange(blocks)].reshape(D, lanes))
    all_features = jnp.concatenate(sides, axis=1).astype(f32)
    all_features = (all_features * scale * gain[:, None]).astype(bf16)
    logits = dot(head, all_features, 1, 0)
    top = jnp.max(logits, axis=0)
    expd = jnp.exp(logits - top)
    onehot = (jnp.arange(head.shape[0])[:, None] + where[1]) == ids
    stats = [
        top,
        jnp.sum(expd, axis=0),
        jnp.sum(expd * logits, axis=0),
        jnp.sum(jnp.where(onehot, logits, 0.0), axis=0),
    ]
    return logits, jnp.stack(stats), all_features


def plain_back(where, ids, rows, logits, head, blocks):
    top, share, coef = rows[0], rows[1], rows[2]
    lanes = logits.shape[1] // lax.axis_size("tp")
    onehot = (jnp.arange(head.shape[0])[:, None] + where[1]) == ids
    dlogits = coef * (jnp.exp(logits - top) * share - onehot.astype(f32))
    dlogits = dlogits.astype(bf16)
    product = dot(head, dlogits, 0, 0).reshape(blocks, D // blocks, -1)
    product = product[where[0] ^ jnp.arange(blocks)]
    return product[..., :lanes], product[..., lanes:].astype(bf16), dlogits


def shards(
    prev_hidden,
    token_embed,
    gain_hidden,
    gain_embed,
    gain_final,
    proj_hidden,
    proj_embed,
    head,
    target_ids,
    valid,
    rest_count,
):
    blocks, cores = lax.axis_size("seq"), lax.axis_size("tp")
    down = orders_of()
    up = [order[::-1] for order in down]
    me = lax.axis_index("seq")
    rows, width = prev_hidden.shape
    features = proj_hidden.shape[1]
    tokens = rows * blocks
    lanes = tokens // cores

    prev_f = prev_hidden.astype(f32)
    embed_f = token_embed.astype(f32)
    sums = lax.psum(
        jnp.stack([jnp.sum(prev_f * prev_f, axis=-1), jnp.sum(embed_f * embed_f, axis=-1)]), "tp"
    )
    scales = lax.rsqrt(sums / D + epsilon)
    scale_prev, scale_embed = scales[0][:, None], scales[1][:, None]
    normed_prev = (prev_f * scale_prev * gain_hidden).astype(bf16)
    normed_embed = (embed_f * scale_embed * gain_embed).astype(bf16)
    main = round(0.75 * width / 128) * 128
    rest = width - main
    first, second, third, ids_here, valid_here, gain_here = lax.optimization_barrier(
        (
            normed_prev[:, :main],
            normed_embed[:, :main],
            jnp.concatenate([normed_prev[:, main:], normed_embed[:, main:]], axis=1),
            target_ids,
            valid,
            gain_final,
        )
    )
    facts = jnp.stack([ids_here // 256, ids_here % 256, valid_here]).astype(bf16)
    facts = dot(jnp.eye(rows, dtype=bf16), jnp.pad(facts, ((0, 5), (0, 0))), 1, 1).astype(bf16)
    gain_parts = jnp.stack(in_parts(gain_here)).astype(bf16).reshape(rows, -1)
    gain_columns = gain_parts.shape[1]
    facts = jnp.concatenate([facts, gain_parts], axis=1)
    facts = jnp.pad(facts, ((0, 0), (0, 128 - facts.shape[1])))

    first = gather(first, down[0]).reshape(tokens, main)
    second = gather(second, down[1]).reshape(tokens, main)
    third = gather(jnp.concatenate([third, facts], axis=1), down[2])
    third = third.reshape(tokens, 2 * rest + 128)

    row = lax.broadcasted_iota(i32, (tokens, 1), 0)
    position = (me ^ (row // rows)) * rows + row % rows
    column = lax.broadcasted_iota(i32, (1, tokens), 1)
    order_prev = position == column
    order_embed = position - 1 == column

    from_prev = dot(proj_hidden[:main], first, 0, 1) + dot(proj_hidden[main:], third[:, :rest], 0, 1)
    from_embed = dot(proj_embed[:main], second, 0, 1) + dot(
        proj_embed[main:], third[:, rest : 2 * rest], 0, 1
    )
    facts_all = third[:, 2 * rest :]
    facts_prev = dot(facts_all, order_prev.astype(bf16), 0, 0)
    partial_value = dot(
        jnp.concatenate([from_prev, from_embed], axis=1),
        jnp.concatenate([order_prev, order_embed], axis=0).astype(f32),
        1,
        0,
        lax.Precision.HIGHEST,
    )
    gain_all = facts_all[:, 8 : 8 + gain_columns].reshape(blocks, 3, features).astype(f32)
    gain_all = gain_all[:, 0] + gain_all[:, 1] + gain_all[:, 2]
    block = jnp.arange(blocks)
    gain_all = dot(
        ((me ^ block)[:, None] == block[None, :]).astype(f32), gain_all, 0, 0, lax.Precision.HIGHEST
    ).reshape(D)
    ids_all = (facts_prev[0:1] * 256 + facts_prev[1:2]).astype(i32)
    valid_all = facts_prev[2]
    core = lax.axis_index("tp")
    cut_of = lambda mask: lax.dynamic_slice_in_dim(partial_value, (core ^ mask) * lanes, lanes, 1)
    mixed_f = cut_of(0)
    for mask in tp_masks():
        mixed_f = mixed_f + from_partner(cut_of(mask), "tp", mask)
    mixed_f = mixed_f.astype(bf16).astype(f32)
    mixed = mixed_f.astype(bf16)
    square_parts = jnp.stack(in_parts(jnp.sum(mixed_f * mixed_f, axis=0))).astype(bf16)
    square_parts = jnp.pad(square_parts, ((0, 13), (0, 0)))
    one, two = cut_in_three(features, 16)
    pieces = [
        gather(part, order)
        for part, order in zip(
            (mixed[:one], mixed[one:two], jnp.concatenate([mixed[two:], square_parts], axis=0)),
            down,
        )
    ]
    for mask in tp_masks():
        pieces = pieces + [from_partner(piece, "tp", mask) for piece in pieces[:3]]
    squares = [
        jnp.sum(piece[:, features - two :][:, :3].astype(f32), axis=(0, 1)) for piece in pieces[2::3]
    ]
    scale_own = lax.rsqrt(squares[0] / D + epsilon)
    scale_final = lax.rsqrt(jnp.concatenate(squares) / D + epsilon)

    vocab_rows = head.shape[0]
    where = jnp.stack([me, lax.axis_index(("seq", "tp")) * vocab_rows]).astype(i32)
    ids = lanes_by_index(ids_all)
    valid_lanes = lanes_by_index(valid_all)
    fits = cores == 2 and lanes % 128 == 0 and vocab_rows % 512 == 0 and 2 * features % 128 == 0
    forward = head_logits if fits else plain_logits
    logits, stats, final_all = forward(where, ids, scale_final[None, :], gain_all, pieces, head)
    stats = stats[:4]
    for bit in range(bits_of("seq")):
        stats = merged([stats, from_partner(stats, "seq", 1 << bit)])
    stats = lanes_by_index(stats)
    stats = merged([stats] + [from_partner(stats, "tp", mask) for mask in tp_masks()])
    row_top, row_total, row_weighted, target_logit = lanes_by_index(stats)
    count = jnp.sum(valid_all) + rest_count[0].astype(f32)
    coef = loss_scale * valid_lanes / count
    row_values = jnp.stack([row_top, 1.0 / row_total, coef])
    row_values = jnp.pad(row_values, ((0, 5), (0, 0)))
    back = head_back if fits else plain_back
    kept, sent, dlogits = back(where, ids, row_values, logits, head, blocks)
    dfinal = kept.reshape(blocks, features, lanes)
    for mask in tp_masks():
        piece = sent[..., (mask - 1) * lanes : mask * lanes]
        dfinal = dfinal + from_partner(piece, "tp", mask).astype(f32).reshape(dfinal.shape)

    def grad_head_piece(index):
        if fits:
            return lambda left, results: grad_head_rows(
                left, final_all, index, 4, results[-1] if results else None
            )
        return lambda left, results: (dot(left, final_all, 1, 1).astype(bf16), left[:8])

    early = [(grad_head_piece(index), dlogits) for index in range(2 if fits else 1)]
    dfinal, results = scatter([dfinal[:, :one], dfinal[:, one:two], dfinal[:, two:]], up, early)
    dfinal = jnp.concatenate(dfinal, axis=0)

    total_dot = (coef * (row_weighted / row_total - target_logit))[:lanes] / scale_own
    dmixed = (
        scale_own * (dfinal * gain_final[:, None]) - mixed_f * (scale_own**3 * (total_dot / D))
    ).astype(bf16)
    dmixed = lanes_by_index(over_cores(dmixed))
    dmixed_prev = dot(dmixed, order_prev.astype(bf16), 1, 1).astype(bf16)
    dmixed_embed = dot(dmixed, order_embed.astype(bf16), 1, 1).astype(bf16)
    back_prev = dot(dmixed_prev, proj_hidden, 0, 1).reshape(blocks, rows, width)
    back_embed = dot(dmixed_embed, proj_embed, 0, 1).reshape(blocks, rows, width)

    def head_grad_end(left, before):
        grad_head = results[-1]
        mark = left[:8]
        if fits:
            for index in (2, 3):
                grad_head, mark = grad_head_rows(left, final_all, index, 4, grad_head)
        return grad_head, mark

    def proj_grad_hidden(given, before):
        rows_all = jnp.concatenate([first, third[:, :rest]], axis=1)
        out = dot(rows_all, given, 0, 1).astype(bf16)
        return out, out[:8]

    def proj_grad_embed(given, before):
        rows_all = jnp.concatenate([second, third[:, rest : 2 * rest]], axis=1)
        out = dot(rows_all, given, 0, 1).astype(bf16)
        return out, out[:8]

    (one, two, three), results = scatter(
        [
            back_prev[..., :main],
            back_embed[..., :main],
            jnp.concatenate([back_prev[..., main:], back_embed[..., main:]], axis=-1),
        ],
        up,
        [
            (head_grad_end, dlogits),
            (proj_grad_hidden, dmixed_prev),
            (proj_grad_embed, dmixed_embed),
        ],
    )
    grad_head, grad_proj_hidden, grad_proj_embed = results
    grad_prev = jnp.concatenate([one, three[:, :rest]], axis=1) * gain_hidden
    grad_embed = jnp.concatenate([two, three[:, rest:]], axis=1) * gain_embed
    dots = lax.psum(
        jnp.stack([jnp.sum(grad_prev * prev_f, axis=-1), jnp.sum(grad_embed * embed_f, axis=-1)]),
        "tp",
    )
    grad_prev_hidden = (
        scale_prev * grad_prev - prev_f * (scale_prev**3 * (dots[0] / D)[:, None])
    ).astype(bf16)
    grad_token_embed = (
        scale_embed * grad_embed - embed_f * (scale_embed**3 * (dots[1] / D)[:, None])
    ).astype(bf16)
    return (grad_prev_hidden, grad_token_embed, grad_proj_hidden, grad_proj_embed, grad_head)


def solution(mesh):
    return jax.shard_map(
        shards,
        mesh=mesh,
        in_specs=(
            P("seq", "tp"),
            P("seq", "tp"),
            P("tp"),
            P("tp"),
            P("seq"),
            P("tp", "seq"),
            P("tp", "seq"),
            P(("seq", "tp"), None),
            P("seq"),
            P("seq"),
            P(),
        ),
        out_specs=(
            P("seq", "tp"),
            P("seq", "tp"),
            P("tp", "seq"),
            P("tp", "seq"),
            P(("seq", "tp"), None),
        ),
        check_vma=False,
    )
```

time: 294 us -> 268 us (0.912)
  Pallas kernels: 31.5 us -> 55 us
  matrix products: 30.7 us -> 14.1 us
  starting transfers between devices: 83.3 us -> 69.7 us
  other arithmetic: 25.9 us -> 17.3 us
  local copies, waits for them, and re-layouts: 15 us -> 9.6 us
  waiting for transfers between devices: 98.1 us -> 92.9 us
    pallas_call x1 -> x5, Pallas kernels: 14.6 us -> 38.3 us  [the longest x4 23.1 us: grad_head_rows(): pl.pallas_call(grad_head_kernel, grid=(D // tile,), in_specs=[pl.BlockSpe...]
    dot_general x12 -> x14, matrix products: 30.7 us -> 14.1 us  [dot(): lax.dot_general(left, right, (((on_left,), (on_right,)), ((), ())), preci...]
    ppermute x60 -> x59, starting transfers between devices: 83.3 us -> 69.7 us  [from_partner(): return lax.ppermute(array, axis, [(i, i ^ mask) for i in range(size)])]
    another operation x21 -> x27, other arithmetic: 12.5 us -> 6.18 us  [the longest x21 4.13 us: gather(): array = jnp.stack([array, from_partner(array, 'seq', 1 << bit)])]
    ppermute x60 -> x59, waiting for transfers between devices: 98.1 us -> 92.9 us  [from_partner(): return lax.ppermute(array, axis, [(i, i ^ mask) for i in range(size)])]
    slice x10 -> x14, local copies, waits for them, and re-layouts: 4.07 us -> 0.92 us  [the longest x1 0.21 us: shards(): back_prev[..., :main]]
    unnamed x63 -> x52, local copies, waits for them, and re-layouts: 6.93 us -> 7.18 us
  transfers between devices with their start and end apart: 60 -> 59, of which waited for: 31 -> 41; matrix products, arithmetic and copies ran while one was open for 13% -> 7% of each run, Pallas kernels for 0% -> 9%
where the time goes in v2:
time: 268 us; the launch traced here: 267 us
  waiting for transfers between devices  92.9 us (35%)
  starting transfers between devices  69.7 us (26%)
  Pallas kernels  55 us (21%)
  other arithmetic  17.3 us (6%)
  matrix products  14.1 us (5%)
  local copies, waits for them, and re-layouts  9.6 us (4%)
  blocking collectives  5.05 us (2%)
  between operations  3.17 us (1%)
    ppermute x59, waiting for transfers between devices, from_partner(): return lax.ppermute(array, axis, [(i, i ^ mask) for i in range(size)])  92.9 us
    ppermute x59, starting transfers between devices, from_partner(): return lax.ppermute(array, axis, [(i, i ^ mask) for i in range(size)])  69.7 us
    pallas_call x4, Pallas kernels, grad_head_rows(): pl.pallas_call(grad_head_kernel, grid=(D // tile,), in_specs=[pl.BlockSpe...  23.1 us
    pallas_call x1, Pallas kernels, head_back(): pl.pallas_call(dfinal_kernel, grid_spec=pltpu.PrefetchScalarGridSpec(num_...  16.8 us
    pallas_call x1, Pallas kernels, head_logits(): pl.pallas_call(logits_kernel, grid_spec=pltpu.PrefetchScalarGridSpec(num_...  15.2 us
    dot_general x14, matrix products, dot(): lax.dot_general(left, right, (((on_left,), (on_right,)), ((), ())), preci...  14.1 us
    unnamed x52, local copies, waits for them, and re-layouts  7.18 us
  transfers between devices with their start and end apart: 59, of which 41 were waited for; matrix products, arithmetic and copies ran while one was open for 7% of the time, Pallas kernels for 9%

profile of v2, /device:TPU:0, one launch (start us, length us, event | category | flops | bytes accessed | tf_op | source)
XLA Modules:
  0.0 266.8 jit_solution(7535439325463739286)
XLA Ops:
  2.7 2.6 psum.14
  9.0 2.9 %collective-permute-start.4 = (bf16[16,1920]{1,0:T(8,128)(2,1)S(1)}, bf16[16,1920]{1,0:T(8,128)(2,1)S(1)}, u32[]{:S(2)}, u32[]{:S(2)}) collective-permute-start(bf16[16,1920]{1,0:T(8,128)(2,1)S(1)} %get-tuple-element.122), channel_id=1, source_target_pairs={{0,2},{2,0},{4,6},{6,4},{8,10},{10,8},{12,14},{14,12},{16,18},{18,... | collective-permute-start | bytes 184328 | tf_op jit(solution)/shard_map/ppermute | solution.py:21
  11.9 2.6 collective-permute-start
  16.3 1.6 collective-permute-start.5
  17.9 3.8 %collective-permute-done = bf16[16,2688]{1,0:T(8,128)(2,1)S(1)} collective-permute-done((bf16[16,2688]{1,0:T(8,128)(2,1)S(1)}, bf16[16,2688]{1,0:T(8,128)(2,1)S(1)}, u32[]{:S(2)}, u32[]{:S(2)}) %collective-permute-start) | collective-permute-done | bytes 86048 | tf_op jit(solution)/shard_map/ppermute | solution.py:21
  23.9 3.0 %collective-permute-start.6 = (bf16[2,2,16,1920]{3,2,1,0:T(8,128)(2,1)S(1)}, bf16[2,2,16,1920]{3,2,1,0:T(8,128)(2,1)S(1)}, u32[]{:S(2)}, u32[]{:S(2)}) collective-permute-start(bf16[2,2,16,1920]{3,2,1,0:T(8,128)(2,1)S(1)} %get-tuple-element.90), channel_id=1, source_target_pairs={{0,16},{2,18},{4,20},{6,22},{8,24},{10,26},{12,28},{14,30},{16,0},... | collective-permute-start | bytes 737288 | tf_op jit(solution)/shard_map/ppermute | solution.py:21
  26.9 6.8 %collective-permute-done.1 = bf16[2,16,2688]{2,1,0:T(8,128)(2,1)S(1)} collective-permute-done((bf16[2,16,2688]{2,1,0:T(8,128)(2,1)S(1)}, bf16[2,16,2688]{2,1,0:T(8,128)(2,1)S(1)}, u32[]{:S(2)}, u32[]{:S(2)}) %collective-permute-start.1) | collective-permute-done | bytes 172064 | tf_op jit(solution)/shard_map/ppermute | solution.py:21
  33.7 1.6 collective-permute-start.2
  36.1 1.9 collective-permute-done.6
  38.7 2.3 collective-permute-done.2
  45.4 1.5 collective-permute-start.11
  46.9 2.5 collective-permute-done.7
  50.9 1.9 fusion.29
  53.3 5.0 %collective-permute-done.11 = bf16[2,2,2,16,2688]{4,3,2,1,0:T(8,128)(2,1)} collective-permute-done((bf16[2,2,2,16,2688]{4,3,2,1,0:T(8,128)(2,1)}, bf16[2,2,2,16,2688]{4,3,2,1,0:T(8,128)(2,1)}, u32[]{:S(2)}, u32[]{:S(2)}) %collective-permute-start.11) | collective-permute-done | bytes 688160 | tf_op jit(solution)/shard_map/ppermute | solution.py:21
  69.7 2.9 %collective-permute-start.22 = (bf16[160,128]{1,0:T(8,128)(2,1)S(1)}, bf16[160,128]{1,0:T(8,128)(2,1)S(1)}, u32[]{:S(2)}, u32[]{:S(2)}) collective-permute-start(bf16[160,128]{1,0:T(8,128)(2,1)S(1)} %get-tuple-element.112), channel_id=1, source_target_pairs={{0,16},{2,18},{4,20},{6,22},{8,24},{10,26},{12,28},{14,30},{16,0},... | collective-permute-start | bytes 122888 | tf_op jit(solution)/shard_map/ppermute | solution.py:21
  72.7 1.6 collective-permute-start.14
  74.6 2.6 collective-permute-start.23
  77.5 2.5 collective-permute-start.19
  81.3 2.7 collective-permute-done.19
  84.0 1.6 collective-permute-start.20
  85.6 1.6 collective-permute-start.24
  89.6 1.7 collective-permute-start.21
  94.7 3.7 %collective-permute-done.21 = bf16[2,2,2,176,128]{4,3,2,1,0:T(8,128)(2,1)S(1)} collective-permute-done((bf16[2,2,2,176,128]{4,3,2,1,0:T(8,128)(2,1)S(1)}, bf16[2,2,2,176,128]{4,3,2,1,0:T(8,128)(2,1)S(1)}, u32[]{:S(2)}, u32[]{:S(2)}) %collective-permute-start.21) | collective-permute-done | bytes 360480 | tf_op jit(solution)/shard_map/ppermute | solution.py:21
  100.3 2.0 collective-permute-done.27.refs_4_
  102.3 15.2 %shard_map.146 = (f32[2048,256]{1,0:T(8,128)S(1)}, f32[8,256]{1,0:T(8,128)S(1)}, bf16[7168,256]{1,0:T(8,128)(2,1)S(1)}) custom-call(s32[2]{0:T(128)S(1)} %pad_add_fusion.1.where, s32[1,256]{1,0:T(1,128)S(1)} %pad_add_fusion.ids, f32[1,256]{1,0:T(1,128)S(1)} %fusion.159.scale, f32[56,128]{1,0:T(8,128)S(1)} %reshape_reshape.15.gain, ...), custom_call_target="tpu_custom_call" | custom-call | flops 7516192768 | bytes 36700160 | tf_op jit(solution)/shard_map/pallas_call | solution.py:168
  117.5 1.8 copy-done
  119.3 1.5 collective-permute-start.28
  120.8 2.1 collective-permute-done.28
  123.4 3.3 %collective-permute-done.29 = f32[4,256]{1,0:T(4,128)S(1)} collective-permute-done((f32[4,256]{1,0:T(4,128)S(1)}, f32[4,256]{1,0:T(4,128)S(1)}, u32[]{:S(2)}, u32[]{:S(2)}) %collective-permute-start.29) | collective-permute-done | bytes 4128 | tf_op jit(solution)/shard_map/ppermute | solution.py:21
  126.7 1.6 collective-permute-start.30
  130.4 2.1 collective-permute-start.31
  133.2 1.8 collective-permute-done.31
  136.4 16.8 %shard_map.147 = (f32[8,2,448,128]{3,2,1,0:T(8,128)S(1)}, bf16[8,2,448,128]{3,2,1,0:T(8,128)(2,1)S(1)}, bf16[2048,256]{1,0:T(8,128)(2,1)S(1)}) custom-call(s32[2]{0:T(128)S(1)} %pad_add_fusion.1.where, s32[1,256]{1,0:T(1,128)S(1)} %pad_add_fusion.ids, f32[8,256]{1,0:T(8,128)S(1)} %select_maximum_fusion.rows, f32[2048,256]{1,0:T(8,128)S(1)} %get-tuple-element.38.logits, ...), custom_call_target="tpu_custom_call" | custom-call | flops 7516192768 | bytes 36700160 | tf_op jit(solution)/shard_map/pallas_call | solution.py:232
  153.5 3.5 %collective-permute-done.33 = bf16[8,2,448,128]{3,2,1,0:T(8,128)(2,1)S(1)} collective-permute-done((bf16[8,2,448,128]{3,2,1,0:T(8,128)(2,1)S(1)}, bf16[8,2,448,128]{3,2,1,0:T(8,128)(2,1)S(1)}, u32[]{:S(2)}, u32[]{:S(2)}) %collective-permute-start.33) | collective-permute-done | bytes 1835040 | tf_op jit(solution)/shard_map/ppermute | solution.py:21
  157.8 1.6 collective-permute-start.42
  161.8 5.8 %shard_map.148 = (bf16[2048,7168]{1,0:T(8,128)(2,1)}, f32[8,128]{1,0:T(8,128)}) custom-call(bf16[2048,256]{1,0:T(8,128)(2,1)S(1)} %get-tuple-element.52.left, bf16[7168,256]{1,0:T(8,128)(2,1)S(1)} %copy-done.1), custom_call_target="tpu_custom_call" | custom-call | flops 1879048192 | bytes 11010048 | tf_op jit(solution)/shard_map/pallas_call | solution.py:276
  167.7 2.3 collective-permute-start.43
  170.8 4.5 %collective-permute-done.43 = bf16[2,2,112,128]{3,2,1,0:T(8,128)(2,1)S(1)} collective-permute-done((bf16[2,2,112,128]{3,2,1,0:T(8,128)(2,1)S(1)}, bf16[2,2,112,128]{3,2,1,0:T(8,128)(2,1)S(1)}, u32[]{:S(2)}, u32[]{:S(2)}) %collective-permute-start.43) | collective-permute-done | bytes 114720 | tf_op jit(solution)/shard_map/ppermute | solution.py:21
  175.3 1.6 collective-permute-start.44
  176.9 2.6 collective-permute-done.44
  181.8 1.6 collective-permute-done.45
  183.6 2.6 collective-permute-done.35
  186.5 1.6 collective-permute-done.40
  188.1 2.0 collective-permute-start.41
  190.9 1.5 collective-permute-start.37
  193.8 2.1 collective-permute-done.37
  196.2 5.8 %shard_map.149 = (bf16[2048,7168]{1,0:T(8,128)(2,1)}, f32[8,128]{1,0:T(8,128)}) custom-call(bf16[2048,256]{1,0:T(8,128)(2,1)S(1)} %get-tuple-element.52.left, bf16[7168,256]{1,0:T(8,128)(2,1)S(1)} %copy-done.1, bf16[2048,7168]{1,0:T(8,128)(2,1)} %get-tuple-element.53.refs_0_), custom_call_target="tpu_custom_call", output_to_operand_aliasing={{0}: (2, {})} | custom-call | flops 1879048192 | bytes 11010048 | tf_op jit(solution)/shard_map/pallas_call | solution.py:276
  204.2 1.7 copy-done.5
  207.4 1.5 collective-permute-start.47
  210.9 5.8 %shard_map.150 = (bf16[2048,7168]{1,0:T(8,128)(2,1)}, f32[8,128]{1,0:T(8,128)}) custom-call(bf16[2048,256]{1,0:T(8,128)(2,1)S(1)} %get-tuple-element.52.left, bf16[7168,256]{1,0:T(8,128)(2,1)S(1)} %copy-done.1, bf16[2048,7168]{1,0:T(8,128)(2,1)} %get-tuple-element.54.refs_0_), custom_call_target="tpu_custom_call", output_to_operand_aliasing={{0}: (2, {})} | custom-call | flops 1879048192 | bytes 11010048 | tf_op jit(solution)/shard_map/pallas_call | solution.py:276
  216.7 5.8 %shard_map.151 = (bf16[2048,7168]{1,0:T(8,128)(2,1)}, f32[8,128]{1,0:T(8,128)}) custom-call(bf16[2048,256]{1,0:T(8,128)(2,1)S(1)} %get-tuple-element.52.left, bf16[7168,256]{1,0:T(8,128)(2,1)S(1)} %copy-done.1, bf16[2048,7168]{1,0:T(8,128)(2,1)} %get-tuple-element.55.refs_0_), custom_call_target="tpu_custom_call", output_to_operand_aliasing={{0}: (2, {})} | custom-call | flops 1879048192 | bytes 11010048 | tf_op jit(solution)/shard_map/pallas_call | solution.py:276
  222.6 2.7 %collective-permute-start.52 = (bf16[2,2,16,1792]{3,2,1,0:T(8,128)(2,1)S(1)}, bf16[2,2,16,1792]{3,2,1,0:T(8,128)(2,1)S(1)}, u32[]{:S(2)}, u32[]{:S(2)}) collective-permute-start(bf16[2,2,16,1792]{3,2,1,0:T(8,128)(2,1)S(1)} %fusion.68), channel_id=1, source_target_pairs={{0,16},{2,18},{4,20},{6,22},{8,24},{10,26},{12,28},{14,30},{16,0},... | collective-permute-start | bytes 688136 | tf_op jit(solution)/shard_map/ppermute | solution.py:21
  225.5 2.0 collective-permute-start.48
  227.6 8.1 %collective-permute-done.52 = bf16[2,2,16,1792]{3,2,1,0:T(8,128)(2,1)S(1)} collective-permute-done((bf16[2,2,16,1792]{3,2,1,0:T(8,128)(2,1)S(1)}, bf16[2,2,16,1792]{3,2,1,0:T(8,128)(2,1)S(1)}, u32[]{:S(2)}, u32[]{:S(2)}) %collective-permute-start.52) | collective-permute-done | bytes 229408 | tf_op jit(solution)/shard_map/ppermute | solution.py:21
  236.6 1.6 collective-permute-start.56
  238.2 2.5 collective-permute-done.53
  241.9 2.7 %convolution_convert_fusion.1 = bf16[3584,448]{0,1:T(8,128)(2,1)} fusion(bf16[448,256]{1,0:T(8,128)(2,1)S(1)} %convolution_convert_fusion.3, bf16[256,896]{1,0:T(8,128)(2,1)S(1)} %get-tuple-element.72, bf16[256,2688]{1,0:T(8,128)(2,1)S(1)} %bitcast.337), kind=kOutput, calls=%fused_computation.1 | convolution fusion | flops 827359232 | bytes 5275648 | tf_op jit(solution)/shard_map/dot_general | solution.py:114
  244.6 2.3 collective-permute-done.54
  247.3 2.1 collective-permute-start.57
  249.3 2.7 %convolution_convert_fusion = bf16[3584,448]{0,1:T(8,128)(2,1)} fusion(bf16[448,256]{1,0:T(8,128)(2,1)S(1)} %convolution_convert_fusion.2, bf16[256,896]{1,0:T(8,128)(2,1)S(1)} %get-tuple-element.71, bf16[256,2688]{1,0:T(8,128)(2,1)S(1)} %bitcast.335), kind=kOutput, calls=%fused_computation | convolution fusion | flops 827359232 | bytes 5275648 | tf_op jit(solution)/shard_map/dot_general | solution.py:114
  254.0 2.2 collective-permute-done.57
  256.7 3.3 %collective-permute-done.50 = bf16[16,2688]{1,0:T(8,128)(2,1)S(1)} collective-permute-done((bf16[16,2688]{1,0:T(8,128)(2,1)S(1)}, bf16[16,2688]{1,0:T(8,128)(2,1)S(1)}, u32[]{:S(2)}, u32[]{:S(2)}) %collective-permute-start.50) | collective-permute-done | bytes 86048 | tf_op jit(solution)/shard_map/ppermute | solution.py:21
  260.1 2.5 collective-permute-done.58
  262.9 2.5 psum.15
  (294 shorter events, 63.8 us)
Async XLA Ops:
  9.0 7.3 %collective-permute-start.4 = (bf16[16,1920]{1,0:T(8,128)(2,1)S(1)}, bf16[16,1920]{1,0:T(8,128)(2,1)S(1)}, u32[]{:S(2)}, u32[]{:S(2)}) collective-permute-start(bf16[16,1920]{1,0:T(8,128)(2,1)S(1)} %get-tuple-element.122), channel_id=1, source_target_pairs={{0,2},{2,0},{4,6},{6,4},{8,10},{10,8},{12,14},{14,12},{16,18},{18,... | collective-permute-start | bytes 184328 | tf_op jit(solution)/shard_map/ppermute | solution.py:21
  11.9 9.8 %collective-permute-start = (bf16[16,2688]{1,0:T(8,128)(2,1)S(1)}, bf16[16,2688]{1,0:T(8,128)(2,1)S(1)}, u32[]{:S(2)}, u32[]{:S(2)}) collective-permute-start(bf16[16,2688]{1,0:T(8,128)(2,1)S(1)} %slice.497), channel_id=1, source_target_pairs={{0,16},{2,18},{4,20},{6,22},{8,24},{10,26},{12,28},{14,30},{16,0},... | collective-permute-start | bytes 258056 | tf_op jit(solution)/shard_map/ppermute | solution.py:21
  14.5 8.3 %collective-permute-start.8 = (bf16[16,2688]{1,0:T(8,128)(2,1)S(1)}, bf16[16,2688]{1,0:T(8,128)(2,1)S(1)}, u32[]{:S(2)}, u32[]{:S(2)}) collective-permute-start(bf16[16,2688]{1,0:T(8,128)(2,1)S(1)} %slice.498), channel_id=1, source_target_pairs={{0,16},{2,18},{4,20},{6,22},{8,24},{10,26},{12,28},{14,30},{16,0},... | collective-permute-start | bytes 258056 | tf_op jit(solution)/shard_map/ppermute | solution.py:21
  16.3 7.6 %collective-permute-start.5 = (bf16[2,16,1920]{2,1,0:T(8,128)(2,1)S(1)}, bf16[2,16,1920]{2,1,0:T(8,128)(2,1)S(1)}, u32[]{:S(2)}, u32[]{:S(2)}) collective-permute-start(bf16[2,16,1920]{2,1,0:T(8,128)(2,1)S(1)} %get-tuple-element.108), channel_id=1, source_target_pairs={{0,4},{2,6},{4,0},{6,2},{8,12},{10,14},{12,8},{14,10},{16,20},{18,... | collective-permute-start | bytes 368648 | tf_op jit(solution)/shard_map/ppermute | solution.py:21
  21.7 12.0 %collective-permute-start.1 = (bf16[2,16,2688]{2,1,0:T(8,128)(2,1)S(1)}, bf16[2,16,2688]{2,1,0:T(8,128)(2,1)S(1)}, u32[]{:S(2)}, u32[]{:S(2)}) collective-permute-start(bf16[2,16,2688]{2,1,0:T(8,128)(2,1)S(1)} %get-tuple-element.96), channel_id=1, source_target_pairs={{0,8},{2,10},{4,12},{6,14},{8,0},{10,2},{12,4},{14,6},{16,24},{18,... | collective-permute-start | bytes 516104 | tf_op jit(solution)/shard_map/ppermute | solution.py:21
  22.8 12.7 %collective-permute-start.9 = (bf16[2,16,2688]{2,1,0:T(8,128)(2,1)S(1)}, bf16[2,16,2688]{2,1,0:T(8,128)(2,1)S(1)}, u32[]{:S(2)}, u32[]{:S(2)}) collective-permute-start(bf16[2,16,2688]{2,1,0:T(8,128)(2,1)S(1)} %get-tuple-element.98), channel_id=1, source_target_pairs={{0,8},{2,10},{4,12},{6,14},{8,0},{10,2},{12,4},{14,6},{16,24},{18,... | collective-permute-start | bytes 516104 | tf_op jit(solution)/shard_map/ppermute | solution.py:21
  23.9 14.2 %collective-permute-start.6 = (bf16[2,2,16,1920]{3,2,1,0:T(8,128)(2,1)S(1)}, bf16[2,2,16,1920]{3,2,1,0:T(8,128)(2,1)S(1)}, u32[]{:S(2)}, u32[]{:S(2)}) collective-permute-start(bf16[2,2,16,1920]{3,2,1,0:T(8,128)(2,1)S(1)} %get-tuple-element.90), channel_id=1, source_target_pairs={{0,16},{2,18},{4,20},{6,22},{8,24},{10,26},{12,28},{14,30},{16,0},... | collective-permute-start | bytes 737288 | tf_op jit(solution)/shard_map/ppermute | solution.py:21
  33.7 7.3 %collective-permute-start.2 = (bf16[2,2,16,2688]{3,2,0,1:T(8,128)(2,1)S(1)}, bf16[2,2,16,2688]{3,2,0,1:T(8,128)(2,1)S(1)}, u32[]{:S(2)}, u32[]{:S(2)}) collective-permute-start(bf16[2,2,16,2688]{3,2,0,1:T(8,128)(2,1)S(1)} %get-tuple-element.82), channel_id=1, source_target_pairs={{0,4},{2,6},{4,0},{6,2},{8,12},{10,14},{12,8},{14,10},{16,20},{18,... | collective-permute-start | bytes 1032200 | tf_op jit(solution)/shard_map/ppermute | solution.py:21
  35.5 8.7 %collective-permute-start.10 = (bf16[2,2,16,2688]{3,2,1,0:T(8,128)(2,1)S(1)}, bf16[2,2,16,2688]{3,2,1,0:T(8,128)(2,1)S(1)}, u32[]{:S(2)}, u32[]{:S(2)}) collective-permute-start(bf16[2,2,16,2688]{3,2,1,0:T(8,128)(2,1)S(1)} %get-tuple-element.84), channel_id=1, source_target_pairs={{0,2},{2,0},{4,6},{6,4},{8,10},{10,8},{12,14},{14,12},{16,18},{18,... | collective-permute-start | bytes 1032200 | tf_op jit(solution)/shard_map/ppermute | solution.py:21
  38.1 11.3 %collective-permute-start.7 = (bf16[2,2,2,16,1920]{4,3,2,1,0:T(8,128)(2,1)S(1)}, bf16[2,2,2,16,1920]{4,3,2,1,0:T(8,128)(2,1)S(1)}, u32[]{:S(2)}, u32[]{:S(2)}) collective-permute-start(bf16[2,2,2,16,1920]{4,3,2,1,0:T(8,128)(2,1)S(1)} %get-tuple-element.78), channel_id=1, source_target_pairs={{0,8},{2,10},{4,12},{6,14},{8,0},{10,2},{12,4},{14,6},{16,24},{18,... | collective-permute-start | bytes 1474568 | tf_op jit(solution)/shard_map/ppermute | solution.py:21
  42.2 17.5 %collective-permute-start.3 = (bf16[2,2,2,16,2688]{4,3,0,1,2:T(8,128)(2,1)}, bf16[2,2,2,16,2688]{4,3,0,1,2:T(8,128)(2,1)}, u32[]{:S(2)}, u32[]{:S(2)}) collective-permute-start(bf16[2,2,2,16,2688]{4,3,0,1,2:T(8,128)(2,1)} %get-tuple-element.74), channel_id=1, source_target_pairs={{0,2},{2,0},{4,6},{6,4},{8,10},{10,8},{12,14},{14,12},{16,18},{18,... | collective-permute-start | bytes 2064392 | tf_op jit(solution)/shard_map/ppermute | solution.py:21
  45.4 13.0 %collective-permute-start.11 = (bf16[2,2,2,16,2688]{4,3,2,1,0:T(8,128)(2,1)}, bf16[2,2,2,16,2688]{4,3,2,1,0:T(8,128)(2,1)}, u32[]{:S(2)}, u32[]{:S(2)}) collective-permute-start(bf16[2,2,2,16,2688]{4,3,2,1,0:T(8,128)(2,1)} %get-tuple-element.76), channel_id=1, source_target_pairs={{0,4},{2,6},{4,0},{6,2},{8,12},{10,14},{12,8},{14,10},{16,20},{18,... | collective-permute-start | bytes 2064392 | tf_op jit(solution)/shard_map/ppermute | solution.py:21
  66.5 1.6 collective-permute-start.12
  68.2 4.4 %collective-permute-start.13 = (bf16[128,128]{1,0:T(8,128)(2,1)S(1)}, bf16[128,128]{1,0:T(8,128)(2,1)S(1)}, u32[]{:S(2)}, u32[]{:S(2)}) collective-permute-start(bf16[128,128]{1,0:T(8,128)(2,1)S(1)} %get-tuple-element.124), channel_id=1, source_target_pairs={{0,2},{2,0},{4,6},{6,4},{8,10},{10,8},{12,14},{14,12},{16,18},{18,... | collective-permute-start | bytes 98312 | tf_op jit(solution)/shard_map/ppermute | solution.py:21
  69.7 4.9 %collective-permute-start.22 = (bf16[160,128]{1,0:T(8,128)(2,1)S(1)}, bf16[160,128]{1,0:T(8,128)(2,1)S(1)}, u32[]{:S(2)}, u32[]{:S(2)}) collective-permute-start(bf16[160,128]{1,0:T(8,128)(2,1)S(1)} %get-tuple-element.112), channel_id=1, source_target_pairs={{0,16},{2,18},{4,20},{6,22},{8,24},{10,26},{12,28},{14,30},{16,0},... | collective-permute-start | bytes 122888 | tf_op jit(solution)/shard_map/ppermute | solution.py:21
  72.6 4.9 %collective-permute-start.18 = (bf16[176,128]{1,0:T(8,128)(2,1)S(1)}, bf16[176,128]{1,0:T(8,128)(2,1)S(1)}, u32[]{:S(2)}, u32[]{:S(2)}) collective-permute-start(bf16[176,128]{1,0:T(8,128)(2,1)S(1)} %get-tuple-element.114), channel_id=1, source_target_pairs={{0,16},{2,18},{4,20},{6,22},{8,24},{10,26},{12,28},{14,30},{16,0},... | collective-permute-start | bytes 135176 | tf_op jit(solution)/shard_map/ppermute | solution.py:21
  72.7 7.4 %collective-permute-start.14 = (bf16[2,128,128]{2,1,0:T(8,128)(2,1)S(1)}, bf16[2,128,128]{2,1,0:T(8,128)(2,1)S(1)}, u32[]{:S(2)}, u32[]{:S(2)}) collective-permute-start(bf16[2,128,128]{2,1,0:T(8,128)(2,1)S(1)} %get-tuple-element.120), channel_id=1, source_target_pairs={{0,4},{2,6},{4,0},{6,2},{8,12},{10,14},{12,8},{14,10},{16,20},{18,... | collective-permute-start | bytes 196616 | tf_op jit(solution)/shard_map/ppermute | solution.py:21
  74.6 11.0 %collective-permute-start.23 = (bf16[2,160,128]{2,1,0:T(8,128)(2,1)S(1)}, bf16[2,160,128]{2,1,0:T(8,128)(2,1)S(1)}, u32[]{:S(2)}, u32[]{:S(2)}) collective-permute-start(bf16[2,160,128]{2,1,0:T(8,128)(2,1)S(1)} %get-tuple-element.118), channel_id=1, source_target_pairs={{0,8},{2,10},{4,12},{6,14},{8,0},{10,2},{12,4},{14,6},{16,24},{18,... | collective-permute-start | bytes 245768 | tf_op jit(solution)/shard_map/ppermute | solution.py:21
  77.5 6.5 %collective-permute-start.19 = (bf16[2,176,128]{2,1,0:T(8,128)(2,1)S(1)}, bf16[2,176,128]{2,1,0:T(8,128)(2,1)S(1)}, u32[]{:S(2)}, u32[]{:S(2)}) collective-permute-start(bf16[2,176,128]{2,1,0:T(8,128)(2,1)S(1)} %get-tuple-element.116), channel_id=1, source_target_pairs={{0,8},{2,10},{4,12},{6,14},{8,0},{10,2},{12,4},{14,6},{16,24},{18,... | collective-permute-start | bytes 270344 | tf_op jit(solution)/shard_map/ppermute | solution.py:21
  80.1 8.0 %collective-permute-start.15 = (bf16[2,2,128,128]{3,2,1,0:T(8,128)(2,1)S(1)}, bf16[2,2,128,128]{3,2,1,0:T(8,128)(2,1)S(1)}, u32[]{:S(2)}, u32[]{:S(2)}) collective-permute-start(bf16[2,2,128,128]{3,2,1,0:T(8,128)(2,1)S(1)} %get-tuple-element.102), channel_id=1, source_target_pairs={{0,16},{2,18},{4,20},{6,22},{8,24},{10,26},{12,28},{14,30},{16,0},... | collective-permute-start | bytes 393224 | tf_op jit(solution)/shard_map/ppermute | solution.py:21
  84.0 5.6 %collective-permute-start.20 = (bf16[2,2,176,128]{3,2,1,0:T(8,128)(2,1)S(1)}, bf16[2,2,176,128]{3,2,1,0:T(8,128)(2,1)S(1)}, u32[]{:S(2)}, u32[]{:S(2)}) collective-permute-start(bf16[2,2,176,128]{3,2,1,0:T(8,128)(2,1)S(1)} %get-tuple-element.94), channel_id=1, source_target_pairs={{0,4},{2,6},{4,0},{6,2},{8,12},{10,14},{12,8},{14,10},{16,20},{18,... | collective-permute-start | bytes 540680 | tf_op jit(solution)/shard_map/ppermute | solution.py:21
  85.6 7.1 %collective-permute-start.24 = (bf16[2,2,160,128]{3,2,1,0:T(8,128)(2,1)S(1)}, bf16[2,2,160,128]{3,2,1,0:T(8,128)(2,1)S(1)}, u32[]{:S(2)}, u32[]{:S(2)}) collective-permute-start(bf16[2,2,160,128]{3,2,1,0:T(8,128)(2,1)S(1)} %get-tuple-element.100), channel_id=1, source_target_pairs={{0,2},{2,0},{4,6},{6,4},{8,10},{10,8},{12,14},{14,12},{16,18},{18,... | collective-permute-start | bytes 491528 | tf_op jit(solution)/shard_map/ppermute | solution.py:21
  88.1 6.4 %collective-permute-start.16 = (bf16[2,2,2,128,128]{4,3,2,1,0:T(8,128)(2,1)S(1)}, bf16[2,2,2,128,128]{4,3,2,1,0:T(8,128)(2,1)S(1)}, u32[]{:S(2)}, u32[]{:S(2)}) collective-permute-start(bf16[2,2,2,128,128]{4,3,2,1,0:T(8,128)(2,1)S(1)} %get-tuple-element.88), channel_id=1, source_target_pairs={{0,8},{2,10},{4,12},{6,14},{8,0},{10,2},{12,4},{14,6},{16,24},{18,... | collective-permute-start | bytes 786440 | tf_op jit(solution)/shard_map/ppermute | solution.py:21
  89.6 8.8 %collective-permute-start.21 = (bf16[2,2,2,176,128]{4,3,2,1,0:T(8,128)(2,1)S(1)}, bf16[2,2,2,176,128]{4,3,2,1,0:T(8,128)(2,1)S(1)}, u32[]{:S(2)}, u32[]{:S(2)}) collective-permute-start(bf16[2,2,2,176,128]{4,3,2,1,0:T(8,128)(2,1)S(1)} %get-tuple-element.80), channel_id=1, source_target_pairs={{0,2},{2,0},{4,6},{6,4},{8,10},{10,8},{12,14},{14,12},{16,18},{18,... | collective-permute-start | bytes 1081352 | tf_op jit(solution)/shard_map/ppermute | solution.py:21
  92.8 7.1 %collective-permute-start.25 = (bf16[2,2,2,160,128]{4,3,2,1,0:T(8,128)(2,1)S(1)}, bf16[2,2,2,160,128]{4,3,2,1,0:T(8,128)(2,1)S(1)}, u32[]{:S(2)}, u32[]{:S(2)}) collective-permute-start(bf16[2,2,2,160,128]{4,3,2,1,0:T(8,128)(2,1)S(1)} %get-tuple-element.86), channel_id=1, source_target_pairs={{0,4},{2,6},{4,0},{6,2},{8,12},{10,14},{12,8},{14,10},{16,20},{18,... | collective-permute-start | bytes 983048 | tf_op jit(solution)/shard_map/ppermute | solution.py:21
  94.7 5.6 %collective-permute-start.17 = (bf16[16,128,128]{2,1,0:T(8,128)(2,1)S(1)}, bf16[16,128,128]{2,1,0:T(8,128)(2,1)S(1)}, u32[]{:S(2)}, u32[]{:S(2)}) collective-permute-start(bf16[16,128,128]{2,1,0:T(8,128)(2,1)S(1)} %bitcast.318), channel_id=1, source_target_pairs={{0,1},{1,0},{2,3},{3,2},{4,5},{5,4},{6,7},{7,6},{8,9},{9,8},{10,11... | collective-permute-start | bytes 1572872 | tf_op jit(solution)/shard_map/ppermute | solution.py:21
  98.6 3.7 %collective-permute-start.26 = (bf16[16,176,128]{2,1,0:T(8,128)(2,1)S(1)}, bf16[16,176,128]{2,1,0:T(8,128)(2,1)S(1)}, u32[]{:S(2)}, u32[]{:S(2)}) collective-permute-start(bf16[16,176,128]{2,1,0:T(8,128)(2,1)S(1)} %bitcast.314), channel_id=1, source_target_pairs={{0,1},{1,0},{2,3},{3,2},{4,5},{5,4},{6,7},{7,6},{8,9},{9,8},{10,11... | collective-permute-start | bytes 2162696 | tf_op jit(solution)/shard_map/ppermute | solution.py:21
  100.1 2.2 collective-permute-start.27
  119.3 3.6 %collective-permute-start.28 = (f32[4,256]{1,0:T(4,128)S(1)}, f32[4,256]{1,0:T(4,128)S(1)}, u32[]{:S(2)}, u32[]{:S(2)}) collective-permute-start(f32[4,256]{1,0:T(4,128)S(1)} %slice.408), channel_id=1, source_target_pairs={{0,2},{2,0},{4,6},{6,4},{8,10},{10,8},{12,14},{14,12},{16,18},{18,... | collective-permute-start | bytes 12296 | tf_op jit(solution)/shard_map/ppermute | solution.py:21
  123.0 3.7 %collective-permute-start.29 = (f32[4,256]{1,0:T(4,128)S(1)}, f32[4,256]{1,0:T(4,128)S(1)}, u32[]{:S(2)}, u32[]{:S(2)}) collective-permute-start(f32[4,256]{1,0:T(4,128)S(1)} %pad_maximum_fusion.28), channel_id=1, source_target_pairs={{0,4},{2,6},{4,0},{6,2},{8,12},{10,14},{12,8},{14,10},{16,20},{18,... | collective-permute-start | bytes 12296 | tf_op jit(solution)/shard_map/ppermute | solution.py:21
  126.7 3.7 %collective-permute-start.30 = (f32[4,256]{1,0:T(4,128)S(1)}, f32[4,256]{1,0:T(4,128)S(1)}, u32[]{:S(2)}, u32[]{:S(2)}) collective-permute-start(f32[4,256]{1,0:T(4,128)S(1)} %pad_maximum_fusion.29), channel_id=1, source_target_pairs={{0,8},{2,10},{4,12},{6,14},{8,0},{10,2},{12,4},{14,6},{16,24},{18,... | collective-permute-start | bytes 12296 | tf_op jit(solution)/shard_map/ppermute | solution.py:21
  130.4 4.6 %collective-permute-start.31 = (f32[4,256]{1,0:T(4,128)S(1)}, f32[4,256]{1,0:T(4,128)S(1)}, u32[]{:S(2)}, u32[]{:S(2)}) collective-permute-start(f32[4,256]{1,0:T(4,128)S(1)} %pad_maximum_fusion.30), channel_id=1, source_target_pairs={{0,16},{2,18},{4,20},{6,22},{8,24},{10,26},{12,28},{14,30},{16,0},... | collective-permute-start | bytes 12296 | tf_op jit(solution)/shard_map/ppermute | solution.py:21
  135.1 1.2 collective-permute-start.32
  136.4 17.0 %copy-start.12 = (bf16[2,2,2,2,16,1920]{5,4,3,2,1,0:T(8,128)(2,1)S(1)}, bf16[2,2,2,2,16,1920]{5,4,3,2,1,0:T(8,128)(2,1)}, u32[]{:S(2)}) copy-start(bf16[2,2,2,2,16,1920]{5,4,3,2,1,0:T(8,128)(2,1)} %copy-done.10) | copy-start | bytes 2949124
  153.2 3.9 %collective-permute-start.33 = (bf16[8,2,448,128]{3,2,1,0:T(8,128)(2,1)S(1)}, bf16[8,2,448,128]{3,2,1,0:T(8,128)(2,1)S(1)}, u32[]{:S(2)}, u32[]{:S(2)}) collective-permute-start(bf16[8,2,448,128]{3,2,1,0:T(8,128)(2,1)S(1)} %get-tuple-element.40), channel_id=1, source_target_pairs={{0,1},{1,0},{2,3},{3,2},{4,5},{5,4},{6,7},{7,6},{8,9},{9,8},{10,11... | collective-permute-start | bytes 5505032 | tf_op jit(solution)/shard_map/ppermute | solution.py:21
  157.8 9.8 %collective-permute-start.42 = (bf16[2,2,2,112,128]{4,3,2,1,0:T(8,128)(2,1)S(1)}, bf16[2,2,2,112,128]{4,3,2,1,0:T(8,128)(2,1)S(1)}, u32[]{:S(2)}, u32[]{:S(2)}) collective-permute-start(bf16[2,2,2,112,128]{4,3,2,1,0:T(8,128)(2,1)S(1)} %fusion.69), channel_id=1, source_target_pairs={{0,8},{2,10},{4,12},{6,14},{8,0},{10,2},{12,4},{14,6},{16,24},{18,... | collective-permute-start | bytes 688136 | tf_op jit(solution)/shard_map/ppermute | solution.py:21
  159.5 10.5 %collective-permute-start.38 = (bf16[2,2,2,160,128]{4,3,0,1,2:T(8,128)(2,1)S(1)}, bf16[2,2,2,160,128]{4,3,0,1,2:T(8,128)(2,1)S(1)}, u32[]{:S(2)}, u32[]{:S(2)}) collective-permute-start(bf16[2,2,2,160,128]{4,3,0,1,2:T(8,128)(2,1)S(1)} %fusion.51), channel_id=1, source_target_pairs={{0,4},{2,6},{4,0},{6,2},{8,12},{10,14},{12,8},{14,10},{16,20},{18,... | collective-permute-start | bytes 983048 | tf_op jit(solution)/shard_map/ppermute | solution.py:21
  160.5 16.4 %collective-permute-start.34 = (bf16[2,2,2,176,128]{4,3,0,1,2:T(8,128)(2,1)S(1)}, bf16[2,2,2,176,128]{4,3,0,1,2:T(8,128)(2,1)S(1)}, u32[]{:S(2)}, u32[]{:S(2)}) collective-permute-start(bf16[2,2,2,176,128]{4,3,0,1,2:T(8,128)(2,1)S(1)} %fusion.45), channel_id=1, source_target_pairs={{0,2},{2,0},{4,6},{6,4},{8,10},{10,8},{12,14},{14,12},{16,18},{18,... | collective-permute-start | bytes 1081352 | tf_op jit(solution)/shard_map/ppermute | solution.py:21
  167.7 7.5 %collective-permute-start.43 = (bf16[2,2,112,128]{3,2,1,0:T(8,128)(2,1)S(1)}, bf16[2,2,112,128]{3,2,1,0:T(8,128)(2,1)S(1)}, u32[]{:S(2)}, u32[]{:S(2)}) collective-permute-start(bf16[2,2,112,128]{3,2,1,0:T(8,128)(2,1)S(1)} %fusion.84), channel_id=1, source_target_pairs={{0,16},{2,18},{4,20},{6,22},{8,24},{10,26},{12,28},{14,30},{16,0},... | collective-permute-start | bytes 344072 | tf_op jit(solution)/shard_map/ppermute | solution.py:21
  170.1 13.4 %collective-permute-start.39 = (bf16[2,2,160,128]{3,2,0,1:T(8,128)(2,1)S(1)}, bf16[2,2,160,128]{3,2,0,1:T(8,128)(2,1)S(1)}, u32[]{:S(2)}, u32[]{:S(2)}) collective-permute-start(bf16[2,2,160,128]{3,2,0,1:T(8,128)(2,1)S(1)} %fusion.79), channel_id=1, source_target_pairs={{0,2},{2,0},{4,6},{6,4},{8,10},{10,8},{12,14},{14,12},{16,18},{18,... | collective-permute-start | bytes 491528 | tf_op jit(solution)/shard_map/ppermute | solution.py:21
  175.3 4.2 %collective-permute-start.44 = (bf16[2,112,128]{2,1,0:T(8,128)(2,1)S(1)}, bf16[2,112,128]{2,1,0:T(8,128)(2,1)S(1)}, u32[]{:S(2)}, u32[]{:S(2)}) collective-permute-start(bf16[2,112,128]{2,1,0:T(8,128)(2,1)S(1)} %fusion.95), channel_id=1, source_target_pairs={{0,4},{2,6},{4,0},{6,2},{8,12},{10,14},{12,8},{14,10},{16,20},{18,... | collective-permute-start | bytes 172040 | tf_op jit(solution)/shard_map/ppermute | solution.py:21
  179.5 3.9 %collective-permute-start.45 = (bf16[112,128]{1,0:T(8,128)(2,1)S(1)}, bf16[112,128]{1,0:T(8,128)(2,1)S(1)}, u32[]{:S(2)}, u32[]{:S(2)}) collective-permute-start(bf16[112,128]{1,0:T(8,128)(2,1)S(1)} %fusion.103), channel_id=1, source_target_pairs={{0,2},{2,0},{4,6},{6,4},{8,10},{10,8},{12,14},{14,12},{16,18},{18,... | collective-permute-start | bytes 86024 | tf_op jit(solution)/shard_map/ppermute | solution.py:21
  180.7 15.3 %copy-start.20 = (f32[448]{0:T(512)S(1)}, f32[448]{0:T(512)}, u32[]{:S(2)}) copy-start(f32[448]{0:T(512)} %param.15) | copy-start | bytes 5380
  180.7 5.6 %collective-permute-start.35 = (bf16[2,2,176,128]{3,2,0,1:T(8,128)(2,1)S(1)}, bf16[2,2,176,128]{3,2,0,1:T(8,128)(2,1)S(1)}, u32[]{:S(2)}, u32[]{:S(2)}) collective-permute-start(bf16[2,2,176,128]{3,2,0,1:T(8,128)(2,1)S(1)} %fusion.73), channel_id=1, source_target_pairs={{0,4},{2,6},{4,0},{6,2},{8,12},{10,14},{12,8},{14,10},{16,20},{18,... | collective-permute-start | bytes 540680 | tf_op jit(solution)/shard_map/ppermute | solution.py:21
  183.5 4.5 %collective-permute-start.40 = (bf16[2,160,128]{2,1,0:T(8,128)(2,1)S(1)}, bf16[2,160,128]{2,1,0:T(8,128)(2,1)S(1)}, u32[]{:S(2)}, u32[]{:S(2)}) collective-permute-start(bf16[2,160,128]{2,1,0:T(8,128)(2,1)S(1)} %fusion.92), channel_id=1, source_target_pairs={{0,8},{2,10},{4,12},{6,14},{8,0},{10,2},{12,4},{14,6},{16,24},{18,... | collective-permute-start | bytes 245768 | tf_op jit(solution)/shard_map/ppermute | solution.py:21
  186.3 4.6 %collective-permute-start.36 = (bf16[2,176,128]{2,1,0:T(8,128)(2,1)S(1)}, bf16[2,176,128]{2,1,0:T(8,128)(2,1)S(1)}, u32[]{:S(2)}, u32[]{:S(2)}) collective-permute-start(bf16[2,176,128]{2,1,0:T(8,128)(2,1)S(1)} %fusion.88), channel_id=1, source_target_pairs={{0,8},{2,10},{4,12},{6,14},{8,0},{10,2},{12,4},{14,6},{16,24},{18,... | collective-permute-start | bytes 270344 | tf_op jit(solution)/shard_map/ppermute | solution.py:21
  188.1 5.7 %collective-permute-start.41 = (bf16[160,128]{1,0:T(8,128)(2,1)S(1)}, bf16[160,128]{1,0:T(8,128)(2,1)S(1)}, u32[]{:S(2)}, u32[]{:S(2)}) collective-permute-start(bf16[160,128]{1,0:T(8,128)(2,1)S(1)} %fusion.99), channel_id=1, source_target_pairs={{0,16},{2,18},{4,20},{6,22},{8,24},{10,26},{12,28},{14,30},{16,0},... | collective-permute-start | bytes 122888 | tf_op jit(solution)/shard_map/ppermute | solution.py:21
  190.9 5.0 %collective-permute-start.37 = (bf16[176,128]{1,0:T(8,128)(2,1)S(1)}, bf16[176,128]{1,0:T(8,128)(2,1)S(1)}, u32[]{:S(2)}, u32[]{:S(2)}) collective-permute-start(bf16[176,128]{1,0:T(8,128)(2,1)S(1)} %fusion.98), channel_id=1, source_target_pairs={{0,16},{2,18},{4,20},{6,22},{8,24},{10,26},{12,28},{14,30},{16,0},... | collective-permute-start | bytes 135176 | tf_op jit(solution)/shard_map/ppermute | solution.py:21
  196.1 5.9 %collective-permute-start.46 = (bf16[448,128]{1,0:T(8,128)(2,1)S(1)}, bf16[448,128]{1,0:T(8,128)(2,1)S(1)}, u32[]{:S(2)}, u32[]{:S(2)}) collective-permute-start(bf16[448,128]{1,0:T(8,128)(2,1)S(1)} %fusion.55), channel_id=1, source_target_pairs={{0,1},{1,0},{2,3},{3,2},{4,5},{5,4},{6,7},{7,6},{8,9},{9,8},{10,11... | collective-permute-start | bytes 344072 | tf_op jit(solution)/shard_map/ppermute | solution.py:21
  207.4 18.0 %collective-permute-start.47 = (bf16[2,2,2,16,2688]{4,3,0,1,2:T(8,128)(2,1)S(1)}, bf16[2,2,2,16,2688]{4,3,0,1,2:T(8,128)(2,1)S(1)}, u32[]{:S(2)}, u32[]{:S(2)}) collective-permute-start(bf16[2,2,2,16,2688]{4,3,0,1,2:T(8,128)(2,1)S(1)} %fusion.34), channel_id=1, source_target_pairs={{0,2},{2,0},{4,6},{6,4},{8,10},{10,8},{12,14},{14,12},{16,18},{18,... | collective-permute-start | bytes 2064392 | tf_op jit(solution)/shard_map/ppermute | solution.py:21
  209.1 13.3 %collective-permute-start.51 = (bf16[2,2,2,16,1792]{4,3,2,1,0:T(8,128)(2,1)S(1)}, bf16[2,2,2,16,1792]{4,3,2,1,0:T(8,128)(2,1)S(1)}, u32[]{:S(2)}, u32[]{:S(2)}) collective-permute-start(bf16[2,2,2,16,1792]{4,3,2,1,0:T(8,128)(2,1)S(1)} %fusion.42), channel_id=1, source_target_pairs={{0,8},{2,10},{4,12},{6,14},{8,0},{10,2},{12,4},{14,6},{16,24},{18,... | collective-permute-start | bytes 1376264 | tf_op jit(solution)/shard_map/ppermute | solution.py:21
  209.7 17.8 %collective-permute-start.55 = (bf16[2,2,2,16,2688]{4,3,0,1,2:T(8,128)(2,1)S(1)}, bf16[2,2,2,16,2688]{4,3,0,1,2:T(8,128)(2,1)S(1)}, u32[]{:S(2)}, u32[]{:S(2)}) collective-permute-start(bf16[2,2,2,16,2688]{4,3,0,1,2:T(8,128)(2,1)S(1)} %fusion.35), channel_id=1, source_target_pairs={{0,4},{2,6},{4,0},{6,2},{8,12},{10,14},{12,8},{14,10},{16,20},{18,... | collective-permute-start | bytes 2064392 | tf_op jit(solution)/shard_map/ppermute | solution.py:21
  222.6 13.2 %collective-permute-start.52 = (bf16[2,2,16,1792]{3,2,1,0:T(8,128)(2,1)S(1)}, bf16[2,2,16,1792]{3,2,1,0:T(8,128)(2,1)S(1)}, u32[]{:S(2)}, u32[]{:S(2)}) collective-permute-start(bf16[2,2,16,1792]{3,2,1,0:T(8,128)(2,1)S(1)} %fusion.68), channel_id=1, source_target_pairs={{0,16},{2,18},{4,20},{6,22},{8,24},{10,26},{12,28},{14,30},{16,0},... | collective-permute-start | bytes 688136 | tf_op jit(solution)/shard_map/ppermute | solution.py:21
  225.5 21.5 %collective-permute-start.48 = (bf16[2,2,16,2688]{3,2,0,1:T(8,128)(2,1)S(1)}, bf16[2,2,16,2688]{3,2,0,1:T(8,128)(2,1)S(1)}, u32[]{:S(2)}, u32[]{:S(2)}) collective-permute-start(bf16[2,2,16,2688]{3,2,0,1:T(8,128)(2,1)S(1)} %fusion.47), channel_id=1, source_target_pairs={{0,4},{2,6},{4,0},{6,2},{8,12},{10,14},{12,8},{14,10},{16,20},{18,... | collective-permute-start | bytes 1032200 | tf_op jit(solution)/shard_map/ppermute | solution.py:21
  227.6 14.3 %copy-start.9 = (bf16[2,2,2,2,16,2688]{5,4,0,1,2,3:T(8,128)(2,1)S(1)}, bf16[2,2,2,2,16,2688]{5,4,0,1,2,3:T(8,128)(2,1)}, u32[]{:S(2)}) copy-start(bf16[2,2,2,2,16,2688]{5,4,0,1,2,3:T(8,128)(2,1)} %copy-done.8) | copy-start | bytes 4128772
  235.8 4.9 %collective-permute-start.53 = (bf16[2,16,1792]{2,1,0:T(8,128)(2,1)S(1)}, bf16[2,16,1792]{2,1,0:T(8,128)(2,1)S(1)}, u32[]{:S(2)}, u32[]{:S(2)}) collective-permute-start(bf16[2,16,1792]{2,1,0:T(8,128)(2,1)S(1)} %fusion.85), channel_id=1, source_target_pairs={{0,4},{2,6},{4,0},{6,2},{8,12},{10,14},{12,8},{14,10},{16,20},{18,... | collective-permute-start | bytes 344072 | tf_op jit(solution)/shard_map/ppermute | solution.py:21
  236.6 10.5 %collective-permute-start.56 = (bf16[2,2,16,2688]{3,2,0,1:T(8,128)(2,1)S(1)}, bf16[2,2,16,2688]{3,2,0,1:T(8,128)(2,1)S(1)}, u32[]{:S(2)}, u32[]{:S(2)}) collective-permute-start(bf16[2,2,16,2688]{3,2,0,1:T(8,128)(2,1)S(1)} %fusion.48), channel_id=1, source_target_pairs={{0,2},{2,0},{4,6},{6,4},{8,10},{10,8},{12,14},{14,12},{16,18},{18,... | collective-permute-start | bytes 1032200 | tf_op jit(solution)/shard_map/ppermute | solution.py:21
  240.7 6.2 %collective-permute-start.54 = (bf16[16,1792]{1,0:T(8,128)(2,1)S(1)}, bf16[16,1792]{1,0:T(8,128)(2,1)S(1)}, u32[]{:S(2)}, u32[]{:S(2)}) collective-permute-start(bf16[16,1792]{1,0:T(8,128)(2,1)S(1)} %fusion.96), channel_id=1, source_target_pairs={{0,2},{2,0},{4,6},{6,4},{8,10},{10,8},{12,14},{14,12},{16,18},{18,... | collective-permute-start | bytes 172040 | tf_op jit(solution)/shard_map/ppermute | solution.py:21
  247.1 6.4 %collective-permute-start.49 = (bf16[2,16,2688]{2,1,0:T(8,128)(2,1)S(1)}, bf16[2,16,2688]{2,1,0:T(8,128)(2,1)S(1)}, u32[]{:S(2)}, u32[]{:S(2)}) collective-permute-start(bf16[2,16,2688]{2,1,0:T(8,128)(2,1)S(1)} %fusion.75), channel_id=1, source_target_pairs={{0,8},{2,10},{4,12},{6,14},{8,0},{10,2},{12,4},{14,6},{16,24},{18,... | collective-permute-start | bytes 516104 | tf_op jit(solution)/shard_map/ppermute | solution.py:21
  247.3 9.0 %collective-permute-start.57 = (bf16[2,16,2688]{2,1,0:T(8,128)(2,1)S(1)}, bf16[2,16,2688]{2,1,0:T(8,128)(2,1)S(1)}, u32[]{:S(2)}, u32[]{:S(2)}) collective-permute-start(bf16[2,16,2688]{2,1,0:T(8,128)(2,1)S(1)} %fusion.76), channel_id=1, source_target_pairs={{0,8},{2,10},{4,12},{6,14},{8,0},{10,2},{12,4},{14,6},{16,24},{18,... | collective-permute-start | bytes 516104 | tf_op jit(solution)/shard_map/ppermute | solution.py:21
  252.0 10.7 %copy-start.19 = (f32[3584]{0:T(1024)S(1)}, f32[3584]{0:T(1024)}, u32[]{:S(2)}) copy-start(f32[3584]{0:T(1024)} %param.14) | copy-start | bytes 43012
  252.0 13.3 %copy-start.22 = (f32[16]{0:T(128)S(1)}, f32[16]{0:T(128)}, u32[]{:S(2)}) copy-start(f32[16]{0:T(128)} %copy-done.21) | copy-start | bytes 196
  253.6 6.4 %collective-permute-start.50 = (bf16[16,2688]{1,0:T(8,128)(2,1)S(1)}, bf16[16,2688]{1,0:T(8,128)(2,1)S(1)}, u32[]{:S(2)}, u32[]{:S(2)}) collective-permute-start(bf16[16,2688]{1,0:T(8,128)(2,1)S(1)} %fusion.90), channel_id=1, source_target_pairs={{0,16},{2,18},{4,20},{6,22},{8,24},{10,26},{12,28},{14,30},{16,0},... | collective-permute-start | bytes 258056 | tf_op jit(solution)/shard_map/ppermute | solution.py:21
  256.3 6.4 %collective-permute-start.58 = (bf16[16,2688]{1,0:T(8,128)(2,1)S(1)}, bf16[16,2688]{1,0:T(8,128)(2,1)S(1)}, u32[]{:S(2)}, u32[]{:S(2)}) collective-permute-start(bf16[16,2688]{1,0:T(8,128)(2,1)S(1)} %fusion.91), channel_id=1, source_target_pairs={{0,16},{2,18},{4,20},{6,22},{8,24},{10,26},{12,28},{14,30},{16,0},... | collective-permute-start | bytes 258056 | tf_op jit(solution)/shard_map/ppermute | solution.py:21
  (21 other events, 77.5 us)

commit v3 on v2

--- a/solution.py
+++ b/solution.py
@@ -25,43 +25,65 @@
     return lax.axis_size(axis).bit_length() - 1
 
 
-def gather(array, order):
-    count, shape = len(order), array.shape
-    for bit in order:
-        array = jnp.stack([array, from_partner(array, "seq", 1 << bit)])
+def zero_of(array, shape):
+    array = array[(0,) * (array.ndim - len(shape))] if array.ndim > len(shape) else array
+    array = array[tuple(slice(0, size) for size in shape[len(shape) - array.ndim :])]
+    return array * 0
+
+
+def in_order(array, order):
+    count = len(order)
     dims = [count - 1 - order.index(bit) for bit in reversed(range(count))]
     array = array.transpose(dims + list(range(count, array.ndim)))
-    return array.reshape((1 << count,) + shape)
-
-
-def scatter(arrays, orders, beside=()):
+    return array.reshape((1 << count,) + array.shape[count:])
+
+
+def gather(first, second, third):
+    high = list(reversed(range(2, bits_of("seq"))))
+    came = []
+    for bit in high:
+        came = [from_partner(first, "seq", 1 << bit), from_partner(second, "seq", 1 << bit)]
+        if bit == high[0]:
+            third = third + zero_of(came[0], third.shape) + zero_of(came[1], third.shape)
+        first, second = jnp.stack([first, came[0]]), jnp.stack([second, came[1]])
+    for bit in (0, 1):
+        first = jnp.stack([first, from_partner(first, "seq", 2 >> bit)])
+        second = jnp.stack([second, from_partner(second, "seq", 1 << bit)])
+        third = jnp.stack([third, from_partner(third, "seq", 1 << bit)])
+    for block in came:
+        third = third + zero_of(block, third.shape[2:])
+    for bit in high:
+        third = jnp.stack([third, from_partner(third, "seq", 1 << bit)])
+    return in_order(first, high + [1, 0]), in_order(second, high + [0, 1]), in_order(third, [0, 1] + high)
+
+
+def scatter(arrays, beside=()):
     count = bits_of("seq")
     arrays = [array.reshape((2,) * count + array.shape[1:]) for array in arrays]
+    low, high = [0, 1], list(range(2, count))
+    orders = [low + high, low[::-1] + high, high + low[::-1]]
     left = [list(reversed(range(count))) for _ in arrays]
     results = []
+    last = None
     for step in range(count):
+        kept, came = [], []
         for k, order in enumerate(orders):
             bit = order[step]
             dim = left[k].index(bit)
             left[k].remove(bit)
             sent = lax.index_in_dim(arrays[k], 1, dim, keepdims=False).astype(bf16)
-            tied = k == 0 and step < len(beside)
-            if tied:
-                work, argument = beside[step]
-                sent, argument = lax.optimization_barrier((sent, argument))
-            came = from_partner(sent, "seq", 1 << bit)
-            if tied:
-                result, mark = work(argument, results)
-                came, mark = lax.optimization_barrier((came, mark))
-                results.append(result)
-            kept = lax.index_in_dim(arrays[k], 0, dim, keepdims=False).astype(f32)
-            arrays[k] = kept + came.astype(f32)
+            kept.append(lax.index_in_dim(arrays[k], 0, dim, keepdims=False).astype(f32))
+            came.append(from_partner(sent, "seq", 1 << bit))
+        sums = [one + other.astype(f32) for one, other in zip(kept, came)]
+        if step < len(beside):
+            result, zeros = beside[step](last, sums[0].shape, results)
+            results.append(result)
+            if zeros is not None:
+                sums[0] = sums[0] + zeros
+        if step < 2:
+            sums[2] = sums[2] + zero_of(came[0], sums[2].shape) + zero_of(came[1], sums[2].shape)
+        arrays, last = sums, came[0]
     return arrays, results
-
-
-def orders_of():
-    down = list(reversed(range(bits_of("seq"))))
-    return [down, down[:-2] + [0, 1], [0, 1] + down[:-2]]
 
 
 def cut_in_three(size, unit):
@@ -262,17 +284,20 @@
 
 
 def grad_head_kernel(left, features, *refs):
-    out, mark = refs[-2:]
+    out, zeros = refs[-2:]
     out[...] = lax.dot_general(
         left[...], features[...], (((1,), (1,)), ((), ())), preferred_element_type=f32
     ).astype(bf16)
-    mark[...] = jnp.zeros_like(mark)
-
-
-def grad_head_rows(left, features, index, count, before):
+
+    @pl.when(pl.program_id(0) == 0)
+    def _():
+        zeros[...] = jnp.zeros_like(zeros)
+
+
+def grad_head_rows(left, features, index, count, later_than, shape, before):
     vocab, tokens = left.shape
     rows, tile = vocab // count, 1024
-    given = () if before is None else (before,)
+    given = (later_than,) if before is None else (later_than, before)
     return pl.pallas_call(
         grad_head_kernel,
         grid=(D // tile,),
@@ -283,13 +308,13 @@
         ],
         out_specs=[
             pl.BlockSpec((rows, tile), lambda i: (index, i)),
-            pl.BlockSpec((8, 128), lambda i: (0, 0)),
+            pl.BlockSpec(shape, lambda i: (0,) * len(shape)),
         ],
         out_shape=[
             jax.ShapeDtypeStruct((vocab, D), bf16),
-            jax.ShapeDtypeStruct((8, 128), f32),
-        ],
-        input_output_aliases={2: 0} if given else {},
+            jax.ShapeDtypeStruct(shape, f32),
+        ],
+        input_output_aliases={3: 0} if before is not None else {},
         compiler_params=pltpu.CompilerParams(vmem_limit_bytes=20 << 20),
         cost_estimate=pl.CostEstimate(
             flops=2 * rows * D * tokens, bytes_accessed=2 * rows * D + 2 * D * tokens, transcendentals=0
@@ -344,8 +369,6 @@
     rest_count,
 ):
     blocks, cores = lax.axis_size("seq"), lax.axis_size("tp")
-    down = orders_of()
-    up = [order[::-1] for order in down]
     me = lax.axis_index("seq")
     rows, width = prev_hidden.shape
     features = proj_hidden.shape[1]
@@ -380,9 +403,8 @@
     facts = jnp.concatenate([facts, gain_parts], axis=1)
     facts = jnp.pad(facts, ((0, 0), (0, 128 - facts.shape[1])))
 
-    first = gather(first, down[0]).reshape(tokens, main)
-    second = gather(second, down[1]).reshape(tokens, main)
-    third = gather(jnp.concatenate([third, facts], axis=1), down[2])
+    first, second, third = gather(first, second, jnp.concatenate([third, facts], axis=1))
+    first, second = first.reshape(tokens, main), second.reshape(tokens, main)
     third = third.reshape(tokens, 2 * rest + 128)
 
     row = lax.broadcasted_iota(i32, (tokens, 1), 0)
@@ -422,13 +444,10 @@
     square_parts = jnp.stack(in_parts(jnp.sum(mixed_f * mixed_f, axis=0))).astype(bf16)
     square_parts = jnp.pad(square_parts, ((0, 13), (0, 0)))
     one, two = cut_in_three(features, 16)
-    pieces = [
-        gather(part, order)
-        for part, order in zip(
-            (mixed[:one], mixed[one:two], jnp.concatenate([mixed[two:], square_parts], axis=0)),
-            down,
-        )
-    ]
+    pieces = gather(
+        mixed[:one], mixed[one:two], jnp.concatenate([mixed[two:], square_parts], axis=0)
+    )
+    pieces = list(pieces)
     for mask in tp_masks():
         pieces = pieces + [from_partner(piece, "tp", mask) for piece in pieces[:3]]
     squares = [
@@ -445,8 +464,9 @@
     forward = head_logits if fits else plain_logits
     logits, stats, final_all = forward(where, ids, scale_final[None, :], gain_all, pieces, head)
     stats = stats[:4]
-    for bit in range(bits_of("seq")):
-        stats = merged([stats, from_partner(stats, "seq", 1 << bit)])
+    for step in range(0, bits_of("seq"), 2):
+        masks = [k << step for k in range(1, min(4, blocks >> step))]
+        stats = merged([stats] + [from_partner(stats, "seq", mask) for mask in masks])
     stats = lanes_by_index(stats)
     stats = merged([stats] + [from_partner(stats, "tp", mask) for mask in tp_masks()])
     row_top, row_total, row_weighted, target_logit = lanes_by_index(stats)
@@ -459,17 +479,24 @@
     dfinal = kept.reshape(blocks, features, lanes)
     for mask in tp_masks():
         piece = sent[..., (mask - 1) * lanes : mask * lanes]
-        dfinal = dfinal + from_partner(piece, "tp", mask).astype(f32).reshape(dfinal.shape)
-
-    def grad_head_piece(index):
-        if fits:
-            return lambda left, results: grad_head_rows(
-                left, final_all, index, 4, results[-1] if results else None
+        from_core = from_partner(piece, "tp", mask)
+        dfinal = dfinal + from_core.astype(f32).reshape(dfinal.shape)
+
+    def grad_head_piece(index, tied):
+        def work(last, shape, results):
+            if not fits:
+                return dot(dlogits, final_all, 1, 1).astype(bf16), None
+            before = results[-1] if results else None
+            shape = shape if tied else (8, 128)
+            out, zeros = grad_head_rows(
+                dlogits, final_all, index, 4, from_core if last is None else last, shape, before
             )
-        return lambda left, results: (dot(left, final_all, 1, 1).astype(bf16), left[:8])
-
-    early = [(grad_head_piece(index), dlogits) for index in range(2 if fits else 1)]
-    dfinal, results = scatter([dfinal[:, :one], dfinal[:, one:two], dfinal[:, two:]], up, early)
+            return out, (zeros if tied else None)
+
+        return work
+
+    early = [grad_head_piece(index, index == 1) for index in range(2 if fits else 1)]
+    dfinal, results = scatter([dfinal[:, :one], dfinal[:, one:two], dfinal[:, two:]], early)
     dfinal = jnp.concatenate(dfinal, axis=0)
 
     total_dot = (coef * (row_weighted / row_total - target_logit))[:lanes] / scale_own
@@ -482,23 +509,18 @@
     back_prev = dot(dmixed_prev, proj_hidden, 0, 1).reshape(blocks, rows, width)
     back_embed = dot(dmixed_embed, proj_embed, 0, 1).reshape(blocks, rows, width)
 
-    def head_grad_end(left, before):
+    def grad_head_end(last, shape, before):
         grad_head = results[-1]
-        mark = left[:8]
         if fits:
             for index in (2, 3):
-                grad_head, mark = grad_head_rows(left, final_all, index, 4, grad_head)
-        return grad_head, mark
-
-    def proj_grad_hidden(given, before):
-        rows_all = jnp.concatenate([first, third[:, :rest]], axis=1)
-        out = dot(rows_all, given, 0, 1).astype(bf16)
-        return out, out[:8]
-
-    def proj_grad_embed(given, before):
-        rows_all = jnp.concatenate([second, third[:, rest : 2 * rest]], axis=1)
-        out = dot(rows_all, given, 0, 1).astype(bf16)
-        return out, out[:8]
+                grad_head, _ = grad_head_rows(
+                    dlogits, final_all, index, 4, dmixed_prev, (8, 128), grad_head
+                )
+        return grad_head, None
+
+    def grad_proj(rows_in, rows_rest, back):
+        rows_all = jnp.concatenate([rows_in, rows_rest], axis=1)
+        return dot(rows_all, back, 0, 1).astype(bf16), None
 
     (one, two, three), results = scatter(
         [
@@ -506,11 +528,10 @@
             back_embed[..., :main],
             jnp.concatenate([back_prev[..., main:], back_embed[..., main:]], axis=-1),
         ],
-        up,
         [
-            (head_grad_end, dlogits),
-            (proj_grad_hidden, dmixed_prev),
-            (proj_grad_embed, dmixed_embed),
+            grad_head_end,
+            lambda *_: grad_proj(first, third[:, :rest], dmixed_prev),
+            lambda *_: grad_proj(second, third[:, rest : 2 * rest], dmixed_embed),
         ],
     )
     grad_head, grad_proj_hidden, grad_proj_embed = results

time: 268 us -> 274 us (1.022)
  waiting for transfers between devices: 92.9 us -> 107 us
  starting transfers between devices: 69.7 us -> 60.6 us
    ppermute x59 -> x61, waiting for transfers between devices: 92.9 us -> 107 us  [from_partner(): return lax.ppermute(array, axis, [(i, i ^ mask) for i in range(size)])]
    ppermute x59 -> x61, starting transfers between devices: 69.7 us -> 60.6 us  [from_partner(): return lax.ppermute(array, axis, [(i, i ^ mask) for i in range(size)])]
  transfers between devices with their start and end apart: 59 -> 61, of which waited for: 41 -> 40; matrix products, arithmetic and copies ran while one was open for 7% -> 7% of each run, Pallas kernels for 9% -> 4%
where the time goes in v3:
time: 274 us; the launch traced here: 273 us
  waiting for transfers between devices  107 us (39%)
  starting transfers between devices  60.6 us (22%)
  Pallas kernels  55.2 us (20%)
  other arithmetic  17.7 us (6%)
  matrix products  14.1 us (5%)
  local copies, waits for them, and re-layouts  9.64 us (4%)
  blocking collectives  5.05 us (2%)
  between operations  3.2 us (1%)
    ppermute x61, waiting for transfers between devices, from_partner(): return lax.ppermute(array, axis, [(i, i ^ mask) for i in range(size)])  107 us
    ppermute x61, starting transfers between devices, from_partner(): return lax.ppermute(array, axis, [(i, i ^ mask) for i in range(size)])  60.6 us
    pallas_call x4, Pallas kernels, grad_head_rows(): pl.pallas_call(grad_head_kernel, grid=(D // tile,), in_specs=[pl.BlockSpe...  23.3 us
    pallas_call x1, Pallas kernels, head_back(): pl.pallas_call(dfinal_kernel, grid_spec=pltpu.PrefetchScalarGridSpec(num_...  16.8 us
    pallas_call x1, Pallas kernels, head_logits(): pl.pallas_call(logits_kernel, grid_spec=pltpu.PrefetchScalarGridSpec(num_...  15.2 us
    dot_general x14, matrix products, dot(): lax.dot_general(left, right, (((on_left,), (on_right,)), ((), ())), preci...  14.1 us
    unnamed x52, local copies, waits for them, and re-layouts  7.21 us
  transfers between devices with their start and end apart: 61, of which 40 were waited for; matrix products, arithmetic and copies ran while one was open for 7% of the time, Pallas kernels for 4%

profile of v3, /device:TPU:0, one launch (start us, length us, event | category | flops | bytes accessed | tf_op | source)
XLA Modules:
  0.0 272.9 jit_solution(5950936466314101098)
XLA Ops:
  2.7 2.6 psum.14
  6.5 4.0 %collective-permute-start = (bf16[16,2688]{1,0:T(8,128)(2,1)S(1)}, bf16[16,2688]{1,0:T(8,128)(2,1)S(1)}, u32[]{:S(2)}, u32[]{:S(2)}) collective-permute-start(bf16[16,2688]{1,0:T(8,128)(2,1)S(1)} %slice.605), channel_id=1, source_target_pairs={{0,16},{2,18},{4,20},{6,22},{8,24},{10,26},{12,28},{14,30},{16,0},... | collective-permute-start | bytes 258056 | tf_op jit(solution)/shard_map/ppermute | solution.py:21
  14.5 3.0 %collective-permute-done = bf16[16,2688]{1,0:T(8,128)(2,1)S(1)} collective-permute-done((bf16[16,2688]{1,0:T(8,128)(2,1)S(1)}, bf16[16,2688]{1,0:T(8,128)(2,1)S(1)}, u32[]{:S(2)}, u32[]{:S(2)}) %collective-permute-start) | collective-permute-done | bytes 86048 | tf_op jit(solution)/shard_map/ppermute | solution.py:21
  17.5 1.4 collective-permute-done.4
  18.9 1.6 collective-permute-start.5
  21.4 1.4 collective-permute-start.1
  23.3 1.6 collective-permute-start.6
  24.9 3.0 %collective-permute-done.7 = bf16[2,16,2688]{2,1,0:T(8,128)(2,1)S(1)} collective-permute-done((bf16[2,16,2688]{2,1,0:T(8,128)(2,1)S(1)}, bf16[2,16,2688]{2,1,0:T(8,128)(2,1)S(1)}, u32[]{:S(2)}, u32[]{:S(2)}) %collective-permute-start.7) | collective-permute-done | bytes 172064 | tf_op jit(solution)/shard_map/ppermute | solution.py:21
  27.9 1.8 collective-permute-done.1
  29.8 1.6 collective-permute-start.2
  32.1 3.0 %collective-permute-start.8 = (bf16[2,2,16,1920]{3,2,1,0:T(8,128)(2,1)S(1)}, bf16[2,2,16,1920]{3,2,1,0:T(8,128)(2,1)S(1)}, u32[]{:S(2)}, u32[]{:S(2)}) collective-permute-start(bf16[2,2,16,1920]{3,2,1,0:T(8,128)(2,1)S(1)} %fusion.61), channel_id=1, source_target_pairs={{0,16},{2,18},{4,20},{6,22},{8,24},{10,26},{12,28},{14,30},{16,0},... | collective-permute-start | bytes 737288 | tf_op jit(solution)/shard_map/ppermute | solution.py:21
  35.2 10.0 %collective-permute-done.8 = bf16[2,2,16,1920]{3,2,1,0:T(8,128)(2,1)S(1)} collective-permute-done((bf16[2,2,16,1920]{3,2,1,0:T(8,128)(2,1)S(1)}, bf16[2,2,16,1920]{3,2,1,0:T(8,128)(2,1)S(1)}, u32[]{:S(2)}, u32[]{:S(2)}) %collective-permute-start.8) | collective-permute-done | bytes 245792 | tf_op jit(solution)/shard_map/ppermute | solution.py:21
  47.1 1.5 collective-permute-start.3
  50.3 7.2 %collective-permute-done.9 = bf16[2,2,2,16,1920]{4,3,2,1,0:T(8,128)(2,1)S(1)} collective-permute-done((bf16[2,2,2,16,1920]{4,3,2,1,0:T(8,128)(2,1)S(1)}, bf16[2,2,2,16,1920]{4,3,2,1,0:T(8,128)(2,1)S(1)}, u32[]{:S(2)}, u32[]{:S(2)}) %collective-permute-start.9) | collective-permute-done | bytes 491552 | tf_op jit(solution)/shard_map/ppermute | solution.py:21
  59.0 1.9 fusion.31
  61.4 5.5 %collective-permute-done.11 = bf16[2,2,2,16,2688]{4,3,2,1,0:T(8,128)(2,1)} collective-permute-done((bf16[2,2,2,16,2688]{4,3,2,1,0:T(8,128)(2,1)}, bf16[2,2,2,16,2688]{4,3,2,1,0:T(8,128)(2,1)}, u32[]{:S(2)}, u32[]{:S(2)}) %collective-permute-start.11) | collective-permute-done | bytes 688160 | tf_op jit(solution)/shard_map/ppermute | solution.py:21
  66.9 1.2 maximum_bitcast_fusion
  71.7 1.3 copy-done.4
  76.7 3.4 %collective-permute-start.14 = (bf16[160,128]{1,0:T(8,128)(2,1)S(1)}, bf16[160,128]{1,0:T(8,128)(2,1)S(1)}, u32[]{:S(2)}, u32[]{:S(2)}) collective-permute-start(bf16[160,128]{1,0:T(8,128)(2,1)S(1)} %get-tuple-element.89), channel_id=1, source_target_pairs={{0,16},{2,18},{4,20},{6,22},{8,24},{10,26},{12,28},{14,30},{16,0},... | collective-permute-start | bytes 122888 | tf_op jit(solution)/shard_map/ppermute | solution.py:21
  80.3 2.4 collective-permute-done.14
  82.7 2.6 collective-permute-done.13
  86.1 3.2 %collective-permute-done.15 = bf16[128,128]{1,0:T(8,128)(2,1)S(1)} collective-permute-done((bf16[128,128]{1,0:T(8,128)(2,1)S(1)}, bf16[128,128]{1,0:T(8,128)(2,1)S(1)}, u32[]{:S(2)}, u32[]{:S(2)}) %collective-permute-start.15) | collective-permute-done | bytes 32800 | tf_op jit(solution)/shard_map/ppermute | solution.py:21
  90.6 1.6 collective-permute-start.22
  92.2 1.5 collective-permute-done.16
  93.7 2.6 collective-permute-start.19
  96.3 4.4 %collective-permute-done.19 = bf16[2,2,128,128]{3,2,1,0:T(8,128)(2,1)S(1)} collective-permute-done((bf16[2,2,128,128]{3,2,1,0:T(8,128)(2,1)S(1)}, bf16[2,2,128,128]{3,2,1,0:T(8,128)(2,1)S(1)}, u32[]{:S(2)}, u32[]{:S(2)}) %collective-permute-start.19) | collective-permute-done | bytes 131104 | tf_op jit(solution)/shard_map/ppermute | solution.py:21
  100.9 1.5 collective-permute-start.23
  103.5 3.7 %collective-permute-done.20 = bf16[2,2,2,128,128]{4,3,2,1,0:T(8,128)(2,1)S(1)} collective-permute-done((bf16[2,2,2,128,128]{4,3,2,1,0:T(8,128)(2,1)S(1)}, bf16[2,2,2,128,128]{4,3,2,1,0:T(8,128)(2,1)S(1)}, u32[]{:S(2)}, u32[]{:S(2)}) %collective-permute-start.20) | collective-permute-done | bytes 262176 | tf_op jit(solution)/shard_map/ppermute | solution.py:21
  109.9 2.0 collective-permute-done.27.refs_4_
  111.9 15.2 %shard_map.146 = (f32[2048,256]{1,0:T(8,128)S(1)}, f32[8,256]{1,0:T(8,128)S(1)}, bf16[7168,256]{1,0:T(8,128)(2,1)S(1)}) custom-call(s32[2]{0:T(128)S(1)} %pad_add_fusion.1.where, s32[1,256]{1,0:T(1,128)S(1)} %pad_add_fusion.ids, f32[1,256]{1,0:T(1,128)S(1)} %fusion.178.scale, f32[56,128]{1,0:T(8,128)S(1)} %reshape_reshape.15.gain, ...), custom_call_target="tpu_custom_call" | custom-call | flops 7516192768 | bytes 36700160 | tf_op jit(solution)/shard_map/pallas_call | solution.py:190
  127.0 1.8 copy-done
  128.9 1.3 collective-permute-start.30
  130.1 1.5 collective-permute-start.29
  133.7 1.5 collective-permute-done.28
  135.3 3.6 %collective-permute-start.33 = (f32[4,256]{1,0:T(4,128)S(1)}, f32[4,256]{1,0:T(4,128)S(1)}, u32[]{:S(2)}, u32[]{:S(2)}) collective-permute-start(f32[4,256]{1,0:T(4,128)S(1)} %fusion.130), channel_id=1, source_target_pairs={{0,24},{2,26},{4,28},{6,30},{8,16},{10,18},{12,20},{14,22},{16,8},... | collective-permute-start | bytes 12296 | tf_op jit(solution)/shard_map/ppermute | solution.py:21
  140.8 2.6 collective-permute-done.32
  144.9 16.8 %shard_map.147 = (f32[8,2,448,128]{3,2,1,0:T(8,128)S(1)}, bf16[8,2,448,128]{3,2,1,0:T(8,128)(2,1)S(1)}, bf16[2048,256]{1,0:T(8,128)(2,1)S(1)}) custom-call(s32[2]{0:T(128)S(1)} %pad_add_fusion.1.where, s32[1,256]{1,0:T(1,128)S(1)} %pad_add_fusion.ids, f32[8,256]{1,0:T(8,128)S(1)} %select_maximum_fusion.rows, f32[2048,256]{1,0:T(8,128)S(1)} %get-tuple-element.29.logits, ...), custom_call_target="tpu_custom_call" | custom-call | flops 7516192768 | bytes 36700160 | tf_op jit(solution)/shard_map/pallas_call | solution.py:254
  161.9 3.6 %collective-permute-done.35.refs_0_ = bf16[8,2,448,128]{3,2,1,0:T(8,128)(2,1)S(1)} collective-permute-done((bf16[8,2,448,128]{3,2,1,0:T(8,128)(2,1)S(1)}, bf16[8,2,448,128]{3,2,1,0:T(8,128)(2,1)S(1)}, u32[]{:S(2)}, u32[]{:S(2)}) %collective-permute-start.35) | collective-permute-done | bytes 1835040 | tf_op jit(solution)/shard_map/ppermute | solution.py:21
  166.9 1.4 collective-permute-start.36
  168.2 5.8 %shard_map.148 = (bf16[2048,7168]{1,0:T(8,128)(2,1)}, f32[8,128]{1,0:T(8,128)}) custom-call(bf16[2048,256]{1,0:T(8,128)(2,1)S(1)} %get-tuple-element.32.left, bf16[7168,256]{1,0:T(8,128)(2,1)S(1)} %copy-done.1, bf16[8,2,448,128]{3,2,1,0:T(8,128)(2,1)S(1)} %collective-permute-done.35.refs_0_), custom_call_target="tpu_custom_call" | custom-call | flops 1879048192 | bytes 11010048 | tf_op jit(solution)/shard_map/pallas_call | solution.py:301
  174.0 2.1 collective-permute-done.40
  176.2 1.3 collective-permute-start.41
  177.7 2.1 collective-permute-start.45
  181.1 5.8 %shard_map.149 = (bf16[2048,7168]{1,0:T(8,128)(2,1)}, f32[2,2,176,128]{3,2,1,0:T(8,128)S(1)}) custom-call(bf16[2048,256]{1,0:T(8,128)(2,1)S(1)} %get-tuple-element.32.left, bf16[7168,256]{1,0:T(8,128)(2,1)S(1)} %copy-done.1, bf16[2,2,2,176,128]{4,3,2,1,0:T(8,128)(2,1)S(1)} %collective-permute-done.36.refs_0_, ...), custom_call_target="tpu_custom_call", output_to_operand_aliasing={{0}: (3, {})} | custom-call | flops 1879048192 | bytes 11010048 | tf_op jit(solution)/shard_map/pallas_call | solution.py:301
  187.0 2.1 collective-permute-start.42
  190.2 1.7 collective-permute-done.42
  193.5 1.4 collective-permute-start.47
  194.8 2.3 collective-permute-done.43
  198.4 3.8 %collective-permute-done.39 = bf16[176,128]{1,0:T(8,128)(2,1)S(1)} collective-permute-done((bf16[176,128]{1,0:T(8,128)(2,1)S(1)}, bf16[176,128]{1,0:T(8,128)(2,1)S(1)}, u32[]{:S(2)}, u32[]{:S(2)}) %collective-permute-start.39) | collective-permute-done | bytes 45088 | tf_op jit(solution)/shard_map/ppermute | solution.py:21
  205.9 1.7 copy-done.5
  209.1 6.0 %shard_map.150 = (bf16[2048,7168]{1,0:T(8,128)(2,1)}, f32[8,128]{1,0:T(8,128)}) custom-call(bf16[2048,256]{1,0:T(8,128)(2,1)S(1)} %get-tuple-element.32.left, bf16[7168,256]{1,0:T(8,128)(2,1)S(1)} %copy-done.1, bf16[448,256]{1,0:T(8,128)(2,1)S(1)} %convolution_convert_fusion.3.refs_0_, ...), custom_call_target="tpu_custom_call", output_to_operand_aliasing={{0}: (3, {})} | custom-call | flops 1879048192 | bytes 11010048 | tf_op jit(solution)/shard_map/pallas_call | solution.py:301
  215.1 5.8 %shard_map.151 = (bf16[2048,7168]{1,0:T(8,128)(2,1)}, f32[8,128]{1,0:T(8,128)}) custom-call(bf16[2048,256]{1,0:T(8,128)(2,1)S(1)} %get-tuple-element.32.left, bf16[7168,256]{1,0:T(8,128)(2,1)S(1)} %copy-done.1, bf16[448,256]{1,0:T(8,128)(2,1)S(1)} %convolution_convert_fusion.3.refs_0_, ...), custom_call_target="tpu_custom_call", output_to_operand_aliasing={{0}: (3, {})} | custom-call | flops 1879048192 | bytes 11010048 | tf_op jit(solution)/shard_map/pallas_call | solution.py:301
  222.2 1.9 collective-permute-start.53
  224.7 2.7 convolution_convert_fusion
  227.4 2.7 convolution_convert_fusion.1
  230.1 8.4 %collective-permute-done.49 = bf16[2,2,2,16,2688]{4,3,2,1,0:T(8,128)(2,1)S(1)} collective-permute-done((bf16[2,2,2,16,2688]{4,3,2,1,0:T(8,128)(2,1)S(1)}, bf16[2,2,2,16,2688]{4,3,2,1,0:T(8,128)(2,1)S(1)}, u32[]{:S(2)}, u32[]{:S(2)}) %collective-permute-start.49) | collective-permute-done | bytes 688160 | tf_op jit(solution)/shard_map/ppermute | solution.py:21
  239.6 2.2 collective-permute-done.54
  242.1 2.5 collective-permute-start.55
  245.1 3.5 %collective-permute-done.50 = bf16[2,2,16,2688]{3,2,1,0:T(8,128)(2,1)S(1)} collective-permute-done((bf16[2,2,16,2688]{3,2,1,0:T(8,128)(2,1)S(1)}, bf16[2,2,16,2688]{3,2,1,0:T(8,128)(2,1)S(1)}, u32[]{:S(2)}, u32[]{:S(2)}) %collective-permute-start.50) | collective-permute-done | bytes 344096 | tf_op jit(solution)/shard_map/ppermute | solution.py:21
  249.7 3.9 %collective-permute-done.55 = bf16[2,2,16,1792]{3,2,1,0:T(8,128)(2,1)S(1)} collective-permute-done((bf16[2,2,16,1792]{3,2,1,0:T(8,128)(2,1)S(1)}, bf16[2,2,16,1792]{3,2,1,0:T(8,128)(2,1)S(1)}, u32[]{:S(2)}, u32[]{:S(2)}) %collective-permute-start.55) | collective-permute-done | bytes 229408 | tf_op jit(solution)/shard_map/ppermute | solution.py:21
  254.5 4.4 %collective-permute-done.57 = bf16[2,16,1792]{2,1,0:T(8,128)(2,1)S(1)} collective-permute-done((bf16[2,16,1792]{2,1,0:T(8,128)(2,1)S(1)}, bf16[2,16,1792]{2,1,0:T(8,128)(2,1)S(1)}, u32[]{:S(2)}, u32[]{:S(2)}) %collective-permute-start.57) | collective-permute-done | bytes 114720 | tf_op jit(solution)/shard_map/ppermute | solution.py:21
  261.0 2.2 collective-permute-done.58
  263.3 4.3 %collective-permute-done.52 = bf16[16,2688]{1,0:T(8,128)(2,1)S(1)} collective-permute-done((bf16[16,2688]{1,0:T(8,128)(2,1)S(1)}, bf16[16,2688]{1,0:T(8,128)(2,1)S(1)}, u32[]{:S(2)}, u32[]{:S(2)}) %collective-permute-start.52) | collective-permute-done | bytes 86048 | tf_op jit(solution)/shard_map/ppermute | solution.py:21
  268.9 2.5 psum.15
  (301 shorter events, 55.0 us)
Async XLA Ops:
  6.5 11.0 %collective-permute-start = (bf16[16,2688]{1,0:T(8,128)(2,1)S(1)}, bf16[16,2688]{1,0:T(8,128)(2,1)S(1)}, u32[]{:S(2)}, u32[]{:S(2)}) collective-permute-start(bf16[16,2688]{1,0:T(8,128)(2,1)S(1)} %slice.605), channel_id=1, source_target_pairs={{0,16},{2,18},{4,20},{6,22},{8,24},{10,26},{12,28},{14,30},{16,0},... | collective-permute-start | bytes 258056 | tf_op jit(solution)/shard_map/ppermute | solution.py:21
  10.5 8.4 %collective-permute-start.4 = (bf16[16,2688]{1,0:T(8,128)(2,1)S(1)}, bf16[16,2688]{1,0:T(8,128)(2,1)S(1)}, u32[]{:S(2)}, u32[]{:S(2)}) collective-permute-start(bf16[16,2688]{1,0:T(8,128)(2,1)S(1)} %slice.606), channel_id=1, source_target_pairs={{0,16},{2,18},{4,20},{6,22},{8,24},{10,26},{12,28},{14,30},{16,0},... | collective-permute-start | bytes 258056 | tf_op jit(solution)/shard_map/ppermute | solution.py:21
  18.9 4.3 %collective-permute-start.5 = (bf16[16,1920]{1,0:T(8,128)(2,1)S(1)}, bf16[16,1920]{1,0:T(8,128)(2,1)S(1)}, u32[]{:S(2)}, u32[]{:S(2)}) collective-permute-start(bf16[16,1920]{1,0:T(8,128)(2,1)S(1)} %fusion.109), channel_id=1, source_target_pairs={{0,2},{2,0},{4,6},{6,4},{8,10},{10,8},{12,14},{14,12},{16,18},{18,... | collective-permute-start | bytes 184328 | tf_op jit(solution)/shard_map/ppermute | solution.py:21
  20.6 7.3 %collective-permute-start.7 = (bf16[2,16,2688]{2,1,0:T(8,128)(2,1)S(1)}, bf16[2,16,2688]{2,1,0:T(8,128)(2,1)S(1)}, u32[]{:S(2)}, u32[]{:S(2)}) collective-permute-start(bf16[2,16,2688]{2,1,0:T(8,128)(2,1)S(1)} %get-tuple-element.74), channel_id=1, source_target_pairs={{0,8},{2,10},{4,12},{6,14},{8,0},{10,2},{12,4},{14,6},{16,24},{18,... | collective-permute-start | bytes 516104 | tf_op jit(solution)/shard_map/ppermute | solution.py:21
  21.4 8.4 %collective-permute-start.1 = (bf16[2,16,2688]{2,1,0:T(8,128)(2,1)S(1)}, bf16[2,16,2688]{2,1,0:T(8,128)(2,1)S(1)}, u32[]{:S(2)}, u32[]{:S(2)}) collective-permute-start(bf16[2,16,2688]{2,1,0:T(8,128)(2,1)S(1)} %get-tuple-element.72), channel_id=1, source_target_pairs={{0,8},{2,10},{4,12},{6,14},{8,0},{10,2},{12,4},{14,6},{16,24},{18,... | collective-permute-start | bytes 516104 | tf_op jit(solution)/shard_map/ppermute | solution.py:21
  23.3 8.8 %collective-permute-start.6 = (bf16[2,16,1920]{2,1,0:T(8,128)(2,1)S(1)}, bf16[2,16,1920]{2,1,0:T(8,128)(2,1)S(1)}, u32[]{:S(2)}, u32[]{:S(2)}) collective-permute-start(bf16[2,16,1920]{2,1,0:T(8,128)(2,1)S(1)} %get-tuple-element.83), channel_id=1, source_target_pairs={{0,4},{2,6},{4,0},{6,2},{8,12},{10,14},{12,8},{14,10},{16,20},{18,... | collective-permute-start | bytes 368648 | tf_op jit(solution)/shard_map/ppermute | solution.py:21
  29.8 16.2 %collective-permute-start.2 = (bf16[2,2,16,2688]{3,2,0,1:T(8,128)(2,1)S(1)}, bf16[2,2,16,2688]{3,2,0,1:T(8,128)(2,1)S(1)}, u32[]{:S(2)}, u32[]{:S(2)}) collective-permute-start(bf16[2,2,16,2688]{3,2,0,1:T(8,128)(2,1)S(1)} %get-tuple-element.60), channel_id=1, source_target_pairs={{0,4},{2,6},{4,0},{6,2},{8,12},{10,14},{12,8},{14,10},{16,20},{18,... | collective-permute-start | bytes 1032200 | tf_op jit(solution)/shard_map/ppermute | solution.py:21
  31.4 17.2 %collective-permute-start.10 = (bf16[2,2,16,2688]{3,2,1,0:T(8,128)(2,1)S(1)}, bf16[2,2,16,2688]{3,2,1,0:T(8,128)(2,1)S(1)}, u32[]{:S(2)}, u32[]{:S(2)}) collective-permute-start(bf16[2,2,16,2688]{3,2,1,0:T(8,128)(2,1)S(1)} %get-tuple-element.62), channel_id=1, source_target_pairs={{0,2},{2,0},{4,6},{6,4},{8,10},{10,8},{12,14},{14,12},{16,18},{18,... | collective-permute-start | bytes 1032200 | tf_op jit(solution)/shard_map/ppermute | solution.py:21
  32.1 13.1 %collective-permute-start.8 = (bf16[2,2,16,1920]{3,2,1,0:T(8,128)(2,1)S(1)}, bf16[2,2,16,1920]{3,2,1,0:T(8,128)(2,1)S(1)}, u32[]{:S(2)}, u32[]{:S(2)}) collective-permute-start(bf16[2,2,16,1920]{3,2,1,0:T(8,128)(2,1)S(1)} %fusion.61), channel_id=1, source_target_pairs={{0,16},{2,18},{4,20},{6,22},{8,24},{10,26},{12,28},{14,30},{16,0},... | collective-permute-start | bytes 737288 | tf_op jit(solution)/shard_map/ppermute | solution.py:21
  45.2 12.3 %collective-permute-start.9 = (bf16[2,2,2,16,1920]{4,3,2,1,0:T(8,128)(2,1)S(1)}, bf16[2,2,2,16,1920]{4,3,2,1,0:T(8,128)(2,1)S(1)}, u32[]{:S(2)}, u32[]{:S(2)}) collective-permute-start(bf16[2,2,2,16,1920]{4,3,2,1,0:T(8,128)(2,1)S(1)} %get-tuple-element.56), channel_id=1, source_target_pairs={{0,8},{2,10},{4,12},{6,14},{8,0},{10,2},{12,4},{14,6},{16,24},{18,... | collective-permute-start | bytes 1474568 | tf_op jit(solution)/shard_map/ppermute | solution.py:21
  47.1 21.1 %collective-permute-start.3 = (bf16[2,2,2,16,2688]{4,3,0,1,2:T(8,128)(2,1)}, bf16[2,2,2,16,2688]{4,3,0,1,2:T(8,128)(2,1)}, u32[]{:S(2)}, u32[]{:S(2)}) collective-permute-start(bf16[2,2,2,16,2688]{4,3,0,1,2:T(8,128)(2,1)} %get-tuple-element.52), channel_id=1, source_target_pairs={{0,2},{2,0},{4,6},{6,4},{8,10},{10,8},{12,14},{14,12},{16,18},{18,... | collective-permute-start | bytes 2064392 | tf_op jit(solution)/shard_map/ppermute | solution.py:21
  49.8 17.1 %collective-permute-start.11 = (bf16[2,2,2,16,2688]{4,3,2,1,0:T(8,128)(2,1)}, bf16[2,2,2,16,2688]{4,3,2,1,0:T(8,128)(2,1)}, u32[]{:S(2)}, u32[]{:S(2)}) collective-permute-start(bf16[2,2,2,16,2688]{4,3,2,1,0:T(8,128)(2,1)} %get-tuple-element.54), channel_id=1, source_target_pairs={{0,4},{2,6},{4,0},{6,2},{8,12},{10,14},{12,8},{14,10},{16,20},{18,... | collective-permute-start | bytes 2064392 | tf_op jit(solution)/shard_map/ppermute | solution.py:21
  75.0 1.6 collective-permute-start.12
  76.7 5.9 %collective-permute-start.14 = (bf16[160,128]{1,0:T(8,128)(2,1)S(1)}, bf16[160,128]{1,0:T(8,128)(2,1)S(1)}, u32[]{:S(2)}, u32[]{:S(2)}) collective-permute-start(bf16[160,128]{1,0:T(8,128)(2,1)S(1)} %get-tuple-element.89), channel_id=1, source_target_pairs={{0,16},{2,18},{4,20},{6,22},{8,24},{10,26},{12,28},{14,30},{16,0},... | collective-permute-start | bytes 122888 | tf_op jit(solution)/shard_map/ppermute | solution.py:21
  80.2 5.2 %collective-permute-start.13 = (bf16[176,128]{1,0:T(8,128)(2,1)S(1)}, bf16[176,128]{1,0:T(8,128)(2,1)S(1)}, u32[]{:S(2)}, u32[]{:S(2)}) collective-permute-start(bf16[176,128]{1,0:T(8,128)(2,1)S(1)} %get-tuple-element.87), channel_id=1, source_target_pairs={{0,16},{2,18},{4,20},{6,22},{8,24},{10,26},{12,28},{14,30},{16,0},... | collective-permute-start | bytes 135176 | tf_op jit(solution)/shard_map/ppermute | solution.py:21
  82.7 7.3 %collective-permute-start.18 = (bf16[2,160,128]{2,1,0:T(8,128)(2,1)S(1)}, bf16[2,160,128]{2,1,0:T(8,128)(2,1)S(1)}, u32[]{:S(2)}, u32[]{:S(2)}) collective-permute-start(bf16[2,160,128]{2,1,0:T(8,128)(2,1)S(1)} %get-tuple-element.93), channel_id=1, source_target_pairs={{0,8},{2,10},{4,12},{6,14},{8,0},{10,2},{12,4},{14,6},{16,24},{18,... | collective-permute-start | bytes 245768 | tf_op jit(solution)/shard_map/ppermute | solution.py:21
  85.4 4.0 %collective-permute-start.15 = (bf16[128,128]{1,0:T(8,128)(2,1)S(1)}, bf16[128,128]{1,0:T(8,128)(2,1)S(1)}, u32[]{:S(2)}, u32[]{:S(2)}) collective-permute-start(bf16[128,128]{1,0:T(8,128)(2,1)S(1)} %fusion.118), channel_id=1, source_target_pairs={{0,2},{2,0},{4,6},{6,4},{8,10},{10,8},{12,14},{14,12},{16,18},{18,... | collective-permute-start | bytes 98312 | tf_op jit(solution)/shard_map/ppermute | solution.py:21
  86.0 4.6 %collective-permute-start.17 = (bf16[2,176,128]{2,1,0:T(8,128)(2,1)S(1)}, bf16[2,176,128]{2,1,0:T(8,128)(2,1)S(1)}, u32[]{:S(2)}, u32[]{:S(2)}) collective-permute-start(bf16[2,176,128]{2,1,0:T(8,128)(2,1)S(1)} %get-tuple-element.91), channel_id=1, source_target_pairs={{0,8},{2,10},{4,12},{6,14},{8,0},{10,2},{12,4},{14,6},{16,24},{18,... | collective-permute-start | bytes 270344 | tf_op jit(solution)/shard_map/ppermute | solution.py:21
  89.4 4.3 %collective-permute-start.16 = (bf16[2,128,128]{2,1,0:T(8,128)(2,1)S(1)}, bf16[2,128,128]{2,1,0:T(8,128)(2,1)S(1)}, u32[]{:S(2)}, u32[]{:S(2)}) collective-permute-start(bf16[2,128,128]{2,1,0:T(8,128)(2,1)S(1)} %get-tuple-element.96), channel_id=1, source_target_pairs={{0,4},{2,6},{4,0},{6,2},{8,12},{10,14},{12,8},{14,10},{16,20},{18,... | collective-permute-start | bytes 196616 | tf_op jit(solution)/shard_map/ppermute | solution.py:21
  90.0 12.4 %collective-permute-start.24 = (bf16[2,2,160,128]{3,2,1,0:T(8,128)(2,1)S(1)}, bf16[2,2,160,128]{3,2,1,0:T(8,128)(2,1)S(1)}, u32[]{:S(2)}, u32[]{:S(2)}) collective-permute-start(bf16[2,2,160,128]{3,2,1,0:T(8,128)(2,1)S(1)} %get-tuple-element.76), channel_id=1, source_target_pairs={{0,2},{2,0},{4,6},{6,4},{8,10},{10,8},{12,14},{14,12},{16,18},{18,... | collective-permute-start | bytes 491528 | tf_op jit(solution)/shard_map/ppermute | solution.py:21
  90.6 10.2 %collective-permute-start.22 = (bf16[2,2,176,128]{3,2,1,0:T(8,128)(2,1)S(1)}, bf16[2,2,176,128]{3,2,1,0:T(8,128)(2,1)S(1)}, u32[]{:S(2)}, u32[]{:S(2)}) collective-permute-start(bf16[2,2,176,128]{3,2,1,0:T(8,128)(2,1)S(1)} %get-tuple-element.70), channel_id=1, source_target_pairs={{0,4},{2,6},{4,0},{6,2},{8,12},{10,14},{12,8},{14,10},{16,20},{18,... | collective-permute-start | bytes 540680 | tf_op jit(solution)/shard_map/ppermute | solution.py:21
  93.7 7.0 %collective-permute-start.19 = (bf16[2,2,128,128]{3,2,1,0:T(8,128)(2,1)S(1)}, bf16[2,2,128,128]{3,2,1,0:T(8,128)(2,1)S(1)}, u32[]{:S(2)}, u32[]{:S(2)}) collective-permute-start(bf16[2,2,128,128]{3,2,1,0:T(8,128)(2,1)S(1)} %fusion.95), channel_id=1, source_target_pairs={{0,16},{2,18},{4,20},{6,22},{8,24},{10,26},{12,28},{14,30},{16,0},... | collective-permute-start | bytes 393224 | tf_op jit(solution)/shard_map/ppermute | solution.py:21
  100.7 6.4 %collective-permute-start.20 = (bf16[2,2,2,128,128]{4,3,2,1,0:T(8,128)(2,1)S(1)}, bf16[2,2,2,128,128]{4,3,2,1,0:T(8,128)(2,1)S(1)}, u32[]{:S(2)}, u32[]{:S(2)}) collective-permute-start(bf16[2,2,2,128,128]{4,3,2,1,0:T(8,128)(2,1)S(1)} %get-tuple-element.66), channel_id=1, source_target_pairs={{0,8},{2,10},{4,12},{6,14},{8,0},{10,2},{12,4},{14,6},{16,24},{18,... | collective-permute-start | bytes 786440 | tf_op jit(solution)/shard_map/ppermute | solution.py:21
  100.9 7.5 %collective-permute-start.23 = (bf16[2,2,2,176,128]{4,3,2,1,0:T(8,128)(2,1)S(1)}, bf16[2,2,2,176,128]{4,3,2,1,0:T(8,128)(2,1)S(1)}, u32[]{:S(2)}, u32[]{:S(2)}) collective-permute-start(bf16[2,2,2,176,128]{4,3,2,1,0:T(8,128)(2,1)S(1)} %get-tuple-element.58), channel_id=1, source_target_pairs={{0,2},{2,0},{4,6},{6,4},{8,10},{10,8},{12,14},{14,12},{16,18},{18,... | collective-permute-start | bytes 1081352 | tf_op jit(solution)/shard_map/ppermute | solution.py:21
  102.4 7.1 %collective-permute-start.25 = (bf16[2,2,2,160,128]{4,3,2,1,0:T(8,128)(2,1)S(1)}, bf16[2,2,2,160,128]{4,3,2,1,0:T(8,128)(2,1)S(1)}, u32[]{:S(2)}, u32[]{:S(2)}) collective-permute-start(bf16[2,2,2,160,128]{4,3,2,1,0:T(8,128)(2,1)S(1)} %get-tuple-element.64), channel_id=1, source_target_pairs={{0,4},{2,6},{4,0},{6,2},{8,12},{10,14},{12,8},{14,10},{16,20},{18,... | collective-permute-start | bytes 983048 | tf_op jit(solution)/shard_map/ppermute | solution.py:21
  107.3 2.6 collective-permute-start.21
  108.5 3.4 %collective-permute-start.26 = (bf16[16,176,128]{2,1,0:T(8,128)(2,1)S(1)}, bf16[16,176,128]{2,1,0:T(8,128)(2,1)S(1)}, u32[]{:S(2)}, u32[]{:S(2)}) collective-permute-start(bf16[16,176,128]{2,1,0:T(8,128)(2,1)S(1)} %bitcast.342), channel_id=1, source_target_pairs={{0,1},{1,0},{2,3},{3,2},{4,5},{5,4},{6,7},{7,6},{8,9},{9,8},{10,11... | collective-permute-start | bytes 2162696 | tf_op jit(solution)/shard_map/ppermute | solution.py:21
  109.7 2.2 collective-permute-start.27
  128.9 4.5 %collective-permute-start.30 = (f32[4,256]{1,0:T(4,128)S(1)}, f32[4,256]{1,0:T(4,128)S(1)}, u32[]{:S(2)}, u32[]{:S(2)}) collective-permute-start(f32[4,256]{1,0:T(4,128)S(1)} %slice.500), channel_id=1, source_target_pairs={{0,6},{2,4},{4,2},{6,0},{8,14},{10,12},{12,10},{14,8},{16,22},{18,... | collective-permute-start | bytes 12296 | tf_op jit(solution)/shard_map/ppermute | solution.py:21
  130.1 3.6 %collective-permute-start.29 = (f32[4,256]{1,0:T(4,128)S(1)}, f32[4,256]{1,0:T(4,128)S(1)}, u32[]{:S(2)}, u32[]{:S(2)}) collective-permute-start(f32[4,256]{1,0:T(4,128)S(1)} %slice.500), channel_id=1, source_target_pairs={{0,4},{2,6},{4,0},{6,2},{8,12},{10,14},{12,8},{14,10},{16,20},{18,... | collective-permute-start | bytes 12296 | tf_op jit(solution)/shard_map/ppermute | solution.py:21
  131.6 3.6 %collective-permute-start.28 = (f32[4,256]{1,0:T(4,128)S(1)}, f32[4,256]{1,0:T(4,128)S(1)}, u32[]{:S(2)}, u32[]{:S(2)}) collective-permute-start(f32[4,256]{1,0:T(4,128)S(1)} %slice.500), channel_id=1, source_target_pairs={{0,2},{2,0},{4,6},{6,4},{8,10},{10,8},{12,14},{14,12},{16,18},{18,... | collective-permute-start | bytes 12296 | tf_op jit(solution)/shard_map/ppermute | solution.py:21
  135.3 5.5 %collective-permute-start.33 = (f32[4,256]{1,0:T(4,128)S(1)}, f32[4,256]{1,0:T(4,128)S(1)}, u32[]{:S(2)}, u32[]{:S(2)}) collective-permute-start(f32[4,256]{1,0:T(4,128)S(1)} %fusion.130), channel_id=1, source_target_pairs={{0,24},{2,26},{4,28},{6,30},{8,16},{10,18},{12,20},{14,22},{16,8},... | collective-permute-start | bytes 12296 | tf_op jit(solution)/shard_map/ppermute | solution.py:21
  138.9 4.5 %collective-permute-start.32 = (f32[4,256]{1,0:T(4,128)S(1)}, f32[4,256]{1,0:T(4,128)S(1)}, u32[]{:S(2)}, u32[]{:S(2)}) collective-permute-start(f32[4,256]{1,0:T(4,128)S(1)} %fusion.130), channel_id=1, source_target_pairs={{0,16},{2,18},{4,20},{6,22},{8,24},{10,26},{12,28},{14,30},{16,0},... | collective-permute-start | bytes 12296 | tf_op jit(solution)/shard_map/ppermute | solution.py:21
  138.9 4.5 %collective-permute-start.31 = (f32[4,256]{1,0:T(4,128)S(1)}, f32[4,256]{1,0:T(4,128)S(1)}, u32[]{:S(2)}, u32[]{:S(2)}) collective-permute-start(f32[4,256]{1,0:T(4,128)S(1)} %fusion.130), channel_id=1, source_target_pairs={{0,8},{2,10},{4,12},{6,14},{8,0},{10,2},{12,4},{14,6},{16,24},{18,... | collective-permute-start | bytes 12296 | tf_op jit(solution)/shard_map/ppermute | solution.py:21
  143.5 1.2 collective-permute-start.34
  161.6 3.9 %collective-permute-start.35 = (bf16[8,2,448,128]{3,2,1,0:T(8,128)(2,1)S(1)}, bf16[8,2,448,128]{3,2,1,0:T(8,128)(2,1)S(1)}, u32[]{:S(2)}, u32[]{:S(2)}) collective-permute-start(bf16[8,2,448,128]{3,2,1,0:T(8,128)(2,1)S(1)} %get-tuple-element.31), channel_id=1, source_target_pairs={{0,1},{1,0},{2,3},{3,2},{4,5},{5,4},{6,7},{7,6},{8,9},{9,8},{10,11... | collective-permute-start | bytes 5505032 | tf_op jit(solution)/shard_map/ppermute | solution.py:21
  166.2 11.4 %collective-permute-start.44 = (bf16[2,2,2,112,128]{4,3,2,1,0:T(8,128)(2,1)S(1)}, bf16[2,2,2,112,128]{4,3,2,1,0:T(8,128)(2,1)S(1)}, u32[]{:S(2)}, u32[]{:S(2)}) collective-permute-start(bf16[2,2,2,112,128]{4,3,2,1,0:T(8,128)(2,1)S(1)} %fusion.78), channel_id=1, source_target_pairs={{0,8},{2,10},{4,12},{6,14},{8,0},{10,2},{12,4},{14,6},{16,24},{18,... | collective-permute-start | bytes 688136 | tf_op jit(solution)/shard_map/ppermute | solution.py:21
  166.3 9.8 %collective-permute-start.40 = (bf16[2,2,2,160,128]{4,3,0,1,2:T(8,128)(2,1)S(1)}, bf16[2,2,2,160,128]{4,3,0,1,2:T(8,128)(2,1)S(1)}, u32[]{:S(2)}, u32[]{:S(2)}) collective-permute-start(bf16[2,2,2,160,128]{4,3,0,1,2:T(8,128)(2,1)S(1)} %fusion.58), channel_id=1, source_target_pairs={{0,4},{2,6},{4,0},{6,2},{8,12},{10,14},{12,8},{14,10},{16,20},{18,... | collective-permute-start | bytes 983048 | tf_op jit(solution)/shard_map/ppermute | solution.py:21
  166.9 10.7 %collective-permute-start.36 = (bf16[2,2,2,176,128]{4,3,2,1,0:T(8,128)(2,1)S(1)}, bf16[2,2,2,176,128]{4,3,2,1,0:T(8,128)(2,1)S(1)}, u32[]{:S(2)}, u32[]{:S(2)}) collective-permute-start(bf16[2,2,2,176,128]{4,3,2,1,0:T(8,128)(2,1)S(1)} %fusion.51), channel_id=1, source_target_pairs={{0,2},{2,0},{4,6},{6,4},{8,10},{10,8},{12,14},{14,12},{16,18},{18,... | collective-permute-start | bytes 1081352 | tf_op jit(solution)/shard_map/ppermute | solution.py:21
  176.2 10.7 %collective-permute-start.41 = (bf16[2,2,160,128]{3,2,0,1:T(8,128)(2,1)S(1)}, bf16[2,2,160,128]{3,2,0,1:T(8,128)(2,1)S(1)}, u32[]{:S(2)}, u32[]{:S(2)}) collective-permute-start(bf16[2,2,160,128]{3,2,0,1:T(8,128)(2,1)S(1)} %fusion.91), channel_id=1, source_target_pairs={{0,2},{2,0},{4,6},{6,4},{8,10},{10,8},{12,14},{14,12},{16,18},{18,... | collective-permute-start | bytes 491528 | tf_op jit(solution)/shard_map/ppermute | solution.py:21
  177.7 11.4 %collective-permute-start.45 = (bf16[2,2,112,128]{3,2,1,0:T(8,128)(2,1)S(1)}, bf16[2,2,112,128]{3,2,1,0:T(8,128)(2,1)S(1)}, u32[]{:S(2)}, u32[]{:S(2)}) collective-permute-start(bf16[2,2,112,128]{3,2,1,0:T(8,128)(2,1)S(1)} %fusion.98), channel_id=1, source_target_pairs={{0,16},{2,18},{4,20},{6,22},{8,24},{10,26},{12,28},{14,30},{16,0},... | collective-permute-start | bytes 344072 | tf_op jit(solution)/shard_map/ppermute | solution.py:21
  179.9 9.2 %collective-permute-start.37 = (bf16[2,2,176,128]{3,2,1,0:T(8,128)(2,1)S(1)}, bf16[2,2,176,128]{3,2,1,0:T(8,128)(2,1)S(1)}, u32[]{:S(2)}, u32[]{:S(2)}) collective-permute-start(bf16[2,2,176,128]{3,2,1,0:T(8,128)(2,1)S(1)} %fusion.85), channel_id=1, source_target_pairs={{0,4},{2,6},{4,0},{6,2},{8,12},{10,14},{12,8},{14,10},{16,20},{18,... | collective-permute-start | bytes 540680 | tf_op jit(solution)/shard_map/ppermute | solution.py:21
  187.0 5.0 %collective-permute-start.42 = (bf16[2,160,128]{2,1,0:T(8,128)(2,1)S(1)}, bf16[2,160,128]{2,1,0:T(8,128)(2,1)S(1)}, u32[]{:S(2)}, u32[]{:S(2)}) collective-permute-start(bf16[2,160,128]{2,1,0:T(8,128)(2,1)S(1)} %fusion.106), channel_id=1, source_target_pairs={{0,8},{2,10},{4,12},{6,14},{8,0},{10,2},{12,4},{14,6},{16,24},{18,... | collective-permute-start | bytes 245768 | tf_op jit(solution)/shard_map/ppermute | solution.py:21
  189.1 13.1 %copy-start.20 = (f32[448]{0:T(512)S(1)}, f32[448]{0:T(512)}, u32[]{:S(2)}) copy-start(f32[448]{0:T(512)} %param.15) | copy-start | bytes 5380
  189.2 4.2 %collective-permute-start.46 = (bf16[2,112,128]{2,1,0:T(8,128)(2,1)S(1)}, bf16[2,112,128]{2,1,0:T(8,128)(2,1)S(1)}, u32[]{:S(2)}, u32[]{:S(2)}) collective-permute-start(bf16[2,112,128]{2,1,0:T(8,128)(2,1)S(1)} %fusion.111), channel_id=1, source_target_pairs={{0,4},{2,6},{4,0},{6,2},{8,12},{10,14},{12,8},{14,10},{16,20},{18,... | collective-permute-start | bytes 172040 | tf_op jit(solution)/shard_map/ppermute | solution.py:21
  189.9 7.3 %collective-permute-start.38 = (bf16[2,176,128]{2,1,0:T(8,128)(2,1)S(1)}, bf16[2,176,128]{2,1,0:T(8,128)(2,1)S(1)}, u32[]{:S(2)}, u32[]{:S(2)}) collective-permute-start(bf16[2,176,128]{2,1,0:T(8,128)(2,1)S(1)} %fusion.102), channel_id=1, source_target_pairs={{0,8},{2,10},{4,12},{6,14},{8,0},{10,2},{12,4},{14,6},{16,24},{18,... | collective-permute-start | bytes 270344 | tf_op jit(solution)/shard_map/ppermute | solution.py:21
  192.0 5.1 %collective-permute-start.43 = (bf16[160,128]{1,0:T(8,128)(2,1)S(1)}, bf16[160,128]{1,0:T(8,128)(2,1)S(1)}, u32[]{:S(2)}, u32[]{:S(2)}) collective-permute-start(bf16[160,128]{1,0:T(8,128)(2,1)S(1)} %fusion.115), channel_id=1, source_target_pairs={{0,16},{2,18},{4,20},{6,22},{8,24},{10,26},{12,28},{14,30},{16,0},... | collective-permute-start | bytes 122888 | tf_op jit(solution)/shard_map/ppermute | solution.py:21
  193.5 4.9 %collective-permute-start.47 = (bf16[112,128]{1,0:T(8,128)(2,1)S(1)}, bf16[112,128]{1,0:T(8,128)(2,1)S(1)}, u32[]{:S(2)}, u32[]{:S(2)}) collective-permute-start(bf16[112,128]{1,0:T(8,128)(2,1)S(1)} %fusion.123), channel_id=1, source_target_pairs={{0,2},{2,0},{4,6},{6,4},{8,10},{10,8},{12,14},{14,12},{16,18},{18,... | collective-permute-start | bytes 86024 | tf_op jit(solution)/shard_map/ppermute | solution.py:21
  197.2 5.0 %collective-permute-start.39 = (bf16[176,128]{1,0:T(8,128)(2,1)S(1)}, bf16[176,128]{1,0:T(8,128)(2,1)S(1)}, u32[]{:S(2)}, u32[]{:S(2)}) collective-permute-start(bf16[176,128]{1,0:T(8,128)(2,1)S(1)} %fusion.114), channel_id=1, source_target_pairs={{0,16},{2,18},{4,20},{6,22},{8,24},{10,26},{12,28},{14,30},{16,0},... | collective-permute-start | bytes 135176 | tf_op jit(solution)/shard_map/ppermute | solution.py:21
  202.4 1.4 collective-permute-start.48
  220.9 17.6 %collective-permute-start.49 = (bf16[2,2,2,16,2688]{4,3,2,1,0:T(8,128)(2,1)S(1)}, bf16[2,2,2,16,2688]{4,3,2,1,0:T(8,128)(2,1)S(1)}, u32[]{:S(2)}, u32[]{:S(2)}) collective-permute-start(bf16[2,2,2,16,2688]{4,3,2,1,0:T(8,128)(2,1)S(1)} %fusion.36), channel_id=1, source_target_pairs={{0,2},{2,0},{4,6},{6,4},{8,10},{10,8},{12,14},{14,12},{16,18},{18,... | collective-permute-start | bytes 2064392 | tf_op jit(solution)/shard_map/ppermute | solution.py:21
  222.2 17.4 %collective-permute-start.53 = (bf16[2,2,2,16,1792]{4,3,2,1,0:T(8,128)(2,1)S(1)}, bf16[2,2,2,16,1792]{4,3,2,1,0:T(8,128)(2,1)S(1)}, u32[]{:S(2)}, u32[]{:S(2)}) collective-permute-start(bf16[2,2,2,16,1792]{4,3,2,1,0:T(8,128)(2,1)S(1)} %fusion.44), channel_id=1, source_target_pairs={{0,8},{2,10},{4,12},{6,14},{8,0},{10,2},{12,4},{14,6},{16,24},{18,... | collective-permute-start | bytes 1376264 | tf_op jit(solution)/shard_map/ppermute | solution.py:21
  224.2 17.6 %collective-permute-start.54 = (bf16[2,2,2,16,2688]{4,3,2,1,0:T(8,128)(2,1)S(1)}, bf16[2,2,2,16,2688]{4,3,2,1,0:T(8,128)(2,1)S(1)}, u32[]{:S(2)}, u32[]{:S(2)}) collective-permute-start(bf16[2,2,2,16,2688]{4,3,2,1,0:T(8,128)(2,1)S(1)} %fusion.37), channel_id=1, source_target_pairs={{0,4},{2,6},{4,0},{6,2},{8,12},{10,14},{12,8},{14,10},{16,20},{18,... | collective-permute-start | bytes 2064392 | tf_op jit(solution)/shard_map/ppermute | solution.py:21
  238.6 10.0 %collective-permute-start.50 = (bf16[2,2,16,2688]{3,2,1,0:T(8,128)(2,1)S(1)}, bf16[2,2,16,2688]{3,2,1,0:T(8,128)(2,1)S(1)}, u32[]{:S(2)}, u32[]{:S(2)}) collective-permute-start(bf16[2,2,16,2688]{3,2,1,0:T(8,128)(2,1)S(1)} %fusion.54), channel_id=1, source_target_pairs={{0,4},{2,6},{4,0},{6,2},{8,12},{10,14},{12,8},{14,10},{16,20},{18,... | collective-permute-start | bytes 1032200 | tf_op jit(solution)/shard_map/ppermute | solution.py:21
  242.1 11.5 %collective-permute-start.55 = (bf16[2,2,16,1792]{3,2,1,0:T(8,128)(2,1)S(1)}, bf16[2,2,16,1792]{3,2,1,0:T(8,128)(2,1)S(1)}, u32[]{:S(2)}, u32[]{:S(2)}) collective-permute-start(bf16[2,2,16,1792]{3,2,1,0:T(8,128)(2,1)S(1)} %fusion.77), channel_id=1, source_target_pairs={{0,16},{2,18},{4,20},{6,22},{8,24},{10,26},{12,28},{14,30},{16,0},... | collective-permute-start | bytes 688136 | tf_op jit(solution)/shard_map/ppermute | solution.py:21
  244.7 8.9 %collective-permute-start.56 = (bf16[2,2,16,2688]{3,2,1,0:T(8,128)(2,1)S(1)}, bf16[2,2,16,2688]{3,2,1,0:T(8,128)(2,1)S(1)}, u32[]{:S(2)}, u32[]{:S(2)}) collective-permute-start(bf16[2,2,16,2688]{3,2,1,0:T(8,128)(2,1)S(1)} %fusion.55), channel_id=1, source_target_pairs={{0,2},{2,0},{4,6},{6,4},{8,10},{10,8},{12,14},{14,12},{16,18},{18,... | collective-permute-start | bytes 1032200 | tf_op jit(solution)/shard_map/ppermute | solution.py:21
  248.7 10.9 %collective-permute-start.51 = (bf16[2,16,2688]{2,1,0:T(8,128)(2,1)S(1)}, bf16[2,16,2688]{2,1,0:T(8,128)(2,1)S(1)}, u32[]{:S(2)}, u32[]{:S(2)}) collective-permute-start(bf16[2,16,2688]{2,1,0:T(8,128)(2,1)S(1)} %fusion.87), channel_id=1, source_target_pairs={{0,8},{2,10},{4,12},{6,14},{8,0},{10,2},{12,4},{14,6},{16,24},{18,... | collective-permute-start | bytes 516104 | tf_op jit(solution)/shard_map/ppermute | solution.py:21
  253.8 5.1 %collective-permute-start.57 = (bf16[2,16,1792]{2,1,0:T(8,128)(2,1)S(1)}, bf16[2,16,1792]{2,1,0:T(8,128)(2,1)S(1)}, u32[]{:S(2)}, u32[]{:S(2)}) collective-permute-start(bf16[2,16,1792]{2,1,0:T(8,128)(2,1)S(1)} %fusion.99), channel_id=1, source_target_pairs={{0,4},{2,6},{4,0},{6,2},{8,12},{10,14},{12,8},{14,10},{16,20},{18,... | collective-permute-start | bytes 344072 | tf_op jit(solution)/shard_map/ppermute | solution.py:21
  254.4 13.3 %copy-start.15 = (bf16[16,3584]{1,0:T(8,128)(2,1)S(1)}, bf16[16,3584]{1,0:T(8,128)(2,1)}, u32[]{:S(2)}) copy-start(bf16[16,3584]{1,0:T(8,128)(2,1)} %param.11) | copy-start | bytes 344068
  254.4 13.3 %copy-start.18 = (f32[3584]{0:T(1024)S(1)}, f32[3584]{0:T(1024)}, u32[]{:S(2)}) copy-start(f32[3584]{0:T(1024)} %param.13) | copy-start | bytes 43012
  254.4 6.5 %collective-permute-start.59 = (bf16[2,16,2688]{2,1,0:T(8,128)(2,1)S(1)}, bf16[2,16,2688]{2,1,0:T(8,128)(2,1)S(1)}, u32[]{:S(2)}, u32[]{:S(2)}) collective-permute-start(bf16[2,16,2688]{2,1,0:T(8,128)(2,1)S(1)} %fusion.88), channel_id=1, source_target_pairs={{0,8},{2,10},{4,12},{6,14},{8,0},{10,2},{12,4},{14,6},{16,24},{18,... | collective-permute-start | bytes 516104 | tf_op jit(solution)/shard_map/ppermute | solution.py:21
  258.9 4.2 %collective-permute-start.58 = (bf16[16,1792]{1,0:T(8,128)(2,1)S(1)}, bf16[16,1792]{1,0:T(8,128)(2,1)S(1)}, u32[]{:S(2)}, u32[]{:S(2)}) collective-permute-start(bf16[16,1792]{1,0:T(8,128)(2,1)S(1)} %fusion.112), channel_id=1, source_target_pairs={{0,2},{2,0},{4,6},{6,4},{8,10},{10,8},{12,14},{14,12},{16,18},{18,... | collective-permute-start | bytes 172040 | tf_op jit(solution)/shard_map/ppermute | solution.py:21
  259.7 7.9 %collective-permute-start.52 = (bf16[16,2688]{1,0:T(8,128)(2,1)S(1)}, bf16[16,2688]{1,0:T(8,128)(2,1)S(1)}, u32[]{:S(2)}, u32[]{:S(2)}) collective-permute-start(bf16[16,2688]{1,0:T(8,128)(2,1)S(1)} %fusion.104), channel_id=1, source_target_pairs={{0,16},{2,18},{4,20},{6,22},{8,24},{10,26},{12,28},{14,30},{16,0},... | collective-permute-start | bytes 258056 | tf_op jit(solution)/shard_map/ppermute | solution.py:21
  263.2 5.4 %collective-permute-start.60 = (bf16[16,2688]{1,0:T(8,128)(2,1)S(1)}, bf16[16,2688]{1,0:T(8,128)(2,1)S(1)}, u32[]{:S(2)}, u32[]{:S(2)}) collective-permute-start(bf16[16,2688]{1,0:T(8,128)(2,1)S(1)} %fusion.105), channel_id=1, source_target_pairs={{0,16},{2,18},{4,20},{6,22},{8,24},{10,26},{12,28},{14,30},{16,0},... | collective-permute-start | bytes 258056 | tf_op jit(solution)/shard_map/ppermute | solution.py:21
  (23 other events, 98.5 us)

commit v4 on v3

--- a/solution.py
+++ b/solution.py
@@ -40,19 +40,21 @@
 
 def gather(first, second, third):
     high = list(reversed(range(2, bits_of("seq"))))
+    array_shape = third.shape
     came = []
     for bit in high:
         came = [from_partner(first, "seq", 1 << bit), from_partner(second, "seq", 1 << bit)]
         if bit == high[0]:
             third = third + zero_of(came[0], third.shape) + zero_of(came[1], third.shape)
         first, second = jnp.stack([first, came[0]]), jnp.stack([second, came[1]])
+    waits = [came]
     for bit in (0, 1):
-        first = jnp.stack([first, from_partner(first, "seq", 2 >> bit)])
-        second = jnp.stack([second, from_partner(second, "seq", 1 << bit)])
+        waits.append([from_partner(first, "seq", 2 >> bit), from_partner(second, "seq", 1 << bit)])
+        first, second = jnp.stack([first, waits[-1][0]]), jnp.stack([second, waits[-1][1]])
         third = jnp.stack([third, from_partner(third, "seq", 1 << bit)])
-    for block in came:
-        third = third + zero_of(block, third.shape[2:])
-    for bit in high:
+    for step, bit in enumerate(high):
+        for block in waits[step] if step < 2 else ():
+            third = third + zero_of(block, array_shape)
         third = jnp.stack([third, from_partner(third, "seq", 1 << bit)])
     return in_order(first, high + [1, 0]), in_order(second, high + [0, 1]), in_order(third, [0, 1] + high)
 
@@ -76,7 +78,7 @@
             came.append(from_partner(sent, "seq", 1 << bit))
         sums = [one + other.astype(f32) for one, other in zip(kept, came)]
         if step < len(beside):
-            result, zeros = beside[step](last, sums[0].shape, results)
+            result, zeros = beside[step](came[2] if last is None else last, sums[0].shape, results)
             results.append(result)
             if zeros is not None:
                 sums[0] = sums[0] + zeros
@@ -489,7 +491,7 @@
             before = results[-1] if results else None
             shape = shape if tied else (8, 128)
             out, zeros = grad_head_rows(
-                dlogits, final_all, index, 4, from_core if last is None else last, shape, before
+                dlogits, final_all, index, 4, last if tied else from_core, shape, before
             )
             return out, (zeros if tied else None)
 
@@ -509,32 +511,32 @@
     back_prev = dot(dmixed_prev, proj_hidden, 0, 1).reshape(blocks, rows, width)
     back_embed = dot(dmixed_embed, proj_embed, 0, 1).reshape(blocks, rows, width)
 
-    def grad_head_end(last, shape, before):
-        grad_head = results[-1]
-        if fits:
-            for index in (2, 3):
-                grad_head, _ = grad_head_rows(
-                    dlogits, final_all, index, 4, dmixed_prev, (8, 128), grad_head
-                )
-        return grad_head, None
+    def grad_head_end(index):
+        def work(last, shape, before):
+            grad_head = before[-1] if before else results[-1]
+            if not fits:
+                return grad_head, None
+            shape = shape if index == 3 else (8, 128)
+            out, zeros = grad_head_rows(dlogits, final_all, index, 4, last, shape, grad_head)
+            return out, (zeros if index == 3 else None)
+
+        return work
 
     def grad_proj(rows_in, rows_rest, back):
         rows_all = jnp.concatenate([rows_in, rows_rest], axis=1)
-        return dot(rows_all, back, 0, 1).astype(bf16), None
-
-    (one, two, three), results = scatter(
+        return dot(rows_all, back, 0, 1).astype(bf16)
+
+    (one, two, three), ends = scatter(
         [
             back_prev[..., :main],
             back_embed[..., :main],
             jnp.concatenate([back_prev[..., main:], back_embed[..., main:]], axis=-1),
         ],
-        [
-            grad_head_end,
-            lambda *_: grad_proj(first, third[:, :rest], dmixed_prev),
-            lambda *_: grad_proj(second, third[:, rest : 2 * rest], dmixed_embed),
-        ],
-    )
-    grad_head, grad_proj_hidden, grad_proj_embed = results
+        [grad_head_end(2), grad_head_end(3)],
+    )
+    grad_head = ends[-1]
+    grad_proj_hidden = grad_proj(first, third[:, :rest], dmixed_prev)
+    grad_proj_embed = grad_proj(second, third[:, rest : 2 * rest], dmixed_embed)
     grad_prev = jnp.concatenate([one, three[:, :rest]], axis=1) * gain_hidden
     grad_embed = jnp.concatenate([two, three[:, rest:]], axis=1) * gain_embed
     dots = lax.psum(

time: 274 us -> 266 us (0.971)
  waiting for transfers between devices: 107 us -> 84.5 us
  starting transfers between devices: 60.6 us -> 71.4 us
  matrix products: 14.1 us -> 16.9 us
    ppermute x61, waiting for transfers between devices: 107 us -> 84.5 us  [from_partner(): return lax.ppermute(array, axis, [(i, i ^ mask) for i in range(size)])]
    ppermute x61, starting transfers between devices: 60.6 us -> 71.4 us  [from_partner(): return lax.ppermute(array, axis, [(i, i ^ mask) for i in range(size)])]
    dot_general x14, matrix products: 14.1 us -> 16.9 us  [dot(): lax.dot_general(left, right, (((on_left,), (on_right,)), ((), ())), preci...]
  transfers between devices with their start and end apart: 61 -> 61, of which waited for: 40 -> 37; matrix products, arithmetic and copies ran while one was open for 7% -> 9% of each run, Pallas kernels for 4% -> 9%
where the time goes in v4:
time: 266 us; the launch traced here: 265 us
  waiting for transfers between devices  84.5 us (32%)
  starting transfers between devices  71.4 us (27%)
  Pallas kernels  55 us (21%)
  other arithmetic  19.7 us (7%)
  matrix products  16.9 us (6%)
  local copies, waits for them, and re-layouts  9.6 us (4%)
  blocking collectives  5.05 us (2%)
  between operations  3.24 us (1%)
    ppermute x61, waiting for transfers between devices, from_partner(): return lax.ppermute(array, axis, [(i, i ^ mask) for i in range(size)])  84.5 us
    ppermute x61, starting transfers between devices, from_partner(): return lax.ppermute(array, axis, [(i, i ^ mask) for i in range(size)])  71.4 us
    pallas_call x4, Pallas kernels, grad_head_rows(): pl.pallas_call(grad_head_kernel, grid=(D // tile,), in_specs=[pl.BlockSpe...  23.1 us
    dot_general x14, matrix products, dot(): lax.dot_general(left, right, (((on_left,), (on_right,)), ((), ())), preci...  16.9 us
    pallas_call x1, Pallas kernels, head_back(): pl.pallas_call(dfinal_kernel, grid_spec=pltpu.PrefetchScalarGridSpec(num_...  16.8 us
    pallas_call x1, Pallas kernels, head_logits(): pl.pallas_call(logits_kernel, grid_spec=pltpu.PrefetchScalarGridSpec(num_...  15.2 us
    unnamed x52, local copies, waits for them, and re-layouts  7.04 us
  transfers between devices with their start and end apart: 61, of which 37 were waited for; matrix products, arithmetic and copies ran while one was open for 9% of the time, Pallas kernels for 9%

profile of v4, /device:TPU:0, one launch (start us, length us, event | category | flops | bytes accessed | tf_op | source)
XLA Modules:
  0.0 265.4 jit_solution(7168047528819808577)
XLA Ops:
  2.7 2.6 psum.14
  6.5 4.0 %collective-permute-start.4 = (bf16[16,2688]{1,0:T(8,128)(2,1)S(1)}, bf16[16,2688]{1,0:T(8,128)(2,1)S(1)}, u32[]{:S(2)}, u32[]{:S(2)}) collective-permute-start(bf16[16,2688]{1,0:T(8,128)(2,1)S(1)} %slice.636), channel_id=1, source_target_pairs={{0,16},{2,18},{4,20},{6,22},{8,24},{10,26},{12,28},{14,30},{16,0},... | collective-permute-start | bytes 258056 | tf_op jit(solution)/shard_map/ppermute | solution.py:21
  14.5 3.0 %collective-permute-done.4 = bf16[16,2688]{1,0:T(8,128)(2,1)S(1)} collective-permute-done((bf16[16,2688]{1,0:T(8,128)(2,1)S(1)}, bf16[16,2688]{1,0:T(8,128)(2,1)S(1)}, u32[]{:S(2)}, u32[]{:S(2)}) %collective-permute-start.4) | collective-permute-done | bytes 86048 | tf_op jit(solution)/shard_map/ppermute | solution.py:21
  18.9 1.6 collective-permute-start.5
  21.4 1.4 collective-permute-start.1
  23.3 1.6 collective-permute-start.6
  24.9 3.0 %collective-permute-done.7 = bf16[2,16,2688]{2,1,0:T(8,128)(2,1)S(1)} collective-permute-done((bf16[2,16,2688]{2,1,0:T(8,128)(2,1)S(1)}, bf16[2,16,2688]{2,1,0:T(8,128)(2,1)S(1)}, u32[]{:S(2)}, u32[]{:S(2)}) %collective-permute-start.7) | collective-permute-done | bytes 172064 | tf_op jit(solution)/shard_map/ppermute | solution.py:21
  27.9 1.8 collective-permute-done.1
  32.1 3.0 %collective-permute-start.8 = (bf16[2,2,16,1920]{3,2,1,0:T(8,128)(2,1)S(1)}, bf16[2,2,16,1920]{3,2,1,0:T(8,128)(2,1)S(1)}, u32[]{:S(2)}, u32[]{:S(2)}) collective-permute-start(bf16[2,2,16,1920]{3,2,1,0:T(8,128)(2,1)S(1)} %fusion.67), channel_id=1, source_target_pairs={{0,16},{2,18},{4,20},{6,22},{8,24},{10,26},{12,28},{14,30},{16,0},... | collective-permute-start | bytes 737288 | tf_op jit(solution)/shard_map/ppermute | solution.py:21
  35.2 2.8 %collective-permute-done.9 = bf16[2,2,16,2688]{3,2,1,0:T(8,128)(2,1)S(1)} collective-permute-done((bf16[2,2,16,2688]{3,2,1,0:T(8,128)(2,1)S(1)}, bf16[2,2,16,2688]{3,2,1,0:T(8,128)(2,1)S(1)}, u32[]{:S(2)}, u32[]{:S(2)}) %collective-permute-start.9) | collective-permute-done | bytes 344096 | tf_op jit(solution)/shard_map/ppermute | solution.py:21
  38.9 6.2 %collective-permute-done.8 = bf16[2,2,16,1920]{3,2,1,0:T(8,128)(2,1)S(1)} collective-permute-done((bf16[2,2,16,1920]{3,2,1,0:T(8,128)(2,1)S(1)}, bf16[2,2,16,1920]{3,2,1,0:T(8,128)(2,1)S(1)}, u32[]{:S(2)}, u32[]{:S(2)}) %collective-permute-start.8) | collective-permute-done | bytes 245792 | tf_op jit(solution)/shard_map/ppermute | solution.py:21
  48.8 1.5 collective-permute-start.3
  50.4 7.1 %collective-permute-done.10 = bf16[2,2,2,16,1920]{4,3,2,1,0:T(8,128)(2,1)S(1)} collective-permute-done((bf16[2,2,2,16,1920]{4,3,2,1,0:T(8,128)(2,1)S(1)}, bf16[2,2,2,16,1920]{4,3,2,1,0:T(8,128)(2,1)S(1)}, u32[]{:S(2)}, u32[]{:S(2)}) %collective-permute-start.10) | collective-permute-done | bytes 491552 | tf_op jit(solution)/shard_map/ppermute | solution.py:21
  58.7 2.7 %fusion.31 = f32[256,448]{0,1:T(8,128)} fusion(bf16[3584,448]{0,1:T(8,128)(2,1)} %param.17, bf16[256,1920]{1,0:T(8,128)(2,1)S(1)} %bitcast.371), kind=kOutput, calls=%fused_computation.39 | convolution fusion | flops 205520896 | bytes 1720320 | tf_op jit(solution)/shard_map/dot_general | solution.py:138
  61.6 1.8 fusion.99
  63.4 1.5 fusion.33
  72.9 1.4 slice_reduce_fusion
  74.4 3.3 %collective-permute-start.14 = (bf16[160,128]{1,0:T(8,128)(2,1)S(1)}, bf16[160,128]{1,0:T(8,128)(2,1)S(1)}, u32[]{:S(2)}, u32[]{:S(2)}) collective-permute-start(bf16[160,128]{1,0:T(8,128)(2,1)S(1)} %get-tuple-element.87), channel_id=1, source_target_pairs={{0,16},{2,18},{4,20},{6,22},{8,24},{10,26},{12,28},{14,30},{16,0},... | collective-permute-start | bytes 122888 | tf_op jit(solution)/shard_map/ppermute | solution.py:21
  77.8 2.1 collective-permute-done.14
  79.9 2.7 %collective-permute-start.18 = (bf16[2,160,128]{2,1,0:T(8,128)(2,1)S(1)}, bf16[2,160,128]{2,1,0:T(8,128)(2,1)S(1)}, u32[]{:S(2)}, u32[]{:S(2)}) collective-permute-start(bf16[2,160,128]{2,1,0:T(8,128)(2,1)S(1)} %get-tuple-element.91), channel_id=1, source_target_pairs={{0,8},{2,10},{4,12},{6,14},{8,0},{10,2},{12,4},{14,6},{16,24},{18,... | collective-permute-start | bytes 245768 | tf_op jit(solution)/shard_map/ppermute | solution.py:21
  82.7 1.6 collective-permute-start.15
  84.2 1.8 collective-permute-start.17
  87.3 1.6 collective-permute-start.21
  88.9 1.6 collective-permute-start.20
  91.7 3.4 %collective-permute-start.19 = (bf16[2,2,128,128]{3,2,1,0:T(8,128)(2,1)S(1)}, bf16[2,2,128,128]{3,2,1,0:T(8,128)(2,1)S(1)}, u32[]{:S(2)}, u32[]{:S(2)}) collective-permute-start(bf16[2,2,128,128]{3,2,1,0:T(8,128)(2,1)S(1)} %fusion.101), channel_id=1, source_target_pairs={{0,16},{2,18},{4,20},{6,22},{8,24},{10,26},{12,28},{14,30},{16,0},... | collective-permute-start | bytes 393224 | tf_op jit(solution)/shard_map/ppermute | solution.py:21
  95.1 4.4 %collective-permute-done.19 = bf16[2,2,128,128]{3,2,1,0:T(8,128)(2,1)S(1)} collective-permute-done((bf16[2,2,128,128]{3,2,1,0:T(8,128)(2,1)S(1)}, bf16[2,2,128,128]{3,2,1,0:T(8,128)(2,1)S(1)}, u32[]{:S(2)}, u32[]{:S(2)}) %collective-permute-start.19) | collective-permute-done | bytes 131104 | tf_op jit(solution)/shard_map/ppermute | solution.py:21
  99.7 1.6 collective-permute-start.24
  101.9 4.1 %collective-permute-done.22 = bf16[2,2,2,128,128]{4,3,2,1,0:T(8,128)(2,1)S(1)} collective-permute-done((bf16[2,2,2,128,128]{4,3,2,1,0:T(8,128)(2,1)S(1)}, bf16[2,2,2,128,128]{4,3,2,1,0:T(8,128)(2,1)S(1)}, u32[]{:S(2)}, u32[]{:S(2)}) %collective-permute-start.22) | collective-permute-done | bytes 262176 | tf_op jit(solution)/shard_map/ppermute | solution.py:21
  108.8 2.0 collective-permute-done.27.refs_4_
  110.8 15.2 %shard_map.146 = (f32[2048,256]{1,0:T(8,128)S(1)}, f32[8,256]{1,0:T(8,128)S(1)}, bf16[7168,256]{1,0:T(8,128)(2,1)S(1)}) custom-call(s32[2]{0:T(128)S(1)} %pad_add_fusion.1.where, s32[1,256]{1,0:T(1,128)S(1)} %pad_add_fusion.ids, f32[1,256]{1,0:T(1,128)S(1)} %fusion.186.scale, f32[56,128]{1,0:T(8,128)S(1)} %reshape_reshape.15.gain, ...), custom_call_target="tpu_custom_call" | custom-call | flops 7516192768 | bytes 36700160 | tf_op jit(solution)/shard_map/pallas_call | solution.py:192
  126.0 1.8 copy-done
  129.0 1.6 collective-permute-start.29
  132.6 1.6 collective-permute-done.28
  134.3 4.0 %collective-permute-start.33 = (f32[4,256]{1,0:T(4,128)S(1)}, f32[4,256]{1,0:T(4,128)S(1)}, u32[]{:S(2)}, u32[]{:S(2)}) collective-permute-start(f32[4,256]{1,0:T(4,128)S(1)} %fusion.138), channel_id=1, source_target_pairs={{0,24},{2,26},{4,28},{6,30},{8,16},{10,18},{12,20},{14,22},{16,8},... | collective-permute-start | bytes 12296 | tf_op jit(solution)/shard_map/ppermute | solution.py:21
  140.3 2.5 collective-permute-done.32
  144.3 16.8 %shard_map.147 = (f32[8,2,448,128]{3,2,1,0:T(8,128)S(1)}, bf16[8,2,448,128]{3,2,1,0:T(8,128)(2,1)S(1)}, bf16[2048,256]{1,0:T(8,128)(2,1)S(1)}) custom-call(s32[2]{0:T(128)S(1)} %pad_add_fusion.1.where, s32[1,256]{1,0:T(1,128)S(1)} %pad_add_fusion.ids, f32[8,256]{1,0:T(8,128)S(1)} %select_maximum_fusion.rows, f32[2048,256]{1,0:T(8,128)S(1)} %get-tuple-element.30.logits, ...), custom_call_target="tpu_custom_call" | custom-call | flops 7516192768 | bytes 36700160 | tf_op jit(solution)/shard_map/pallas_call | solution.py:256
  161.3 3.6 %collective-permute-done.35.refs_0_ = bf16[8,2,448,128]{3,2,1,0:T(8,128)(2,1)S(1)} collective-permute-done((bf16[8,2,448,128]{3,2,1,0:T(8,128)(2,1)S(1)}, bf16[8,2,448,128]{3,2,1,0:T(8,128)(2,1)S(1)}, u32[]{:S(2)}, u32[]{:S(2)}) %collective-permute-start.35) | collective-permute-done | bytes 1835040 | tf_op jit(solution)/shard_map/ppermute | solution.py:21
  167.6 5.8 %shard_map.148 = (bf16[2048,7168]{1,0:T(8,128)(2,1)}, f32[8,128]{1,0:T(8,128)}) custom-call(bf16[2048,256]{1,0:T(8,128)(2,1)S(1)} %get-tuple-element.33.left, bf16[7168,256]{1,0:T(8,128)(2,1)S(1)} %copy-done.1, bf16[8,2,448,128]{3,2,1,0:T(8,128)(2,1)S(1)} %collective-permute-done.35.refs_0_), custom_call_target="tpu_custom_call" | custom-call | flops 1879048192 | bytes 11010048 | tf_op jit(solution)/shard_map/pallas_call | solution.py:303
  173.3 2.3 collective-permute-done.40
  176.7 2.1 collective-permute-start.45
  178.9 1.9 collective-permute-start.37
  180.9 5.8 %shard_map.149 = (bf16[2048,7168]{1,0:T(8,128)(2,1)}, f32[2,2,176,128]{3,2,1,0:T(8,128)S(1)}) custom-call(bf16[2048,256]{1,0:T(8,128)(2,1)S(1)} %get-tuple-element.33.left, bf16[7168,256]{1,0:T(8,128)(2,1)S(1)} %copy-done.1, bf16[2,2,2,176,128]{4,3,2,1,0:T(8,128)(2,1)S(1)} %collective-permute-done.36.refs_0_, ...), custom_call_target="tpu_custom_call", output_to_operand_aliasing={{0}: (3, {})} | custom-call | flops 1879048192 | bytes 11010048 | tf_op jit(solution)/shard_map/pallas_call | solution.py:303
  186.7 2.0 collective-permute-start.42
  189.2 1.9 collective-permute-done.42
  193.8 2.8 %collective-permute-done.43 = bf16[160,128]{1,0:T(8,128)(2,1)S(1)} collective-permute-done((bf16[160,128]{1,0:T(8,128)(2,1)S(1)}, bf16[160,128]{1,0:T(8,128)(2,1)S(1)}, u32[]{:S(2)}, u32[]{:S(2)}) %collective-permute-start.43) | collective-permute-done | bytes 40992 | tf_op jit(solution)/shard_map/ppermute | solution.py:21
  197.6 4.1 %collective-permute-done.39 = bf16[176,128]{1,0:T(8,128)(2,1)S(1)} collective-permute-done((bf16[176,128]{1,0:T(8,128)(2,1)S(1)}, bf16[176,128]{1,0:T(8,128)(2,1)S(1)}, u32[]{:S(2)}, u32[]{:S(2)}) %collective-permute-start.39) | collective-permute-done | bytes 45088 | tf_op jit(solution)/shard_map/ppermute | solution.py:21
  205.5 1.7 copy-done.5
  210.9 1.5 collective-permute-start.51
  212.4 2.7 %convolution_convert_fusion.1 = bf16[3584,448]{0,1:T(8,128)(2,1)} fusion(bf16[448,256]{1,0:T(8,128)(2,1)S(1)} %convolution_convert_fusion.3, bf16[256,896]{1,0:T(8,128)(2,1)S(1)} %get-tuple-element.52, bf16[256,2688]{1,0:T(8,128)(2,1)S(1)} %bitcast.367), kind=kOutput, calls=%fused_computation.1 | convolution fusion | flops 827359232 | bytes 5275648 | tf_op jit(solution)/shard_map/dot_general | solution.py:138
  215.1 2.7 %convolution_convert_fusion = bf16[3584,448]{0,1:T(8,128)(2,1)} fusion(bf16[448,256]{1,0:T(8,128)(2,1)S(1)} %convolution_convert_fusion.2, bf16[256,896]{1,0:T(8,128)(2,1)S(1)} %get-tuple-element.51, bf16[256,2688]{1,0:T(8,128)(2,1)S(1)} %bitcast.365), kind=kOutput, calls=%fused_computation | convolution fusion | flops 827359232 | bytes 5275648 | tf_op jit(solution)/shard_map/dot_general | solution.py:138
  217.8 5.2 %collective-permute-done.51.refs_0_ = bf16[2,2,2,16,1792]{4,3,2,1,0:T(8,128)(2,1)S(1)} collective-permute-done((bf16[2,2,2,16,1792]{4,3,2,1,0:T(8,128)(2,1)S(1)}, bf16[2,2,2,16,1792]{4,3,2,1,0:T(8,128)(2,1)S(1)}, u32[]{:S(2)}, u32[]{:S(2)}) %collective-permute-start.51) | collective-permute-done | bytes 458784 | tf_op jit(solution)/shard_map/ppermute | solution.py:21
  223.0 3.2 %collective-permute-done.49.refs_0_ = bf16[2,2,2,16,2688]{4,3,2,1,0:T(8,128)(2,1)S(1)} collective-permute-done((bf16[2,2,2,16,2688]{4,3,2,1,0:T(8,128)(2,1)S(1)}, bf16[2,2,2,16,2688]{4,3,2,1,0:T(8,128)(2,1)S(1)}, u32[]{:S(2)}, u32[]{:S(2)}) %collective-permute-start.49) | collective-permute-done | bytes 688160 | tf_op jit(solution)/shard_map/ppermute | solution.py:21
  230.4 5.8 %shard_map.150 = (bf16[2048,7168]{1,0:T(8,128)(2,1)}, f32[8,128]{1,0:T(8,128)}) custom-call(bf16[2048,256]{1,0:T(8,128)(2,1)S(1)} %get-tuple-element.33.left, bf16[7168,256]{1,0:T(8,128)(2,1)S(1)} %copy-done.1, bf16[2,2,2,16,1792]{4,3,2,1,0:T(8,128)(2,1)S(1)} %collective-permute-done.51.refs_0_, ...), custom_call_target="tpu_custom_call", output_to_operand_aliasing={{0}: (3, {})} | custom-call | flops 1879048192 | bytes 11010048 | tf_op jit(solution)/shard_map/pallas_call | solution.py:303
  236.2 5.8 %shard_map.151 = (bf16[2048,7168]{1,0:T(8,128)(2,1)}, f32[2,2,16,2688]{3,2,1,0:T(8,128)S(1)}) custom-call(bf16[2048,256]{1,0:T(8,128)(2,1)S(1)} %get-tuple-element.33.left, bf16[7168,256]{1,0:T(8,128)(2,1)S(1)} %copy-done.1, bf16[2,2,2,16,2688]{4,3,2,1,0:T(8,128)(2,1)S(1)} %collective-permute-done.49.refs_0_, ...), custom_call_target="tpu_custom_call", output_to_operand_aliasing={{0}: (3, {})} | custom-call | flops 1879048192 | bytes 11010048 | tf_op jit(solution)/shard_map/pallas_call | solution.py:303
  242.2 1.4 collective-permute-start.57
  243.8 2.5 collective-permute-start.52
  247.1 1.8 collective-permute-start.58
  248.8 1.7 collective-permute-done.52
  250.6 1.8 collective-permute-done.59
  252.4 1.4 collective-permute-start.60
  253.9 1.6 collective-permute-start.53
  255.5 2.4 collective-permute-done.60
  258.1 3.1 %collective-permute-done.53 = bf16[16,2688]{1,0:T(8,128)(2,1)S(1)} collective-permute-done((bf16[16,2688]{1,0:T(8,128)(2,1)S(1)}, bf16[16,2688]{1,0:T(8,128)(2,1)S(1)}, u32[]{:S(2)}, u32[]{:S(2)}) %collective-permute-start.53) | collective-permute-done | bytes 86048 | tf_op jit(solution)/shard_map/ppermute | solution.py:21
  261.4 2.5 psum.15
  (312 shorter events, 60.6 us)
Async XLA Ops:
  6.5 11.0 %collective-permute-start.4 = (bf16[16,2688]{1,0:T(8,128)(2,1)S(1)}, bf16[16,2688]{1,0:T(8,128)(2,1)S(1)}, u32[]{:S(2)}, u32[]{:S(2)}) collective-permute-start(bf16[16,2688]{1,0:T(8,128)(2,1)S(1)} %slice.636), channel_id=1, source_target_pairs={{0,16},{2,18},{4,20},{6,22},{8,24},{10,26},{12,28},{14,30},{16,0},... | collective-permute-start | bytes 258056 | tf_op jit(solution)/shard_map/ppermute | solution.py:21
  10.5 8.4 %collective-permute-start = (bf16[16,2688]{1,0:T(8,128)(2,1)S(1)}, bf16[16,2688]{1,0:T(8,128)(2,1)S(1)}, u32[]{:S(2)}, u32[]{:S(2)}) collective-permute-start(bf16[16,2688]{1,0:T(8,128)(2,1)S(1)} %slice.635), channel_id=1, source_target_pairs={{0,16},{2,18},{4,20},{6,22},{8,24},{10,26},{12,28},{14,30},{16,0},... | collective-permute-start | bytes 258056 | tf_op jit(solution)/shard_map/ppermute | solution.py:21
  10.6 20.1 %copy-start.22 = (s32[256]{0:T(256)}, s32[256]{0:T(256)S(1)}, u32[]{:S(2)}) copy-start(s32[256]{0:T(256)S(1)} %get-tuple-element.151) | copy-start | bytes 3076
  18.9 4.3 %collective-permute-start.5 = (bf16[16,1920]{1,0:T(8,128)(2,1)S(1)}, bf16[16,1920]{1,0:T(8,128)(2,1)S(1)}, u32[]{:S(2)}, u32[]{:S(2)}) collective-permute-start(bf16[16,1920]{1,0:T(8,128)(2,1)S(1)} %fusion.115), channel_id=1, source_target_pairs={{0,2},{2,0},{4,6},{6,4},{8,10},{10,8},{12,14},{14,12},{16,18},{18,... | collective-permute-start | bytes 184328 | tf_op jit(solution)/shard_map/ppermute | solution.py:21
  20.6 7.3 %collective-permute-start.7 = (bf16[2,16,2688]{2,1,0:T(8,128)(2,1)S(1)}, bf16[2,16,2688]{2,1,0:T(8,128)(2,1)S(1)}, u32[]{:S(2)}, u32[]{:S(2)}) collective-permute-start(bf16[2,16,2688]{2,1,0:T(8,128)(2,1)S(1)} %get-tuple-element.72), channel_id=1, source_target_pairs={{0,8},{2,10},{4,12},{6,14},{8,0},{10,2},{12,4},{14,6},{16,24},{18,... | collective-permute-start | bytes 516104 | tf_op jit(solution)/shard_map/ppermute | solution.py:21
  21.4 8.4 %collective-permute-start.1 = (bf16[2,16,2688]{2,1,0:T(8,128)(2,1)S(1)}, bf16[2,16,2688]{2,1,0:T(8,128)(2,1)S(1)}, u32[]{:S(2)}, u32[]{:S(2)}) collective-permute-start(bf16[2,16,2688]{2,1,0:T(8,128)(2,1)S(1)} %get-tuple-element.70), channel_id=1, source_target_pairs={{0,8},{2,10},{4,12},{6,14},{8,0},{10,2},{12,4},{14,6},{16,24},{18,... | collective-permute-start | bytes 516104 | tf_op jit(solution)/shard_map/ppermute | solution.py:21
  23.3 8.8 %collective-permute-start.6 = (bf16[2,16,1920]{2,1,0:T(8,128)(2,1)S(1)}, bf16[2,16,1920]{2,1,0:T(8,128)(2,1)S(1)}, u32[]{:S(2)}, u32[]{:S(2)}) collective-permute-start(bf16[2,16,1920]{2,1,0:T(8,128)(2,1)S(1)} %get-tuple-element.81), channel_id=1, source_target_pairs={{0,4},{2,6},{4,0},{6,2},{8,12},{10,14},{12,8},{14,10},{16,20},{18,... | collective-permute-start | bytes 368648 | tf_op jit(solution)/shard_map/ppermute | solution.py:21
  29.8 8.2 %collective-permute-start.9 = (bf16[2,2,16,2688]{3,2,1,0:T(8,128)(2,1)S(1)}, bf16[2,2,16,2688]{3,2,1,0:T(8,128)(2,1)S(1)}, u32[]{:S(2)}, u32[]{:S(2)}) collective-permute-start(bf16[2,2,16,2688]{3,2,1,0:T(8,128)(2,1)S(1)} %get-tuple-element.62), channel_id=1, source_target_pairs={{0,2},{2,0},{4,6},{6,4},{8,10},{10,8},{12,14},{14,12},{16,18},{18,... | collective-permute-start | bytes 1032200 | tf_op jit(solution)/shard_map/ppermute | solution.py:21
  30.7 8.2 %collective-permute-start.2 = (bf16[2,2,16,2688]{3,2,1,0:T(8,128)(2,1)S(1)}, bf16[2,2,16,2688]{3,2,1,0:T(8,128)(2,1)S(1)}, u32[]{:S(2)}, u32[]{:S(2)}) collective-permute-start(bf16[2,2,16,2688]{3,2,1,0:T(8,128)(2,1)S(1)} %get-tuple-element.60), channel_id=1, source_target_pairs={{0,4},{2,6},{4,0},{6,2},{8,12},{10,14},{12,8},{14,10},{16,20},{18,... | collective-permute-start | bytes 1032200 | tf_op jit(solution)/shard_map/ppermute | solution.py:21
  32.1 13.1 %collective-permute-start.8 = (bf16[2,2,16,1920]{3,2,1,0:T(8,128)(2,1)S(1)}, bf16[2,2,16,1920]{3,2,1,0:T(8,128)(2,1)S(1)}, u32[]{:S(2)}, u32[]{:S(2)}) collective-permute-start(bf16[2,2,16,1920]{3,2,1,0:T(8,128)(2,1)S(1)} %fusion.67), channel_id=1, source_target_pairs={{0,16},{2,18},{4,20},{6,22},{8,24},{10,26},{12,28},{14,30},{16,0},... | collective-permute-start | bytes 737288 | tf_op jit(solution)/shard_map/ppermute | solution.py:21
  45.2 12.3 %collective-permute-start.10 = (bf16[2,2,2,16,1920]{4,3,2,1,0:T(8,128)(2,1)S(1)}, bf16[2,2,2,16,1920]{4,3,2,1,0:T(8,128)(2,1)S(1)}, u32[]{:S(2)}, u32[]{:S(2)}) collective-permute-start(bf16[2,2,2,16,1920]{4,3,2,1,0:T(8,128)(2,1)S(1)} %fusion.46), channel_id=1, source_target_pairs={{0,8},{2,10},{4,12},{6,14},{8,0},{10,2},{12,4},{14,6},{16,24},{18,... | collective-permute-start | bytes 1474568 | tf_op jit(solution)/shard_map/ppermute | solution.py:21
  47.2 17.7 %collective-permute-start.11 = (bf16[2,2,2,16,2688]{4,3,2,1,0:T(8,128)(2,1)}, bf16[2,2,2,16,2688]{4,3,2,1,0:T(8,128)(2,1)}, u32[]{:S(2)}, u32[]{:S(2)}) collective-permute-start(bf16[2,2,2,16,2688]{4,3,2,1,0:T(8,128)(2,1)} %get-tuple-element.56), channel_id=1, source_target_pairs={{0,4},{2,6},{4,0},{6,2},{8,12},{10,14},{12,8},{14,10},{16,20},{18,... | collective-permute-start | bytes 2064392 | tf_op jit(solution)/shard_map/ppermute | solution.py:21
  48.8 17.5 %collective-permute-start.3 = (bf16[2,2,2,16,2688]{4,3,2,1,0:T(8,128)(2,1)}, bf16[2,2,2,16,2688]{4,3,2,1,0:T(8,128)(2,1)}, u32[]{:S(2)}, u32[]{:S(2)}) collective-permute-start(bf16[2,2,2,16,2688]{4,3,2,1,0:T(8,128)(2,1)} %get-tuple-element.54), channel_id=1, source_target_pairs={{0,2},{2,0},{4,6},{6,4},{8,10},{10,8},{12,14},{14,12},{16,18},{18,... | collective-permute-start | bytes 2064392 | tf_op jit(solution)/shard_map/ppermute | solution.py:21
  72.4 1.9 collective-permute-start.12
  74.4 5.5 %collective-permute-start.14 = (bf16[160,128]{1,0:T(8,128)(2,1)S(1)}, bf16[160,128]{1,0:T(8,128)(2,1)S(1)}, u32[]{:S(2)}, u32[]{:S(2)}) collective-permute-start(bf16[160,128]{1,0:T(8,128)(2,1)S(1)} %get-tuple-element.87), channel_id=1, source_target_pairs={{0,16},{2,18},{4,20},{6,22},{8,24},{10,26},{12,28},{14,30},{16,0},... | collective-permute-start | bytes 122888 | tf_op jit(solution)/shard_map/ppermute | solution.py:21
  77.7 5.0 %collective-permute-start.13 = (bf16[176,128]{1,0:T(8,128)(2,1)S(1)}, bf16[176,128]{1,0:T(8,128)(2,1)S(1)}, u32[]{:S(2)}, u32[]{:S(2)}) collective-permute-start(bf16[176,128]{1,0:T(8,128)(2,1)S(1)} %get-tuple-element.85), channel_id=1, source_target_pairs={{0,16},{2,18},{4,20},{6,22},{8,24},{10,26},{12,28},{14,30},{16,0},... | collective-permute-start | bytes 135176 | tf_op jit(solution)/shard_map/ppermute | solution.py:21
  79.9 7.3 %collective-permute-start.18 = (bf16[2,160,128]{2,1,0:T(8,128)(2,1)S(1)}, bf16[2,160,128]{2,1,0:T(8,128)(2,1)S(1)}, u32[]{:S(2)}, u32[]{:S(2)}) collective-permute-start(bf16[2,160,128]{2,1,0:T(8,128)(2,1)S(1)} %get-tuple-element.91), channel_id=1, source_target_pairs={{0,8},{2,10},{4,12},{6,14},{8,0},{10,2},{12,4},{14,6},{16,24},{18,... | collective-permute-start | bytes 245768 | tf_op jit(solution)/shard_map/ppermute | solution.py:21
  82.7 4.0 %collective-permute-start.15 = (bf16[128,128]{1,0:T(8,128)(2,1)S(1)}, bf16[128,128]{1,0:T(8,128)(2,1)S(1)}, u32[]{:S(2)}, u32[]{:S(2)}) collective-permute-start(bf16[128,128]{1,0:T(8,128)(2,1)S(1)} %fusion.126), channel_id=1, source_target_pairs={{0,2},{2,0},{4,6},{6,4},{8,10},{10,8},{12,14},{14,12},{16,18},{18,... | collective-permute-start | bytes 98312 | tf_op jit(solution)/shard_map/ppermute | solution.py:21
  84.2 4.6 %collective-permute-start.17 = (bf16[2,176,128]{2,1,0:T(8,128)(2,1)S(1)}, bf16[2,176,128]{2,1,0:T(8,128)(2,1)S(1)}, u32[]{:S(2)}, u32[]{:S(2)}) collective-permute-start(bf16[2,176,128]{2,1,0:T(8,128)(2,1)S(1)} %get-tuple-element.89), channel_id=1, source_target_pairs={{0,8},{2,10},{4,12},{6,14},{8,0},{10,2},{12,4},{14,6},{16,24},{18,... | collective-permute-start | bytes 270344 | tf_op jit(solution)/shard_map/ppermute | solution.py:21
  86.7 5.0 %collective-permute-start.16 = (bf16[2,128,128]{2,1,0:T(8,128)(2,1)S(1)}, bf16[2,128,128]{2,1,0:T(8,128)(2,1)S(1)}, u32[]{:S(2)}, u32[]{:S(2)}) collective-permute-start(bf16[2,128,128]{2,1,0:T(8,128)(2,1)S(1)} %get-tuple-element.94), channel_id=1, source_target_pairs={{0,4},{2,6},{4,0},{6,2},{8,12},{10,14},{12,8},{14,10},{16,20},{18,... | collective-permute-start | bytes 196616 | tf_op jit(solution)/shard_map/ppermute | solution.py:21
  87.3 7.8 %collective-permute-start.21 = (bf16[2,2,160,128]{3,2,1,0:T(8,128)(2,1)S(1)}, bf16[2,2,160,128]{3,2,1,0:T(8,128)(2,1)S(1)}, u32[]{:S(2)}, u32[]{:S(2)}) collective-permute-start(bf16[2,2,160,128]{3,2,1,0:T(8,128)(2,1)S(1)} %get-tuple-element.74), channel_id=1, source_target_pairs={{0,2},{2,0},{4,6},{6,4},{8,10},{10,8},{12,14},{14,12},{16,18},{18,... | collective-permute-start | bytes 491528 | tf_op jit(solution)/shard_map/ppermute | solution.py:21
  88.9 6.3 %collective-permute-start.20 = (bf16[2,2,176,128]{3,2,1,0:T(8,128)(2,1)S(1)}, bf16[2,2,176,128]{3,2,1,0:T(8,128)(2,1)S(1)}, u32[]{:S(2)}, u32[]{:S(2)}) collective-permute-start(bf16[2,2,176,128]{3,2,1,0:T(8,128)(2,1)S(1)} %get-tuple-element.68), channel_id=1, source_target_pairs={{0,4},{2,6},{4,0},{6,2},{8,12},{10,14},{12,8},{14,10},{16,20},{18,... | collective-permute-start | bytes 540680 | tf_op jit(solution)/shard_map/ppermute | solution.py:21
  91.7 7.8 %collective-permute-start.19 = (bf16[2,2,128,128]{3,2,1,0:T(8,128)(2,1)S(1)}, bf16[2,2,128,128]{3,2,1,0:T(8,128)(2,1)S(1)}, u32[]{:S(2)}, u32[]{:S(2)}) collective-permute-start(bf16[2,2,128,128]{3,2,1,0:T(8,128)(2,1)S(1)} %fusion.101), channel_id=1, source_target_pairs={{0,16},{2,18},{4,20},{6,22},{8,24},{10,26},{12,28},{14,30},{16,0},... | collective-permute-start | bytes 393224 | tf_op jit(solution)/shard_map/ppermute | solution.py:21
  99.5 6.4 %collective-permute-start.22 = (bf16[2,2,2,128,128]{4,3,2,1,0:T(8,128)(2,1)S(1)}, bf16[2,2,2,128,128]{4,3,2,1,0:T(8,128)(2,1)S(1)}, u32[]{:S(2)}, u32[]{:S(2)}) collective-permute-start(bf16[2,2,2,128,128]{4,3,2,1,0:T(8,128)(2,1)S(1)} %fusion.65), channel_id=1, source_target_pairs={{0,8},{2,10},{4,12},{6,14},{8,0},{10,2},{12,4},{14,6},{16,24},{18,... | collective-permute-start | bytes 786440 | tf_op jit(solution)/shard_map/ppermute | solution.py:21
  99.7 7.5 %collective-permute-start.24 = (bf16[2,2,2,176,128]{4,3,2,1,0:T(8,128)(2,1)S(1)}, bf16[2,2,2,176,128]{4,3,2,1,0:T(8,128)(2,1)S(1)}, u32[]{:S(2)}, u32[]{:S(2)}) collective-permute-start(bf16[2,2,2,176,128]{4,3,2,1,0:T(8,128)(2,1)S(1)} %get-tuple-element.58), channel_id=1, source_target_pairs={{0,2},{2,0},{4,6},{6,4},{8,10},{10,8},{12,14},{14,12},{16,18},{18,... | collective-permute-start | bytes 1081352 | tf_op jit(solution)/shard_map/ppermute | solution.py:21
  101.4 7.1 %collective-permute-start.25 = (bf16[2,2,2,160,128]{4,3,2,1,0:T(8,128)(2,1)S(1)}, bf16[2,2,2,160,128]{4,3,2,1,0:T(8,128)(2,1)S(1)}, u32[]{:S(2)}, u32[]{:S(2)}) collective-permute-start(bf16[2,2,2,160,128]{4,3,2,1,0:T(8,128)(2,1)S(1)} %get-tuple-element.64), channel_id=1, source_target_pairs={{0,4},{2,6},{4,0},{6,2},{8,12},{10,14},{12,8},{14,10},{16,20},{18,... | collective-permute-start | bytes 983048 | tf_op jit(solution)/shard_map/ppermute | solution.py:21
  106.1 2.7 %collective-permute-start.23 = (bf16[16,128,128]{2,1,0:T(8,128)(2,1)S(1)}, bf16[16,128,128]{2,1,0:T(8,128)(2,1)S(1)}, u32[]{:S(2)}, u32[]{:S(2)}) collective-permute-start(bf16[16,128,128]{2,1,0:T(8,128)(2,1)S(1)} %bitcast.348), channel_id=1, source_target_pairs={{0,1},{1,0},{2,3},{3,2},{4,5},{5,4},{6,7},{7,6},{8,9},{9,8},{10,11... | collective-permute-start | bytes 1572872 | tf_op jit(solution)/shard_map/ppermute | solution.py:21
  107.3 3.5 %collective-permute-start.26 = (bf16[16,176,128]{2,1,0:T(8,128)(2,1)S(1)}, bf16[16,176,128]{2,1,0:T(8,128)(2,1)S(1)}, u32[]{:S(2)}, u32[]{:S(2)}) collective-permute-start(bf16[16,176,128]{2,1,0:T(8,128)(2,1)S(1)} %bitcast.344), channel_id=1, source_target_pairs={{0,1},{1,0},{2,3},{3,2},{4,5},{5,4},{6,7},{7,6},{8,9},{9,8},{10,11... | collective-permute-start | bytes 2162696 | tf_op jit(solution)/shard_map/ppermute | solution.py:21
  108.6 2.2 collective-permute-start.27
  127.8 4.5 %collective-permute-start.30 = (f32[4,256]{1,0:T(4,128)S(1)}, f32[4,256]{1,0:T(4,128)S(1)}, u32[]{:S(2)}, u32[]{:S(2)}) collective-permute-start(f32[4,256]{1,0:T(4,128)S(1)} %slice.530), channel_id=1, source_target_pairs={{0,6},{2,4},{4,2},{6,0},{8,14},{10,12},{12,10},{14,8},{16,22},{18,... | collective-permute-start | bytes 12296 | tf_op jit(solution)/shard_map/ppermute | solution.py:21
  129.0 3.6 %collective-permute-start.29 = (f32[4,256]{1,0:T(4,128)S(1)}, f32[4,256]{1,0:T(4,128)S(1)}, u32[]{:S(2)}, u32[]{:S(2)}) collective-permute-start(f32[4,256]{1,0:T(4,128)S(1)} %slice.530), channel_id=1, source_target_pairs={{0,4},{2,6},{4,0},{6,2},{8,12},{10,14},{12,8},{14,10},{16,20},{18,... | collective-permute-start | bytes 12296 | tf_op jit(solution)/shard_map/ppermute | solution.py:21
  130.6 3.6 %collective-permute-start.28 = (f32[4,256]{1,0:T(4,128)S(1)}, f32[4,256]{1,0:T(4,128)S(1)}, u32[]{:S(2)}, u32[]{:S(2)}) collective-permute-start(f32[4,256]{1,0:T(4,128)S(1)} %slice.530), channel_id=1, source_target_pairs={{0,2},{2,0},{4,6},{6,4},{8,10},{10,8},{12,14},{14,12},{16,18},{18,... | collective-permute-start | bytes 12296 | tf_op jit(solution)/shard_map/ppermute | solution.py:21
  134.3 6.0 %collective-permute-start.33 = (f32[4,256]{1,0:T(4,128)S(1)}, f32[4,256]{1,0:T(4,128)S(1)}, u32[]{:S(2)}, u32[]{:S(2)}) collective-permute-start(f32[4,256]{1,0:T(4,128)S(1)} %fusion.138), channel_id=1, source_target_pairs={{0,24},{2,26},{4,28},{6,30},{8,16},{10,18},{12,20},{14,22},{16,8},... | collective-permute-start | bytes 12296 | tf_op jit(solution)/shard_map/ppermute | solution.py:21
  138.3 4.5 %collective-permute-start.32 = (f32[4,256]{1,0:T(4,128)S(1)}, f32[4,256]{1,0:T(4,128)S(1)}, u32[]{:S(2)}, u32[]{:S(2)}) collective-permute-start(f32[4,256]{1,0:T(4,128)S(1)} %fusion.138), channel_id=1, source_target_pairs={{0,16},{2,18},{4,20},{6,22},{8,24},{10,26},{12,28},{14,30},{16,0},... | collective-permute-start | bytes 12296 | tf_op jit(solution)/shard_map/ppermute | solution.py:21
  138.3 4.5 %collective-permute-start.31 = (f32[4,256]{1,0:T(4,128)S(1)}, f32[4,256]{1,0:T(4,128)S(1)}, u32[]{:S(2)}, u32[]{:S(2)}) collective-permute-start(f32[4,256]{1,0:T(4,128)S(1)} %fusion.138), channel_id=1, source_target_pairs={{0,8},{2,10},{4,12},{6,14},{8,0},{10,2},{12,4},{14,6},{16,24},{18,... | collective-permute-start | bytes 12296 | tf_op jit(solution)/shard_map/ppermute | solution.py:21
  142.9 1.2 collective-permute-start.34
  161.0 3.9 %collective-permute-start.35 = (bf16[8,2,448,128]{3,2,1,0:T(8,128)(2,1)S(1)}, bf16[8,2,448,128]{3,2,1,0:T(8,128)(2,1)S(1)}, u32[]{:S(2)}, u32[]{:S(2)}) collective-permute-start(bf16[8,2,448,128]{3,2,1,0:T(8,128)(2,1)S(1)} %get-tuple-element.32), channel_id=1, source_target_pairs={{0,1},{1,0},{2,3},{3,2},{4,5},{5,4},{6,7},{7,6},{8,9},{9,8},{10,11... | collective-permute-start | bytes 5505032 | tf_op jit(solution)/shard_map/ppermute | solution.py:21
  165.7 10.9 %collective-permute-start.44 = (bf16[2,2,2,112,128]{4,3,2,1,0:T(8,128)(2,1)S(1)}, bf16[2,2,2,112,128]{4,3,2,1,0:T(8,128)(2,1)S(1)}, u32[]{:S(2)}, u32[]{:S(2)}) collective-permute-start(bf16[2,2,2,112,128]{4,3,2,1,0:T(8,128)(2,1)S(1)} %fusion.84), channel_id=1, source_target_pairs={{0,8},{2,10},{4,12},{6,14},{8,0},{10,2},{12,4},{14,6},{16,24},{18,... | collective-permute-start | bytes 688136 | tf_op jit(solution)/shard_map/ppermute | solution.py:21
  165.8 9.8 %collective-permute-start.40 = (bf16[2,2,2,160,128]{4,3,0,1,2:T(8,128)(2,1)S(1)}, bf16[2,2,2,160,128]{4,3,0,1,2:T(8,128)(2,1)S(1)}, u32[]{:S(2)}, u32[]{:S(2)}) collective-permute-start(bf16[2,2,2,160,128]{4,3,0,1,2:T(8,128)(2,1)S(1)} %fusion.62), channel_id=1, source_target_pairs={{0,4},{2,6},{4,0},{6,2},{8,12},{10,14},{12,8},{14,10},{16,20},{18,... | collective-permute-start | bytes 983048 | tf_op jit(solution)/shard_map/ppermute | solution.py:21
  166.4 10.2 %collective-permute-start.36 = (bf16[2,2,2,176,128]{4,3,2,1,0:T(8,128)(2,1)S(1)}, bf16[2,2,2,176,128]{4,3,2,1,0:T(8,128)(2,1)S(1)}, u32[]{:S(2)}, u32[]{:S(2)}) collective-permute-start(bf16[2,2,2,176,128]{4,3,2,1,0:T(8,128)(2,1)S(1)} %fusion.55), channel_id=1, source_target_pairs={{0,2},{2,0},{4,6},{6,4},{8,10},{10,8},{12,14},{14,12},{16,18},{18,... | collective-permute-start | bytes 1081352 | tf_op jit(solution)/shard_map/ppermute | solution.py:21
  175.8 10.9 %collective-permute-start.41 = (bf16[2,2,160,128]{3,2,0,1:T(8,128)(2,1)S(1)}, bf16[2,2,160,128]{3,2,0,1:T(8,128)(2,1)S(1)}, u32[]{:S(2)}, u32[]{:S(2)}) collective-permute-start(bf16[2,2,160,128]{3,2,0,1:T(8,128)(2,1)S(1)} %fusion.97), channel_id=1, source_target_pairs={{0,2},{2,0},{4,6},{6,4},{8,10},{10,8},{12,14},{14,12},{16,18},{18,... | collective-permute-start | bytes 491528 | tf_op jit(solution)/shard_map/ppermute | solution.py:21
  176.7 11.9 %collective-permute-start.45 = (bf16[2,2,112,128]{3,2,1,0:T(8,128)(2,1)S(1)}, bf16[2,2,112,128]{3,2,1,0:T(8,128)(2,1)S(1)}, u32[]{:S(2)}, u32[]{:S(2)}) collective-permute-start(bf16[2,2,112,128]{3,2,1,0:T(8,128)(2,1)S(1)} %fusion.104), channel_id=1, source_target_pairs={{0,16},{2,18},{4,20},{6,22},{8,24},{10,26},{12,28},{14,30},{16,0},... | collective-permute-start | bytes 344072 | tf_op jit(solution)/shard_map/ppermute | solution.py:21
  178.9 9.7 %collective-permute-start.37 = (bf16[2,2,176,128]{3,2,1,0:T(8,128)(2,1)S(1)}, bf16[2,2,176,128]{3,2,1,0:T(8,128)(2,1)S(1)}, u32[]{:S(2)}, u32[]{:S(2)}) collective-permute-start(bf16[2,2,176,128]{3,2,1,0:T(8,128)(2,1)S(1)} %fusion.91), channel_id=1, source_target_pairs={{0,4},{2,6},{4,0},{6,2},{8,12},{10,14},{12,8},{14,10},{16,20},{18,... | collective-permute-start | bytes 540680 | tf_op jit(solution)/shard_map/ppermute | solution.py:21
  186.7 4.5 %collective-permute-start.42 = (bf16[2,160,128]{2,1,0:T(8,128)(2,1)S(1)}, bf16[2,160,128]{2,1,0:T(8,128)(2,1)S(1)}, u32[]{:S(2)}, u32[]{:S(2)}) collective-permute-start(bf16[2,160,128]{2,1,0:T(8,128)(2,1)S(1)} %fusion.112), channel_id=1, source_target_pairs={{0,8},{2,10},{4,12},{6,14},{8,0},{10,2},{12,4},{14,6},{16,24},{18,... | collective-permute-start | bytes 245768 | tf_op jit(solution)/shard_map/ppermute | solution.py:21
  188.7 4.2 %collective-permute-start.46 = (bf16[2,112,128]{2,1,0:T(8,128)(2,1)S(1)}, bf16[2,112,128]{2,1,0:T(8,128)(2,1)S(1)}, u32[]{:S(2)}, u32[]{:S(2)}) collective-permute-start(bf16[2,112,128]{2,1,0:T(8,128)(2,1)S(1)} %fusion.117), channel_id=1, source_target_pairs={{0,4},{2,6},{4,0},{6,2},{8,12},{10,14},{12,8},{14,10},{16,20},{18,... | collective-permute-start | bytes 172040 | tf_op jit(solution)/shard_map/ppermute | solution.py:21
  188.9 7.7 %collective-permute-start.38 = (bf16[2,176,128]{2,1,0:T(8,128)(2,1)S(1)}, bf16[2,176,128]{2,1,0:T(8,128)(2,1)S(1)}, u32[]{:S(2)}, u32[]{:S(2)}) collective-permute-start(bf16[2,176,128]{2,1,0:T(8,128)(2,1)S(1)} %fusion.108), channel_id=1, source_target_pairs={{0,8},{2,10},{4,12},{6,14},{8,0},{10,2},{12,4},{14,6},{16,24},{18,... | collective-permute-start | bytes 270344 | tf_op jit(solution)/shard_map/ppermute | solution.py:21
  191.2 5.4 %collective-permute-start.43 = (bf16[160,128]{1,0:T(8,128)(2,1)S(1)}, bf16[160,128]{1,0:T(8,128)(2,1)S(1)}, u32[]{:S(2)}, u32[]{:S(2)}) collective-permute-start(bf16[160,128]{1,0:T(8,128)(2,1)S(1)} %fusion.121), channel_id=1, source_target_pairs={{0,16},{2,18},{4,20},{6,22},{8,24},{10,26},{12,28},{14,30},{16,0},... | collective-permute-start | bytes 122888 | tf_op jit(solution)/shard_map/ppermute | solution.py:21
  193.0 4.6 %collective-permute-start.47 = (bf16[112,128]{1,0:T(8,128)(2,1)S(1)}, bf16[112,128]{1,0:T(8,128)(2,1)S(1)}, u32[]{:S(2)}, u32[]{:S(2)}) collective-permute-start(bf16[112,128]{1,0:T(8,128)(2,1)S(1)} %fusion.131), channel_id=1, source_target_pairs={{0,2},{2,0},{4,6},{6,4},{8,10},{10,8},{12,14},{14,12},{16,18},{18,... | collective-permute-start | bytes 86024 | tf_op jit(solution)/shard_map/ppermute | solution.py:21
  196.7 5.0 %collective-permute-start.39 = (bf16[176,128]{1,0:T(8,128)(2,1)S(1)}, bf16[176,128]{1,0:T(8,128)(2,1)S(1)}, u32[]{:S(2)}, u32[]{:S(2)}) collective-permute-start(bf16[176,128]{1,0:T(8,128)(2,1)S(1)} %fusion.120), channel_id=1, source_target_pairs={{0,16},{2,18},{4,20},{6,22},{8,24},{10,26},{12,28},{14,30},{16,0},... | collective-permute-start | bytes 135176 | tf_op jit(solution)/shard_map/ppermute | solution.py:21
  201.9 1.4 collective-permute-start.48
  208.7 17.6 %collective-permute-start.49 = (bf16[2,2,2,16,2688]{4,3,2,1,0:T(8,128)(2,1)S(1)}, bf16[2,2,2,16,2688]{4,3,2,1,0:T(8,128)(2,1)S(1)}, u32[]{:S(2)}, u32[]{:S(2)}) collective-permute-start(bf16[2,2,2,16,2688]{4,3,2,1,0:T(8,128)(2,1)S(1)} %fusion.36), channel_id=1, source_target_pairs={{0,2},{2,0},{4,6},{6,4},{8,10},{10,8},{12,14},{14,12},{16,18},{18,... | collective-permute-start | bytes 2064392 | tf_op jit(solution)/shard_map/ppermute | solution.py:21
  209.6 17.3 %collective-permute-start.54 = (bf16[2,2,2,16,2688]{4,3,0,1,2:T(8,128)(2,1)S(1)}, bf16[2,2,2,16,2688]{4,3,0,1,2:T(8,128)(2,1)S(1)}, u32[]{:S(2)}, u32[]{:S(2)}) collective-permute-start(bf16[2,2,2,16,2688]{4,3,0,1,2:T(8,128)(2,1)S(1)} %fusion.37), channel_id=1, source_target_pairs={{0,4},{2,6},{4,0},{6,2},{8,12},{10,14},{12,8},{14,10},{16,20},{18,... | collective-permute-start | bytes 2064392 | tf_op jit(solution)/shard_map/ppermute | solution.py:21
  210.9 12.1 %collective-permute-start.51 = (bf16[2,2,2,16,1792]{4,3,2,1,0:T(8,128)(2,1)S(1)}, bf16[2,2,2,16,1792]{4,3,2,1,0:T(8,128)(2,1)S(1)}, u32[]{:S(2)}, u32[]{:S(2)}) collective-permute-start(bf16[2,2,2,16,1792]{4,3,2,1,0:T(8,128)(2,1)S(1)} %fusion.47), channel_id=1, source_target_pairs={{0,8},{2,10},{4,12},{6,14},{8,0},{10,2},{12,4},{14,6},{16,24},{18,... | collective-permute-start | bytes 1376264 | tf_op jit(solution)/shard_map/ppermute | solution.py:21
  227.2 14.8 %collective-permute-start.55 = (bf16[2,2,16,1792]{3,2,1,0:T(8,128)(2,1)S(1)}, bf16[2,2,16,1792]{3,2,1,0:T(8,128)(2,1)S(1)}, u32[]{:S(2)}, u32[]{:S(2)}) collective-permute-start(bf16[2,2,16,1792]{3,2,1,0:T(8,128)(2,1)S(1)} %fusion.83), channel_id=1, source_target_pairs={{0,16},{2,18},{4,20},{6,22},{8,24},{10,26},{12,28},{14,30},{16,0},... | collective-permute-start | bytes 688136 | tf_op jit(solution)/shard_map/ppermute | solution.py:21
  228.5 13.5 %collective-permute-start.50 = (bf16[2,2,16,2688]{3,2,1,0:T(8,128)(2,1)S(1)}, bf16[2,2,16,2688]{3,2,1,0:T(8,128)(2,1)S(1)}, u32[]{:S(2)}, u32[]{:S(2)}) collective-permute-start(bf16[2,2,16,2688]{3,2,1,0:T(8,128)(2,1)S(1)} %fusion.58), channel_id=1, source_target_pairs={{0,4},{2,6},{4,0},{6,2},{8,12},{10,14},{12,8},{14,10},{16,20},{18,... | collective-permute-start | bytes 1032200 | tf_op jit(solution)/shard_map/ppermute | solution.py:21
  230.0 12.0 %collective-permute-start.56 = (bf16[2,2,16,2688]{3,2,0,1:T(8,128)(2,1)S(1)}, bf16[2,2,16,2688]{3,2,0,1:T(8,128)(2,1)S(1)}, u32[]{:S(2)}, u32[]{:S(2)}) collective-permute-start(bf16[2,2,16,2688]{3,2,0,1:T(8,128)(2,1)S(1)} %fusion.59), channel_id=1, source_target_pairs={{0,2},{2,0},{4,6},{6,4},{8,10},{10,8},{12,14},{14,12},{16,18},{18,... | collective-permute-start | bytes 1032200 | tf_op jit(solution)/shard_map/ppermute | solution.py:21
  242.2 4.9 %collective-permute-start.57 = (bf16[2,16,1792]{2,1,0:T(8,128)(2,1)S(1)}, bf16[2,16,1792]{2,1,0:T(8,128)(2,1)S(1)}, u32[]{:S(2)}, u32[]{:S(2)}) collective-permute-start(bf16[2,16,1792]{2,1,0:T(8,128)(2,1)S(1)} %fusion.105), channel_id=1, source_target_pairs={{0,4},{2,6},{4,0},{6,2},{8,12},{10,14},{12,8},{14,10},{16,20},{18,... | collective-permute-start | bytes 344072 | tf_op jit(solution)/shard_map/ppermute | solution.py:21
  243.8 6.8 %collective-permute-start.52 = (bf16[2,16,2688]{2,1,0:T(8,128)(2,1)S(1)}, bf16[2,16,2688]{2,1,0:T(8,128)(2,1)S(1)}, u32[]{:S(2)}, u32[]{:S(2)}) collective-permute-start(bf16[2,16,2688]{2,1,0:T(8,128)(2,1)S(1)} %fusion.93), channel_id=1, source_target_pairs={{0,8},{2,10},{4,12},{6,14},{8,0},{10,2},{12,4},{14,6},{16,24},{18,... | collective-permute-start | bytes 516104 | tf_op jit(solution)/shard_map/ppermute | solution.py:21
  246.4 6.0 %collective-permute-start.59 = (bf16[2,16,2688]{2,1,0:T(8,128)(2,1)S(1)}, bf16[2,16,2688]{2,1,0:T(8,128)(2,1)S(1)}, u32[]{:S(2)}, u32[]{:S(2)}) collective-permute-start(bf16[2,16,2688]{2,1,0:T(8,128)(2,1)S(1)} %fusion.94), channel_id=1, source_target_pairs={{0,8},{2,10},{4,12},{6,14},{8,0},{10,2},{12,4},{14,6},{16,24},{18,... | collective-permute-start | bytes 516104 | tf_op jit(solution)/shard_map/ppermute | solution.py:21
  247.1 14.2 %copy-start.14 = (bf16[16,3584]{1,0:T(8,128)(2,1)S(1)}, bf16[16,3584]{1,0:T(8,128)(2,1)}, u32[]{:S(2)}) copy-start(bf16[16,3584]{1,0:T(8,128)(2,1)} %param.11) | copy-start | bytes 344068
  247.1 14.2 %copy-start.17 = (f32[3584]{0:T(1024)S(1)}, f32[3584]{0:T(1024)}, u32[]{:S(2)}) copy-start(f32[3584]{0:T(1024)} %param.13) | copy-start | bytes 43012
  247.1 6.8 %collective-permute-start.58 = (bf16[16,1792]{1,0:T(8,128)(2,1)S(1)}, bf16[16,1792]{1,0:T(8,128)(2,1)S(1)}, u32[]{:S(2)}, u32[]{:S(2)}) collective-permute-start(bf16[16,1792]{1,0:T(8,128)(2,1)S(1)} %fusion.118), channel_id=1, source_target_pairs={{0,2},{2,0},{4,6},{6,4},{8,10},{10,8},{12,14},{14,12},{16,18},{18,... | collective-permute-start | bytes 172040 | tf_op jit(solution)/shard_map/ppermute | solution.py:21
  252.4 5.4 %collective-permute-start.60 = (bf16[16,2688]{1,0:T(8,128)(2,1)S(1)}, bf16[16,2688]{1,0:T(8,128)(2,1)S(1)}, u32[]{:S(2)}, u32[]{:S(2)}) collective-permute-start(bf16[16,2688]{1,0:T(8,128)(2,1)S(1)} %fusion.111), channel_id=1, source_target_pairs={{0,16},{2,18},{4,20},{6,22},{8,24},{10,26},{12,28},{14,30},{16,0},... | collective-permute-start | bytes 258056 | tf_op jit(solution)/shard_map/ppermute | solution.py:21
  253.9 7.3 %collective-permute-start.53 = (bf16[16,2688]{1,0:T(8,128)(2,1)S(1)}, bf16[16,2688]{1,0:T(8,128)(2,1)S(1)}, u32[]{:S(2)}, u32[]{:S(2)}) collective-permute-start(bf16[16,2688]{1,0:T(8,128)(2,1)S(1)} %fusion.110), channel_id=1, source_target_pairs={{0,16},{2,18},{4,20},{6,22},{8,24},{10,26},{12,28},{14,30},{16,0},... | collective-permute-start | bytes 258056 | tf_op jit(solution)/shard_map/ppermute | solution.py:21
  (23 other events, 110.1 us)

commit v5 on v4

--- a/solution.py
+++ b/solution.py
@@ -40,50 +40,62 @@
 
 def gather(first, second, third):
     high = list(reversed(range(2, bits_of("seq"))))
-    array_shape = third.shape
+    third_shape = third.shape
     came = []
     for bit in high:
         came = [from_partner(first, "seq", 1 << bit), from_partner(second, "seq", 1 << bit)]
         if bit == high[0]:
             third = third + zero_of(came[0], third.shape) + zero_of(came[1], third.shape)
         first, second = jnp.stack([first, came[0]]), jnp.stack([second, came[1]])
-    waits = [came]
     for bit in (0, 1):
-        waits.append([from_partner(first, "seq", 2 >> bit), from_partner(second, "seq", 1 << bit)])
-        first, second = jnp.stack([first, waits[-1][0]]), jnp.stack([second, waits[-1][1]])
+        first = jnp.stack([first, from_partner(first, "seq", 2 >> bit)])
+        second = jnp.stack([second, from_partner(second, "seq", 1 << bit)])
         third = jnp.stack([third, from_partner(third, "seq", 1 << bit)])
-    for step, bit in enumerate(high):
-        for block in waits[step] if step < 2 else ():
-            third = third + zero_of(block, array_shape)
-        third = jnp.stack([third, from_partner(third, "seq", 1 << bit)])
-    return in_order(first, high + [1, 0]), in_order(second, high + [0, 1]), in_order(third, [0, 1] + high)
+    for block in came:
+        third = third + zero_of(block, third_shape)
+    far = range(1, 1 << len(high))
+    third = jnp.stack([third] + [from_partner(third, "seq", place << 2) for place in far])
+    third = third.reshape((-1,) + third_shape)
+    return in_order(first, high + [1, 0]), in_order(second, high + [0, 1]), third
 
 
 def scatter(arrays, beside=()):
     count = bits_of("seq")
-    arrays = [array.reshape((2,) * count + array.shape[1:]) for array in arrays]
     low, high = [0, 1], list(range(2, count))
-    orders = [low + high, low[::-1] + high, high + low[::-1]]
-    left = [list(reversed(range(count))) for _ in arrays]
+    third = arrays[2].reshape((1 << len(high), 2, 2) + arrays[2].shape[1:])
+    far = [
+        from_partner(third[place].astype(bf16), "seq", place << 2)
+        for place in range(1, 1 << len(high))
+    ]
+    arrays = [array.reshape((2,) * count + array.shape[1:]) for array in arrays[:2]]
+    orders = [low + high, low[::-1] + high, [None, None, 1, 0] + [None] * len(high[2:])]
+    left = [list(reversed(range(count))), list(reversed(range(count))), [1, 0]]
     results = []
-    last = None
+    last = far[0]
     for step in range(count):
-        kept, came = [], []
-        for k, order in enumerate(orders):
-            bit = order[step]
+        sums, came = [], []
+        for k, array in enumerate(arrays):
+            bit = orders[k][step]
+            if bit is None:
+                sums.append(array)
+                continue
             dim = left[k].index(bit)
             left[k].remove(bit)
-            sent = lax.index_in_dim(arrays[k], 1, dim, keepdims=False).astype(bf16)
-            kept.append(lax.index_in_dim(arrays[k], 0, dim, keepdims=False).astype(f32))
+            sent = lax.index_in_dim(array, 1, dim, keepdims=False).astype(bf16)
+            kept = lax.index_in_dim(array, 0, dim, keepdims=False).astype(f32)
             came.append(from_partner(sent, "seq", 1 << bit))
-        sums = [one + other.astype(f32) for one, other in zip(kept, came)]
+            sums.append(kept + came[-1].astype(f32))
         if step < len(beside):
-            result, zeros = beside[step](came[2] if last is None else last, sums[0].shape, results)
+            result, zeros = beside[step](last, sums[0].shape, results)
             results.append(result)
             if zeros is not None:
                 sums[0] = sums[0] + zeros
-        if step < 2:
-            sums[2] = sums[2] + zero_of(came[0], sums[2].shape) + zero_of(came[1], sums[2].shape)
+        if step == 1:
+            total = third[0].astype(f32)
+            for block in far:
+                total = total + block.astype(f32)
+            shape = third.shape[3:]
+            sums.append(total + zero_of(came[0], shape) + zero_of(came[1], shape))
         arrays, last = sums, came[0]
     return arrays, results
 
@@ -155,17 +167,15 @@
     def _():
         for device in range(blocks):
             for side in range(2):
-                start = device * features
+                done = 0
                 columns = slice(side * lanes, (side + 1) * lanes)
                 for piece in pieces[3 * side : 3 * side + 3]:
-                    rows = min(piece.shape[1], (device + 1) * features - start)
-                    all_features[start : start + rows, columns] = piece[where[0] ^ device][:rows]
-                    start += rows
-        columns_of_gain = gain[...].T
-        for k in range(gain.shape[0]):
-            part = slice(128 * k, 128 * (k + 1))
-            values = all_features[part, :].astype(f32) * scale[...] * columns_of_gain[:, k : k + 1]
-            all_features[part, :] = values.astype(bf16)
+                    rows = min(piece.shape[1], features - done)
+                    values = piece[where[0] ^ device][:rows].astype(f32) * scale[:, columns]
+                    values = values * gain[done : done + rows, device : device + 1]
+                    start = device * features + done
+                    all_features[start : start + rows, columns] = values.astype(bf16)
+                    done += rows
         stats[...] = jnp.zeros_like(stats)
         stats[0:1, :] = jnp.full((1, stats.shape[1]), -jnp.inf, f32)
 
@@ -187,7 +197,7 @@
 def head_logits(where, ids, scale, gain, pieces, head):
     vocab, tokens = head.shape[0], ids.shape[1]
     tile = 512
-    gain = gain.reshape(-1, 128)
+    gain = gain.reshape(pieces[0].shape[0], -1).T
     whole = lambda array: pl.BlockSpec(array.shape, lambda i, w: (0,) * array.ndim)
     return pl.pallas_call(
         logits_kernel,
@@ -235,15 +245,15 @@
             entries = lax.broadcasted_iota(i32, probs.shape, 0) + (where[1] + start)
             dlogits = coef * (probs - (entries == ids[...]).astype(f32))
             plain[start : start + tile, :] = dlogits.astype(bf16)
-            turned[:, start : start + tile] = dlogits.T.astype(bf16)
-
-    product = jnp.dot(turned[...], head[...], preferred_element_type=f32).T
-    half = product.shape[0] // 2
+            turned[:, start : start + tile] = dlogits.astype(bf16).T
+
+    product = jnp.dot(turned[...], head[...], preferred_element_type=f32)
+    mine, other = product[:lanes].T, product[lanes:].astype(bf16).T
+    half = mine.shape[0] // 2
     flip = where[0] & 1
     for piece in range(2):
-        block = product[piece * half : (piece + 1) * half]
-        kept[0, piece ^ flip] = block[:, :lanes]
-        sent[0, piece ^ flip] = block[:, lanes:].astype(bf16)
+        kept[0, piece ^ flip] = mine[piece * half : (piece + 1) * half]
+        sent[0, piece ^ flip] = other[piece * half : (piece + 1) * half]
 
 
 def head_back(where, ids, rows, logits, head, blocks):
@@ -490,9 +500,8 @@
                 return dot(dlogits, final_all, 1, 1).astype(bf16), None
             before = results[-1] if results else None
             shape = shape if tied else (8, 128)
-            out, zeros = grad_head_rows(
-                dlogits, final_all, index, 4, last if tied else from_core, shape, before
-            )
+            later_than = last if tied else from_core
+            out, zeros = grad_head_rows(dlogits, final_all, index, 4, later_than, shape, before)
             return out, (zeros if tied else None)
 
         return work
@@ -516,9 +525,7 @@
             grad_head = before[-1] if before else results[-1]
             if not fits:
                 return grad_head, None
-            shape = shape if index == 3 else (8, 128)
-            out, zeros = grad_head_rows(dlogits, final_all, index, 4, last, shape, grad_head)
-            return out, (zeros if index == 3 else None)
+            return grad_head_rows(dlogits, final_all, index, 4, last, shape, grad_head)
 
         return work
 

time: 266 us -> 265 us (level)
  starting transfers between devices: 71.4 us -> 78.7 us
  other arithmetic: 19.7 us -> 13 us
  waiting for transfers between devices: 84.5 us -> 90.4 us
  matrix products: 16.9 us -> 12.2 us
  local copies, waits for them, and re-layouts: 9.6 us -> 6.08 us
    ppermute x61 -> x65, starting transfers between devices: 71.4 us -> 78.7 us  [from_partner(): return lax.ppermute(array, axis, [(i, i ^ mask) for i in range(size)])]
    ppermute x61 -> x65, waiting for transfers between devices: 84.5 us -> 90.4 us  [from_partner(): return lax.ppermute(array, axis, [(i, i ^ mask) for i in range(size)])]
    dot_general x14, matrix products: 16.9 us -> 12.2 us  [dot(): lax.dot_general(left, right, (((on_left,), (on_right,)), ((), ())), preci...]
    unnamed x52 -> x36, local copies, waits for them, and re-layouts: 7.04 us -> 3.81 us
  transfers between devices with their start and end apart: 61 -> 65, of which waited for: 37 -> 38; matrix products, arithmetic and copies ran while one was open for 9% -> 6% of each run, Pallas kernels for 9% -> 9%
where the time goes in v5:
time: 265 us; the launch traced here: 264 us
  waiting for transfers between devices  90.4 us (34%)
  starting transfers between devices  78.7 us (30%)
  Pallas kernels  55.7 us (21%)
  other arithmetic  13 us (5%)
  matrix products  12.2 us (5%)
  local copies, waits for them, and re-layouts  6.08 us (2%)
  blocking collectives  5.05 us (2%)
  between operations  3.18 us (1%)
    ppermute x65, waiting for transfers between devices, from_partner(): return lax.ppermute(array, axis, [(i, i ^ mask) for i in range(size)])  90.4 us
    ppermute x65, starting transfers between devices, from_partner(): return lax.ppermute(array, axis, [(i, i ^ mask) for i in range(size)])  78.7 us
    pallas_call x4, Pallas kernels, grad_head_rows(): pl.pallas_call(grad_head_kernel, grid=(D // tile,), in_specs=[pl.BlockSpe...  23.2 us
    pallas_call x1, Pallas kernels, head_back(): pl.pallas_call(dfinal_kernel, grid_spec=pltpu.PrefetchScalarGridSpec(num_...  16.7 us
    pallas_call x1, Pallas kernels, head_logits(): pl.pallas_call(logits_kernel, grid_spec=pltpu.PrefetchScalarGridSpec(num_...  15.9 us
    dot_general x14, matrix products, dot(): lax.dot_general(left, right, (((on_left,), (on_right,)), ((), ())), preci...  12.2 us
  transfers between devices with their start and end apart: 65, of which 38 were waited for; matrix products, arithmetic and copies ran while one was open for 6% of the time, Pallas kernels for 9%

profile of v5, /device:TPU:0, one launch (start us, length us, event | category | flops | bytes accessed | tf_op | source)
XLA Modules:
  0.0 264.4 jit_solution(428717396979208725)
XLA Ops:
  2.7 2.6 psum.14
  6.5 4.0 %collective-permute-start.4 = (bf16[16,2688]{1,0:T(8,128)(2,1)S(1)}, bf16[16,2688]{1,0:T(8,128)(2,1)S(1)}, u32[]{:S(2)}, u32[]{:S(2)}) collective-permute-start(bf16[16,2688]{1,0:T(8,128)(2,1)S(1)} %slice.615), channel_id=1, source_target_pairs={{0,16},{2,18},{4,20},{6,22},{8,24},{10,26},{12,28},{14,30},{16,0},... | collective-permute-start | bytes 258056 | tf_op jit(solution)/shard_map/ppermute | solution.py:21
  13.4 4.1 %collective-permute-done.4 = bf16[16,2688]{1,0:T(8,128)(2,1)S(1)} collective-permute-done((bf16[16,2688]{1,0:T(8,128)(2,1)S(1)}, bf16[16,2688]{1,0:T(8,128)(2,1)S(1)}, u32[]{:S(2)}, u32[]{:S(2)}) %collective-permute-start.4) | collective-permute-done | bytes 86048 | tf_op jit(solution)/shard_map/ppermute | solution.py:21
  17.5 1.4 collective-permute-done
  18.9 1.6 collective-permute-start.5
  21.4 1.4 collective-permute-start.1
  23.3 1.6 collective-permute-start.6
  24.9 3.0 %collective-permute-done.7 = bf16[2,16,2688]{2,1,0:T(8,128)(2,1)S(1)} collective-permute-done((bf16[2,16,2688]{2,1,0:T(8,128)(2,1)S(1)}, bf16[2,16,2688]{2,1,0:T(8,128)(2,1)S(1)}, u32[]{:S(2)}, u32[]{:S(2)}) %collective-permute-start.7) | collective-permute-done | bytes 172064 | tf_op jit(solution)/shard_map/ppermute | solution.py:21
  27.9 1.8 collective-permute-done.1
  30.7 1.4 collective-permute-start.2
  32.1 4.2 %collective-permute-start.10 = (bf16[2,2,16,1920]{3,2,1,0:T(8,128)(2,1)S(1)}, bf16[2,2,16,1920]{3,2,1,0:T(8,128)(2,1)S(1)}, u32[]{:S(2)}, u32[]{:S(2)}) collective-permute-start(bf16[2,2,16,1920]{3,2,1,0:T(8,128)(2,1)S(1)} %fusion.55), channel_id=1, source_target_pairs={{0,24},{2,26},{4,28},{6,30},{8,16},{10,18},{12,20},{14,22},{16,8},... | collective-permute-start | bytes 737288 | tf_op jit(solution)/shard_map/ppermute | solution.py:21
  37.0 6.2 %collective-permute-done.10 = bf16[2,2,16,1920]{3,2,1,0:T(8,128)(2,1)S(1)} collective-permute-done((bf16[2,2,16,1920]{3,2,1,0:T(8,128)(2,1)S(1)}, bf16[2,2,16,1920]{3,2,1,0:T(8,128)(2,1)S(1)}, u32[]{:S(2)}, u32[]{:S(2)}) %collective-permute-start.10) | collective-permute-done | bytes 245792 | tf_op jit(solution)/shard_map/ppermute | solution.py:21
  43.2 12.4 %collective-permute-done.9 = bf16[2,2,16,1920]{3,2,1,0:T(8,128)(2,1)S(1)} collective-permute-done((bf16[2,2,16,1920]{3,2,1,0:T(8,128)(2,1)S(1)}, bf16[2,2,16,1920]{3,2,1,0:T(8,128)(2,1)S(1)}, u32[]{:S(2)}, u32[]{:S(2)}) %collective-permute-start.9) | collective-permute-done | bytes 245792 | tf_op jit(solution)/shard_map/ppermute | solution.py:21
  57.4 1.6 collective-permute-start.3
  60.0 13.2 %collective-permute-done.12 = bf16[2,2,2,16,2688]{4,3,2,1,0:T(8,128)(2,1)S(1)} collective-permute-done((bf16[2,2,2,16,2688]{4,3,2,1,0:T(8,128)(2,1)S(1)}, bf16[2,2,2,16,2688]{4,3,2,1,0:T(8,128)(2,1)S(1)}, u32[]{:S(2)}, u32[]{:S(2)}) %collective-permute-start.12) | collective-permute-done | bytes 688160 | tf_op jit(solution)/shard_map/ppermute | solution.py:21
  78.3 2.9 %collective-permute-start.14 = (bf16[176,128]{1,0:T(8,128)(2,1)S(1)}, bf16[176,128]{1,0:T(8,128)(2,1)S(1)}, u32[]{:S(2)}, u32[]{:S(2)}) collective-permute-start(bf16[176,128]{1,0:T(8,128)(2,1)S(1)} %get-tuple-element.93), channel_id=1, source_target_pairs={{0,16},{2,18},{4,20},{6,22},{8,24},{10,26},{12,28},{14,30},{16,0},... | collective-permute-start | bytes 135176 | tf_op jit(solution)/shard_map/ppermute | solution.py:21
  81.2 2.1 collective-permute-done.15
  84.3 1.6 collective-permute-start.16
  85.9 1.3 collective-permute-start.18
  88.3 1.6 collective-permute-start.17
  89.9 1.6 collective-permute-start.26
  93.3 2.2 collective-permute-start.22
  96.0 1.8 collective-permute-start.20
  97.8 1.3 collective-permute-start.25
  99.2 1.4 collective-permute-start.27
  100.7 3.6 %collective-permute-done.21 = bf16[2,2,128,128]{3,2,1,0:T(8,128)(2,1)S(1)} collective-permute-done((bf16[2,2,128,128]{3,2,1,0:T(8,128)(2,1)S(1)}, bf16[2,2,128,128]{3,2,1,0:T(8,128)(2,1)S(1)}, u32[]{:S(2)}, u32[]{:S(2)}) %collective-permute-start.21) | collective-permute-done | bytes 131104 | tf_op jit(solution)/shard_map/ppermute | solution.py:21
  107.0 1.6 collective-permute-done.29.refs_4_
  108.6 15.9 %shard_map.146 = (f32[2048,256]{1,0:T(8,128)S(1)}, f32[8,256]{1,0:T(8,128)S(1)}, bf16[7168,256]{1,0:T(8,128)(2,1)S(1)}) custom-call(s32[2]{0:T(128)S(1)} %pad_add_fusion.1.where, s32[1,256]{1,0:T(1,128)S(1)} %pad_add_fusion.ids, f32[1,256]{1,0:T(1,128)S(1)} %fusion.171.scale, f32[448,16]{1,0:T(8,128)S(1)} %fusion.109.gain, ...), custom_call_target="tpu_custom_call" | custom-call | flops 7516192768 | bytes 36700160 | tf_op jit(solution)/shard_map/pallas_call | solution.py:202
  124.5 1.8 copy-done
  126.4 2.1 collective-permute-start.32
  132.8 2.4 collective-permute-start.35
  135.2 2.0 collective-permute-start.33
  141.1 16.7 %shard_map.147 = (f32[8,2,448,128]{3,2,1,0:T(8,128)S(1)}, bf16[8,2,448,128]{3,2,1,0:T(8,128)(2,1)S(1)}, bf16[2048,256]{1,0:T(8,128)(2,1)S(1)}) custom-call(s32[2]{0:T(128)S(1)} %pad_add_fusion.1.where, s32[1,256]{1,0:T(1,128)S(1)} %pad_add_fusion.ids, f32[8,256]{1,0:T(8,128)S(1)} %select_maximum_fusion.rows, f32[2048,256]{1,0:T(8,128)S(1)} %get-tuple-element.31.logits, ...), custom_call_target="tpu_custom_call" | custom-call | flops 7516192768 | bytes 36700160 | tf_op jit(solution)/shard_map/pallas_call | solution.py:266
  158.1 3.6 %collective-permute-done.37.refs_0_ = bf16[8,2,448,128]{3,2,1,0:T(8,128)(2,1)S(1)} collective-permute-done((bf16[8,2,448,128]{3,2,1,0:T(8,128)(2,1)S(1)}, bf16[8,2,448,128]{3,2,1,0:T(8,128)(2,1)S(1)}, u32[]{:S(2)}, u32[]{:S(2)}) %collective-permute-start.37) | collective-permute-done | bytes 1835040 | tf_op jit(solution)/shard_map/ppermute | solution.py:21
  162.6 1.6 collective-permute-start.48
  165.3 1.8 collective-permute-start.46
  167.1 1.6 collective-permute-start.42
  169.6 5.8 %shard_map.148 = (bf16[2048,7168]{1,0:T(8,128)(2,1)}, f32[8,128]{1,0:T(8,128)}) custom-call(bf16[2048,256]{1,0:T(8,128)(2,1)S(1)} %get-tuple-element.34.left, bf16[7168,256]{1,0:T(8,128)(2,1)S(1)} %copy-done.1, bf16[8,2,448,128]{3,2,1,0:T(8,128)(2,1)S(1)} %collective-permute-done.37.refs_0_), custom_call_target="tpu_custom_call" | custom-call | flops 1879048192 | bytes 11010048 | tf_op jit(solution)/shard_map/pallas_call | solution.py:313
  177.0 2.0 collective-permute-done.38.refs_0_
  179.2 5.8 %shard_map.149 = (bf16[2048,7168]{1,0:T(8,128)(2,1)}, f32[2,2,176,128]{3,2,1,0:T(8,128)S(1)}) custom-call(bf16[2048,256]{1,0:T(8,128)(2,1)S(1)} %get-tuple-element.34.left, bf16[7168,256]{1,0:T(8,128)(2,1)S(1)} %copy-done.1, bf16[2,2,2,176,128]{4,3,2,1,0:T(8,128)(2,1)S(1)} %collective-permute-done.38.refs_0_, ...), custom_call_target="tpu_custom_call", output_to_operand_aliasing={{0}: (3, {})} | custom-call | flops 1879048192 | bytes 11010048 | tf_op jit(solution)/shard_map/pallas_call | solution.py:313
  185.6 2.1 collective-permute-start.49
  187.7 1.8 collective-permute-start.40
  189.7 1.5 collective-permute-start.45
  192.1 3.3 %collective-permute-done.45 = bf16[160,128]{1,0:T(8,128)(2,1)S(1)} collective-permute-done((bf16[160,128]{1,0:T(8,128)(2,1)S(1)}, bf16[160,128]{1,0:T(8,128)(2,1)S(1)}, u32[]{:S(2)}, u32[]{:S(2)}) %collective-permute-start.45) | collective-permute-done | bytes 40992 | tf_op jit(solution)/shard_map/ppermute | solution.py:21
  196.3 4.4 %collective-permute-done.41 = bf16[176,128]{1,0:T(8,128)(2,1)S(1)} collective-permute-done((bf16[176,128]{1,0:T(8,128)(2,1)S(1)}, bf16[176,128]{1,0:T(8,128)(2,1)S(1)}, u32[]{:S(2)}, u32[]{:S(2)}) %collective-permute-start.41) | collective-permute-done | bytes 45088 | tf_op jit(solution)/shard_map/ppermute | solution.py:21
  204.5 1.7 copy-done.5
  209.4 2.8 %collective-permute-start.53 = (bf16[2,2,16,1792]{3,2,1,0:T(8,128)(2,1)S(1)}, bf16[2,2,16,1792]{3,2,1,0:T(8,128)(2,1)S(1)}, u32[]{:S(2)}, u32[]{:S(2)}) collective-permute-start(bf16[2,2,16,1792]{3,2,1,0:T(8,128)(2,1)S(1)} %bitcast.370), channel_id=1, source_target_pairs={{0,8},{2,10},{4,12},{6,14},{8,0},{10,2},{12,4},{14,6},{16,24},{18,... | collective-permute-start | bytes 688136 | tf_op jit(solution)/shard_map/ppermute | solution.py:21
  212.3 1.6 collective-permute-start.59
  214.7 2.7 %convolution_convert_fusion.1 = bf16[3584,448]{0,1:T(8,128)(2,1)} fusion(bf16[448,256]{1,0:T(8,128)(2,1)S(1)} %convolution_convert_fusion.3, bf16[256,896]{1,0:T(8,128)(2,1)S(1)} %get-tuple-element.57, bf16[256,2688]{1,0:T(8,128)(2,1)S(1)} %bitcast.336), kind=kOutput, calls=%fused_computation.1 | convolution fusion | flops 827359232 | bytes 5275648 | tf_op jit(solution)/shard_map/dot_general | solution.py:150
  217.4 2.7 %convolution_convert_fusion = bf16[3584,448]{0,1:T(8,128)(2,1)} fusion(bf16[448,256]{1,0:T(8,128)(2,1)S(1)} %convolution_convert_fusion.2, bf16[256,896]{1,0:T(8,128)(2,1)S(1)} %get-tuple-element.56, bf16[256,2688]{1,0:T(8,128)(2,1)S(1)} %bitcast.334), kind=kOutput, calls=%fused_computation | convolution fusion | flops 827359232 | bytes 5275648 | tf_op jit(solution)/shard_map/dot_general | solution.py:150
  220.1 3.2 %collective-permute-done.53.refs_0_ = bf16[2,2,16,1792]{3,2,1,0:T(8,128)(2,1)S(1)} collective-permute-done((bf16[2,2,16,1792]{3,2,1,0:T(8,128)(2,1)S(1)}, bf16[2,2,16,1792]{3,2,1,0:T(8,128)(2,1)S(1)}, u32[]{:S(2)}, u32[]{:S(2)}) %collective-permute-start.53) | collective-permute-done | bytes 229408 | tf_op jit(solution)/shard_map/ppermute | solution.py:21
  223.3 5.8 %shard_map.150 = (bf16[2048,7168]{1,0:T(8,128)(2,1)}, f32[2,2,2,16,2688]{4,3,2,1,0:T(8,128)S(1)}) custom-call(bf16[2048,256]{1,0:T(8,128)(2,1)S(1)} %get-tuple-element.34.left, bf16[7168,256]{1,0:T(8,128)(2,1)S(1)} %copy-done.1, bf16[2,2,16,1792]{3,2,1,0:T(8,128)(2,1)S(1)} %collective-permute-done.53.refs_0_, ...), custom_call_target="tpu_custom_call", output_to_operand_aliasing={{0}: (3, {})} | custom-call | flops 1879048192 | bytes 11010048 | tf_op jit(solution)/shard_map/pallas_call | solution.py:313
  230.7 2.9 %collective-permute-start.54 = (bf16[2,2,16,2688]{3,2,1,0:T(8,128)(2,1)S(1)}, bf16[2,2,16,2688]{3,2,1,0:T(8,128)(2,1)S(1)}, u32[]{:S(2)}, u32[]{:S(2)}) collective-permute-start(bf16[2,2,16,2688]{3,2,1,0:T(8,128)(2,1)S(1)} %fusion.48), channel_id=1, source_target_pairs={{0,4},{2,6},{4,0},{6,2},{8,12},{10,14},{12,8},{14,10},{16,20},{18,... | collective-permute-start | bytes 1032200 | tf_op jit(solution)/shard_map/ppermute | solution.py:21
  233.6 5.8 %shard_map.151 = (bf16[2048,7168]{1,0:T(8,128)(2,1)}, f32[2,2,16,2688]{3,2,1,0:T(8,128)S(1)}) custom-call(bf16[2048,256]{1,0:T(8,128)(2,1)S(1)} %get-tuple-element.34.left, bf16[7168,256]{1,0:T(8,128)(2,1)S(1)} %copy-done.1, bf16[2,2,2,16,2688]{4,3,2,1,0:T(8,128)(2,1)S(1)} %collective-permute-done.52.refs_0_, ...), custom_call_target="tpu_custom_call", output_to_operand_aliasing={{0}: (3, {})} | custom-call | flops 1879048192 | bytes 11010048 | tf_op jit(solution)/shard_map/pallas_call | solution.py:313
  239.4 1.4 collective-permute-done.54
  241.1 1.8 collective-permute-start.61
  243.0 2.5 collective-permute-start.55
  246.0 1.5 collective-permute-start.62
  247.5 2.3 collective-permute-done.55
  249.8 1.8 collective-permute-done.63
  251.7 2.1 collective-permute-start.64
  254.8 2.4 collective-permute-done.64
  257.3 2.8 %collective-permute-done.56 = bf16[16,2688]{1,0:T(8,128)(2,1)S(1)} collective-permute-done((bf16[16,2688]{1,0:T(8,128)(2,1)S(1)}, bf16[16,2688]{1,0:T(8,128)(2,1)S(1)}, u32[]{:S(2)}, u32[]{:S(2)}) %collective-permute-start.56) | collective-permute-done | bytes 86048 | tf_op jit(solution)/shard_map/ppermute | solution.py:21
  260.4 2.5 psum.15
  (293 shorter events, 51.2 us)
Async XLA Ops:
  6.5 11.0 %collective-permute-start.4 = (bf16[16,2688]{1,0:T(8,128)(2,1)S(1)}, bf16[16,2688]{1,0:T(8,128)(2,1)S(1)}, u32[]{:S(2)}, u32[]{:S(2)}) collective-permute-start(bf16[16,2688]{1,0:T(8,128)(2,1)S(1)} %slice.615), channel_id=1, source_target_pairs={{0,16},{2,18},{4,20},{6,22},{8,24},{10,26},{12,28},{14,30},{16,0},... | collective-permute-start | bytes 258056 | tf_op jit(solution)/shard_map/ppermute | solution.py:21
  10.5 8.4 %collective-permute-start = (bf16[16,2688]{1,0:T(8,128)(2,1)S(1)}, bf16[16,2688]{1,0:T(8,128)(2,1)S(1)}, u32[]{:S(2)}, u32[]{:S(2)}) collective-permute-start(bf16[16,2688]{1,0:T(8,128)(2,1)S(1)} %slice.614), channel_id=1, source_target_pairs={{0,16},{2,18},{4,20},{6,22},{8,24},{10,26},{12,28},{14,30},{16,0},... | collective-permute-start | bytes 258056 | tf_op jit(solution)/shard_map/ppermute | solution.py:21
  18.9 4.3 %collective-permute-start.5 = (bf16[16,1920]{1,0:T(8,128)(2,1)S(1)}, bf16[16,1920]{1,0:T(8,128)(2,1)S(1)}, u32[]{:S(2)}, u32[]{:S(2)}) collective-permute-start(bf16[16,1920]{1,0:T(8,128)(2,1)S(1)} %fusion.96), channel_id=1, source_target_pairs={{0,2},{2,0},{4,6},{6,4},{8,10},{10,8},{12,14},{14,12},{16,18},{18,... | collective-permute-start | bytes 184328 | tf_op jit(solution)/shard_map/ppermute | solution.py:21
  20.6 7.3 %collective-permute-start.7 = (bf16[2,16,2688]{2,1,0:T(8,128)(2,1)S(1)}, bf16[2,16,2688]{2,1,0:T(8,128)(2,1)S(1)}, u32[]{:S(2)}, u32[]{:S(2)}) collective-permute-start(bf16[2,16,2688]{2,1,0:T(8,128)(2,1)S(1)} %get-tuple-element.80), channel_id=1, source_target_pairs={{0,8},{2,10},{4,12},{6,14},{8,0},{10,2},{12,4},{14,6},{16,24},{18,... | collective-permute-start | bytes 516104 | tf_op jit(solution)/shard_map/ppermute | solution.py:21
  21.4 8.4 %collective-permute-start.1 = (bf16[2,16,2688]{2,1,0:T(8,128)(2,1)S(1)}, bf16[2,16,2688]{2,1,0:T(8,128)(2,1)S(1)}, u32[]{:S(2)}, u32[]{:S(2)}) collective-permute-start(bf16[2,16,2688]{2,1,0:T(8,128)(2,1)S(1)} %get-tuple-element.78), channel_id=1, source_target_pairs={{0,8},{2,10},{4,12},{6,14},{8,0},{10,2},{12,4},{14,6},{16,24},{18,... | collective-permute-start | bytes 516104 | tf_op jit(solution)/shard_map/ppermute | solution.py:21
  23.3 8.8 %collective-permute-start.6 = (bf16[2,16,1920]{2,1,0:T(8,128)(2,1)S(1)}, bf16[2,16,1920]{2,1,0:T(8,128)(2,1)S(1)}, u32[]{:S(2)}, u32[]{:S(2)}) collective-permute-start(bf16[2,16,1920]{2,1,0:T(8,128)(2,1)S(1)} %get-tuple-element.89), channel_id=1, source_target_pairs={{0,4},{2,6},{4,0},{6,2},{8,12},{10,14},{12,8},{14,10},{16,20},{18,... | collective-permute-start | bytes 368648 | tf_op jit(solution)/shard_map/ppermute | solution.py:21
  29.8 26.9 %collective-permute-start.11 = (bf16[2,2,16,2688]{3,2,1,0:T(8,128)(2,1)S(1)}, bf16[2,2,16,2688]{3,2,1,0:T(8,128)(2,1)S(1)}, u32[]{:S(2)}, u32[]{:S(2)}) collective-permute-start(bf16[2,2,16,2688]{3,2,1,0:T(8,128)(2,1)S(1)} %get-tuple-element.70), channel_id=1, source_target_pairs={{0,2},{2,0},{4,6},{6,4},{8,10},{10,8},{12,14},{14,12},{16,18},{18,... | collective-permute-start | bytes 1032200 | tf_op jit(solution)/shard_map/ppermute | solution.py:21
  30.7 26.7 %collective-permute-start.2 = (bf16[2,2,16,2688]{3,2,1,0:T(8,128)(2,1)S(1)}, bf16[2,2,16,2688]{3,2,1,0:T(8,128)(2,1)S(1)}, u32[]{:S(2)}, u32[]{:S(2)}) collective-permute-start(bf16[2,2,16,2688]{3,2,1,0:T(8,128)(2,1)S(1)} %get-tuple-element.68), channel_id=1, source_target_pairs={{0,4},{2,6},{4,0},{6,2},{8,12},{10,14},{12,8},{14,10},{16,20},{18,... | collective-permute-start | bytes 1032200 | tf_op jit(solution)/shard_map/ppermute | solution.py:21
  32.1 11.1 %collective-permute-start.10 = (bf16[2,2,16,1920]{3,2,1,0:T(8,128)(2,1)S(1)}, bf16[2,2,16,1920]{3,2,1,0:T(8,128)(2,1)S(1)}, u32[]{:S(2)}, u32[]{:S(2)}) collective-permute-start(bf16[2,2,16,1920]{3,2,1,0:T(8,128)(2,1)S(1)} %fusion.55), channel_id=1, source_target_pairs={{0,24},{2,26},{4,28},{6,30},{8,16},{10,18},{12,20},{14,22},{16,8},... | collective-permute-start | bytes 737288 | tf_op jit(solution)/shard_map/ppermute | solution.py:21
  36.3 19.4 %collective-permute-start.9 = (bf16[2,2,16,1920]{3,2,1,0:T(8,128)(2,1)S(1)}, bf16[2,2,16,1920]{3,2,1,0:T(8,128)(2,1)S(1)}, u32[]{:S(2)}, u32[]{:S(2)}) collective-permute-start(bf16[2,2,16,1920]{3,2,1,0:T(8,128)(2,1)S(1)} %fusion.55), channel_id=1, source_target_pairs={{0,16},{2,18},{4,20},{6,22},{8,24},{10,26},{12,28},{14,30},{16,0},... | collective-permute-start | bytes 737288 | tf_op jit(solution)/shard_map/ppermute | solution.py:21
  36.3 19.4 %collective-permute-start.8 = (bf16[2,2,16,1920]{3,2,1,0:T(8,128)(2,1)S(1)}, bf16[2,2,16,1920]{3,2,1,0:T(8,128)(2,1)S(1)}, u32[]{:S(2)}, u32[]{:S(2)}) collective-permute-start(bf16[2,2,16,1920]{3,2,1,0:T(8,128)(2,1)S(1)} %fusion.55), channel_id=1, source_target_pairs={{0,8},{2,10},{4,12},{6,14},{8,0},{10,2},{12,4},{14,6},{16,24},{18,... | collective-permute-start | bytes 737288 | tf_op jit(solution)/shard_map/ppermute | solution.py:21
  56.8 16.5 %collective-permute-start.12 = (bf16[2,2,2,16,2688]{4,3,2,1,0:T(8,128)(2,1)S(1)}, bf16[2,2,2,16,2688]{4,3,2,1,0:T(8,128)(2,1)S(1)}, u32[]{:S(2)}, u32[]{:S(2)}) collective-permute-start(bf16[2,2,2,16,2688]{4,3,2,1,0:T(8,128)(2,1)S(1)} %get-tuple-element.64), channel_id=1, source_target_pairs={{0,4},{2,6},{4,0},{6,2},{8,12},{10,14},{12,8},{14,10},{16,20},{18,... | collective-permute-start | bytes 2064392 | tf_op jit(solution)/shard_map/ppermute | solution.py:21
  57.4 16.2 %collective-permute-start.3 = (bf16[2,2,2,16,2688]{4,3,2,1,0:T(8,128)(2,1)S(1)}, bf16[2,2,2,16,2688]{4,3,2,1,0:T(8,128)(2,1)S(1)}, u32[]{:S(2)}, u32[]{:S(2)}) collective-permute-start(bf16[2,2,2,16,2688]{4,3,2,1,0:T(8,128)(2,1)S(1)} %get-tuple-element.62), channel_id=1, source_target_pairs={{0,2},{2,0},{4,6},{6,4},{8,10},{10,8},{12,14},{14,12},{16,18},{18,... | collective-permute-start | bytes 2064392 | tf_op jit(solution)/shard_map/ppermute | solution.py:21
  76.5 1.6 collective-permute-start.13
  78.2 5.1 %collective-permute-start.15 = (bf16[160,128]{1,0:T(8,128)(2,1)S(1)}, bf16[160,128]{1,0:T(8,128)(2,1)S(1)}, u32[]{:S(2)}, u32[]{:S(2)}) collective-permute-start(bf16[160,128]{1,0:T(8,128)(2,1)S(1)} %get-tuple-element.95), channel_id=1, source_target_pairs={{0,16},{2,18},{4,20},{6,22},{8,24},{10,26},{12,28},{14,30},{16,0},... | collective-permute-start | bytes 122888 | tf_op jit(solution)/shard_map/ppermute | solution.py:21
  78.3 6.0 %collective-permute-start.14 = (bf16[176,128]{1,0:T(8,128)(2,1)S(1)}, bf16[176,128]{1,0:T(8,128)(2,1)S(1)}, u32[]{:S(2)}, u32[]{:S(2)}) collective-permute-start(bf16[176,128]{1,0:T(8,128)(2,1)S(1)} %get-tuple-element.93), channel_id=1, source_target_pairs={{0,16},{2,18},{4,20},{6,22},{8,24},{10,26},{12,28},{14,30},{16,0},... | collective-permute-start | bytes 135176 | tf_op jit(solution)/shard_map/ppermute | solution.py:21
  83.3 6.6 %collective-permute-start.19 = (bf16[2,160,128]{2,1,0:T(8,128)(2,1)S(1)}, bf16[2,160,128]{2,1,0:T(8,128)(2,1)S(1)}, u32[]{:S(2)}, u32[]{:S(2)}) collective-permute-start(bf16[2,160,128]{2,1,0:T(8,128)(2,1)S(1)} %get-tuple-element.99), channel_id=1, source_target_pairs={{0,8},{2,10},{4,12},{6,14},{8,0},{10,2},{12,4},{14,6},{16,24},{18,... | collective-permute-start | bytes 245768 | tf_op jit(solution)/shard_map/ppermute | solution.py:21
  84.3 4.0 %collective-permute-start.16 = (bf16[128,128]{1,0:T(8,128)(2,1)S(1)}, bf16[128,128]{1,0:T(8,128)(2,1)S(1)}, u32[]{:S(2)}, u32[]{:S(2)}) collective-permute-start(bf16[128,128]{1,0:T(8,128)(2,1)S(1)} %fusion.107), channel_id=1, source_target_pairs={{0,2},{2,0},{4,6},{6,4},{8,10},{10,8},{12,14},{14,12},{16,18},{18,... | collective-permute-start | bytes 98312 | tf_op jit(solution)/shard_map/ppermute | solution.py:21
  85.9 5.6 %collective-permute-start.18 = (bf16[2,176,128]{2,1,0:T(8,128)(2,1)S(1)}, bf16[2,176,128]{2,1,0:T(8,128)(2,1)S(1)}, u32[]{:S(2)}, u32[]{:S(2)}) collective-permute-start(bf16[2,176,128]{2,1,0:T(8,128)(2,1)S(1)} %get-tuple-element.97), channel_id=1, source_target_pairs={{0,8},{2,10},{4,12},{6,14},{8,0},{10,2},{12,4},{14,6},{16,24},{18,... | collective-permute-start | bytes 270344 | tf_op jit(solution)/shard_map/ppermute | solution.py:21
  88.3 5.0 %collective-permute-start.17 = (bf16[2,128,128]{2,1,0:T(8,128)(2,1)S(1)}, bf16[2,128,128]{2,1,0:T(8,128)(2,1)S(1)}, u32[]{:S(2)}, u32[]{:S(2)}) collective-permute-start(bf16[2,128,128]{2,1,0:T(8,128)(2,1)S(1)} %get-tuple-element.102), channel_id=1, source_target_pairs={{0,4},{2,6},{4,0},{6,2},{8,12},{10,14},{12,8},{14,10},{16,20},{18,... | collective-permute-start | bytes 196616 | tf_op jit(solution)/shard_map/ppermute | solution.py:21
  89.9 9.2 %collective-permute-start.26 = (bf16[2,2,160,128]{3,2,1,0:T(8,128)(2,1)S(1)}, bf16[2,2,160,128]{3,2,1,0:T(8,128)(2,1)S(1)}, u32[]{:S(2)}, u32[]{:S(2)}) collective-permute-start(bf16[2,2,160,128]{3,2,1,0:T(8,128)(2,1)S(1)} %get-tuple-element.82), channel_id=1, source_target_pairs={{0,2},{2,0},{4,6},{6,4},{8,10},{10,8},{12,14},{14,12},{16,18},{18,... | collective-permute-start | bytes 491528 | tf_op jit(solution)/shard_map/ppermute | solution.py:21
  91.5 6.2 %collective-permute-start.24 = (bf16[2,2,176,128]{3,2,1,0:T(8,128)(2,1)S(1)}, bf16[2,2,176,128]{3,2,1,0:T(8,128)(2,1)S(1)}, u32[]{:S(2)}, u32[]{:S(2)}) collective-permute-start(bf16[2,2,176,128]{3,2,1,0:T(8,128)(2,1)S(1)} %get-tuple-element.76), channel_id=1, source_target_pairs={{0,4},{2,6},{4,0},{6,2},{8,12},{10,14},{12,8},{14,10},{16,20},{18,... | collective-permute-start | bytes 540680 | tf_op jit(solution)/shard_map/ppermute | solution.py:21
  93.3 7.4 %collective-permute-start.22 = (bf16[2,2,128,128]{3,2,1,0:T(8,128)(2,1)S(1)}, bf16[2,2,128,128]{3,2,1,0:T(8,128)(2,1)S(1)}, u32[]{:S(2)}, u32[]{:S(2)}) collective-permute-start(bf16[2,2,128,128]{3,2,1,0:T(8,128)(2,1)S(1)} %fusion.83), channel_id=1, source_target_pairs={{0,24},{2,26},{4,28},{6,30},{8,16},{10,18},{12,20},{14,22},{16,8},... | collective-permute-start | bytes 393224 | tf_op jit(solution)/shard_map/ppermute | solution.py:21
  95.5 8.8 %collective-permute-start.21 = (bf16[2,2,128,128]{3,2,1,0:T(8,128)(2,1)S(1)}, bf16[2,2,128,128]{3,2,1,0:T(8,128)(2,1)S(1)}, u32[]{:S(2)}, u32[]{:S(2)}) collective-permute-start(bf16[2,2,128,128]{3,2,1,0:T(8,128)(2,1)S(1)} %fusion.83), channel_id=1, source_target_pairs={{0,16},{2,18},{4,20},{6,22},{8,24},{10,26},{12,28},{14,30},{16,0},... | collective-permute-start | bytes 393224 | tf_op jit(solution)/shard_map/ppermute | solution.py:21
  96.0 8.3 %collective-permute-start.20 = (bf16[2,2,128,128]{3,2,1,0:T(8,128)(2,1)S(1)}, bf16[2,2,128,128]{3,2,1,0:T(8,128)(2,1)S(1)}, u32[]{:S(2)}, u32[]{:S(2)}) collective-permute-start(bf16[2,2,128,128]{3,2,1,0:T(8,128)(2,1)S(1)} %fusion.83), channel_id=1, source_target_pairs={{0,8},{2,10},{4,12},{6,14},{8,0},{10,2},{12,4},{14,6},{16,24},{18,... | collective-permute-start | bytes 393224 | tf_op jit(solution)/shard_map/ppermute | solution.py:21
  97.8 7.5 %collective-permute-start.25 = (bf16[2,2,2,176,128]{4,3,2,1,0:T(8,128)(2,1)S(1)}, bf16[2,2,2,176,128]{4,3,2,1,0:T(8,128)(2,1)S(1)}, u32[]{:S(2)}, u32[]{:S(2)}) collective-permute-start(bf16[2,2,2,176,128]{4,3,2,1,0:T(8,128)(2,1)S(1)} %get-tuple-element.66), channel_id=1, source_target_pairs={{0,2},{2,0},{4,6},{6,4},{8,10},{10,8},{12,14},{14,12},{16,18},{18,... | collective-permute-start | bytes 1081352 | tf_op jit(solution)/shard_map/ppermute | solution.py:21
  99.2 7.1 %collective-permute-start.27 = (bf16[2,2,2,160,128]{4,3,2,1,0:T(8,128)(2,1)S(1)}, bf16[2,2,2,160,128]{4,3,2,1,0:T(8,128)(2,1)S(1)}, u32[]{:S(2)}, u32[]{:S(2)}) collective-permute-start(bf16[2,2,2,160,128]{4,3,2,1,0:T(8,128)(2,1)S(1)} %get-tuple-element.72), channel_id=1, source_target_pairs={{0,4},{2,6},{4,0},{6,2},{8,12},{10,14},{12,8},{14,10},{16,20},{18,... | collective-permute-start | bytes 983048 | tf_op jit(solution)/shard_map/ppermute | solution.py:21
  104.4 2.6 collective-permute-start.23
  105.4 3.2 %collective-permute-start.28 = (bf16[16,176,128]{2,1,0:T(8,128)(2,1)S(1)}, bf16[16,176,128]{2,1,0:T(8,128)(2,1)S(1)}, u32[]{:S(2)}, u32[]{:S(2)}) collective-permute-start(bf16[16,176,128]{2,1,0:T(8,128)(2,1)S(1)} %bitcast.315), channel_id=1, source_target_pairs={{0,1},{1,0},{2,3},{3,2},{4,5},{5,4},{6,7},{7,6},{8,9},{9,8},{10,11... | collective-permute-start | bytes 2162696 | tf_op jit(solution)/shard_map/ppermute | solution.py:21
  106.5 2.2 collective-permute-start.29
  126.4 4.5 %collective-permute-start.32 = (f32[4,256]{1,0:T(4,128)S(1)}, f32[4,256]{1,0:T(4,128)S(1)}, u32[]{:S(2)}, u32[]{:S(2)}) collective-permute-start(f32[4,256]{1,0:T(4,128)S(1)} %slice.512), channel_id=1, source_target_pairs={{0,6},{2,4},{4,2},{6,0},{8,14},{10,12},{12,10},{14,8},{16,22},{18,... | collective-permute-start | bytes 12296 | tf_op jit(solution)/shard_map/ppermute | solution.py:21
  128.4 3.6 %collective-permute-start.31 = (f32[4,256]{1,0:T(4,128)S(1)}, f32[4,256]{1,0:T(4,128)S(1)}, u32[]{:S(2)}, u32[]{:S(2)}) collective-permute-start(f32[4,256]{1,0:T(4,128)S(1)} %slice.512), channel_id=1, source_target_pairs={{0,4},{2,6},{4,0},{6,2},{8,12},{10,14},{12,8},{14,10},{16,20},{18,... | collective-permute-start | bytes 12296 | tf_op jit(solution)/shard_map/ppermute | solution.py:21
  129.1 3.6 %collective-permute-start.30 = (f32[4,256]{1,0:T(4,128)S(1)}, f32[4,256]{1,0:T(4,128)S(1)}, u32[]{:S(2)}, u32[]{:S(2)}) collective-permute-start(f32[4,256]{1,0:T(4,128)S(1)} %slice.512), channel_id=1, source_target_pairs={{0,2},{2,0},{4,6},{6,4},{8,10},{10,8},{12,14},{14,12},{16,18},{18,... | collective-permute-start | bytes 12296 | tf_op jit(solution)/shard_map/ppermute | solution.py:21
  132.8 5.8 %collective-permute-start.35 = (f32[4,256]{1,0:T(4,128)S(1)}, f32[4,256]{1,0:T(4,128)S(1)}, u32[]{:S(2)}, u32[]{:S(2)}) collective-permute-start(f32[4,256]{1,0:T(4,128)S(1)} %fusion.123), channel_id=1, source_target_pairs={{0,24},{2,26},{4,28},{6,30},{8,16},{10,18},{12,20},{14,22},{16,8},... | collective-permute-start | bytes 12296 | tf_op jit(solution)/shard_map/ppermute | solution.py:21
  135.2 4.5 %collective-permute-start.34 = (f32[4,256]{1,0:T(4,128)S(1)}, f32[4,256]{1,0:T(4,128)S(1)}, u32[]{:S(2)}, u32[]{:S(2)}) collective-permute-start(f32[4,256]{1,0:T(4,128)S(1)} %fusion.123), channel_id=1, source_target_pairs={{0,16},{2,18},{4,20},{6,22},{8,24},{10,26},{12,28},{14,30},{16,0},... | collective-permute-start | bytes 12296 | tf_op jit(solution)/shard_map/ppermute | solution.py:21
  135.2 4.5 %collective-permute-start.33 = (f32[4,256]{1,0:T(4,128)S(1)}, f32[4,256]{1,0:T(4,128)S(1)}, u32[]{:S(2)}, u32[]{:S(2)}) collective-permute-start(f32[4,256]{1,0:T(4,128)S(1)} %fusion.123), channel_id=1, source_target_pairs={{0,8},{2,10},{4,12},{6,14},{8,0},{10,2},{12,4},{14,6},{16,24},{18,... | collective-permute-start | bytes 12296 | tf_op jit(solution)/shard_map/ppermute | solution.py:21
  157.8 3.9 %collective-permute-start.37 = (bf16[8,2,448,128]{3,2,1,0:T(8,128)(2,1)S(1)}, bf16[8,2,448,128]{3,2,1,0:T(8,128)(2,1)S(1)}, u32[]{:S(2)}, u32[]{:S(2)}) collective-permute-start(bf16[8,2,448,128]{3,2,1,0:T(8,128)(2,1)S(1)} %get-tuple-element.33), channel_id=1, source_target_pairs={{0,1},{1,0},{2,3},{3,2},{4,5},{5,4},{6,7},{7,6},{8,9},{9,8},{10,11... | collective-permute-start | bytes 5505032 | tf_op jit(solution)/shard_map/ppermute | solution.py:21
  162.6 22.8 %collective-permute-start.48 = (bf16[2,2,112,128]{3,2,1,0:T(8,128)(2,1)S(1)}, bf16[2,2,112,128]{3,2,1,0:T(8,128)(2,1)S(1)}, u32[]{:S(2)}, u32[]{:S(2)}) collective-permute-start(bf16[2,2,112,128]{3,2,1,0:T(8,128)(2,1)S(1)} %bitcast.383), channel_id=1, source_target_pairs={{0,24},{2,26},{4,28},{6,30},{8,16},{10,18},{12,20},{14,22},{16,8},... | collective-permute-start | bytes 344072 | tf_op jit(solution)/shard_map/ppermute | solution.py:21
  164.2 21.3 %collective-permute-start.47 = (bf16[2,2,112,128]{3,2,1,0:T(8,128)(2,1)S(1)}, bf16[2,2,112,128]{3,2,1,0:T(8,128)(2,1)S(1)}, u32[]{:S(2)}, u32[]{:S(2)}) collective-permute-start(bf16[2,2,112,128]{3,2,1,0:T(8,128)(2,1)S(1)} %bitcast.382), channel_id=1, source_target_pairs={{0,16},{2,18},{4,20},{6,22},{8,24},{10,26},{12,28},{14,30},{16,0},... | collective-permute-start | bytes 344072 | tf_op jit(solution)/shard_map/ppermute | solution.py:21
  165.3 20.2 %collective-permute-start.46 = (bf16[2,2,112,128]{3,2,1,0:T(8,128)(2,1)S(1)}, bf16[2,2,112,128]{3,2,1,0:T(8,128)(2,1)S(1)}, u32[]{:S(2)}, u32[]{:S(2)}) collective-permute-start(bf16[2,2,112,128]{3,2,1,0:T(8,128)(2,1)S(1)} %bitcast.381), channel_id=1, source_target_pairs={{0,8},{2,10},{4,12},{6,14},{8,0},{10,2},{12,4},{14,6},{16,24},{18,... | collective-permute-start | bytes 344072 | tf_op jit(solution)/shard_map/ppermute | solution.py:21
  167.1 9.0 %collective-permute-start.42 = (bf16[2,2,2,160,128]{4,3,1,0,2:T(8,128)(2,1)S(1)}, bf16[2,2,2,160,128]{4,3,1,0,2:T(8,128)(2,1)S(1)}, u32[]{:S(2)}, u32[]{:S(2)}) collective-permute-start(bf16[2,2,2,160,128]{4,3,1,0,2:T(8,128)(2,1)S(1)} %fusion.52), channel_id=1, source_target_pairs={{0,4},{2,6},{4,0},{6,2},{8,12},{10,14},{12,8},{14,10},{16,20},{18,... | collective-permute-start | bytes 983048 | tf_op jit(solution)/shard_map/ppermute | solution.py:21
  168.8 10.3 %collective-permute-start.38 = (bf16[2,2,2,176,128]{4,3,2,1,0:T(8,128)(2,1)S(1)}, bf16[2,2,2,176,128]{4,3,2,1,0:T(8,128)(2,1)S(1)}, u32[]{:S(2)}, u32[]{:S(2)}) collective-permute-start(bf16[2,2,2,176,128]{4,3,2,1,0:T(8,128)(2,1)S(1)} %fusion.45), channel_id=1, source_target_pairs={{0,2},{2,0},{4,6},{6,4},{8,10},{10,8},{12,14},{14,12},{16,18},{18,... | collective-permute-start | bytes 1081352 | tf_op jit(solution)/shard_map/ppermute | solution.py:21
  176.2 8.8 %collective-permute-start.43 = (bf16[2,2,160,128]{3,2,1,0:T(8,128)(2,1)S(1)}, bf16[2,2,160,128]{3,2,1,0:T(8,128)(2,1)S(1)}, u32[]{:S(2)}, u32[]{:S(2)}) collective-permute-start(bf16[2,2,160,128]{3,2,1,0:T(8,128)(2,1)S(1)} %fusion.79), channel_id=1, source_target_pairs={{0,2},{2,0},{4,6},{6,4},{8,10},{10,8},{12,14},{14,12},{16,18},{18,... | collective-permute-start | bytes 491528 | tf_op jit(solution)/shard_map/ppermute | solution.py:21
  179.2 6.3 %collective-permute-start.39 = (bf16[2,2,176,128]{3,2,1,0:T(8,128)(2,1)S(1)}, bf16[2,2,176,128]{3,2,1,0:T(8,128)(2,1)S(1)}, u32[]{:S(2)}, u32[]{:S(2)}) collective-permute-start(bf16[2,2,176,128]{3,2,1,0:T(8,128)(2,1)S(1)} %fusion.73), channel_id=1, source_target_pairs={{0,4},{2,6},{4,0},{6,2},{8,12},{10,14},{12,8},{14,10},{16,20},{18,... | collective-permute-start | bytes 540680 | tf_op jit(solution)/shard_map/ppermute | solution.py:21
  185.1 4.6 %collective-permute-start.44 = (bf16[2,160,128]{2,1,0:T(8,128)(2,1)S(1)}, bf16[2,160,128]{2,1,0:T(8,128)(2,1)S(1)}, u32[]{:S(2)}, u32[]{:S(2)}) collective-permute-start(bf16[2,160,128]{2,1,0:T(8,128)(2,1)S(1)} %fusion.93), channel_id=1, source_target_pairs={{0,8},{2,10},{4,12},{6,14},{8,0},{10,2},{12,4},{14,6},{16,24},{18,... | collective-permute-start | bytes 245768 | tf_op jit(solution)/shard_map/ppermute | solution.py:21
  185.6 5.7 %collective-permute-start.49 = (bf16[2,112,128]{2,1,0:T(8,128)(2,1)S(1)}, bf16[2,112,128]{2,1,0:T(8,128)(2,1)S(1)}, u32[]{:S(2)}, u32[]{:S(2)}) collective-permute-start(bf16[2,112,128]{2,1,0:T(8,128)(2,1)S(1)} %fusion.98), channel_id=1, source_target_pairs={{0,4},{2,6},{4,0},{6,2},{8,12},{10,14},{12,8},{14,10},{16,20},{18,... | collective-permute-start | bytes 172040 | tf_op jit(solution)/shard_map/ppermute | solution.py:21
  187.7 7.7 %collective-permute-start.40 = (bf16[2,176,128]{2,1,0:T(8,128)(2,1)S(1)}, bf16[2,176,128]{2,1,0:T(8,128)(2,1)S(1)}, u32[]{:S(2)}, u32[]{:S(2)}) collective-permute-start(bf16[2,176,128]{2,1,0:T(8,128)(2,1)S(1)} %fusion.89), channel_id=1, source_target_pairs={{0,8},{2,10},{4,12},{6,14},{8,0},{10,2},{12,4},{14,6},{16,24},{18,... | collective-permute-start | bytes 270344 | tf_op jit(solution)/shard_map/ppermute | solution.py:21
  189.7 5.6 %collective-permute-start.45 = (bf16[160,128]{1,0:T(8,128)(2,1)S(1)}, bf16[160,128]{1,0:T(8,128)(2,1)S(1)}, u32[]{:S(2)}, u32[]{:S(2)}) collective-permute-start(bf16[160,128]{1,0:T(8,128)(2,1)S(1)} %fusion.104), channel_id=1, source_target_pairs={{0,16},{2,18},{4,20},{6,22},{8,24},{10,26},{12,28},{14,30},{16,0},... | collective-permute-start | bytes 122888 | tf_op jit(solution)/shard_map/ppermute | solution.py:21
  191.3 5.0 %collective-permute-start.50 = (bf16[112,128]{1,0:T(8,128)(2,1)S(1)}, bf16[112,128]{1,0:T(8,128)(2,1)S(1)}, u32[]{:S(2)}, u32[]{:S(2)}) collective-permute-start(bf16[112,128]{1,0:T(8,128)(2,1)S(1)} %fusion.112), channel_id=1, source_target_pairs={{0,2},{2,0},{4,6},{6,4},{8,10},{10,8},{12,14},{14,12},{16,18},{18,... | collective-permute-start | bytes 86024 | tf_op jit(solution)/shard_map/ppermute | solution.py:21
  195.4 5.3 %collective-permute-start.41 = (bf16[176,128]{1,0:T(8,128)(2,1)S(1)}, bf16[176,128]{1,0:T(8,128)(2,1)S(1)}, u32[]{:S(2)}, u32[]{:S(2)}) collective-permute-start(bf16[176,128]{1,0:T(8,128)(2,1)S(1)} %fusion.103), channel_id=1, source_target_pairs={{0,16},{2,18},{4,20},{6,22},{8,24},{10,26},{12,28},{14,30},{16,0},... | collective-permute-start | bytes 135176 | tf_op jit(solution)/shard_map/ppermute | solution.py:21
  200.9 1.4 collective-permute-start.51
  207.7 33.2 %collective-permute-start.58 = (bf16[2,2,16,1792]{3,2,1,0:T(8,128)(2,1)S(1)}, bf16[2,2,16,1792]{3,2,1,0:T(8,128)(2,1)S(1)}, u32[]{:S(2)}, u32[]{:S(2)}) collective-permute-start(bf16[2,2,16,1792]{3,2,1,0:T(8,128)(2,1)S(1)} %bitcast.369), channel_id=1, source_target_pairs={{0,24},{2,26},{4,28},{6,30},{8,16},{10,18},{12,20},{14,22},{16,8},... | collective-permute-start | bytes 688136 | tf_op jit(solution)/shard_map/ppermute | solution.py:21
  208.2 32.7 %collective-permute-start.57 = (bf16[2,2,16,1792]{3,2,1,0:T(8,128)(2,1)S(1)}, bf16[2,2,16,1792]{3,2,1,0:T(8,128)(2,1)S(1)}, u32[]{:S(2)}, u32[]{:S(2)}) collective-permute-start(bf16[2,2,16,1792]{3,2,1,0:T(8,128)(2,1)S(1)} %bitcast.368), channel_id=1, source_target_pairs={{0,16},{2,18},{4,20},{6,22},{8,24},{10,26},{12,28},{14,30},{16,0},... | collective-permute-start | bytes 688136 | tf_op jit(solution)/shard_map/ppermute | solution.py:21
  209.4 13.9 %collective-permute-start.53 = (bf16[2,2,16,1792]{3,2,1,0:T(8,128)(2,1)S(1)}, bf16[2,2,16,1792]{3,2,1,0:T(8,128)(2,1)S(1)}, u32[]{:S(2)}, u32[]{:S(2)}) collective-permute-start(bf16[2,2,16,1792]{3,2,1,0:T(8,128)(2,1)S(1)} %bitcast.370), channel_id=1, source_target_pairs={{0,8},{2,10},{4,12},{6,14},{8,0},{10,2},{12,4},{14,6},{16,24},{18,... | collective-permute-start | bytes 688136 | tf_op jit(solution)/shard_map/ppermute | solution.py:21
  212.3 16.8 %collective-permute-start.59 = (bf16[2,2,2,16,2688]{4,3,1,0,2:T(8,128)(2,1)S(1)}, bf16[2,2,2,16,2688]{4,3,1,0,2:T(8,128)(2,1)S(1)}, u32[]{:S(2)}, u32[]{:S(2)}) collective-permute-start(bf16[2,2,2,16,2688]{4,3,1,0,2:T(8,128)(2,1)S(1)} %fusion.36), channel_id=1, source_target_pairs={{0,4},{2,6},{4,0},{6,2},{8,12},{10,14},{12,8},{14,10},{16,20},{18,... | collective-permute-start | bytes 2064392 | tf_op jit(solution)/shard_map/ppermute | solution.py:21
  214.0 16.4 %collective-permute-start.52 = (bf16[2,2,2,16,2688]{4,3,2,1,0:T(8,128)(2,1)S(1)}, bf16[2,2,2,16,2688]{4,3,2,1,0:T(8,128)(2,1)S(1)}, u32[]{:S(2)}, u32[]{:S(2)}) collective-permute-start(bf16[2,2,2,16,2688]{4,3,2,1,0:T(8,128)(2,1)S(1)} %fusion.35), channel_id=1, source_target_pairs={{0,2},{2,0},{4,6},{6,4},{8,10},{10,8},{12,14},{14,12},{16,18},{18,... | collective-permute-start | bytes 2064392 | tf_op jit(solution)/shard_map/ppermute | solution.py:21
  229.3 10.1 %collective-permute-start.60 = (bf16[2,2,16,2688]{3,2,1,0:T(8,128)(2,1)S(1)}, bf16[2,2,16,2688]{3,2,1,0:T(8,128)(2,1)S(1)}, u32[]{:S(2)}, u32[]{:S(2)}) collective-permute-start(bf16[2,2,16,2688]{3,2,1,0:T(8,128)(2,1)S(1)} %fusion.49), channel_id=1, source_target_pairs={{0,2},{2,0},{4,6},{6,4},{8,10},{10,8},{12,14},{14,12},{16,18},{18,... | collective-permute-start | bytes 1032200 | tf_op jit(solution)/shard_map/ppermute | solution.py:21
  230.7 10.2 %collective-permute-start.54 = (bf16[2,2,16,2688]{3,2,1,0:T(8,128)(2,1)S(1)}, bf16[2,2,16,2688]{3,2,1,0:T(8,128)(2,1)S(1)}, u32[]{:S(2)}, u32[]{:S(2)}) collective-permute-start(bf16[2,2,16,2688]{3,2,1,0:T(8,128)(2,1)S(1)} %fusion.48), channel_id=1, source_target_pairs={{0,4},{2,6},{4,0},{6,2},{8,12},{10,14},{12,8},{14,10},{16,20},{18,... | collective-permute-start | bytes 1032200 | tf_op jit(solution)/shard_map/ppermute | solution.py:21
  241.1 4.9 %collective-permute-start.61 = (bf16[2,16,1792]{2,1,0:T(8,128)(2,1)S(1)}, bf16[2,16,1792]{2,1,0:T(8,128)(2,1)S(1)}, u32[]{:S(2)}, u32[]{:S(2)}) collective-permute-start(bf16[2,16,1792]{2,1,0:T(8,128)(2,1)S(1)} %fusion.86), channel_id=1, source_target_pairs={{0,4},{2,6},{4,0},{6,2},{8,12},{10,14},{12,8},{14,10},{16,20},{18,... | collective-permute-start | bytes 344072 | tf_op jit(solution)/shard_map/ppermute | solution.py:21
  243.0 6.8 %collective-permute-start.55 = (bf16[2,16,2688]{2,1,0:T(8,128)(2,1)S(1)}, bf16[2,16,2688]{2,1,0:T(8,128)(2,1)S(1)}, u32[]{:S(2)}, u32[]{:S(2)}) collective-permute-start(bf16[2,16,2688]{2,1,0:T(8,128)(2,1)S(1)} %fusion.75), channel_id=1, source_target_pairs={{0,8},{2,10},{4,12},{6,14},{8,0},{10,2},{12,4},{14,6},{16,24},{18,... | collective-permute-start | bytes 516104 | tf_op jit(solution)/shard_map/ppermute | solution.py:21
  245.7 5.9 %collective-permute-start.63 = (bf16[2,16,2688]{2,1,0:T(8,128)(2,1)S(1)}, bf16[2,16,2688]{2,1,0:T(8,128)(2,1)S(1)}, u32[]{:S(2)}, u32[]{:S(2)}) collective-permute-start(bf16[2,16,2688]{2,1,0:T(8,128)(2,1)S(1)} %fusion.76), channel_id=1, source_target_pairs={{0,8},{2,10},{4,12},{6,14},{8,0},{10,2},{12,4},{14,6},{16,24},{18,... | collective-permute-start | bytes 516104 | tf_op jit(solution)/shard_map/ppermute | solution.py:21
  246.0 7.8 %collective-permute-start.62 = (bf16[16,1792]{1,0:T(8,128)(2,1)S(1)}, bf16[16,1792]{1,0:T(8,128)(2,1)S(1)}, u32[]{:S(2)}, u32[]{:S(2)}) collective-permute-start(bf16[16,1792]{1,0:T(8,128)(2,1)S(1)} %fusion.99), channel_id=1, source_target_pairs={{0,2},{2,0},{4,6},{6,4},{8,10},{10,8},{12,14},{14,12},{16,18},{18,... | collective-permute-start | bytes 172040 | tf_op jit(solution)/shard_map/ppermute | solution.py:21
  251.7 5.4 %collective-permute-start.64 = (bf16[16,2688]{1,0:T(8,128)(2,1)S(1)}, bf16[16,2688]{1,0:T(8,128)(2,1)S(1)}, u32[]{:S(2)}, u32[]{:S(2)}) collective-permute-start(bf16[16,2688]{1,0:T(8,128)(2,1)S(1)} %fusion.92), channel_id=1, source_target_pairs={{0,16},{2,18},{4,20},{6,22},{8,24},{10,26},{12,28},{14,30},{16,0},... | collective-permute-start | bytes 258056 | tf_op jit(solution)/shard_map/ppermute | solution.py:21
  253.9 6.3 %collective-permute-start.56 = (bf16[16,2688]{1,0:T(8,128)(2,1)S(1)}, bf16[16,2688]{1,0:T(8,128)(2,1)S(1)}, u32[]{:S(2)}, u32[]{:S(2)}) collective-permute-start(bf16[16,2688]{1,0:T(8,128)(2,1)S(1)} %fusion.91), channel_id=1, source_target_pairs={{0,16},{2,18},{4,20},{6,22},{8,24},{10,26},{12,28},{14,30},{16,0},... | collective-permute-start | bytes 258056 | tf_op jit(solution)/shard_map/ppermute | solution.py:21
  (19 other events, 172.3 us)

commit v6 on v5

--- a/solution.py
+++ b/solution.py
@@ -38,7 +38,7 @@
     return array.reshape((1 << count,) + array.shape[count:])
 
 
-def gather(first, second, third):
+def gather(first, second, third, last=False):
     high = list(reversed(range(2, bits_of("seq"))))
     third_shape = third.shape
     came = []
@@ -48,14 +48,16 @@
             third = third + zero_of(came[0], third.shape) + zero_of(came[1], third.shape)
         first, second = jnp.stack([first, came[0]]), jnp.stack([second, came[1]])
     for bit in (0, 1):
-        first = jnp.stack([first, from_partner(first, "seq", 2 >> bit)])
-        second = jnp.stack([second, from_partner(second, "seq", 1 << bit)])
+        ends = [from_partner(first, "seq", 2 >> bit), from_partner(second, "seq", 1 << bit)]
+        first, second = jnp.stack([first, ends[0]]), jnp.stack([second, ends[1]])
         third = jnp.stack([third, from_partner(third, "seq", 1 << bit)])
     for block in came:
         third = third + zero_of(block, third_shape)
     far = range(1, 1 << len(high))
     third = jnp.stack([third] + [from_partner(third, "seq", place << 2) for place in far])
     third = third.reshape((-1,) + third_shape)
+    for block in ends if last else ():
+        third = third + zero_of(block, third_shape)
     return in_order(first, high + [1, 0]), in_order(second, high + [0, 1]), third
 
 
@@ -301,26 +303,26 @@
         left[...], features[...], (((1,), (1,)), ((), ())), preferred_element_type=f32
     ).astype(bf16)
 
-    @pl.when(pl.program_id(0) == 0)
+    @pl.when((pl.program_id(0) == 0) & (pl.program_id(1) == 0))
     def _():
         zeros[...] = jnp.zeros_like(zeros)
 
 
-def grad_head_rows(left, features, index, count, later_than, shape, before):
+def grad_head_rows(left, features, start, count, later_than, shape, before):
     vocab, tokens = left.shape
-    rows, tile = vocab // count, 1024
+    rows, tile = 256, 1792
     given = (later_than,) if before is None else (later_than, before)
     return pl.pallas_call(
         grad_head_kernel,
-        grid=(D // tile,),
+        grid=(D // tile, count),
         in_specs=[
-            pl.BlockSpec((rows, tokens), lambda i: (index, 0)),
-            pl.BlockSpec((tile, tokens), lambda i: (i, 0)),
+            pl.BlockSpec((rows, tokens), lambda i, j: (start + j, 0)),
+            pl.BlockSpec((tile, tokens), lambda i, j: (i, 0)),
             *[pl.BlockSpec(memory_space=pl.ANY) for _ in given],
         ],
         out_specs=[
-            pl.BlockSpec((rows, tile), lambda i: (index, i)),
-            pl.BlockSpec(shape, lambda i: (0,) * len(shape)),
+            pl.BlockSpec((rows, tile), lambda i, j: (start + j, i)),
+            pl.BlockSpec(shape, lambda i, j: (0,) * len(shape)),
         ],
         out_shape=[
             jax.ShapeDtypeStruct((vocab, D), bf16),
@@ -329,7 +331,9 @@
         input_output_aliases={3: 0} if before is not None else {},
         compiler_params=pltpu.CompilerParams(vmem_limit_bytes=20 << 20),
         cost_estimate=pl.CostEstimate(
-            flops=2 * rows * D * tokens, bytes_accessed=2 * rows * D + 2 * D * tokens, transcendentals=0
+            flops=2 * count * rows * D * tokens,
+            bytes_accessed=2 * count * rows * D + 2 * D * tokens,
+            transcendentals=0,
         ),
     )(left, features, *given)
 
@@ -415,7 +419,7 @@
     facts = jnp.concatenate([facts, gain_parts], axis=1)
     facts = jnp.pad(facts, ((0, 0), (0, 128 - facts.shape[1])))
 
-    first, second, third = gather(first, second, jnp.concatenate([third, facts], axis=1))
+    first, second, third = gather(first, second, jnp.concatenate([third, facts], axis=1), True)
     first, second = first.reshape(tokens, main), second.reshape(tokens, main)
     third = third.reshape(tokens, 2 * rest + 128)
 
@@ -472,7 +476,7 @@
     where = jnp.stack([me, lax.axis_index(("seq", "tp")) * vocab_rows]).astype(i32)
     ids = lanes_by_index(ids_all)
     valid_lanes = lanes_by_index(valid_all)
-    fits = cores == 2 and lanes % 128 == 0 and vocab_rows % 512 == 0 and 2 * features % 128 == 0
+    fits = cores == 2 and lanes % 128 == 0 and vocab_rows % 2048 == 0 and 2 * features % 128 == 0
     forward = head_logits if fits else plain_logits
     logits, stats, final_all = forward(where, ids, scale_final[None, :], gain_all, pieces, head)
     stats = stats[:4]
@@ -494,19 +498,24 @@
         from_core = from_partner(piece, "tp", mask)
         dfinal = dfinal + from_core.astype(f32).reshape(dfinal.shape)
 
-    def grad_head_piece(index, tied):
+    def grad_head_piece(start, count, tied):
         def work(last, shape, results):
             if not fits:
                 return dot(dlogits, final_all, 1, 1).astype(bf16), None
             before = results[-1] if results else None
             shape = shape if tied else (8, 128)
             later_than = last if tied else from_core
-            out, zeros = grad_head_rows(dlogits, final_all, index, 4, later_than, shape, before)
+            out, zeros = grad_head_rows(dlogits, final_all, start, count, later_than, shape, before)
             return out, (zeros if tied else None)
 
         return work
 
-    early = [grad_head_piece(index, index == 1) for index in range(2 if fits else 1)]
+    quarter = vocab_rows // 1024
+    early = [grad_head_piece(0, quarter, False)]
+    if fits:
+        early.append(grad_head_piece(quarter, quarter // 2, True))
+    ahead = quarter + quarter // 2
+    behind = vocab_rows // 256 - ahead - quarter
     dfinal, results = scatter([dfinal[:, :one], dfinal[:, one:two], dfinal[:, two:]], early)
     dfinal = jnp.concatenate(dfinal, axis=0)
 
@@ -520,12 +529,12 @@
     back_prev = dot(dmixed_prev, proj_hidden, 0, 1).reshape(blocks, rows, width)
     back_embed = dot(dmixed_embed, proj_embed, 0, 1).reshape(blocks, rows, width)
 
-    def grad_head_end(index):
+    def grad_head_end(start, count):
         def work(last, shape, before):
             grad_head = before[-1] if before else results[-1]
             if not fits:
                 return grad_head, None
-            return grad_head_rows(dlogits, final_all, index, 4, last, shape, grad_head)
+            return grad_head_rows(dlogits, final_all, start, count, last, shape, grad_head)
 
         return work
 
@@ -539,7 +548,7 @@
             back_embed[..., :main],
             jnp.concatenate([back_prev[..., main:], back_embed[..., main:]], axis=-1),
         ],
-        [grad_head_end(2), grad_head_end(3)],
+        [grad_head_end(ahead, behind), grad_head_end(ahead + behind, quarter)],
     )
     grad_head = ends[-1]
     grad_proj_hidden = grad_proj(first, third[:, :rest], dmixed_prev)

time: 265 us -> 267 us (level)
  starting transfers between devices: 78.7 us -> 73.4 us
  waiting for transfers between devices: 90.4 us -> 95 us
    ppermute x65, starting transfers between devices: 78.7 us -> 73.4 us  [from_partner(): return lax.ppermute(array, axis, [(i, i ^ mask) for i in range(size)])]
    ppermute x65, waiting for transfers between devices: 90.4 us -> 95 us  [from_partner(): return lax.ppermute(array, axis, [(i, i ^ mask) for i in range(size)])]
  transfers between devices with their start and end apart: 65 -> 65, of which waited for: 38 -> 40; matrix products, arithmetic and copies ran while one was open for 6% -> 5% of each run, Pallas kernels for 9% -> 9%
where the time goes in v6:
time: 267 us; the launch traced here: 266 us
  waiting for transfers between devices  95 us (36%)
  starting transfers between devices  73.4 us (27%)
  Pallas kernels  56.2 us (21%)
  other arithmetic  13.2 us (5%)
  matrix products  12.2 us (5%)
  local copies, waits for them, and re-layouts  7.73 us (3%)
  blocking collectives  5.05 us (2%)
  between operations  3.18 us (1%)
    ppermute x65, waiting for transfers between devices, from_partner(): return lax.ppermute(array, axis, [(i, i ^ mask) for i in range(size)])  95 us
    ppermute x65, starting transfers between devices, from_partner(): return lax.ppermute(array, axis, [(i, i ^ mask) for i in range(size)])  73.4 us
    pallas_call x4, Pallas kernels, grad_head_rows(): pl.pallas_call(grad_head_kernel, grid=(D // tile, count), in_specs=[pl.Bl...  23.7 us
    pallas_call x1, Pallas kernels, head_back(): pl.pallas_call(dfinal_kernel, grid_spec=pltpu.PrefetchScalarGridSpec(num_...  16.7 us
    pallas_call x1, Pallas kernels, head_logits(): pl.pallas_call(logits_kernel, grid_spec=pltpu.PrefetchScalarGridSpec(num_...  15.9 us
    dot_general x14, matrix products, dot(): lax.dot_general(left, right, (((on_left,), (on_right,)), ((), ())), preci...  12.2 us
    unnamed x36, local copies, waits for them, and re-layouts  5.46 us
  transfers between devices with their start and end apart: 65, of which 40 were waited for; matrix products, arithmetic and copies ran while one was open for 5% of the time, Pallas kernels for 9%

profile of v6, /device:TPU:0, one launch (start us, length us, event | category | flops | bytes accessed | tf_op | source)
XLA Modules:
  0.0 265.9 jit_solution(6005213321264176639)
XLA Ops:
  2.7 2.6 psum.14
  6.5 4.0 %collective-permute-start.4 = (bf16[16,2688]{1,0:T(8,128)(2,1)S(1)}, bf16[16,2688]{1,0:T(8,128)(2,1)S(1)}, u32[]{:S(2)}, u32[]{:S(2)}) collective-permute-start(bf16[16,2688]{1,0:T(8,128)(2,1)S(1)} %slice.631), channel_id=1, source_target_pairs={{0,16},{2,18},{4,20},{6,22},{8,24},{10,26},{12,28},{14,30},{16,0},... | collective-permute-start | bytes 258056 | tf_op jit(solution)/shard_map/ppermute | solution.py:21
  13.4 4.1 %collective-permute-done.4 = bf16[16,2688]{1,0:T(8,128)(2,1)S(1)} collective-permute-done((bf16[16,2688]{1,0:T(8,128)(2,1)S(1)}, bf16[16,2688]{1,0:T(8,128)(2,1)S(1)}, u32[]{:S(2)}, u32[]{:S(2)}) %collective-permute-start.4) | collective-permute-done | bytes 86048 | tf_op jit(solution)/shard_map/ppermute | solution.py:21
  17.5 1.4 collective-permute-done
  18.9 1.6 collective-permute-start.5
  21.4 1.4 collective-permute-start.1
  23.3 1.6 collective-permute-start.6
  24.9 3.0 %collective-permute-done.7 = bf16[2,16,2688]{2,1,0:T(8,128)(2,1)S(1)} collective-permute-done((bf16[2,16,2688]{2,1,0:T(8,128)(2,1)S(1)}, bf16[2,16,2688]{2,1,0:T(8,128)(2,1)S(1)}, u32[]{:S(2)}, u32[]{:S(2)}) %collective-permute-start.7) | collective-permute-done | bytes 172064 | tf_op jit(solution)/shard_map/ppermute | solution.py:21
  27.9 1.8 collective-permute-done.1
  30.7 1.4 collective-permute-start.2
  32.1 4.2 %collective-permute-start.10 = (bf16[2,2,16,1920]{3,2,1,0:T(8,128)(2,1)S(1)}, bf16[2,2,16,1920]{3,2,1,0:T(8,128)(2,1)S(1)}, u32[]{:S(2)}, u32[]{:S(2)}) collective-permute-start(bf16[2,2,16,1920]{3,2,1,0:T(8,128)(2,1)S(1)} %fusion.55), channel_id=1, source_target_pairs={{0,24},{2,26},{4,28},{6,30},{8,16},{10,18},{12,20},{14,22},{16,8},... | collective-permute-start | bytes 737288 | tf_op jit(solution)/shard_map/ppermute | solution.py:21
  38.1 1.6 collective-permute-start.12
  39.7 3.5 %collective-permute-done.10 = bf16[2,2,16,1920]{3,2,1,0:T(8,128)(2,1)S(1)} collective-permute-done((bf16[2,2,16,1920]{3,2,1,0:T(8,128)(2,1)S(1)}, bf16[2,2,16,1920]{3,2,1,0:T(8,128)(2,1)S(1)}, u32[]{:S(2)}, u32[]{:S(2)}) %collective-permute-start.10) | collective-permute-done | bytes 245792 | tf_op jit(solution)/shard_map/ppermute | solution.py:21
  43.2 12.4 %collective-permute-done.9 = bf16[2,2,16,1920]{3,2,1,0:T(8,128)(2,1)S(1)} collective-permute-done((bf16[2,2,16,1920]{3,2,1,0:T(8,128)(2,1)S(1)}, bf16[2,2,16,1920]{3,2,1,0:T(8,128)(2,1)S(1)}, u32[]{:S(2)}, u32[]{:S(2)}) %collective-permute-start.9) | collective-permute-done | bytes 245792 | tf_op jit(solution)/shard_map/ppermute | solution.py:21
  56.0 1.6 collective-permute-start.3
  57.5 14.9 %collective-permute-done.3 = bf16[2,2,2,16,2688]{4,3,2,1,0:T(8,128)(2,1)S(1)} collective-permute-done((bf16[2,2,2,16,2688]{4,3,2,1,0:T(8,128)(2,1)S(1)}, bf16[2,2,2,16,2688]{4,3,2,1,0:T(8,128)(2,1)S(1)}, u32[]{:S(2)}, u32[]{:S(2)}) %collective-permute-start.3) | collective-permute-done | bytes 688160 | tf_op jit(solution)/shard_map/ppermute | solution.py:21
  73.8 1.6 copy-done.4
  80.4 2.9 %collective-permute-start.14 = (bf16[176,128]{1,0:T(8,128)(2,1)S(1)}, bf16[176,128]{1,0:T(8,128)(2,1)S(1)}, u32[]{:S(2)}, u32[]{:S(2)}) collective-permute-start(bf16[176,128]{1,0:T(8,128)(2,1)S(1)} %get-tuple-element.93), channel_id=1, source_target_pairs={{0,16},{2,18},{4,20},{6,22},{8,24},{10,26},{12,28},{14,30},{16,0},... | collective-permute-start | bytes 135176 | tf_op jit(solution)/shard_map/ppermute | solution.py:21
  83.3 2.1 collective-permute-done.15
  86.5 1.6 collective-permute-start.16
  88.1 1.3 collective-permute-start.18
  91.1 1.6 collective-permute-start.26
  92.7 1.6 collective-permute-start.24
  95.5 2.2 collective-permute-start.22
  98.3 1.7 collective-permute-start.20
  102.5 4.0 %collective-permute-done.21 = bf16[2,2,128,128]{3,2,1,0:T(8,128)(2,1)S(1)} collective-permute-done((bf16[2,2,128,128]{3,2,1,0:T(8,128)(2,1)S(1)}, bf16[2,2,128,128]{3,2,1,0:T(8,128)(2,1)S(1)}, u32[]{:S(2)}, u32[]{:S(2)}) %collective-permute-start.21) | collective-permute-done | bytes 131104 | tf_op jit(solution)/shard_map/ppermute | solution.py:21
  109.1 1.8 collective-permute-done.29.refs_4_
  110.8 15.9 %shard_map.146 = (f32[2048,256]{1,0:T(8,128)S(1)}, f32[8,256]{1,0:T(8,128)S(1)}, bf16[7168,256]{1,0:T(8,128)(2,1)S(1)}) custom-call(s32[2]{0:T(128)S(1)} %pad_add_fusion.1.where, s32[1,256]{1,0:T(1,128)S(1)} %pad_add_fusion.ids, f32[1,256]{1,0:T(1,128)S(1)} %fusion.171.scale, f32[448,16]{1,0:T(8,128)S(1)} %fusion.109.gain, ...), custom_call_target="tpu_custom_call" | custom-call | flops 7516192768 | bytes 36700160 | tf_op jit(solution)/shard_map/pallas_call | solution.py:204
  126.7 1.8 copy-done
  128.5 1.2 collective-permute-start.32
  129.8 1.4 collective-permute-start.31
  133.4 1.4 collective-permute-done.30
  134.8 2.6 collective-permute-start.35
  137.4 1.9 collective-permute-start.33
  140.6 1.3 collective-permute-done.34
  143.3 16.7 %shard_map.147 = (f32[8,2,448,128]{3,2,1,0:T(8,128)S(1)}, bf16[8,2,448,128]{3,2,1,0:T(8,128)(2,1)S(1)}, bf16[2048,256]{1,0:T(8,128)(2,1)S(1)}) custom-call(s32[2]{0:T(128)S(1)} %pad_add_fusion.1.where, s32[1,256]{1,0:T(1,128)S(1)} %pad_add_fusion.ids, f32[8,256]{1,0:T(8,128)S(1)} %select_maximum_fusion.rows, f32[2048,256]{1,0:T(8,128)S(1)} %get-tuple-element.31.logits, ...), custom_call_target="tpu_custom_call" | custom-call | flops 7516192768 | bytes 36700160 | tf_op jit(solution)/shard_map/pallas_call | solution.py:268
  160.3 3.6 %collective-permute-done.37.refs_0_ = bf16[8,2,448,128]{3,2,1,0:T(8,128)(2,1)S(1)} collective-permute-done((bf16[8,2,448,128]{3,2,1,0:T(8,128)(2,1)S(1)}, bf16[8,2,448,128]{3,2,1,0:T(8,128)(2,1)S(1)}, u32[]{:S(2)}, u32[]{:S(2)}) %collective-permute-start.37) | collective-permute-done | bytes 1835040 | tf_op jit(solution)/shard_map/ppermute | solution.py:21
  164.8 1.5 collective-permute-start.48
  167.3 1.9 collective-permute-start.46
  170.7 5.9 %shard_map.148 = (bf16[2048,7168]{1,0:T(8,128)(2,1)}, f32[8,128]{1,0:T(8,128)}) custom-call(bf16[2048,256]{1,0:T(8,128)(2,1)S(1)} %get-tuple-element.34.left, bf16[7168,256]{1,0:T(8,128)(2,1)S(1)} %copy-done.1, bf16[8,2,448,128]{3,2,1,0:T(8,128)(2,1)S(1)} %collective-permute-done.37.refs_0_), custom_call_target="tpu_custom_call" | custom-call | flops 1879048192 | bytes 11010048 | tf_op jit(solution)/shard_map/pallas_call | solution.py:315
  176.6 1.7 collective-permute-done.42
  179.5 2.5 collective-permute-start.39
  181.9 3.2 %shard_map.149 = (bf16[2048,7168]{1,0:T(8,128)(2,1)}, f32[2,2,176,128]{3,2,1,0:T(8,128)S(1)}) custom-call(bf16[2048,256]{1,0:T(8,128)(2,1)S(1)} %get-tuple-element.34.left, bf16[7168,256]{1,0:T(8,128)(2,1)S(1)} %copy-done.1, bf16[2,2,2,176,128]{4,3,2,1,0:T(8,128)(2,1)S(1)} %collective-permute-done.38.refs_0_, ...), custom_call_target="tpu_custom_call", output_to_operand_aliasing={{0}: (3, {})} | custom-call | flops 939524096 | bytes 7340032 | tf_op jit(solution)/shard_map/pallas_call | solution.py:315
  185.7 2.5 collective-permute-start.49
  188.4 1.7 collective-permute-done.44
  191.7 3.6 %collective-permute-done.45 = bf16[160,128]{1,0:T(8,128)(2,1)S(1)} collective-permute-done((bf16[160,128]{1,0:T(8,128)(2,1)S(1)}, bf16[160,128]{1,0:T(8,128)(2,1)S(1)}, u32[]{:S(2)}, u32[]{:S(2)}) %collective-permute-start.45) | collective-permute-done | bytes 40992 | tf_op jit(solution)/shard_map/ppermute | solution.py:21
  196.1 4.3 %collective-permute-done.41 = bf16[176,128]{1,0:T(8,128)(2,1)S(1)} collective-permute-done((bf16[176,128]{1,0:T(8,128)(2,1)S(1)}, bf16[176,128]{1,0:T(8,128)(2,1)S(1)}, u32[]{:S(2)}, u32[]{:S(2)}) %collective-permute-start.41) | collective-permute-done | bytes 45088 | tf_op jit(solution)/shard_map/ppermute | solution.py:21
  204.2 1.7 copy-done.5
  207.5 2.1 collective-permute-start.58
  209.5 2.4 collective-permute-start.53
  213.6 2.7 %convolution_convert_fusion.1 = bf16[3584,448]{0,1:T(8,128)(2,1)} fusion(bf16[448,256]{1,0:T(8,128)(2,1)S(1)} %convolution_convert_fusion.3, bf16[256,896]{1,0:T(8,128)(2,1)S(1)} %get-tuple-element.57, bf16[256,2688]{1,0:T(8,128)(2,1)S(1)} %bitcast.347), kind=kOutput, calls=%fused_computation.1 | convolution fusion | flops 827359232 | bytes 5275648 | tf_op jit(solution)/shard_map/dot_general | solution.py:152
  216.3 2.7 %convolution_convert_fusion = bf16[3584,448]{0,1:T(8,128)(2,1)} fusion(bf16[448,256]{1,0:T(8,128)(2,1)S(1)} %convolution_convert_fusion.2, bf16[256,896]{1,0:T(8,128)(2,1)S(1)} %get-tuple-element.56, bf16[256,2688]{1,0:T(8,128)(2,1)S(1)} %bitcast.345), kind=kOutput, calls=%fused_computation | convolution fusion | flops 827359232 | bytes 5275648 | tf_op jit(solution)/shard_map/dot_general | solution.py:152
  219.0 5.6 %collective-permute-done.53.refs_0_ = bf16[2,2,16,1792]{3,2,1,0:T(8,128)(2,1)S(1)} collective-permute-done((bf16[2,2,16,1792]{3,2,1,0:T(8,128)(2,1)S(1)}, bf16[2,2,16,1792]{3,2,1,0:T(8,128)(2,1)S(1)}, u32[]{:S(2)}, u32[]{:S(2)}) %collective-permute-start.53) | collective-permute-done | bytes 229408 | tf_op jit(solution)/shard_map/ppermute | solution.py:21
  224.6 8.7 %shard_map.150 = (bf16[2048,7168]{1,0:T(8,128)(2,1)}, f32[2,2,2,16,2688]{4,3,2,1,0:T(8,128)S(1)}) custom-call(bf16[2048,256]{1,0:T(8,128)(2,1)S(1)} %get-tuple-element.34.left, bf16[7168,256]{1,0:T(8,128)(2,1)S(1)} %copy-done.1, bf16[2,2,16,1792]{3,2,1,0:T(8,128)(2,1)S(1)} %collective-permute-done.53.refs_0_, ...), custom_call_target="tpu_custom_call", output_to_operand_aliasing={{0}: (3, {})} | custom-call | flops 2818572288 | bytes 14680064 | tf_op jit(solution)/shard_map/pallas_call | solution.py:315
  235.0 5.9 %shard_map.151 = (bf16[2048,7168]{1,0:T(8,128)(2,1)}, f32[2,2,16,2688]{3,2,1,0:T(8,128)S(1)}) custom-call(bf16[2048,256]{1,0:T(8,128)(2,1)S(1)} %get-tuple-element.34.left, bf16[7168,256]{1,0:T(8,128)(2,1)S(1)} %copy-done.1, bf16[2,2,2,16,2688]{4,3,2,1,0:T(8,128)(2,1)S(1)} %collective-permute-done.52.refs_0_, ...), custom_call_target="tpu_custom_call", output_to_operand_aliasing={{0}: (3, {})} | custom-call | flops 1879048192 | bytes 11010048 | tf_op jit(solution)/shard_map/pallas_call | solution.py:315
  241.0 1.9 collective-permute-done.60
  244.5 2.5 collective-permute-start.55
  247.2 1.4 collective-permute-done.61
  248.7 1.5 collective-permute-start.62
  251.3 1.8 collective-permute-done.63
  253.1 2.5 collective-permute-start.64
  256.2 2.4 collective-permute-done.64
  258.8 2.9 %collective-permute-done.56 = bf16[16,2688]{1,0:T(8,128)(2,1)S(1)} collective-permute-done((bf16[16,2688]{1,0:T(8,128)(2,1)S(1)}, bf16[16,2688]{1,0:T(8,128)(2,1)S(1)}, u32[]{:S(2)}, u32[]{:S(2)}) %collective-permute-start.56) | collective-permute-done | bytes 86048 | tf_op jit(solution)/shard_map/ppermute | solution.py:21
  261.9 2.5 psum.15
  (298 shorter events, 51.7 us)
Async XLA Ops:
  6.5 11.0 %collective-permute-start.4 = (bf16[16,2688]{1,0:T(8,128)(2,1)S(1)}, bf16[16,2688]{1,0:T(8,128)(2,1)S(1)}, u32[]{:S(2)}, u32[]{:S(2)}) collective-permute-start(bf16[16,2688]{1,0:T(8,128)(2,1)S(1)} %slice.631), channel_id=1, source_target_pairs={{0,16},{2,18},{4,20},{6,22},{8,24},{10,26},{12,28},{14,30},{16,0},... | collective-permute-start | bytes 258056 | tf_op jit(solution)/shard_map/ppermute | solution.py:21
  10.5 8.4 %collective-permute-start = (bf16[16,2688]{1,0:T(8,128)(2,1)S(1)}, bf16[16,2688]{1,0:T(8,128)(2,1)S(1)}, u32[]{:S(2)}, u32[]{:S(2)}) collective-permute-start(bf16[16,2688]{1,0:T(8,128)(2,1)S(1)} %slice.630), channel_id=1, source_target_pairs={{0,16},{2,18},{4,20},{6,22},{8,24},{10,26},{12,28},{14,30},{16,0},... | collective-permute-start | bytes 258056 | tf_op jit(solution)/shard_map/ppermute | solution.py:21
  18.9 4.3 %collective-permute-start.5 = (bf16[16,1920]{1,0:T(8,128)(2,1)S(1)}, bf16[16,1920]{1,0:T(8,128)(2,1)S(1)}, u32[]{:S(2)}, u32[]{:S(2)}) collective-permute-start(bf16[16,1920]{1,0:T(8,128)(2,1)S(1)} %fusion.96), channel_id=1, source_target_pairs={{0,2},{2,0},{4,6},{6,4},{8,10},{10,8},{12,14},{14,12},{16,18},{18,... | collective-permute-start | bytes 184328 | tf_op jit(solution)/shard_map/ppermute | solution.py:21
  20.6 7.3 %collective-permute-start.7 = (bf16[2,16,2688]{2,1,0:T(8,128)(2,1)S(1)}, bf16[2,16,2688]{2,1,0:T(8,128)(2,1)S(1)}, u32[]{:S(2)}, u32[]{:S(2)}) collective-permute-start(bf16[2,16,2688]{2,1,0:T(8,128)(2,1)S(1)} %get-tuple-element.80), channel_id=1, source_target_pairs={{0,8},{2,10},{4,12},{6,14},{8,0},{10,2},{12,4},{14,6},{16,24},{18,... | collective-permute-start | bytes 516104 | tf_op jit(solution)/shard_map/ppermute | solution.py:21
  21.4 8.4 %collective-permute-start.1 = (bf16[2,16,2688]{2,1,0:T(8,128)(2,1)S(1)}, bf16[2,16,2688]{2,1,0:T(8,128)(2,1)S(1)}, u32[]{:S(2)}, u32[]{:S(2)}) collective-permute-start(bf16[2,16,2688]{2,1,0:T(8,128)(2,1)S(1)} %get-tuple-element.78), channel_id=1, source_target_pairs={{0,8},{2,10},{4,12},{6,14},{8,0},{10,2},{12,4},{14,6},{16,24},{18,... | collective-permute-start | bytes 516104 | tf_op jit(solution)/shard_map/ppermute | solution.py:21
  23.3 8.8 %collective-permute-start.6 = (bf16[2,16,1920]{2,1,0:T(8,128)(2,1)S(1)}, bf16[2,16,1920]{2,1,0:T(8,128)(2,1)S(1)}, u32[]{:S(2)}, u32[]{:S(2)}) collective-permute-start(bf16[2,16,1920]{2,1,0:T(8,128)(2,1)S(1)} %get-tuple-element.89), channel_id=1, source_target_pairs={{0,4},{2,6},{4,0},{6,2},{8,12},{10,14},{12,8},{14,10},{16,20},{18,... | collective-permute-start | bytes 368648 | tf_op jit(solution)/shard_map/ppermute | solution.py:21
  29.8 8.2 %collective-permute-start.11 = (bf16[2,2,16,2688]{3,2,1,0:T(8,128)(2,1)S(1)}, bf16[2,2,16,2688]{3,2,1,0:T(8,128)(2,1)S(1)}, u32[]{:S(2)}, u32[]{:S(2)}) collective-permute-start(bf16[2,2,16,2688]{3,2,1,0:T(8,128)(2,1)S(1)} %get-tuple-element.70), channel_id=1, source_target_pairs={{0,2},{2,0},{4,6},{6,4},{8,10},{10,8},{12,14},{14,12},{16,18},{18,... | collective-permute-start | bytes 1032200 | tf_op jit(solution)/shard_map/ppermute | solution.py:21
  30.7 25.2 %collective-permute-start.2 = (bf16[2,2,16,2688]{3,2,1,0:T(8,128)(2,1)S(1)}, bf16[2,2,16,2688]{3,2,1,0:T(8,128)(2,1)S(1)}, u32[]{:S(2)}, u32[]{:S(2)}) collective-permute-start(bf16[2,2,16,2688]{3,2,1,0:T(8,128)(2,1)S(1)} %get-tuple-element.68), channel_id=1, source_target_pairs={{0,4},{2,6},{4,0},{6,2},{8,12},{10,14},{12,8},{14,10},{16,20},{18,... | collective-permute-start | bytes 1032200 | tf_op jit(solution)/shard_map/ppermute | solution.py:21
  32.1 11.1 %collective-permute-start.10 = (bf16[2,2,16,1920]{3,2,1,0:T(8,128)(2,1)S(1)}, bf16[2,2,16,1920]{3,2,1,0:T(8,128)(2,1)S(1)}, u32[]{:S(2)}, u32[]{:S(2)}) collective-permute-start(bf16[2,2,16,1920]{3,2,1,0:T(8,128)(2,1)S(1)} %fusion.55), channel_id=1, source_target_pairs={{0,24},{2,26},{4,28},{6,30},{8,16},{10,18},{12,20},{14,22},{16,8},... | collective-permute-start | bytes 737288 | tf_op jit(solution)/shard_map/ppermute | solution.py:21
  36.3 19.4 %collective-permute-start.9 = (bf16[2,2,16,1920]{3,2,1,0:T(8,128)(2,1)S(1)}, bf16[2,2,16,1920]{3,2,1,0:T(8,128)(2,1)S(1)}, u32[]{:S(2)}, u32[]{:S(2)}) collective-permute-start(bf16[2,2,16,1920]{3,2,1,0:T(8,128)(2,1)S(1)} %fusion.55), channel_id=1, source_target_pairs={{0,16},{2,18},{4,20},{6,22},{8,24},{10,26},{12,28},{14,30},{16,0},... | collective-permute-start | bytes 737288 | tf_op jit(solution)/shard_map/ppermute | solution.py:21
  36.3 19.4 %collective-permute-start.8 = (bf16[2,2,16,1920]{3,2,1,0:T(8,128)(2,1)S(1)}, bf16[2,2,16,1920]{3,2,1,0:T(8,128)(2,1)S(1)}, u32[]{:S(2)}, u32[]{:S(2)}) collective-permute-start(bf16[2,2,16,1920]{3,2,1,0:T(8,128)(2,1)S(1)} %fusion.55), channel_id=1, source_target_pairs={{0,8},{2,10},{4,12},{6,14},{8,0},{10,2},{12,4},{14,6},{16,24},{18,... | collective-permute-start | bytes 737288 | tf_op jit(solution)/shard_map/ppermute | solution.py:21
  38.1 19.4 %collective-permute-start.12 = (bf16[2,2,2,16,2688]{4,3,2,1,0:T(8,128)(2,1)S(1)}, bf16[2,2,2,16,2688]{4,3,2,1,0:T(8,128)(2,1)S(1)}, u32[]{:S(2)}, u32[]{:S(2)}) collective-permute-start(bf16[2,2,2,16,2688]{4,3,2,1,0:T(8,128)(2,1)S(1)} %get-tuple-element.64), channel_id=1, source_target_pairs={{0,4},{2,6},{4,0},{6,2},{8,12},{10,14},{12,8},{14,10},{16,20},{18,... | collective-permute-start | bytes 2064392 | tf_op jit(solution)/shard_map/ppermute | solution.py:21
  56.0 16.5 %collective-permute-start.3 = (bf16[2,2,2,16,2688]{4,3,2,1,0:T(8,128)(2,1)S(1)}, bf16[2,2,2,16,2688]{4,3,2,1,0:T(8,128)(2,1)S(1)}, u32[]{:S(2)}, u32[]{:S(2)}) collective-permute-start(bf16[2,2,2,16,2688]{4,3,2,1,0:T(8,128)(2,1)S(1)} %get-tuple-element.62), channel_id=1, source_target_pairs={{0,2},{2,0},{4,6},{6,4},{8,10},{10,8},{12,14},{14,12},{16,18},{18,... | collective-permute-start | bytes 2064392 | tf_op jit(solution)/shard_map/ppermute | solution.py:21
  78.7 1.6 collective-permute-start.13
  80.3 5.2 %collective-permute-start.15 = (bf16[160,128]{1,0:T(8,128)(2,1)S(1)}, bf16[160,128]{1,0:T(8,128)(2,1)S(1)}, u32[]{:S(2)}, u32[]{:S(2)}) collective-permute-start(bf16[160,128]{1,0:T(8,128)(2,1)S(1)} %get-tuple-element.95), channel_id=1, source_target_pairs={{0,16},{2,18},{4,20},{6,22},{8,24},{10,26},{12,28},{14,30},{16,0},... | collective-permute-start | bytes 122888 | tf_op jit(solution)/shard_map/ppermute | solution.py:21
  80.4 6.0 %collective-permute-start.14 = (bf16[176,128]{1,0:T(8,128)(2,1)S(1)}, bf16[176,128]{1,0:T(8,128)(2,1)S(1)}, u32[]{:S(2)}, u32[]{:S(2)}) collective-permute-start(bf16[176,128]{1,0:T(8,128)(2,1)S(1)} %get-tuple-element.93), channel_id=1, source_target_pairs={{0,16},{2,18},{4,20},{6,22},{8,24},{10,26},{12,28},{14,30},{16,0},... | collective-permute-start | bytes 135176 | tf_op jit(solution)/shard_map/ppermute | solution.py:21
  85.5 5.6 %collective-permute-start.19 = (bf16[2,160,128]{2,1,0:T(8,128)(2,1)S(1)}, bf16[2,160,128]{2,1,0:T(8,128)(2,1)S(1)}, u32[]{:S(2)}, u32[]{:S(2)}) collective-permute-start(bf16[2,160,128]{2,1,0:T(8,128)(2,1)S(1)} %get-tuple-element.99), channel_id=1, source_target_pairs={{0,8},{2,10},{4,12},{6,14},{8,0},{10,2},{12,4},{14,6},{16,24},{18,... | collective-permute-start | bytes 245768 | tf_op jit(solution)/shard_map/ppermute | solution.py:21
  86.5 4.0 %collective-permute-start.16 = (bf16[128,128]{1,0:T(8,128)(2,1)S(1)}, bf16[128,128]{1,0:T(8,128)(2,1)S(1)}, u32[]{:S(2)}, u32[]{:S(2)}) collective-permute-start(bf16[128,128]{1,0:T(8,128)(2,1)S(1)} %fusion.107), channel_id=1, source_target_pairs={{0,2},{2,0},{4,6},{6,4},{8,10},{10,8},{12,14},{14,12},{16,18},{18,... | collective-permute-start | bytes 98312 | tf_op jit(solution)/shard_map/ppermute | solution.py:21
  88.1 4.6 %collective-permute-start.18 = (bf16[2,176,128]{2,1,0:T(8,128)(2,1)S(1)}, bf16[2,176,128]{2,1,0:T(8,128)(2,1)S(1)}, u32[]{:S(2)}, u32[]{:S(2)}) collective-permute-start(bf16[2,176,128]{2,1,0:T(8,128)(2,1)S(1)} %get-tuple-element.97), channel_id=1, source_target_pairs={{0,8},{2,10},{4,12},{6,14},{8,0},{10,2},{12,4},{14,6},{16,24},{18,... | collective-permute-start | bytes 270344 | tf_op jit(solution)/shard_map/ppermute | solution.py:21
  90.5 5.0 %collective-permute-start.17 = (bf16[2,128,128]{2,1,0:T(8,128)(2,1)S(1)}, bf16[2,128,128]{2,1,0:T(8,128)(2,1)S(1)}, u32[]{:S(2)}, u32[]{:S(2)}) collective-permute-start(bf16[2,128,128]{2,1,0:T(8,128)(2,1)S(1)} %get-tuple-element.102), channel_id=1, source_target_pairs={{0,4},{2,6},{4,0},{6,2},{8,12},{10,14},{12,8},{14,10},{16,20},{18,... | collective-permute-start | bytes 196616 | tf_op jit(solution)/shard_map/ppermute | solution.py:21
  91.1 10.1 %collective-permute-start.26 = (bf16[2,2,160,128]{3,2,1,0:T(8,128)(2,1)S(1)}, bf16[2,2,160,128]{3,2,1,0:T(8,128)(2,1)S(1)}, u32[]{:S(2)}, u32[]{:S(2)}) collective-permute-start(bf16[2,2,160,128]{3,2,1,0:T(8,128)(2,1)S(1)} %get-tuple-element.82), channel_id=1, source_target_pairs={{0,2},{2,0},{4,6},{6,4},{8,10},{10,8},{12,14},{14,12},{16,18},{18,... | collective-permute-start | bytes 491528 | tf_op jit(solution)/shard_map/ppermute | solution.py:21
  92.7 7.3 %collective-permute-start.24 = (bf16[2,2,176,128]{3,2,1,0:T(8,128)(2,1)S(1)}, bf16[2,2,176,128]{3,2,1,0:T(8,128)(2,1)S(1)}, u32[]{:S(2)}, u32[]{:S(2)}) collective-permute-start(bf16[2,2,176,128]{3,2,1,0:T(8,128)(2,1)S(1)} %get-tuple-element.76), channel_id=1, source_target_pairs={{0,4},{2,6},{4,0},{6,2},{8,12},{10,14},{12,8},{14,10},{16,20},{18,... | collective-permute-start | bytes 540680 | tf_op jit(solution)/shard_map/ppermute | solution.py:21
  95.5 7.0 %collective-permute-start.22 = (bf16[2,2,128,128]{3,2,1,0:T(8,128)(2,1)S(1)}, bf16[2,2,128,128]{3,2,1,0:T(8,128)(2,1)S(1)}, u32[]{:S(2)}, u32[]{:S(2)}) collective-permute-start(bf16[2,2,128,128]{3,2,1,0:T(8,128)(2,1)S(1)} %fusion.83), channel_id=1, source_target_pairs={{0,24},{2,26},{4,28},{6,30},{8,16},{10,18},{12,20},{14,22},{16,8},... | collective-permute-start | bytes 393224 | tf_op jit(solution)/shard_map/ppermute | solution.py:21
  97.6 8.8 %collective-permute-start.21 = (bf16[2,2,128,128]{3,2,1,0:T(8,128)(2,1)S(1)}, bf16[2,2,128,128]{3,2,1,0:T(8,128)(2,1)S(1)}, u32[]{:S(2)}, u32[]{:S(2)}) collective-permute-start(bf16[2,2,128,128]{3,2,1,0:T(8,128)(2,1)S(1)} %fusion.83), channel_id=1, source_target_pairs={{0,16},{2,18},{4,20},{6,22},{8,24},{10,26},{12,28},{14,30},{16,0},... | collective-permute-start | bytes 393224 | tf_op jit(solution)/shard_map/ppermute | solution.py:21
  98.3 8.2 %collective-permute-start.20 = (bf16[2,2,128,128]{3,2,1,0:T(8,128)(2,1)S(1)}, bf16[2,2,128,128]{3,2,1,0:T(8,128)(2,1)S(1)}, u32[]{:S(2)}, u32[]{:S(2)}) collective-permute-start(bf16[2,2,128,128]{3,2,1,0:T(8,128)(2,1)S(1)} %fusion.83), channel_id=1, source_target_pairs={{0,8},{2,10},{4,12},{6,14},{8,0},{10,2},{12,4},{14,6},{16,24},{18,... | collective-permute-start | bytes 393224 | tf_op jit(solution)/shard_map/ppermute | solution.py:21
  100.0 7.5 %collective-permute-start.25 = (bf16[2,2,2,176,128]{4,3,2,1,0:T(8,128)(2,1)S(1)}, bf16[2,2,2,176,128]{4,3,2,1,0:T(8,128)(2,1)S(1)}, u32[]{:S(2)}, u32[]{:S(2)}) collective-permute-start(bf16[2,2,2,176,128]{4,3,2,1,0:T(8,128)(2,1)S(1)} %get-tuple-element.66), channel_id=1, source_target_pairs={{0,2},{2,0},{4,6},{6,4},{8,10},{10,8},{12,14},{14,12},{16,18},{18,... | collective-permute-start | bytes 1081352 | tf_op jit(solution)/shard_map/ppermute | solution.py:21
  101.2 7.1 %collective-permute-start.27 = (bf16[2,2,2,160,128]{4,3,2,1,0:T(8,128)(2,1)S(1)}, bf16[2,2,2,160,128]{4,3,2,1,0:T(8,128)(2,1)S(1)}, u32[]{:S(2)}, u32[]{:S(2)}) collective-permute-start(bf16[2,2,2,160,128]{4,3,2,1,0:T(8,128)(2,1)S(1)} %get-tuple-element.72), channel_id=1, source_target_pairs={{0,4},{2,6},{4,0},{6,2},{8,12},{10,14},{12,8},{14,10},{16,20},{18,... | collective-permute-start | bytes 983048 | tf_op jit(solution)/shard_map/ppermute | solution.py:21
  106.6 2.5 collective-permute-start.23
  107.6 3.2 %collective-permute-start.28 = (bf16[16,176,128]{2,1,0:T(8,128)(2,1)S(1)}, bf16[16,176,128]{2,1,0:T(8,128)(2,1)S(1)}, u32[]{:S(2)}, u32[]{:S(2)}) collective-permute-start(bf16[16,176,128]{2,1,0:T(8,128)(2,1)S(1)} %bitcast.326), channel_id=1, source_target_pairs={{0,1},{1,0},{2,3},{3,2},{4,5},{5,4},{6,7},{7,6},{8,9},{9,8},{10,11... | collective-permute-start | bytes 2162696 | tf_op jit(solution)/shard_map/ppermute | solution.py:21
  108.5 2.3 collective-permute-start.29
  128.5 4.5 %collective-permute-start.32 = (f32[4,256]{1,0:T(4,128)S(1)}, f32[4,256]{1,0:T(4,128)S(1)}, u32[]{:S(2)}, u32[]{:S(2)}) collective-permute-start(f32[4,256]{1,0:T(4,128)S(1)} %slice.528), channel_id=1, source_target_pairs={{0,6},{2,4},{4,2},{6,0},{8,14},{10,12},{12,10},{14,8},{16,22},{18,... | collective-permute-start | bytes 12296 | tf_op jit(solution)/shard_map/ppermute | solution.py:21
  129.8 3.6 %collective-permute-start.31 = (f32[4,256]{1,0:T(4,128)S(1)}, f32[4,256]{1,0:T(4,128)S(1)}, u32[]{:S(2)}, u32[]{:S(2)}) collective-permute-start(f32[4,256]{1,0:T(4,128)S(1)} %slice.528), channel_id=1, source_target_pairs={{0,4},{2,6},{4,0},{6,2},{8,12},{10,14},{12,8},{14,10},{16,20},{18,... | collective-permute-start | bytes 12296 | tf_op jit(solution)/shard_map/ppermute | solution.py:21
  131.1 3.6 %collective-permute-start.30 = (f32[4,256]{1,0:T(4,128)S(1)}, f32[4,256]{1,0:T(4,128)S(1)}, u32[]{:S(2)}, u32[]{:S(2)}) collective-permute-start(f32[4,256]{1,0:T(4,128)S(1)} %slice.528), channel_id=1, source_target_pairs={{0,2},{2,0},{4,6},{6,4},{8,10},{10,8},{12,14},{14,12},{16,18},{18,... | collective-permute-start | bytes 12296 | tf_op jit(solution)/shard_map/ppermute | solution.py:21
  134.8 5.8 %collective-permute-start.35 = (f32[4,256]{1,0:T(4,128)S(1)}, f32[4,256]{1,0:T(4,128)S(1)}, u32[]{:S(2)}, u32[]{:S(2)}) collective-permute-start(f32[4,256]{1,0:T(4,128)S(1)} %fusion.123), channel_id=1, source_target_pairs={{0,24},{2,26},{4,28},{6,30},{8,16},{10,18},{12,20},{14,22},{16,8},... | collective-permute-start | bytes 12296 | tf_op jit(solution)/shard_map/ppermute | solution.py:21
  137.4 4.5 %collective-permute-start.34 = (f32[4,256]{1,0:T(4,128)S(1)}, f32[4,256]{1,0:T(4,128)S(1)}, u32[]{:S(2)}, u32[]{:S(2)}) collective-permute-start(f32[4,256]{1,0:T(4,128)S(1)} %fusion.123), channel_id=1, source_target_pairs={{0,16},{2,18},{4,20},{6,22},{8,24},{10,26},{12,28},{14,30},{16,0},... | collective-permute-start | bytes 12296 | tf_op jit(solution)/shard_map/ppermute | solution.py:21
  137.4 4.5 %collective-permute-start.33 = (f32[4,256]{1,0:T(4,128)S(1)}, f32[4,256]{1,0:T(4,128)S(1)}, u32[]{:S(2)}, u32[]{:S(2)}) collective-permute-start(f32[4,256]{1,0:T(4,128)S(1)} %fusion.123), channel_id=1, source_target_pairs={{0,8},{2,10},{4,12},{6,14},{8,0},{10,2},{12,4},{14,6},{16,24},{18,... | collective-permute-start | bytes 12296 | tf_op jit(solution)/shard_map/ppermute | solution.py:21
  160.0 3.9 %collective-permute-start.37 = (bf16[8,2,448,128]{3,2,1,0:T(8,128)(2,1)S(1)}, bf16[8,2,448,128]{3,2,1,0:T(8,128)(2,1)S(1)}, u32[]{:S(2)}, u32[]{:S(2)}) collective-permute-start(bf16[8,2,448,128]{3,2,1,0:T(8,128)(2,1)S(1)} %get-tuple-element.33), channel_id=1, source_target_pairs={{0,1},{1,0},{2,3},{3,2},{4,5},{5,4},{6,7},{7,6},{8,9},{9,8},{10,11... | collective-permute-start | bytes 5505032 | tf_op jit(solution)/shard_map/ppermute | solution.py:21
  164.8 20.8 %collective-permute-start.48 = (bf16[2,2,112,128]{3,2,1,0:T(8,128)(2,1)S(1)}, bf16[2,2,112,128]{3,2,1,0:T(8,128)(2,1)S(1)}, u32[]{:S(2)}, u32[]{:S(2)}) collective-permute-start(bf16[2,2,112,128]{3,2,1,0:T(8,128)(2,1)S(1)} %bitcast.389), channel_id=1, source_target_pairs={{0,24},{2,26},{4,28},{6,30},{8,16},{10,18},{12,20},{14,22},{16,8},... | collective-permute-start | bytes 344072 | tf_op jit(solution)/shard_map/ppermute | solution.py:21
  166.3 19.2 %collective-permute-start.47 = (bf16[2,2,112,128]{3,2,1,0:T(8,128)(2,1)S(1)}, bf16[2,2,112,128]{3,2,1,0:T(8,128)(2,1)S(1)}, u32[]{:S(2)}, u32[]{:S(2)}) collective-permute-start(bf16[2,2,112,128]{3,2,1,0:T(8,128)(2,1)S(1)} %bitcast.388), channel_id=1, source_target_pairs={{0,16},{2,18},{4,20},{6,22},{8,24},{10,26},{12,28},{14,30},{16,0},... | collective-permute-start | bytes 344072 | tf_op jit(solution)/shard_map/ppermute | solution.py:21
  167.3 18.3 %collective-permute-start.46 = (bf16[2,2,112,128]{3,2,1,0:T(8,128)(2,1)S(1)}, bf16[2,2,112,128]{3,2,1,0:T(8,128)(2,1)S(1)}, u32[]{:S(2)}, u32[]{:S(2)}) collective-permute-start(bf16[2,2,112,128]{3,2,1,0:T(8,128)(2,1)S(1)} %bitcast.387), channel_id=1, source_target_pairs={{0,8},{2,10},{4,12},{6,14},{8,0},{10,2},{12,4},{14,6},{16,24},{18,... | collective-permute-start | bytes 344072 | tf_op jit(solution)/shard_map/ppermute | solution.py:21
  169.3 9.0 %collective-permute-start.42 = (bf16[2,2,2,160,128]{4,3,1,0,2:T(8,128)(2,1)S(1)}, bf16[2,2,2,160,128]{4,3,1,0,2:T(8,128)(2,1)S(1)}, u32[]{:S(2)}, u32[]{:S(2)}) collective-permute-start(bf16[2,2,2,160,128]{4,3,1,0,2:T(8,128)(2,1)S(1)} %fusion.52), channel_id=1, source_target_pairs={{0,4},{2,6},{4,0},{6,2},{8,12},{10,14},{12,8},{14,10},{16,20},{18,... | collective-permute-start | bytes 983048 | tf_op jit(solution)/shard_map/ppermute | solution.py:21
  169.9 9.4 %collective-permute-start.38 = (bf16[2,2,2,176,128]{4,3,2,1,0:T(8,128)(2,1)S(1)}, bf16[2,2,2,176,128]{4,3,2,1,0:T(8,128)(2,1)S(1)}, u32[]{:S(2)}, u32[]{:S(2)}) collective-permute-start(bf16[2,2,2,176,128]{4,3,2,1,0:T(8,128)(2,1)S(1)} %fusion.45), channel_id=1, source_target_pairs={{0,2},{2,0},{4,6},{6,4},{8,10},{10,8},{12,14},{14,12},{16,18},{18,... | collective-permute-start | bytes 1081352 | tf_op jit(solution)/shard_map/ppermute | solution.py:21
  178.4 6.7 %collective-permute-start.43 = (bf16[2,2,160,128]{3,2,1,0:T(8,128)(2,1)S(1)}, bf16[2,2,160,128]{3,2,1,0:T(8,128)(2,1)S(1)}, u32[]{:S(2)}, u32[]{:S(2)}) collective-permute-start(bf16[2,2,160,128]{3,2,1,0:T(8,128)(2,1)S(1)} %fusion.79), channel_id=1, source_target_pairs={{0,2},{2,0},{4,6},{6,4},{8,10},{10,8},{12,14},{14,12},{16,18},{18,... | collective-permute-start | bytes 491528 | tf_op jit(solution)/shard_map/ppermute | solution.py:21
  179.5 6.1 %collective-permute-start.39 = (bf16[2,2,176,128]{3,2,1,0:T(8,128)(2,1)S(1)}, bf16[2,2,176,128]{3,2,1,0:T(8,128)(2,1)S(1)}, u32[]{:S(2)}, u32[]{:S(2)}) collective-permute-start(bf16[2,2,176,128]{3,2,1,0:T(8,128)(2,1)S(1)} %fusion.73), channel_id=1, source_target_pairs={{0,4},{2,6},{4,0},{6,2},{8,12},{10,14},{12,8},{14,10},{16,20},{18,... | collective-permute-start | bytes 540680 | tf_op jit(solution)/shard_map/ppermute | solution.py:21
  185.2 4.9 %collective-permute-start.44 = (bf16[2,160,128]{2,1,0:T(8,128)(2,1)S(1)}, bf16[2,160,128]{2,1,0:T(8,128)(2,1)S(1)}, u32[]{:S(2)}, u32[]{:S(2)}) collective-permute-start(bf16[2,160,128]{2,1,0:T(8,128)(2,1)S(1)} %fusion.93), channel_id=1, source_target_pairs={{0,8},{2,10},{4,12},{6,14},{8,0},{10,2},{12,4},{14,6},{16,24},{18,... | collective-permute-start | bytes 245768 | tf_op jit(solution)/shard_map/ppermute | solution.py:21
  185.7 5.3 %collective-permute-start.49 = (bf16[2,112,128]{2,1,0:T(8,128)(2,1)S(1)}, bf16[2,112,128]{2,1,0:T(8,128)(2,1)S(1)}, u32[]{:S(2)}, u32[]{:S(2)}) collective-permute-start(bf16[2,112,128]{2,1,0:T(8,128)(2,1)S(1)} %fusion.98), channel_id=1, source_target_pairs={{0,4},{2,6},{4,0},{6,2},{8,12},{10,14},{12,8},{14,10},{16,20},{18,... | collective-permute-start | bytes 172040 | tf_op jit(solution)/shard_map/ppermute | solution.py:21
  188.4 7.0 %collective-permute-start.40 = (bf16[2,176,128]{2,1,0:T(8,128)(2,1)S(1)}, bf16[2,176,128]{2,1,0:T(8,128)(2,1)S(1)}, u32[]{:S(2)}, u32[]{:S(2)}) collective-permute-start(bf16[2,176,128]{2,1,0:T(8,128)(2,1)S(1)} %fusion.89), channel_id=1, source_target_pairs={{0,8},{2,10},{4,12},{6,14},{8,0},{10,2},{12,4},{14,6},{16,24},{18,... | collective-permute-start | bytes 270344 | tf_op jit(solution)/shard_map/ppermute | solution.py:21
  190.2 5.2 %collective-permute-start.45 = (bf16[160,128]{1,0:T(8,128)(2,1)S(1)}, bf16[160,128]{1,0:T(8,128)(2,1)S(1)}, u32[]{:S(2)}, u32[]{:S(2)}) collective-permute-start(bf16[160,128]{1,0:T(8,128)(2,1)S(1)} %fusion.104), channel_id=1, source_target_pairs={{0,16},{2,18},{4,20},{6,22},{8,24},{10,26},{12,28},{14,30},{16,0},... | collective-permute-start | bytes 122888 | tf_op jit(solution)/shard_map/ppermute | solution.py:21
  191.0 5.1 %collective-permute-start.50 = (bf16[112,128]{1,0:T(8,128)(2,1)S(1)}, bf16[112,128]{1,0:T(8,128)(2,1)S(1)}, u32[]{:S(2)}, u32[]{:S(2)}) collective-permute-start(bf16[112,128]{1,0:T(8,128)(2,1)S(1)} %fusion.112), channel_id=1, source_target_pairs={{0,2},{2,0},{4,6},{6,4},{8,10},{10,8},{12,14},{14,12},{16,18},{18,... | collective-permute-start | bytes 86024 | tf_op jit(solution)/shard_map/ppermute | solution.py:21
  195.4 5.1 %collective-permute-start.41 = (bf16[176,128]{1,0:T(8,128)(2,1)S(1)}, bf16[176,128]{1,0:T(8,128)(2,1)S(1)}, u32[]{:S(2)}, u32[]{:S(2)}) collective-permute-start(bf16[176,128]{1,0:T(8,128)(2,1)S(1)} %fusion.103), channel_id=1, source_target_pairs={{0,16},{2,18},{4,20},{6,22},{8,24},{10,26},{12,28},{14,30},{16,0},... | collective-permute-start | bytes 135176 | tf_op jit(solution)/shard_map/ppermute | solution.py:21
  200.6 1.4 collective-permute-start.51
  207.5 36.1 %collective-permute-start.58 = (bf16[2,2,16,1792]{3,2,1,0:T(8,128)(2,1)S(1)}, bf16[2,2,16,1792]{3,2,1,0:T(8,128)(2,1)S(1)}, u32[]{:S(2)}, u32[]{:S(2)}) collective-permute-start(bf16[2,2,16,1792]{3,2,1,0:T(8,128)(2,1)S(1)} %bitcast.375), channel_id=1, source_target_pairs={{0,24},{2,26},{4,28},{6,30},{8,16},{10,18},{12,20},{14,22},{16,8},... | collective-permute-start | bytes 688136 | tf_op jit(solution)/shard_map/ppermute | solution.py:21
  209.5 34.0 %collective-permute-start.57 = (bf16[2,2,16,1792]{3,2,1,0:T(8,128)(2,1)S(1)}, bf16[2,2,16,1792]{3,2,1,0:T(8,128)(2,1)S(1)}, u32[]{:S(2)}, u32[]{:S(2)}) collective-permute-start(bf16[2,2,16,1792]{3,2,1,0:T(8,128)(2,1)S(1)} %bitcast.374), channel_id=1, source_target_pairs={{0,16},{2,18},{4,20},{6,22},{8,24},{10,26},{12,28},{14,30},{16,0},... | collective-permute-start | bytes 688136 | tf_op jit(solution)/shard_map/ppermute | solution.py:21
  209.5 15.1 %collective-permute-start.53 = (bf16[2,2,16,1792]{3,2,1,0:T(8,128)(2,1)S(1)}, bf16[2,2,16,1792]{3,2,1,0:T(8,128)(2,1)S(1)}, u32[]{:S(2)}, u32[]{:S(2)}) collective-permute-start(bf16[2,2,16,1792]{3,2,1,0:T(8,128)(2,1)S(1)} %bitcast.376), channel_id=1, source_target_pairs={{0,8},{2,10},{4,12},{6,14},{8,0},{10,2},{12,4},{14,6},{16,24},{18,... | collective-permute-start | bytes 688136 | tf_op jit(solution)/shard_map/ppermute | solution.py:21
  212.0 21.3 %collective-permute-start.59 = (bf16[2,2,2,16,2688]{4,3,1,0,2:T(8,128)(2,1)S(1)}, bf16[2,2,2,16,2688]{4,3,1,0,2:T(8,128)(2,1)S(1)}, u32[]{:S(2)}, u32[]{:S(2)}) collective-permute-start(bf16[2,2,2,16,2688]{4,3,1,0,2:T(8,128)(2,1)S(1)} %fusion.36), channel_id=1, source_target_pairs={{0,4},{2,6},{4,0},{6,2},{8,12},{10,14},{12,8},{14,10},{16,20},{18,... | collective-permute-start | bytes 2064392 | tf_op jit(solution)/shard_map/ppermute | solution.py:21
  212.6 21.6 %collective-permute-start.52 = (bf16[2,2,2,16,2688]{4,3,2,1,0:T(8,128)(2,1)S(1)}, bf16[2,2,2,16,2688]{4,3,2,1,0:T(8,128)(2,1)S(1)}, u32[]{:S(2)}, u32[]{:S(2)}) collective-permute-start(bf16[2,2,2,16,2688]{4,3,2,1,0:T(8,128)(2,1)S(1)} %fusion.35), channel_id=1, source_target_pairs={{0,2},{2,0},{4,6},{6,4},{8,10},{10,8},{12,14},{14,12},{16,18},{18,... | collective-permute-start | bytes 2064392 | tf_op jit(solution)/shard_map/ppermute | solution.py:21
  233.5 9.3 %collective-permute-start.60 = (bf16[2,2,16,2688]{3,2,1,0:T(8,128)(2,1)S(1)}, bf16[2,2,16,2688]{3,2,1,0:T(8,128)(2,1)S(1)}, u32[]{:S(2)}, u32[]{:S(2)}) collective-permute-start(bf16[2,2,16,2688]{3,2,1,0:T(8,128)(2,1)S(1)} %fusion.49), channel_id=1, source_target_pairs={{0,2},{2,0},{4,6},{6,4},{8,10},{10,8},{12,14},{14,12},{16,18},{18,... | collective-permute-start | bytes 1032200 | tf_op jit(solution)/shard_map/ppermute | solution.py:21
  234.5 9.1 %collective-permute-start.54 = (bf16[2,2,16,2688]{3,2,1,0:T(8,128)(2,1)S(1)}, bf16[2,2,16,2688]{3,2,1,0:T(8,128)(2,1)S(1)}, u32[]{:S(2)}, u32[]{:S(2)}) collective-permute-start(bf16[2,2,16,2688]{3,2,1,0:T(8,128)(2,1)S(1)} %fusion.48), channel_id=1, source_target_pairs={{0,4},{2,6},{4,0},{6,2},{8,12},{10,14},{12,8},{14,10},{16,20},{18,... | collective-permute-start | bytes 1032200 | tf_op jit(solution)/shard_map/ppermute | solution.py:21
  243.8 4.9 %collective-permute-start.61 = (bf16[2,16,1792]{2,1,0:T(8,128)(2,1)S(1)}, bf16[2,16,1792]{2,1,0:T(8,128)(2,1)S(1)}, u32[]{:S(2)}, u32[]{:S(2)}) collective-permute-start(bf16[2,16,1792]{2,1,0:T(8,128)(2,1)S(1)} %fusion.86), channel_id=1, source_target_pairs={{0,4},{2,6},{4,0},{6,2},{8,12},{10,14},{12,8},{14,10},{16,20},{18,... | collective-permute-start | bytes 344072 | tf_op jit(solution)/shard_map/ppermute | solution.py:21
  244.5 6.8 %collective-permute-start.55 = (bf16[2,16,2688]{2,1,0:T(8,128)(2,1)S(1)}, bf16[2,16,2688]{2,1,0:T(8,128)(2,1)S(1)}, u32[]{:S(2)}, u32[]{:S(2)}) collective-permute-start(bf16[2,16,2688]{2,1,0:T(8,128)(2,1)S(1)} %fusion.75), channel_id=1, source_target_pairs={{0,8},{2,10},{4,12},{6,14},{8,0},{10,2},{12,4},{14,6},{16,24},{18,... | collective-permute-start | bytes 516104 | tf_op jit(solution)/shard_map/ppermute | solution.py:21
  247.1 6.0 %collective-permute-start.63 = (bf16[2,16,2688]{2,1,0:T(8,128)(2,1)S(1)}, bf16[2,16,2688]{2,1,0:T(8,128)(2,1)S(1)}, u32[]{:S(2)}, u32[]{:S(2)}) collective-permute-start(bf16[2,16,2688]{2,1,0:T(8,128)(2,1)S(1)} %fusion.76), channel_id=1, source_target_pairs={{0,8},{2,10},{4,12},{6,14},{8,0},{10,2},{12,4},{14,6},{16,24},{18,... | collective-permute-start | bytes 516104 | tf_op jit(solution)/shard_map/ppermute | solution.py:21
  248.7 7.0 %collective-permute-start.62 = (bf16[16,1792]{1,0:T(8,128)(2,1)S(1)}, bf16[16,1792]{1,0:T(8,128)(2,1)S(1)}, u32[]{:S(2)}, u32[]{:S(2)}) collective-permute-start(bf16[16,1792]{1,0:T(8,128)(2,1)S(1)} %fusion.99), channel_id=1, source_target_pairs={{0,2},{2,0},{4,6},{6,4},{8,10},{10,8},{12,14},{14,12},{16,18},{18,... | collective-permute-start | bytes 172040 | tf_op jit(solution)/shard_map/ppermute | solution.py:21
  253.1 5.5 %collective-permute-start.64 = (bf16[16,2688]{1,0:T(8,128)(2,1)S(1)}, bf16[16,2688]{1,0:T(8,128)(2,1)S(1)}, u32[]{:S(2)}, u32[]{:S(2)}) collective-permute-start(bf16[16,2688]{1,0:T(8,128)(2,1)S(1)} %fusion.92), channel_id=1, source_target_pairs={{0,16},{2,18},{4,20},{6,22},{8,24},{10,26},{12,28},{14,30},{16,0},... | collective-permute-start | bytes 258056 | tf_op jit(solution)/shard_map/ppermute | solution.py:21
  255.7 6.0 %collective-permute-start.56 = (bf16[16,2688]{1,0:T(8,128)(2,1)S(1)}, bf16[16,2688]{1,0:T(8,128)(2,1)S(1)}, u32[]{:S(2)}, u32[]{:S(2)}) collective-permute-start(bf16[16,2688]{1,0:T(8,128)(2,1)S(1)} %fusion.91), channel_id=1, source_target_pairs={{0,16},{2,18},{4,20},{6,22},{8,24},{10,26},{12,28},{14,30},{16,0},... | collective-permute-start | bytes 258056 | tf_op jit(solution)/shard_map/ppermute | solution.py:21
  (19 other events, 157.4 us)

commit v7 on v6

--- a/solution.py
+++ b/solution.py
@@ -38,7 +38,13 @@
     return array.reshape((1 << count,) + array.shape[count:])
 
 
-def gather(first, second, third, last=False):
+def gather_alone(array, order):
+    for bit in order:
+        array = jnp.stack([array, from_partner(array, "seq", 1 << bit)])
+    return in_order(array, order)
+
+
+def gather(first, second, third):
     high = list(reversed(range(2, bits_of("seq"))))
     third_shape = third.shape
     came = []
@@ -56,8 +62,6 @@
     far = range(1, 1 << len(high))
     third = jnp.stack([third] + [from_partner(third, "seq", place << 2) for place in far])
     third = third.reshape((-1,) + third_shape)
-    for block in ends if last else ():
-        third = third + zero_of(block, third_shape)
     return in_order(first, high + [1, 0]), in_order(second, high + [0, 1]), third
 
 
@@ -419,7 +423,10 @@
     facts = jnp.concatenate([facts, gain_parts], axis=1)
     facts = jnp.pad(facts, ((0, 0), (0, 128 - facts.shape[1])))
 
-    first, second, third = gather(first, second, jnp.concatenate([third, facts], axis=1), True)
+    high = list(reversed(range(2, bits_of("seq"))))
+    first = gather_alone(first, high + [1, 0])
+    second = gather_alone(second, high + [0, 1])
+    third = gather_alone(jnp.concatenate([third, facts], axis=1), [0, 1] + high)
     first, second = first.reshape(tokens, main), second.reshape(tokens, main)
     third = third.reshape(tokens, 2 * rest + 128)
 
@@ -515,7 +522,6 @@
     if fits:
         early.append(grad_head_piece(quarter, quarter // 2, True))
     ahead = quarter + quarter // 2
-    behind = vocab_rows // 256 - ahead - quarter
     dfinal, results = scatter([dfinal[:, :one], dfinal[:, one:two], dfinal[:, two:]], early)
     dfinal = jnp.concatenate(dfinal, axis=0)
 
@@ -548,7 +554,11 @@
             back_embed[..., :main],
             jnp.concatenate([back_prev[..., main:], back_embed[..., main:]], axis=-1),
         ],
-        [grad_head_end(ahead, behind), grad_head_end(ahead + behind, quarter)],
+        [
+            grad_head_end(ahead, quarter),
+            grad_head_end(ahead + quarter, quarter),
+            grad_head_end(ahead + 2 * quarter, quarter // 2),
+        ],
     )
     grad_head = ends[-1]
     grad_proj_hidden = grad_proj(first, third[:, :rest], dmixed_prev)

time: 267 us -> 250 us (0.936)
  waiting for transfers between devices: 95 us -> 71.4 us
  starting transfers between devices: 73.4 us -> 80.4 us
    ppermute x65 -> x64, waiting for transfers between devices: 95 us -> 71.4 us  [from_partner(): return lax.ppermute(array, axis, [(i, i ^ mask) for i in range(size)])]
    ppermute x65 -> x64, starting transfers between devices: 73.4 us -> 80.4 us  [from_partner(): return lax.ppermute(array, axis, [(i, i ^ mask) for i in range(size)])]
    pallas_call x4 -> x5, Pallas kernels: 23.7 us -> 24.2 us  [grad_head_rows(): pl.pallas_call(grad_head_kernel, grid=(D // tile, count), in_specs=[pl.Bl...]
  transfers between devices with their start and end apart: 65 -> 64, of which waited for: 40 -> 37; matrix products, arithmetic and copies ran while one was open for 5% -> 5% of each run, Pallas kernels for 9% -> 10%
where the time goes in v7:
time: 250 us
  starting transfers between devices  80.4 us (32%)
  waiting for transfers between devices  71.4 us (29%)
  Pallas kernels  56.7 us (23%)
  other arithmetic  12.9 us (5%)
  matrix products  12.2 us (5%)
  local copies, waits for them, and re-layouts  8.02 us (3%)
  blocking collectives  5.05 us (2%)
  between operations  3.1 us (1%)
    ppermute x64, starting transfers between devices, from_partner(): return lax.ppermute(array, axis, [(i, i ^ mask) for i in range(size)])  80.4 us
    ppermute x64, waiting for transfers between devices, from_partner(): return lax.ppermute(array, axis, [(i, i ^ mask) for i in range(size)])  71.4 us
    pallas_call x5, Pallas kernels, grad_head_rows(): pl.pallas_call(grad_head_kernel, grid=(D // tile, count), in_specs=[pl.Bl...  24.2 us
    pallas_call x1, Pallas kernels, head_back(): pl.pallas_call(dfinal_kernel, grid_spec=pltpu.PrefetchScalarGridSpec(num_...  16.7 us
    pallas_call x1, Pallas kernels, head_logits(): pl.pallas_call(logits_kernel, grid_spec=pltpu.PrefetchScalarGridSpec(num_...  15.9 us
    dot_general x14, matrix products, dot(): lax.dot_general(left, right, (((on_left,), (on_right,)), ((), ())), preci...  12.2 us
    unnamed x36, local copies, waits for them, and re-layouts  5.62 us
  transfers between devices with their start and end apart: 64, of which 37 were waited for; matrix products, arithmetic and copies ran while one was open for 5% of the time, Pallas kernels for 10%

profile of v7, /device:TPU:0, one launch (start us, length us, event | category | flops | bytes accessed | tf_op | source)
XLA Modules:
  0.0 249.9 jit_solution(4630537534069290420)
XLA Ops:
  2.7 2.6 %psum.14 = f32[2,16]{1,0:T(2,128)S(1)} all-reduce(f32[2,16]{1,0:T(2,128)S(1)} %pad_maximum_fusion.30), channel_id=1, replica_groups=mesh['seq'=16,'tp'=2] {'tp'}, use_global_device_ids=true, to_apply=%region_2.0 | all-reduce | flops 32 | bytes 256 | tf_op jit(solution)/shard_map/psum | solution.py:400
  9.0 2.9 %collective-permute-start.4 = (bf16[16,1920]{1,0:T(8,128)(2,1)S(1)}, bf16[16,1920]{1,0:T(8,128)(2,1)S(1)}, u32[]{:S(2)}, u32[]{:S(2)}) collective-permute-start(bf16[16,1920]{1,0:T(8,128)(2,1)S(1)} %get-tuple-element.111), channel_id=1, source_target_pairs={{0,2},{2,0},{4,6},{6,4},{8,10},{10,8},{12,14},{14,12},{16,18},{18,... | collective-permute-start | bytes 184328 | tf_op jit(solution)/shard_map/ppermute | solution.py:21
  11.9 2.6 %collective-permute-start.8 = (bf16[16,2688]{1,0:T(8,128)(2,1)S(1)}, bf16[16,2688]{1,0:T(8,128)(2,1)S(1)}, u32[]{:S(2)}, u32[]{:S(2)}) collective-permute-start(bf16[16,2688]{1,0:T(8,128)(2,1)S(1)} %slice.591), channel_id=1, source_target_pairs={{0,16},{2,18},{4,20},{6,22},{8,24},{10,26},{12,28},{14,30},{16,0},... | collective-permute-start | bytes 258056 | tf_op jit(solution)/shard_map/ppermute | solution.py:21
  15.2 1.6 collective-permute-start.5
  16.7 4.9 %collective-permute-done.8 = bf16[16,2688]{1,0:T(8,128)(2,1)S(1)} collective-permute-done((bf16[16,2688]{1,0:T(8,128)(2,1)S(1)}, bf16[16,2688]{1,0:T(8,128)(2,1)S(1)}, u32[]{:S(2)}, u32[]{:S(2)}) %collective-permute-start.8) | collective-permute-done | bytes 86048 | tf_op jit(solution)/shard_map/ppermute | solution.py:21
  23.9 3.0 %collective-permute-start.6 = (bf16[2,2,16,1920]{3,2,1,0:T(8,128)(2,1)S(1)}, bf16[2,2,16,1920]{3,2,1,0:T(8,128)(2,1)S(1)}, u32[]{:S(2)}, u32[]{:S(2)}) collective-permute-start(bf16[2,2,16,1920]{3,2,1,0:T(8,128)(2,1)S(1)} %get-tuple-element.80), channel_id=1, source_target_pairs={{0,16},{2,18},{4,20},{6,22},{8,24},{10,26},{12,28},{14,30},{16,0},... | collective-permute-start | bytes 737288 | tf_op jit(solution)/shard_map/ppermute | solution.py:21
  26.9 6.8 %collective-permute-done.9 = bf16[2,16,2688]{2,1,0:T(8,128)(2,1)S(1)} collective-permute-done((bf16[2,16,2688]{2,1,0:T(8,128)(2,1)S(1)}, bf16[2,16,2688]{2,1,0:T(8,128)(2,1)S(1)}, u32[]{:S(2)}, u32[]{:S(2)}) %collective-permute-start.9) | collective-permute-done | bytes 172064 | tf_op jit(solution)/shard_map/ppermute | solution.py:21
  35.5 1.6 collective-permute-start.2
  38.7 2.3 collective-permute-done.10
  41.1 1.6 collective-permute-start.11
  42.7 2.8 %collective-permute-done.2 = bf16[2,2,16,2688]{3,2,1,0:T(8,128)(2,1)S(1)} collective-permute-done((bf16[2,2,16,2688]{3,2,1,0:T(8,128)(2,1)S(1)}, bf16[2,2,16,2688]{3,2,1,0:T(8,128)(2,1)S(1)}, u32[]{:S(2)}, u32[]{:S(2)}) %collective-permute-start.2) | collective-permute-done | bytes 344096 | tf_op jit(solution)/shard_map/ppermute | solution.py:21
  45.5 1.5 collective-permute-start.3
  47.0 2.4 collective-permute-done.7
  49.8 1.8 copy-done.2
  53.3 4.5 %collective-permute-done.11 = bf16[2,2,2,16,2688]{4,3,2,1,0:T(8,128)(2,1)S(1)} collective-permute-done((bf16[2,2,2,16,2688]{4,3,2,1,0:T(8,128)(2,1)S(1)}, bf16[2,2,2,16,2688]{4,3,2,1,0:T(8,128)(2,1)S(1)}, u32[]{:S(2)}, u32[]{:S(2)}) %collective-permute-start.11) | collective-permute-done | bytes 688160 | tf_op jit(solution)/shard_map/ppermute | solution.py:21
  62.5 2.8 %collective-permute-start.14 = (bf16[160,128]{1,0:T(8,128)(2,1)S(1)}, bf16[160,128]{1,0:T(8,128)(2,1)S(1)}, u32[]{:S(2)}, u32[]{:S(2)}) collective-permute-start(bf16[160,128]{1,0:T(8,128)(2,1)S(1)} %get-tuple-element.102), channel_id=1, source_target_pairs={{0,16},{2,18},{4,20},{6,22},{8,24},{10,26},{12,28},{14,30},{16,0},... | collective-permute-start | bytes 122888 | tf_op jit(solution)/shard_map/ppermute | solution.py:21
  65.5 2.0 collective-permute-done.14
  67.5 2.5 collective-permute-start.18
  70.9 2.5 %collective-permute-start.17 = (bf16[2,176,128]{2,1,0:T(8,128)(2,1)S(1)}, bf16[2,176,128]{2,1,0:T(8,128)(2,1)S(1)}, u32[]{:S(2)}, u32[]{:S(2)}) collective-permute-start(bf16[2,176,128]{2,1,0:T(8,128)(2,1)S(1)} %get-tuple-element.104), channel_id=1, source_target_pairs={{0,8},{2,10},{4,12},{6,14},{8,0},{10,2},{12,4},{14,6},{16,24},{18,... | collective-permute-start | bytes 270344 | tf_op jit(solution)/shard_map/ppermute | solution.py:21
  74.3 1.6 collective-permute-start.16
  77.6 1.7 collective-permute-done.16
  79.4 3.3 %collective-permute-start.21 = (bf16[2,2,128,128]{3,2,1,0:T(8,128)(2,1)S(1)}, bf16[2,2,128,128]{3,2,1,0:T(8,128)(2,1)S(1)}, u32[]{:S(2)}, u32[]{:S(2)}) collective-permute-start(bf16[2,2,128,128]{3,2,1,0:T(8,128)(2,1)S(1)} %fusion.82), channel_id=1, source_target_pairs={{0,24},{2,26},{4,28},{6,30},{8,16},{10,18},{12,20},{14,22},{16,8},... | collective-permute-start | bytes 393224 | tf_op jit(solution)/shard_map/ppermute | solution.py:21
  84.7 1.6 collective-permute-start.26
  87.3 4.1 %collective-permute-done.20 = bf16[2,2,128,128]{3,2,1,0:T(8,128)(2,1)S(1)} collective-permute-done((bf16[2,2,128,128]{3,2,1,0:T(8,128)(2,1)S(1)}, bf16[2,2,128,128]{3,2,1,0:T(8,128)(2,1)S(1)}, u32[]{:S(2)}, u32[]{:S(2)}) %collective-permute-start.20) | collective-permute-done | bytes 131104 | tf_op jit(solution)/shard_map/ppermute | solution.py:21
  93.5 1.9 collective-permute-done.28.refs_4_
  95.4 15.9 %shard_map.146 = (f32[2048,256]{1,0:T(8,128)S(1)}, f32[8,256]{1,0:T(8,128)S(1)}, bf16[7168,256]{1,0:T(8,128)(2,1)S(1)}) custom-call(s32[2]{0:T(128)S(1)} %pad_add_fusion.1.where, s32[1,256]{1,0:T(1,128)S(1)} %pad_add_fusion.ids, f32[1,256]{1,0:T(1,128)S(1)} %fusion.168.scale, f32[448,16]{1,0:T(8,128)S(1)} %fusion.106.gain, ...), custom_call_target="tpu_custom_call" | custom-call | flops 7516192768 | bytes 36700160 | tf_op jit(solution)/shard_map/pallas_call | solution.py:208
  111.3 1.8 copy-done
  113.1 1.8 collective-permute-start.31
  119.1 2.7 %collective-permute-start.34 = (f32[4,256]{1,0:T(4,128)S(1)}, f32[4,256]{1,0:T(4,128)S(1)}, u32[]{:S(2)}, u32[]{:S(2)}) collective-permute-start(f32[4,256]{1,0:T(4,128)S(1)} %fusion.120), channel_id=1, source_target_pairs={{0,24},{2,26},{4,28},{6,30},{8,16},{10,18},{12,20},{14,22},{16,8},... | collective-permute-start | bytes 12296 | tf_op jit(solution)/shard_map/ppermute | solution.py:21
  121.8 1.7 collective-permute-start.32
  124.9 1.4 collective-permute-done.33
  127.7 16.7 %shard_map.147 = (f32[8,2,448,128]{3,2,1,0:T(8,128)S(1)}, bf16[8,2,448,128]{3,2,1,0:T(8,128)(2,1)S(1)}, bf16[2048,256]{1,0:T(8,128)(2,1)S(1)}) custom-call(s32[2]{0:T(128)S(1)} %pad_add_fusion.1.where, s32[1,256]{1,0:T(1,128)S(1)} %pad_add_fusion.ids, f32[8,256]{1,0:T(8,128)S(1)} %select_maximum_fusion.rows, f32[2048,256]{1,0:T(8,128)S(1)} %get-tuple-element.33.logits, ...), custom_call_target="tpu_custom_call" | custom-call | flops 7516192768 | bytes 36700160 | tf_op jit(solution)/shard_map/pallas_call | solution.py:272
  144.7 3.6 %collective-permute-done.36.refs_0_ = bf16[8,2,448,128]{3,2,1,0:T(8,128)(2,1)S(1)} collective-permute-done((bf16[8,2,448,128]{3,2,1,0:T(8,128)(2,1)S(1)}, bf16[8,2,448,128]{3,2,1,0:T(8,128)(2,1)S(1)}, u32[]{:S(2)}, u32[]{:S(2)}) %collective-permute-start.36) | collective-permute-done | bytes 1835040 | tf_op jit(solution)/shard_map/ppermute | solution.py:21
  149.2 1.5 collective-permute-start.47
  151.6 2.1 collective-permute-start.45
  153.7 1.7 collective-permute-start.41
  155.5 1.8 collective-permute-start.37
  157.3 5.9 %shard_map.148 = (bf16[2048,7168]{1,0:T(8,128)(2,1)}, f32[8,128]{1,0:T(8,128)}) custom-call(bf16[2048,256]{1,0:T(8,128)(2,1)S(1)} %get-tuple-element.36.left, bf16[7168,256]{1,0:T(8,128)(2,1)S(1)} %copy-done.1, bf16[8,2,448,128]{3,2,1,0:T(8,128)(2,1)S(1)} %collective-permute-done.36.refs_0_), custom_call_target="tpu_custom_call" | custom-call | flops 1879048192 | bytes 11010048 | tf_op jit(solution)/shard_map/pallas_call | solution.py:319
  165.2 1.3 collective-permute-start.38
  166.5 3.2 %shard_map.149 = (bf16[2048,7168]{1,0:T(8,128)(2,1)}, f32[2,2,176,128]{3,2,1,0:T(8,128)S(1)}) custom-call(bf16[2048,256]{1,0:T(8,128)(2,1)S(1)} %get-tuple-element.36.left, bf16[7168,256]{1,0:T(8,128)(2,1)S(1)} %copy-done.1, bf16[2,2,2,176,128]{4,3,2,1,0:T(8,128)(2,1)S(1)} %collective-permute-done.37.refs_0_, ...), custom_call_target="tpu_custom_call", output_to_operand_aliasing={{0}: (3, {})} | custom-call | flops 939524096 | bytes 7340032 | tf_op jit(solution)/shard_map/pallas_call | solution.py:319
  170.9 1.3 collective-permute-start.48
  174.3 1.5 collective-permute-start.44
  175.8 2.4 collective-permute-start.49
  178.2 2.2 collective-permute-done.44
  180.8 4.6 %collective-permute-done.40 = bf16[176,128]{1,0:T(8,128)(2,1)S(1)} collective-permute-done((bf16[176,128]{1,0:T(8,128)(2,1)S(1)}, bf16[176,128]{1,0:T(8,128)(2,1)S(1)}, u32[]{:S(2)}, u32[]{:S(2)}) %collective-permute-start.40) | collective-permute-done | bytes 45088 | tf_op jit(solution)/shard_map/ppermute | solution.py:21
  189.2 1.7 copy-done.5
  192.5 1.7 collective-permute-start.57
  194.2 2.7 %collective-permute-start.52 = (bf16[2,2,16,1792]{3,2,1,0:T(8,128)(2,1)S(1)}, bf16[2,2,16,1792]{3,2,1,0:T(8,128)(2,1)S(1)}, u32[]{:S(2)}, u32[]{:S(2)}) collective-permute-start(bf16[2,2,16,1792]{3,2,1,0:T(8,128)(2,1)S(1)} %bitcast.363), channel_id=1, source_target_pairs={{0,8},{2,10},{4,12},{6,14},{8,0},{10,2},{12,4},{14,6},{16,24},{18,... | collective-permute-start | bytes 688136 | tf_op jit(solution)/shard_map/ppermute | solution.py:21
  198.1 1.8 collective-permute-start.51
  199.9 2.7 %convolution_convert_fusion.1 = bf16[3584,448]{0,1:T(8,128)(2,1)} fusion(bf16[448,256]{1,0:T(8,128)(2,1)S(1)} %convolution_convert_fusion.3, bf16[256,896]{1,0:T(8,128)(2,1)S(1)} %get-tuple-element.61, bf16[256,2688]{1,0:T(8,128)(2,1)S(1)} %bitcast.337), kind=kOutput, calls=%fused_computation.1 | convolution fusion | flops 827359232 | bytes 5275648 | tf_op jit(solution)/shard_map/dot_general | solution.py:156
  202.6 2.7 %convolution_convert_fusion = bf16[3584,448]{0,1:T(8,128)(2,1)} fusion(bf16[448,256]{1,0:T(8,128)(2,1)S(1)} %convolution_convert_fusion.2, bf16[256,896]{1,0:T(8,128)(2,1)S(1)} %get-tuple-element.60, bf16[256,2688]{1,0:T(8,128)(2,1)S(1)} %bitcast.335), kind=kOutput, calls=%fused_computation | convolution fusion | flops 827359232 | bytes 5275648 | tf_op jit(solution)/shard_map/dot_general | solution.py:156
  205.3 4.0 %collective-permute-done.52.refs_0_ = bf16[2,2,16,1792]{3,2,1,0:T(8,128)(2,1)S(1)} collective-permute-done((bf16[2,2,16,1792]{3,2,1,0:T(8,128)(2,1)S(1)}, bf16[2,2,16,1792]{3,2,1,0:T(8,128)(2,1)S(1)}, u32[]{:S(2)}, u32[]{:S(2)}) %collective-permute-start.52) | collective-permute-done | bytes 229408 | tf_op jit(solution)/shard_map/ppermute | solution.py:21
  209.3 6.0 %shard_map.150 = (bf16[2048,7168]{1,0:T(8,128)(2,1)}, f32[2,2,2,16,2688]{4,3,2,1,0:T(8,128)S(1)}) custom-call(bf16[2048,256]{1,0:T(8,128)(2,1)S(1)} %get-tuple-element.36.left, bf16[7168,256]{1,0:T(8,128)(2,1)S(1)} %copy-done.1, bf16[2,2,16,1792]{3,2,1,0:T(8,128)(2,1)S(1)} %collective-permute-done.52.refs_0_, ...), custom_call_target="tpu_custom_call", output_to_operand_aliasing={{0}: (3, {})} | custom-call | flops 1879048192 | bytes 11010048 | tf_op jit(solution)/shard_map/pallas_call | solution.py:319
  215.5 1.5 collective-permute-start.59
  218.2 6.0 %shard_map.151 = (bf16[2048,7168]{1,0:T(8,128)(2,1)}, f32[2,2,16,2688]{3,2,1,0:T(8,128)S(1)}) custom-call(bf16[2048,256]{1,0:T(8,128)(2,1)S(1)} %get-tuple-element.36.left, bf16[7168,256]{1,0:T(8,128)(2,1)S(1)} %copy-done.1, bf16[2,2,2,16,2688]{4,3,2,1,0:T(8,128)(2,1)S(1)} %copy.74.refs_0_, ...), custom_call_target="tpu_custom_call", output_to_operand_aliasing={{0}: (3, {})} | custom-call | flops 1879048192 | bytes 11010048 | tf_op jit(solution)/shard_map/pallas_call | solution.py:319
  224.8 1.5 collective-permute-done.53.refs_0_
  227.6 2.5 %collective-permute-start.54 = (bf16[2,16,2688]{2,1,0:T(8,128)(2,1)S(1)}, bf16[2,16,2688]{2,1,0:T(8,128)(2,1)S(1)}, u32[]{:S(2)}, u32[]{:S(2)}) collective-permute-start(bf16[2,16,2688]{2,1,0:T(8,128)(2,1)S(1)} %fusion.74), channel_id=1, source_target_pairs={{0,8},{2,10},{4,12},{6,14},{8,0},{10,2},{12,4},{14,6},{16,24},{18,... | collective-permute-start | bytes 516104 | tf_op jit(solution)/shard_map/ppermute | solution.py:21
  230.3 3.2 %shard_map.152 = (bf16[2048,7168]{1,0:T(8,128)(2,1)}, f32[2,16,2688]{2,1,0:T(8,128)S(1)}) custom-call(bf16[2048,256]{1,0:T(8,128)(2,1)S(1)} %get-tuple-element.36.left, bf16[7168,256]{1,0:T(8,128)(2,1)S(1)} %copy-done.1, bf16[2,2,16,2688]{3,2,1,0:T(8,128)(2,1)S(1)} %collective-permute-done.53.refs_0_, ...), custom_call_target="tpu_custom_call", output_to_operand_aliasing={{0}: (3, {})} | custom-call | flops 939524096 | bytes 7340032 | tf_op jit(solution)/shard_map/pallas_call | solution.py:319
  234.5 1.8 collective-permute-done.62
  236.3 3.4 %collective-permute-start.63 = (bf16[16,2688]{1,0:T(8,128)(2,1)S(1)}, bf16[16,2688]{1,0:T(8,128)(2,1)S(1)}, u32[]{:S(2)}, u32[]{:S(2)}) collective-permute-start(bf16[16,2688]{1,0:T(8,128)(2,1)S(1)} %fusion.91), channel_id=1, source_target_pairs={{0,16},{2,18},{4,20},{6,22},{8,24},{10,26},{12,28},{14,30},{16,0},... | collective-permute-start | bytes 258056 | tf_op jit(solution)/shard_map/ppermute | solution.py:21
  239.7 1.3 collective-permute-start.55
  241.0 2.1 collective-permute-done.63
  243.3 2.4 collective-permute-done.55
  245.9 2.5 psum.15
  (291 shorter events, 53.5 us)
Async XLA Ops:
  9.0 6.1 %collective-permute-start.4 = (bf16[16,1920]{1,0:T(8,128)(2,1)S(1)}, bf16[16,1920]{1,0:T(8,128)(2,1)S(1)}, u32[]{:S(2)}, u32[]{:S(2)}) collective-permute-start(bf16[16,1920]{1,0:T(8,128)(2,1)S(1)} %get-tuple-element.111), channel_id=1, source_target_pairs={{0,2},{2,0},{4,6},{6,4},{8,10},{10,8},{12,14},{14,12},{16,18},{18,... | collective-permute-start | bytes 184328 | tf_op jit(solution)/shard_map/ppermute | solution.py:21
  11.9 9.8 %collective-permute-start.8 = (bf16[16,2688]{1,0:T(8,128)(2,1)S(1)}, bf16[16,2688]{1,0:T(8,128)(2,1)S(1)}, u32[]{:S(2)}, u32[]{:S(2)}) collective-permute-start(bf16[16,2688]{1,0:T(8,128)(2,1)S(1)} %slice.591), channel_id=1, source_target_pairs={{0,16},{2,18},{4,20},{6,22},{8,24},{10,26},{12,28},{14,30},{16,0},... | collective-permute-start | bytes 258056 | tf_op jit(solution)/shard_map/ppermute | solution.py:21
  14.5 8.3 %collective-permute-start = (bf16[16,2688]{1,0:T(8,128)(2,1)S(1)}, bf16[16,2688]{1,0:T(8,128)(2,1)S(1)}, u32[]{:S(2)}, u32[]{:S(2)}) collective-permute-start(bf16[16,2688]{1,0:T(8,128)(2,1)S(1)} %slice.590), channel_id=1, source_target_pairs={{0,16},{2,18},{4,20},{6,22},{8,24},{10,26},{12,28},{14,30},{16,0},... | collective-permute-start | bytes 258056 | tf_op jit(solution)/shard_map/ppermute | solution.py:21
  15.2 8.7 %collective-permute-start.5 = (bf16[2,16,1920]{2,1,0:T(8,128)(2,1)S(1)}, bf16[2,16,1920]{2,1,0:T(8,128)(2,1)S(1)}, u32[]{:S(2)}, u32[]{:S(2)}) collective-permute-start(bf16[2,16,1920]{2,1,0:T(8,128)(2,1)S(1)} %get-tuple-element.96), channel_id=1, source_target_pairs={{0,4},{2,6},{4,0},{6,2},{8,12},{10,14},{12,8},{14,10},{16,20},{18,... | collective-permute-start | bytes 368648 | tf_op jit(solution)/shard_map/ppermute | solution.py:21
  21.7 12.0 %collective-permute-start.9 = (bf16[2,16,2688]{2,1,0:T(8,128)(2,1)S(1)}, bf16[2,16,2688]{2,1,0:T(8,128)(2,1)S(1)}, u32[]{:S(2)}, u32[]{:S(2)}) collective-permute-start(bf16[2,16,2688]{2,1,0:T(8,128)(2,1)S(1)} %get-tuple-element.88), channel_id=1, source_target_pairs={{0,8},{2,10},{4,12},{6,14},{8,0},{10,2},{12,4},{14,6},{16,24},{18,... | collective-permute-start | bytes 516104 | tf_op jit(solution)/shard_map/ppermute | solution.py:21
  22.8 12.7 %collective-permute-start.1 = (bf16[2,16,2688]{2,1,0:T(8,128)(2,1)S(1)}, bf16[2,16,2688]{2,1,0:T(8,128)(2,1)S(1)}, u32[]{:S(2)}, u32[]{:S(2)}) collective-permute-start(bf16[2,16,2688]{2,1,0:T(8,128)(2,1)S(1)} %get-tuple-element.86), channel_id=1, source_target_pairs={{0,8},{2,10},{4,12},{6,14},{8,0},{10,2},{12,4},{14,6},{16,24},{18,... | collective-permute-start | bytes 516104 | tf_op jit(solution)/shard_map/ppermute | solution.py:21
  23.9 14.2 %collective-permute-start.6 = (bf16[2,2,16,1920]{3,2,1,0:T(8,128)(2,1)S(1)}, bf16[2,2,16,1920]{3,2,1,0:T(8,128)(2,1)S(1)}, u32[]{:S(2)}, u32[]{:S(2)}) collective-permute-start(bf16[2,2,16,1920]{3,2,1,0:T(8,128)(2,1)S(1)} %get-tuple-element.80), channel_id=1, source_target_pairs={{0,16},{2,18},{4,20},{6,22},{8,24},{10,26},{12,28},{14,30},{16,0},... | collective-permute-start | bytes 737288 | tf_op jit(solution)/shard_map/ppermute | solution.py:21
  33.7 7.3 %collective-permute-start.10 = (bf16[2,2,16,2688]{3,2,1,0:T(8,128)(2,1)S(1)}, bf16[2,2,16,2688]{3,2,1,0:T(8,128)(2,1)S(1)}, u32[]{:S(2)}, u32[]{:S(2)}) collective-permute-start(bf16[2,2,16,2688]{3,2,1,0:T(8,128)(2,1)S(1)} %get-tuple-element.76), channel_id=1, source_target_pairs={{0,2},{2,0},{4,6},{6,4},{8,10},{10,8},{12,14},{14,12},{16,18},{18,... | collective-permute-start | bytes 1032200 | tf_op jit(solution)/shard_map/ppermute | solution.py:21
  35.5 9.9 %collective-permute-start.2 = (bf16[2,2,16,2688]{3,2,1,0:T(8,128)(2,1)S(1)}, bf16[2,2,16,2688]{3,2,1,0:T(8,128)(2,1)S(1)}, u32[]{:S(2)}, u32[]{:S(2)}) collective-permute-start(bf16[2,2,16,2688]{3,2,1,0:T(8,128)(2,1)S(1)} %get-tuple-element.74), channel_id=1, source_target_pairs={{0,4},{2,6},{4,0},{6,2},{8,12},{10,14},{12,8},{14,10},{16,20},{18,... | collective-permute-start | bytes 1032200 | tf_op jit(solution)/shard_map/ppermute | solution.py:21
  38.1 11.3 %collective-permute-start.7 = (bf16[2,2,2,16,1920]{4,3,2,1,0:T(8,128)(2,1)S(1)}, bf16[2,2,2,16,1920]{4,3,2,1,0:T(8,128)(2,1)S(1)}, u32[]{:S(2)}, u32[]{:S(2)}) collective-permute-start(bf16[2,2,2,16,1920]{4,3,2,1,0:T(8,128)(2,1)S(1)} %get-tuple-element.70), channel_id=1, source_target_pairs={{0,8},{2,10},{4,12},{6,14},{8,0},{10,2},{12,4},{14,6},{16,24},{18,... | collective-permute-start | bytes 1474568 | tf_op jit(solution)/shard_map/ppermute | solution.py:21
  41.1 16.6 %collective-permute-start.11 = (bf16[2,2,2,16,2688]{4,3,2,1,0:T(8,128)(2,1)S(1)}, bf16[2,2,2,16,2688]{4,3,2,1,0:T(8,128)(2,1)S(1)}, u32[]{:S(2)}, u32[]{:S(2)}) collective-permute-start(bf16[2,2,2,16,2688]{4,3,2,1,0:T(8,128)(2,1)S(1)} %get-tuple-element.68), channel_id=1, source_target_pairs={{0,4},{2,6},{4,0},{6,2},{8,12},{10,14},{12,8},{14,10},{16,20},{18,... | collective-permute-start | bytes 2064392 | tf_op jit(solution)/shard_map/ppermute | solution.py:21
  45.5 12.4 %collective-permute-start.3 = (bf16[2,2,2,16,2688]{4,3,2,1,0:T(8,128)(2,1)S(1)}, bf16[2,2,2,16,2688]{4,3,2,1,0:T(8,128)(2,1)S(1)}, u32[]{:S(2)}, u32[]{:S(2)}) collective-permute-start(bf16[2,2,2,16,2688]{4,3,2,1,0:T(8,128)(2,1)S(1)} %get-tuple-element.66), channel_id=1, source_target_pairs={{0,2},{2,0},{4,6},{6,4},{8,10},{10,8},{12,14},{14,12},{16,18},{18,... | collective-permute-start | bytes 2064392 | tf_op jit(solution)/shard_map/ppermute | solution.py:21
  60.8 1.6 collective-permute-start.12
  62.5 5.0 %collective-permute-start.14 = (bf16[160,128]{1,0:T(8,128)(2,1)S(1)}, bf16[160,128]{1,0:T(8,128)(2,1)S(1)}, u32[]{:S(2)}, u32[]{:S(2)}) collective-permute-start(bf16[160,128]{1,0:T(8,128)(2,1)S(1)} %get-tuple-element.102), channel_id=1, source_target_pairs={{0,16},{2,18},{4,20},{6,22},{8,24},{10,26},{12,28},{14,30},{16,0},... | collective-permute-start | bytes 122888 | tf_op jit(solution)/shard_map/ppermute | solution.py:21
  65.3 4.9 %collective-permute-start.13 = (bf16[176,128]{1,0:T(8,128)(2,1)S(1)}, bf16[176,128]{1,0:T(8,128)(2,1)S(1)}, u32[]{:S(2)}, u32[]{:S(2)}) collective-permute-start(bf16[176,128]{1,0:T(8,128)(2,1)S(1)} %get-tuple-element.100), channel_id=1, source_target_pairs={{0,16},{2,18},{4,20},{6,22},{8,24},{10,26},{12,28},{14,30},{16,0},... | collective-permute-start | bytes 135176 | tf_op jit(solution)/shard_map/ppermute | solution.py:21
  67.5 8.4 %collective-permute-start.18 = (bf16[2,160,128]{2,1,0:T(8,128)(2,1)S(1)}, bf16[2,160,128]{2,1,0:T(8,128)(2,1)S(1)}, u32[]{:S(2)}, u32[]{:S(2)}) collective-permute-start(bf16[2,160,128]{2,1,0:T(8,128)(2,1)S(1)} %get-tuple-element.106), channel_id=1, source_target_pairs={{0,8},{2,10},{4,12},{6,14},{8,0},{10,2},{12,4},{14,6},{16,24},{18,... | collective-permute-start | bytes 245768 | tf_op jit(solution)/shard_map/ppermute | solution.py:21
  70.3 4.0 %collective-permute-start.15 = (bf16[128,128]{1,0:T(8,128)(2,1)S(1)}, bf16[128,128]{1,0:T(8,128)(2,1)S(1)}, u32[]{:S(2)}, u32[]{:S(2)}) collective-permute-start(bf16[128,128]{1,0:T(8,128)(2,1)S(1)} %fusion.104), channel_id=1, source_target_pairs={{0,2},{2,0},{4,6},{6,4},{8,10},{10,8},{12,14},{14,12},{16,18},{18,... | collective-permute-start | bytes 98312 | tf_op jit(solution)/shard_map/ppermute | solution.py:21
  70.9 5.7 %collective-permute-start.17 = (bf16[2,176,128]{2,1,0:T(8,128)(2,1)S(1)}, bf16[2,176,128]{2,1,0:T(8,128)(2,1)S(1)}, u32[]{:S(2)}, u32[]{:S(2)}) collective-permute-start(bf16[2,176,128]{2,1,0:T(8,128)(2,1)S(1)} %get-tuple-element.104), channel_id=1, source_target_pairs={{0,8},{2,10},{4,12},{6,14},{8,0},{10,2},{12,4},{14,6},{16,24},{18,... | collective-permute-start | bytes 270344 | tf_op jit(solution)/shard_map/ppermute | solution.py:21
  74.3 5.0 %collective-permute-start.16 = (bf16[2,128,128]{2,1,0:T(8,128)(2,1)S(1)}, bf16[2,128,128]{2,1,0:T(8,128)(2,1)S(1)}, u32[]{:S(2)}, u32[]{:S(2)}) collective-permute-start(bf16[2,128,128]{2,1,0:T(8,128)(2,1)S(1)} %get-tuple-element.109), channel_id=1, source_target_pairs={{0,4},{2,6},{4,0},{6,2},{8,12},{10,14},{12,8},{14,10},{16,20},{18,... | collective-permute-start | bytes 196616 | tf_op jit(solution)/shard_map/ppermute | solution.py:21
  75.9 8.7 %collective-permute-start.25 = (bf16[2,2,160,128]{3,2,1,0:T(8,128)(2,1)S(1)}, bf16[2,2,160,128]{3,2,1,0:T(8,128)(2,1)S(1)}, u32[]{:S(2)}, u32[]{:S(2)}) collective-permute-start(bf16[2,2,160,128]{3,2,1,0:T(8,128)(2,1)S(1)} %get-tuple-element.90), channel_id=1, source_target_pairs={{0,2},{2,0},{4,6},{6,4},{8,10},{10,8},{12,14},{14,12},{16,18},{18,... | collective-permute-start | bytes 491528 | tf_op jit(solution)/shard_map/ppermute | solution.py:21
  76.7 7.1 %collective-permute-start.23 = (bf16[2,2,176,128]{3,2,1,0:T(8,128)(2,1)S(1)}, bf16[2,2,176,128]{3,2,1,0:T(8,128)(2,1)S(1)}, u32[]{:S(2)}, u32[]{:S(2)}) collective-permute-start(bf16[2,2,176,128]{3,2,1,0:T(8,128)(2,1)S(1)} %get-tuple-element.84), channel_id=1, source_target_pairs={{0,4},{2,6},{4,0},{6,2},{8,12},{10,14},{12,8},{14,10},{16,20},{18,... | collective-permute-start | bytes 540680 | tf_op jit(solution)/shard_map/ppermute | solution.py:21
  79.4 7.9 %collective-permute-start.21 = (bf16[2,2,128,128]{3,2,1,0:T(8,128)(2,1)S(1)}, bf16[2,2,128,128]{3,2,1,0:T(8,128)(2,1)S(1)}, u32[]{:S(2)}, u32[]{:S(2)}) collective-permute-start(bf16[2,2,128,128]{3,2,1,0:T(8,128)(2,1)S(1)} %fusion.82), channel_id=1, source_target_pairs={{0,24},{2,26},{4,28},{6,30},{8,16},{10,18},{12,20},{14,22},{16,8},... | collective-permute-start | bytes 393224 | tf_op jit(solution)/shard_map/ppermute | solution.py:21
  82.7 8.7 %collective-permute-start.20 = (bf16[2,2,128,128]{3,2,1,0:T(8,128)(2,1)S(1)}, bf16[2,2,128,128]{3,2,1,0:T(8,128)(2,1)S(1)}, u32[]{:S(2)}, u32[]{:S(2)}) collective-permute-start(bf16[2,2,128,128]{3,2,1,0:T(8,128)(2,1)S(1)} %fusion.82), channel_id=1, source_target_pairs={{0,16},{2,18},{4,20},{6,22},{8,24},{10,26},{12,28},{14,30},{16,0},... | collective-permute-start | bytes 393224 | tf_op jit(solution)/shard_map/ppermute | solution.py:21
  83.1 8.3 %collective-permute-start.19 = (bf16[2,2,128,128]{3,2,1,0:T(8,128)(2,1)S(1)}, bf16[2,2,128,128]{3,2,1,0:T(8,128)(2,1)S(1)}, u32[]{:S(2)}, u32[]{:S(2)}) collective-permute-start(bf16[2,2,128,128]{3,2,1,0:T(8,128)(2,1)S(1)} %fusion.82), channel_id=1, source_target_pairs={{0,8},{2,10},{4,12},{6,14},{8,0},{10,2},{12,4},{14,6},{16,24},{18,... | collective-permute-start | bytes 393224 | tf_op jit(solution)/shard_map/ppermute | solution.py:21
  83.9 7.7 %collective-permute-start.24 = (bf16[2,2,2,176,128]{4,3,2,1,0:T(8,128)(2,1)S(1)}, bf16[2,2,2,176,128]{4,3,2,1,0:T(8,128)(2,1)S(1)}, u32[]{:S(2)}, u32[]{:S(2)}) collective-permute-start(bf16[2,2,2,176,128]{4,3,2,1,0:T(8,128)(2,1)S(1)} %get-tuple-element.72), channel_id=1, source_target_pairs={{0,2},{2,0},{4,6},{6,4},{8,10},{10,8},{12,14},{14,12},{16,18},{18,... | collective-permute-start | bytes 1081352 | tf_op jit(solution)/shard_map/ppermute | solution.py:21
  84.7 7.6 %collective-permute-start.26 = (bf16[2,2,2,160,128]{4,3,2,1,0:T(8,128)(2,1)S(1)}, bf16[2,2,2,160,128]{4,3,2,1,0:T(8,128)(2,1)S(1)}, u32[]{:S(2)}, u32[]{:S(2)}) collective-permute-start(bf16[2,2,2,160,128]{4,3,2,1,0:T(8,128)(2,1)S(1)} %get-tuple-element.78), channel_id=1, source_target_pairs={{0,4},{2,6},{4,0},{6,2},{8,12},{10,14},{12,8},{14,10},{16,20},{18,... | collective-permute-start | bytes 983048 | tf_op jit(solution)/shard_map/ppermute | solution.py:21
  91.5 2.0 collective-permute-start.22
  91.7 3.7 %collective-permute-start.27 = (bf16[16,176,128]{2,1,0:T(8,128)(2,1)S(1)}, bf16[16,176,128]{2,1,0:T(8,128)(2,1)S(1)}, u32[]{:S(2)}, u32[]{:S(2)}) collective-permute-start(bf16[16,176,128]{2,1,0:T(8,128)(2,1)S(1)} %bitcast.316), channel_id=1, source_target_pairs={{0,1},{1,0},{2,3},{3,2},{4,5},{5,4},{6,7},{7,6},{8,9},{9,8},{10,11... | collective-permute-start | bytes 2162696 | tf_op jit(solution)/shard_map/ppermute | solution.py:21
  92.4 3.1 %collective-permute-start.28 = (bf16[16,160,128]{2,1,0:T(8,128)(2,1)S(1)}, bf16[16,160,128]{2,1,0:T(8,128)(2,1)S(1)}, u32[]{:S(2)}, u32[]{:S(2)}) collective-permute-start(bf16[16,160,128]{2,1,0:T(8,128)(2,1)S(1)} %bitcast.318), channel_id=1, source_target_pairs={{0,1},{1,0},{2,3},{3,2},{4,5},{5,4},{6,7},{7,6},{8,9},{9,8},{10,11... | collective-permute-start | bytes 1966088 | tf_op jit(solution)/shard_map/ppermute | solution.py:21
  113.1 4.5 %collective-permute-start.31 = (f32[4,256]{1,0:T(4,128)S(1)}, f32[4,256]{1,0:T(4,128)S(1)}, u32[]{:S(2)}, u32[]{:S(2)}) collective-permute-start(f32[4,256]{1,0:T(4,128)S(1)} %slice.488), channel_id=1, source_target_pairs={{0,6},{2,4},{4,2},{6,0},{8,14},{10,12},{12,10},{14,8},{16,22},{18,... | collective-permute-start | bytes 12296 | tf_op jit(solution)/shard_map/ppermute | solution.py:21
  114.9 3.6 %collective-permute-start.30 = (f32[4,256]{1,0:T(4,128)S(1)}, f32[4,256]{1,0:T(4,128)S(1)}, u32[]{:S(2)}, u32[]{:S(2)}) collective-permute-start(f32[4,256]{1,0:T(4,128)S(1)} %slice.488), channel_id=1, source_target_pairs={{0,4},{2,6},{4,0},{6,2},{8,12},{10,14},{12,8},{14,10},{16,20},{18,... | collective-permute-start | bytes 12296 | tf_op jit(solution)/shard_map/ppermute | solution.py:21
  115.4 3.6 %collective-permute-start.29 = (f32[4,256]{1,0:T(4,128)S(1)}, f32[4,256]{1,0:T(4,128)S(1)}, u32[]{:S(2)}, u32[]{:S(2)}) collective-permute-start(f32[4,256]{1,0:T(4,128)S(1)} %slice.488), channel_id=1, source_target_pairs={{0,2},{2,0},{4,6},{6,4},{8,10},{10,8},{12,14},{14,12},{16,18},{18,... | collective-permute-start | bytes 12296 | tf_op jit(solution)/shard_map/ppermute | solution.py:21
  119.1 5.8 %collective-permute-start.34 = (f32[4,256]{1,0:T(4,128)S(1)}, f32[4,256]{1,0:T(4,128)S(1)}, u32[]{:S(2)}, u32[]{:S(2)}) collective-permute-start(f32[4,256]{1,0:T(4,128)S(1)} %fusion.120), channel_id=1, source_target_pairs={{0,24},{2,26},{4,28},{6,30},{8,16},{10,18},{12,20},{14,22},{16,8},... | collective-permute-start | bytes 12296 | tf_op jit(solution)/shard_map/ppermute | solution.py:21
  121.8 4.5 %collective-permute-start.33 = (f32[4,256]{1,0:T(4,128)S(1)}, f32[4,256]{1,0:T(4,128)S(1)}, u32[]{:S(2)}, u32[]{:S(2)}) collective-permute-start(f32[4,256]{1,0:T(4,128)S(1)} %fusion.120), channel_id=1, source_target_pairs={{0,16},{2,18},{4,20},{6,22},{8,24},{10,26},{12,28},{14,30},{16,0},... | collective-permute-start | bytes 12296 | tf_op jit(solution)/shard_map/ppermute | solution.py:21
  121.8 4.5 %collective-permute-start.32 = (f32[4,256]{1,0:T(4,128)S(1)}, f32[4,256]{1,0:T(4,128)S(1)}, u32[]{:S(2)}, u32[]{:S(2)}) collective-permute-start(f32[4,256]{1,0:T(4,128)S(1)} %fusion.120), channel_id=1, source_target_pairs={{0,8},{2,10},{4,12},{6,14},{8,0},{10,2},{12,4},{14,6},{16,24},{18,... | collective-permute-start | bytes 12296 | tf_op jit(solution)/shard_map/ppermute | solution.py:21
  126.4 1.2 collective-permute-start.35
  144.4 3.9 %collective-permute-start.36 = (bf16[8,2,448,128]{3,2,1,0:T(8,128)(2,1)S(1)}, bf16[8,2,448,128]{3,2,1,0:T(8,128)(2,1)S(1)}, u32[]{:S(2)}, u32[]{:S(2)}) collective-permute-start(bf16[8,2,448,128]{3,2,1,0:T(8,128)(2,1)S(1)} %get-tuple-element.35), channel_id=1, source_target_pairs={{0,1},{1,0},{2,3},{3,2},{4,5},{5,4},{6,7},{7,6},{8,9},{9,8},{10,11... | collective-permute-start | bytes 5505032 | tf_op jit(solution)/shard_map/ppermute | solution.py:21
  149.2 21.5 %collective-permute-start.47 = (bf16[2,2,112,128]{3,2,1,0:T(8,128)(2,1)S(1)}, bf16[2,2,112,128]{3,2,1,0:T(8,128)(2,1)S(1)}, u32[]{:S(2)}, u32[]{:S(2)}) collective-permute-start(bf16[2,2,112,128]{3,2,1,0:T(8,128)(2,1)S(1)} %bitcast.379), channel_id=1, source_target_pairs={{0,24},{2,26},{4,28},{6,30},{8,16},{10,18},{12,20},{14,22},{16,8},... | collective-permute-start | bytes 344072 | tf_op jit(solution)/shard_map/ppermute | solution.py:21
  150.7 20.0 %collective-permute-start.46 = (bf16[2,2,112,128]{3,2,1,0:T(8,128)(2,1)S(1)}, bf16[2,2,112,128]{3,2,1,0:T(8,128)(2,1)S(1)}, u32[]{:S(2)}, u32[]{:S(2)}) collective-permute-start(bf16[2,2,112,128]{3,2,1,0:T(8,128)(2,1)S(1)} %bitcast.378), channel_id=1, source_target_pairs={{0,16},{2,18},{4,20},{6,22},{8,24},{10,26},{12,28},{14,30},{16,0},... | collective-permute-start | bytes 344072 | tf_op jit(solution)/shard_map/ppermute | solution.py:21
  151.6 19.2 %collective-permute-start.45 = (bf16[2,2,112,128]{3,2,1,0:T(8,128)(2,1)S(1)}, bf16[2,2,112,128]{3,2,1,0:T(8,128)(2,1)S(1)}, u32[]{:S(2)}, u32[]{:S(2)}) collective-permute-start(bf16[2,2,112,128]{3,2,1,0:T(8,128)(2,1)S(1)} %bitcast.377), channel_id=1, source_target_pairs={{0,8},{2,10},{4,12},{6,14},{8,0},{10,2},{12,4},{14,6},{16,24},{18,... | collective-permute-start | bytes 344072 | tf_op jit(solution)/shard_map/ppermute | solution.py:21
  153.7 9.5 %collective-permute-start.41 = (bf16[2,2,2,160,128]{4,3,1,0,2:T(8,128)(2,1)S(1)}, bf16[2,2,2,160,128]{4,3,1,0,2:T(8,128)(2,1)S(1)}, u32[]{:S(2)}, u32[]{:S(2)}) collective-permute-start(bf16[2,2,2,160,128]{4,3,1,0,2:T(8,128)(2,1)S(1)} %fusion.53), channel_id=1, source_target_pairs={{0,4},{2,6},{4,0},{6,2},{8,12},{10,14},{12,8},{14,10},{16,20},{18,... | collective-permute-start | bytes 983048 | tf_op jit(solution)/shard_map/ppermute | solution.py:21
  155.5 9.6 %collective-permute-start.37 = (bf16[2,2,2,176,128]{4,3,2,1,0:T(8,128)(2,1)S(1)}, bf16[2,2,2,176,128]{4,3,2,1,0:T(8,128)(2,1)S(1)}, u32[]{:S(2)}, u32[]{:S(2)}) collective-permute-start(bf16[2,2,2,176,128]{4,3,2,1,0:T(8,128)(2,1)S(1)} %fusion.45), channel_id=1, source_target_pairs={{0,2},{2,0},{4,6},{6,4},{8,10},{10,8},{12,14},{14,12},{16,18},{18,... | collective-permute-start | bytes 1081352 | tf_op jit(solution)/shard_map/ppermute | solution.py:21
  163.3 6.3 %collective-permute-start.42 = (bf16[2,2,160,128]{3,2,1,0:T(8,128)(2,1)S(1)}, bf16[2,2,160,128]{3,2,1,0:T(8,128)(2,1)S(1)}, u32[]{:S(2)}, u32[]{:S(2)}) collective-permute-start(bf16[2,2,160,128]{3,2,1,0:T(8,128)(2,1)S(1)} %fusion.78), channel_id=1, source_target_pairs={{0,2},{2,0},{4,6},{6,4},{8,10},{10,8},{12,14},{14,12},{16,18},{18,... | collective-permute-start | bytes 491528 | tf_op jit(solution)/shard_map/ppermute | solution.py:21
  165.2 5.6 %collective-permute-start.38 = (bf16[2,2,176,128]{3,2,1,0:T(8,128)(2,1)S(1)}, bf16[2,2,176,128]{3,2,1,0:T(8,128)(2,1)S(1)}, u32[]{:S(2)}, u32[]{:S(2)}) collective-permute-start(bf16[2,2,176,128]{3,2,1,0:T(8,128)(2,1)S(1)} %fusion.72), channel_id=1, source_target_pairs={{0,4},{2,6},{4,0},{6,2},{8,12},{10,14},{12,8},{14,10},{16,20},{18,... | collective-permute-start | bytes 540680 | tf_op jit(solution)/shard_map/ppermute | solution.py:21
  169.7 4.5 %collective-permute-start.43 = (bf16[2,160,128]{2,1,0:T(8,128)(2,1)S(1)}, bf16[2,160,128]{2,1,0:T(8,128)(2,1)S(1)}, u32[]{:S(2)}, u32[]{:S(2)}) collective-permute-start(bf16[2,160,128]{2,1,0:T(8,128)(2,1)S(1)} %fusion.92), channel_id=1, source_target_pairs={{0,8},{2,10},{4,12},{6,14},{8,0},{10,2},{12,4},{14,6},{16,24},{18,... | collective-permute-start | bytes 245768 | tf_op jit(solution)/shard_map/ppermute | solution.py:21
  170.9 4.9 %collective-permute-start.48 = (bf16[2,112,128]{2,1,0:T(8,128)(2,1)S(1)}, bf16[2,112,128]{2,1,0:T(8,128)(2,1)S(1)}, u32[]{:S(2)}, u32[]{:S(2)}) collective-permute-start(bf16[2,112,128]{2,1,0:T(8,128)(2,1)S(1)} %fusion.95), channel_id=1, source_target_pairs={{0,4},{2,6},{4,0},{6,2},{8,12},{10,14},{12,8},{14,10},{16,20},{18,... | collective-permute-start | bytes 172040 | tf_op jit(solution)/shard_map/ppermute | solution.py:21
  172.3 8.1 %collective-permute-start.39 = (bf16[2,176,128]{2,1,0:T(8,128)(2,1)S(1)}, bf16[2,176,128]{2,1,0:T(8,128)(2,1)S(1)}, u32[]{:S(2)}, u32[]{:S(2)}) collective-permute-start(bf16[2,176,128]{2,1,0:T(8,128)(2,1)S(1)} %fusion.88), channel_id=1, source_target_pairs={{0,8},{2,10},{4,12},{6,14},{8,0},{10,2},{12,4},{14,6},{16,24},{18,... | collective-permute-start | bytes 270344 | tf_op jit(solution)/shard_map/ppermute | solution.py:21
  174.3 6.1 %collective-permute-start.44 = (bf16[160,128]{1,0:T(8,128)(2,1)S(1)}, bf16[160,128]{1,0:T(8,128)(2,1)S(1)}, u32[]{:S(2)}, u32[]{:S(2)}) collective-permute-start(bf16[160,128]{1,0:T(8,128)(2,1)S(1)} %fusion.101), channel_id=1, source_target_pairs={{0,16},{2,18},{4,20},{6,22},{8,24},{10,26},{12,28},{14,30},{16,0},... | collective-permute-start | bytes 122888 | tf_op jit(solution)/shard_map/ppermute | solution.py:21
  175.8 5.0 %collective-permute-start.49 = (bf16[112,128]{1,0:T(8,128)(2,1)S(1)}, bf16[112,128]{1,0:T(8,128)(2,1)S(1)}, u32[]{:S(2)}, u32[]{:S(2)}) collective-permute-start(bf16[112,128]{1,0:T(8,128)(2,1)S(1)} %fusion.109), channel_id=1, source_target_pairs={{0,2},{2,0},{4,6},{6,4},{8,10},{10,8},{12,14},{14,12},{16,18},{18,... | collective-permute-start | bytes 86024 | tf_op jit(solution)/shard_map/ppermute | solution.py:21
  180.4 5.0 %collective-permute-start.40 = (bf16[176,128]{1,0:T(8,128)(2,1)S(1)}, bf16[176,128]{1,0:T(8,128)(2,1)S(1)}, u32[]{:S(2)}, u32[]{:S(2)}) collective-permute-start(bf16[176,128]{1,0:T(8,128)(2,1)S(1)} %fusion.100), channel_id=1, source_target_pairs={{0,16},{2,18},{4,20},{6,22},{8,24},{10,26},{12,28},{14,30},{16,0},... | collective-permute-start | bytes 135176 | tf_op jit(solution)/shard_map/ppermute | solution.py:21
  185.6 1.4 collective-permute-start.50
  192.5 33.9 %collective-permute-start.57 = (bf16[2,2,16,1792]{3,2,1,0:T(8,128)(2,1)S(1)}, bf16[2,2,16,1792]{3,2,1,0:T(8,128)(2,1)S(1)}, u32[]{:S(2)}, u32[]{:S(2)}) collective-permute-start(bf16[2,2,16,1792]{3,2,1,0:T(8,128)(2,1)S(1)} %bitcast.362), channel_id=1, source_target_pairs={{0,24},{2,26},{4,28},{6,30},{8,16},{10,18},{12,20},{14,22},{16,8},... | collective-permute-start | bytes 688136 | tf_op jit(solution)/shard_map/ppermute | solution.py:21
  194.2 32.2 %collective-permute-start.56 = (bf16[2,2,16,1792]{3,2,1,0:T(8,128)(2,1)S(1)}, bf16[2,2,16,1792]{3,2,1,0:T(8,128)(2,1)S(1)}, u32[]{:S(2)}, u32[]{:S(2)}) collective-permute-start(bf16[2,2,16,1792]{3,2,1,0:T(8,128)(2,1)S(1)} %bitcast.361), channel_id=1, source_target_pairs={{0,16},{2,18},{4,20},{6,22},{8,24},{10,26},{12,28},{14,30},{16,0},... | collective-permute-start | bytes 688136 | tf_op jit(solution)/shard_map/ppermute | solution.py:21
  194.2 15.1 %collective-permute-start.52 = (bf16[2,2,16,1792]{3,2,1,0:T(8,128)(2,1)S(1)}, bf16[2,2,16,1792]{3,2,1,0:T(8,128)(2,1)S(1)}, u32[]{:S(2)}, u32[]{:S(2)}) collective-permute-start(bf16[2,2,16,1792]{3,2,1,0:T(8,128)(2,1)S(1)} %bitcast.363), channel_id=1, source_target_pairs={{0,8},{2,10},{4,12},{6,14},{8,0},{10,2},{12,4},{14,6},{16,24},{18,... | collective-permute-start | bytes 688136 | tf_op jit(solution)/shard_map/ppermute | solution.py:21
  197.0 18.3 %collective-permute-start.58 = (bf16[2,2,2,16,2688]{4,3,1,0,2:T(8,128)(2,1)S(1)}, bf16[2,2,2,16,2688]{4,3,1,0,2:T(8,128)(2,1)S(1)}, u32[]{:S(2)}, u32[]{:S(2)}) collective-permute-start(bf16[2,2,2,16,2688]{4,3,1,0,2:T(8,128)(2,1)S(1)} %fusion.36), channel_id=1, source_target_pairs={{0,4},{2,6},{4,0},{6,2},{8,12},{10,14},{12,8},{14,10},{16,20},{18,... | collective-permute-start | bytes 2064392 | tf_op jit(solution)/shard_map/ppermute | solution.py:21
  198.1 18.9 %collective-permute-start.51 = (bf16[2,2,2,16,2688]{4,3,0,1,2:T(8,128)(2,1)S(1)}, bf16[2,2,2,16,2688]{4,3,0,1,2:T(8,128)(2,1)S(1)}, u32[]{:S(2)}, u32[]{:S(2)}) collective-permute-start(bf16[2,2,2,16,2688]{4,3,0,1,2:T(8,128)(2,1)S(1)} %fusion.35), channel_id=1, source_target_pairs={{0,2},{2,0},{4,6},{6,4},{8,10},{10,8},{12,14},{14,12},{16,18},{18,... | collective-permute-start | bytes 2064392 | tf_op jit(solution)/shard_map/ppermute | solution.py:21
  215.5 9.4 %collective-permute-start.59 = (bf16[2,2,16,2688]{3,2,1,0:T(8,128)(2,1)S(1)}, bf16[2,2,16,2688]{3,2,1,0:T(8,128)(2,1)S(1)}, u32[]{:S(2)}, u32[]{:S(2)}) collective-permute-start(bf16[2,2,16,2688]{3,2,1,0:T(8,128)(2,1)S(1)} %fusion.49), channel_id=1, source_target_pairs={{0,2},{2,0},{4,6},{6,4},{8,10},{10,8},{12,14},{14,12},{16,18},{18,... | collective-permute-start | bytes 1032200 | tf_op jit(solution)/shard_map/ppermute | solution.py:21
  217.3 9.1 %collective-permute-start.53 = (bf16[2,2,16,2688]{3,2,1,0:T(8,128)(2,1)S(1)}, bf16[2,2,16,2688]{3,2,1,0:T(8,128)(2,1)S(1)}, u32[]{:S(2)}, u32[]{:S(2)}) collective-permute-start(bf16[2,2,16,2688]{3,2,1,0:T(8,128)(2,1)S(1)} %copy.72), channel_id=1, source_target_pairs={{0,4},{2,6},{4,0},{6,2},{8,12},{10,14},{12,8},{14,10},{16,20},{18,... | collective-permute-start | bytes 1032200 | tf_op jit(solution)/shard_map/ppermute | solution.py:21
  226.6 7.0 %collective-permute-start.60 = (bf16[2,16,1792]{2,1,0:T(8,128)(2,1)S(1)}, bf16[2,16,1792]{2,1,0:T(8,128)(2,1)S(1)}, u32[]{:S(2)}, u32[]{:S(2)}) collective-permute-start(bf16[2,16,1792]{2,1,0:T(8,128)(2,1)S(1)} %fusion.85), channel_id=1, source_target_pairs={{0,4},{2,6},{4,0},{6,2},{8,12},{10,14},{12,8},{14,10},{16,20},{18,... | collective-permute-start | bytes 344072 | tf_op jit(solution)/shard_map/ppermute | solution.py:21
  227.6 6.8 %collective-permute-start.54 = (bf16[2,16,2688]{2,1,0:T(8,128)(2,1)S(1)}, bf16[2,16,2688]{2,1,0:T(8,128)(2,1)S(1)}, u32[]{:S(2)}, u32[]{:S(2)}) collective-permute-start(bf16[2,16,2688]{2,1,0:T(8,128)(2,1)S(1)} %fusion.74), channel_id=1, source_target_pairs={{0,8},{2,10},{4,12},{6,14},{8,0},{10,2},{12,4},{14,6},{16,24},{18,... | collective-permute-start | bytes 516104 | tf_op jit(solution)/shard_map/ppermute | solution.py:21
  230.2 6.0 %collective-permute-start.62 = (bf16[2,16,2688]{2,1,0:T(8,128)(2,1)S(1)}, bf16[2,16,2688]{2,1,0:T(8,128)(2,1)S(1)}, u32[]{:S(2)}, u32[]{:S(2)}) collective-permute-start(bf16[2,16,2688]{2,1,0:T(8,128)(2,1)S(1)} %fusion.75), channel_id=1, source_target_pairs={{0,8},{2,10},{4,12},{6,14},{8,0},{10,2},{12,4},{14,6},{16,24},{18,... | collective-permute-start | bytes 516104 | tf_op jit(solution)/shard_map/ppermute | solution.py:21
  233.6 6.1 %collective-permute-start.61 = (bf16[16,1792]{1,0:T(8,128)(2,1)S(1)}, bf16[16,1792]{1,0:T(8,128)(2,1)S(1)}, u32[]{:S(2)}, u32[]{:S(2)}) collective-permute-start(bf16[16,1792]{1,0:T(8,128)(2,1)S(1)} %fusion.96), channel_id=1, source_target_pairs={{0,2},{2,0},{4,6},{6,4},{8,10},{10,8},{12,14},{14,12},{16,18},{18,... | collective-permute-start | bytes 172040 | tf_op jit(solution)/shard_map/ppermute | solution.py:21
  236.3 6.8 %collective-permute-start.63 = (bf16[16,2688]{1,0:T(8,128)(2,1)S(1)}, bf16[16,2688]{1,0:T(8,128)(2,1)S(1)}, u32[]{:S(2)}, u32[]{:S(2)}) collective-permute-start(bf16[16,2688]{1,0:T(8,128)(2,1)S(1)} %fusion.91), channel_id=1, source_target_pairs={{0,16},{2,18},{4,20},{6,22},{8,24},{10,26},{12,28},{14,30},{16,0},... | collective-permute-start | bytes 258056 | tf_op jit(solution)/shard_map/ppermute | solution.py:21
  239.7 5.9 %collective-permute-start.55 = (bf16[16,2688]{1,0:T(8,128)(2,1)S(1)}, bf16[16,2688]{1,0:T(8,128)(2,1)S(1)}, u32[]{:S(2)}, u32[]{:S(2)}) collective-permute-start(bf16[16,2688]{1,0:T(8,128)(2,1)S(1)} %fusion.90), channel_id=1, source_target_pairs={{0,16},{2,18},{4,20},{6,22},{8,24},{10,26},{12,28},{14,30},{16,0},... | collective-permute-start | bytes 258056 | tf_op jit(solution)/shard_map/ppermute | solution.py:21
  (18 other events, 147.9 us)

commit v8 on v7

--- a/solution.py
+++ b/solution.py
@@ -202,7 +202,7 @@
 
 def head_logits(where, ids, scale, gain, pieces, head):
     vocab, tokens = head.shape[0], ids.shape[1]
-    tile = 512
+    tile = 256
     gain = gain.reshape(pieces[0].shape[0], -1).T
     whole = lambda array: pl.BlockSpec(array.shape, lambda i, w: (0,) * array.ndim)
     return pl.pallas_call(
@@ -424,11 +424,12 @@
     facts = jnp.pad(facts, ((0, 0), (0, 128 - facts.shape[1])))
 
     high = list(reversed(range(2, bits_of("seq"))))
-    first = gather_alone(first, high + [1, 0])
+    first = gather_alone(jnp.concatenate([first, facts], axis=1), high + [1, 0])
     second = gather_alone(second, high + [0, 1])
-    third = gather_alone(jnp.concatenate([third, facts], axis=1), [0, 1] + high)
-    first, second = first.reshape(tokens, main), second.reshape(tokens, main)
-    third = third.reshape(tokens, 2 * rest + 128)
+    third = gather_alone(third, [0, 1] + high)
+    first, second = first.reshape(tokens, main + 128), second.reshape(tokens, main)
+    first, facts_all = first[:, :main], first[:, main:]
+    third = third.reshape(tokens, 2 * rest)
 
     row = lax.broadcasted_iota(i32, (tokens, 1), 0)
     position = (me ^ (row // rows)) * rows + row % rows
@@ -440,7 +441,6 @@
     from_embed = dot(proj_embed[:main], second, 0, 1) + dot(
         proj_embed[main:], third[:, rest : 2 * rest], 0, 1
     )
-    facts_all = third[:, 2 * rest :]
     facts_prev = dot(facts_all, order_prev.astype(bf16), 0, 0)
     partial_value = dot(
         jnp.concatenate([from_prev, from_embed], axis=1),

time: 250 us -> 256 us (1.024)
  starting transfers between devices: 80.4 us -> 75.4 us
  other arithmetic: 12.9 us -> 16.4 us
  local copies, waits for them, and re-layouts: 8.02 us -> 11 us
    ppermute x64, starting transfers between devices: 80.4 us -> 75.4 us  [from_partner(): return lax.ppermute(array, axis, [(i, i ^ mask) for i in range(size)])]
    unnamed x36 -> x66, local copies, waits for them, and re-layouts: 5.62 us -> 8.48 us
  transfers between devices with their start and end apart: 64 -> 64, of which waited for: 37 -> 38; matrix products, arithmetic and copies ran while one was open for 5% -> 6% of each run, Pallas kernels for 10% -> 9%
where the time goes in v8:
time: 256 us; the launch traced here: 255 us
  starting transfers between devices  75.4 us (29%)
  waiting for transfers between devices  73.7 us (29%)
  Pallas kernels  58.5 us (23%)
  other arithmetic  16.4 us (6%)
  matrix products  12.2 us (5%)
  local copies, waits for them, and re-layouts  11 us (4%)
  blocking collectives  5.05 us (2%)
  between operations  3.24 us (1%)
    ppermute x64, starting transfers between devices, from_partner(): return lax.ppermute(array, axis, [(i, i ^ mask) for i in range(size)])  75.4 us
    ppermute x64, waiting for transfers between devices, from_partner(): return lax.ppermute(array, axis, [(i, i ^ mask) for i in range(size)])  73.7 us
    pallas_call x5, Pallas kernels, grad_head_rows(): pl.pallas_call(grad_head_kernel, grid=(D // tile, count), in_specs=[pl.Bl...  24.2 us
    pallas_call x1, Pallas kernels, head_logits(): pl.pallas_call(logits_kernel, grid_spec=pltpu.PrefetchScalarGridSpec(num_...  17.6 us
    pallas_call x1, Pallas kernels, head_back(): pl.pallas_call(dfinal_kernel, grid_spec=pltpu.PrefetchScalarGridSpec(num_...  16.7 us
    dot_general x14, matrix products, dot(): lax.dot_general(left, right, (((on_left,), (on_right,)), ((), ())), preci...  12.2 us
    unnamed x66, local copies, waits for them, and re-layouts  8.48 us
  transfers between devices with their start and end apart: 64, of which 38 were waited for; matrix products, arithmetic and copies ran while one was open for 6% of the time, Pallas kernels for 9%

profile of v8, /device:TPU:0, one launch (start us, length us, event | category | flops | bytes accessed | tf_op | source)
XLA Modules:
  0.0 255.5 jit_solution(12603975506003254329)
XLA Ops:
  2.7 2.6 %psum.14 = f32[2,16]{1,0:T(2,128)S(1)} all-reduce(f32[2,16]{1,0:T(2,128)S(1)} %pad_maximum_fusion.30), channel_id=1, replica_groups=mesh['seq'=16,'tp'=2] {'tp'}, use_global_device_ids=true, to_apply=%region_2.0 | all-reduce | flops 32 | bytes 256 | tf_op jit(solution)/shard_map/psum | solution.py:400
  7.1 2.9 %collective-permute-start.4 = (bf16[16,1792]{1,0:T(8,128)(2,1)S(1)}, bf16[16,1792]{1,0:T(8,128)(2,1)S(1)}, u32[]{:S(2)}, u32[]{:S(2)}) collective-permute-start(bf16[16,1792]{1,0:T(8,128)(2,1)S(1)} %pad_maximum_fusion.22), channel_id=1, source_target_pairs={{0,2},{2,0},{4,6},{6,4},{8,10},{10,8},{12,14},{14,12},{16,18},{18,... | collective-permute-start | bytes 172040 | tf_op jit(solution)/shard_map/ppermute | solution.py:21
  10.0 2.6 %collective-permute-start.8 = (bf16[16,2688]{1,0:T(8,128)(2,1)S(1)}, bf16[16,2688]{1,0:T(8,128)(2,1)S(1)}, u32[]{:S(2)}, u32[]{:S(2)}) collective-permute-start(bf16[16,2688]{1,0:T(8,128)(2,1)S(1)} %slice.595), channel_id=1, source_target_pairs={{0,16},{2,18},{4,20},{6,22},{8,24},{10,26},{12,28},{14,30},{16,0},... | collective-permute-start | bytes 258056 | tf_op jit(solution)/shard_map/ppermute | solution.py:21
  15.8 1.6 collective-permute-start.5
  17.4 2.5 collective-permute-start.9
  19.9 2.3 collective-permute-done
  22.4 2.8 %collective-permute-start.6 = (bf16[2,2,16,1792]{3,2,1,0:T(8,128)(2,1)S(1)}, bf16[2,2,16,1792]{3,2,1,0:T(8,128)(2,1)S(1)}, u32[]{:S(2)}, u32[]{:S(2)}) collective-permute-start(bf16[2,2,16,1792]{3,2,1,0:T(8,128)(2,1)S(1)} %get-tuple-element.82), channel_id=1, source_target_pairs={{0,16},{2,18},{4,20},{6,22},{8,24},{10,26},{12,28},{14,30},{16,0},... | collective-permute-start | bytes 688136 | tf_op jit(solution)/shard_map/ppermute | solution.py:21
  26.4 7.3 %collective-permute-done.1 = bf16[2,16,2816]{2,1,0:T(8,128)(2,1)S(1)} collective-permute-done((bf16[2,16,2816]{2,1,0:T(8,128)(2,1)S(1)}, bf16[2,16,2816]{2,1,0:T(8,128)(2,1)S(1)}, u32[]{:S(2)}, u32[]{:S(2)}) %collective-permute-start.1) | collective-permute-done | bytes 180256 | tf_op jit(solution)/shard_map/ppermute | solution.py:21
  33.7 1.6 collective-permute-start.2
  36.6 1.6 collective-permute-start.11
  38.2 6.9 %collective-permute-done.2 = bf16[2,2,16,2816]{3,2,1,0:T(8,128)(2,1)S(1)} collective-permute-done((bf16[2,2,16,2816]{3,2,1,0:T(8,128)(2,1)S(1)}, bf16[2,2,16,2816]{3,2,1,0:T(8,128)(2,1)S(1)}, u32[]{:S(2)}, u32[]{:S(2)}) %collective-permute-start.2) | collective-permute-done | bytes 360480 | tf_op jit(solution)/shard_map/ppermute | solution.py:21
  46.8 2.1 copy-done.4
  49.3 8.6 %collective-permute-done.11 = bf16[2,2,2,16,2688]{4,3,2,1,0:T(8,128)(2,1)S(1)} collective-permute-done((bf16[2,2,2,16,2688]{4,3,2,1,0:T(8,128)(2,1)S(1)}, bf16[2,2,2,16,2688]{4,3,2,1,0:T(8,128)(2,1)S(1)}, u32[]{:S(2)}, u32[]{:S(2)}) %collective-permute-start.11) | collective-permute-done | bytes 688160 | tf_op jit(solution)/shard_map/ppermute | solution.py:21
  60.2 1.5 copy-done.2
  65.6 2.7 %collective-permute-start.13 = (bf16[176,128]{1,0:T(8,128)(2,1)S(1)}, bf16[176,128]{1,0:T(8,128)(2,1)S(1)}, u32[]{:S(2)}, u32[]{:S(2)}) collective-permute-start(bf16[176,128]{1,0:T(8,128)(2,1)S(1)} %get-tuple-element.98), channel_id=1, source_target_pairs={{0,16},{2,18},{4,20},{6,22},{8,24},{10,26},{12,28},{14,30},{16,0},... | collective-permute-start | bytes 135176 | tf_op jit(solution)/shard_map/ppermute | solution.py:21
  68.3 2.4 collective-permute-done.14
  72.5 1.4 collective-permute-start.17
  73.8 1.9 collective-permute-done.15
  75.7 1.6 collective-permute-start.16
  78.7 2.0 collective-permute-done.16
  80.7 2.1 collective-permute-start.21
  83.6 1.6 collective-permute-start.19
  86.1 1.5 collective-permute-start.26
  87.7 4.1 %collective-permute-done.20 = bf16[2,2,128,128]{3,2,1,0:T(8,128)(2,1)S(1)} collective-permute-done((bf16[2,2,128,128]{3,2,1,0:T(8,128)(2,1)S(1)}, bf16[2,2,128,128]{3,2,1,0:T(8,128)(2,1)S(1)}, u32[]{:S(2)}, u32[]{:S(2)}) %collective-permute-start.20) | collective-permute-done | bytes 131104 | tf_op jit(solution)/shard_map/ppermute | solution.py:21
  94.1 1.9 collective-permute-done.28.refs_4_
  96.1 17.6 %shard_map.146 = (f32[2048,256]{1,0:T(8,128)S(1)}, f32[8,256]{1,0:T(8,128)S(1)}, bf16[7168,256]{1,0:T(8,128)(2,1)S(1)}) custom-call(s32[2]{0:T(128)S(1)} %pad_add_fusion.1.where, s32[1,256]{1,0:T(1,128)S(1)} %pad_add_fusion.ids, f32[1,256]{1,0:T(1,128)S(1)} %fusion.162.scale, f32[448,16]{1,0:T(8,128)S(1)} %fusion.100.gain, ...), custom_call_target="tpu_custom_call" | custom-call | flops 7516192768 | bytes 36700160 | tf_op jit(solution)/shard_map/pallas_call | solution.py:208
  113.7 1.8 copy-done
  115.5 1.8 collective-permute-start.31
  122.6 2.4 collective-permute-start.34
  125.0 2.0 collective-permute-start.32
  132.9 16.7 %shard_map.147 = (f32[8,2,448,128]{3,2,1,0:T(8,128)S(1)}, bf16[8,2,448,128]{3,2,1,0:T(8,128)(2,1)S(1)}, bf16[2048,256]{1,0:T(8,128)(2,1)S(1)}) custom-call(s32[2]{0:T(128)S(1)} %pad_add_fusion.1.where, s32[1,256]{1,0:T(1,128)S(1)} %pad_add_fusion.ids, f32[8,256]{1,0:T(8,128)S(1)} %select_maximum_fusion.rows, f32[2048,256]{1,0:T(8,128)S(1)} %get-tuple-element.33.logits, ...), custom_call_target="tpu_custom_call" | custom-call | flops 7516192768 | bytes 36700160 | tf_op jit(solution)/shard_map/pallas_call | solution.py:272
  149.8 3.6 %collective-permute-done.36.refs_0_ = bf16[8,2,448,128]{3,2,1,0:T(8,128)(2,1)S(1)} collective-permute-done((bf16[8,2,448,128]{3,2,1,0:T(8,128)(2,1)S(1)}, bf16[8,2,448,128]{3,2,1,0:T(8,128)(2,1)S(1)}, u32[]{:S(2)}, u32[]{:S(2)}) %collective-permute-start.36) | collective-permute-done | bytes 1835040 | tf_op jit(solution)/shard_map/ppermute | solution.py:21
  154.5 1.6 collective-permute-start.47
  157.1 1.8 collective-permute-start.45
  160.3 1.3 collective-permute-start.37
  161.6 5.9 %shard_map.148 = (bf16[2048,7168]{1,0:T(8,128)(2,1)}, f32[8,128]{1,0:T(8,128)}) custom-call(bf16[2048,256]{1,0:T(8,128)(2,1)S(1)} %get-tuple-element.36.left, bf16[7168,256]{1,0:T(8,128)(2,1)S(1)} %copy-done.1, bf16[8,2,448,128]{3,2,1,0:T(8,128)(2,1)S(1)} %collective-permute-done.36.refs_0_), custom_call_target="tpu_custom_call" | custom-call | flops 1879048192 | bytes 11010048 | tf_op jit(solution)/shard_map/pallas_call | solution.py:319
  170.8 3.2 %shard_map.149 = (bf16[2048,7168]{1,0:T(8,128)(2,1)}, f32[2,2,176,128]{3,2,1,0:T(8,128)S(1)}) custom-call(bf16[2048,256]{1,0:T(8,128)(2,1)S(1)} %get-tuple-element.36.left, bf16[7168,256]{1,0:T(8,128)(2,1)S(1)} %copy-done.1, bf16[2,2,2,176,128]{4,3,2,1,0:T(8,128)(2,1)S(1)} %collective-permute-done.37.refs_0_, ...), custom_call_target="tpu_custom_call", output_to_operand_aliasing={{0}: (3, {})} | custom-call | flops 939524096 | bytes 7340032 | tf_op jit(solution)/shard_map/pallas_call | solution.py:319
  174.7 1.5 collective-permute-done.38
  176.7 1.4 collective-permute-start.39
  180.6 2.0 collective-permute-start.49
  182.6 2.3 collective-permute-done.44
  185.4 4.6 %collective-permute-done.40 = bf16[176,128]{1,0:T(8,128)(2,1)S(1)} collective-permute-done((bf16[176,128]{1,0:T(8,128)(2,1)S(1)}, bf16[176,128]{1,0:T(8,128)(2,1)S(1)}, u32[]{:S(2)}, u32[]{:S(2)}) %collective-permute-start.40) | collective-permute-done | bytes 45088 | tf_op jit(solution)/shard_map/ppermute | solution.py:21
  193.7 1.7 copy-done.3
  197.0 1.8 collective-permute-start.57
  198.8 2.7 %collective-permute-start.52 = (bf16[2,2,16,1792]{3,2,1,0:T(8,128)(2,1)S(1)}, bf16[2,2,16,1792]{3,2,1,0:T(8,128)(2,1)S(1)}, u32[]{:S(2)}, u32[]{:S(2)}) collective-permute-start(bf16[2,2,16,1792]{3,2,1,0:T(8,128)(2,1)S(1)} %bitcast.361), channel_id=1, source_target_pairs={{0,8},{2,10},{4,12},{6,14},{8,0},{10,2},{12,4},{14,6},{16,24},{18,... | collective-permute-start | bytes 688136 | tf_op jit(solution)/shard_map/ppermute | solution.py:21
  201.6 1.3 collective-permute-start.58
  203.0 1.6 collective-permute-start.51
  204.6 2.7 %convolution_convert_fusion = bf16[3584,448]{0,1:T(8,128)(2,1)} fusion(bf16[448,256]{1,0:T(8,128)(2,1)S(1)} %convolution_convert_fusion.2, bf16[256,896]{1,0:T(8,128)(2,1)S(1)} %get-tuple-element.60, bf16[256,2688]{1,0:T(8,128)(2,1)S(1)} %bitcast.341), kind=kOutput, calls=%fused_computation | convolution fusion | flops 827359232 | bytes 5275648 | tf_op jit(solution)/shard_map/dot_general | solution.py:156
  207.3 2.7 %convolution_convert_fusion.1 = bf16[3584,448]{0,1:T(8,128)(2,1)} fusion(bf16[448,256]{1,0:T(8,128)(2,1)S(1)} %convolution_convert_fusion.3, bf16[256,896]{1,0:T(8,128)(2,1)S(1)} %get-tuple-element.61, bf16[256,2688]{1,0:T(8,128)(2,1)S(1)} %slice.598), kind=kOutput, calls=%fused_computation.1 | convolution fusion | flops 827359232 | bytes 5275648 | tf_op jit(solution)/shard_map/dot_general | solution.py:156
  210.0 4.2 %collective-permute-done.52.refs_0_ = bf16[2,2,16,1792]{3,2,1,0:T(8,128)(2,1)S(1)} collective-permute-done((bf16[2,2,16,1792]{3,2,1,0:T(8,128)(2,1)S(1)}, bf16[2,2,16,1792]{3,2,1,0:T(8,128)(2,1)S(1)}, u32[]{:S(2)}, u32[]{:S(2)}) %collective-permute-start.52) | collective-permute-done | bytes 229408 | tf_op jit(solution)/shard_map/ppermute | solution.py:21
  214.2 6.0 %shard_map.150 = (bf16[2048,7168]{1,0:T(8,128)(2,1)}, f32[2,2,2,16,2688]{4,3,2,1,0:T(8,128)S(1)}) custom-call(bf16[2048,256]{1,0:T(8,128)(2,1)S(1)} %get-tuple-element.36.left, bf16[7168,256]{1,0:T(8,128)(2,1)S(1)} %copy-done.1, bf16[2,2,16,1792]{3,2,1,0:T(8,128)(2,1)S(1)} %collective-permute-done.52.refs_0_, ...), custom_call_target="tpu_custom_call", output_to_operand_aliasing={{0}: (3, {})} | custom-call | flops 1879048192 | bytes 11010048 | tf_op jit(solution)/shard_map/pallas_call | solution.py:319
  220.4 1.4 collective-permute-start.59
  222.0 1.8 collective-permute-start.53
  223.8 6.0 %shard_map.151 = (bf16[2048,7168]{1,0:T(8,128)(2,1)}, f32[2,2,16,2688]{3,2,1,0:T(8,128)S(1)}) custom-call(bf16[2048,256]{1,0:T(8,128)(2,1)S(1)} %get-tuple-element.36.left, bf16[7168,256]{1,0:T(8,128)(2,1)S(1)} %copy-done.1, bf16[2,2,2,16,2688]{4,3,2,1,0:T(8,128)(2,1)S(1)} %copy.74.refs_0_, ...), custom_call_target="tpu_custom_call", output_to_operand_aliasing={{0}: (3, {})} | custom-call | flops 1879048192 | bytes 11010048 | tf_op jit(solution)/shard_map/pallas_call | solution.py:319
  230.1 1.3 collective-permute-done.53.refs_0_
  231.7 1.7 collective-permute-start.60
  233.5 2.5 collective-permute-start.54
  236.2 3.2 %shard_map.152 = (bf16[2048,7168]{1,0:T(8,128)(2,1)}, f32[2,16,2688]{2,1,0:T(8,128)S(1)}) custom-call(bf16[2048,256]{1,0:T(8,128)(2,1)S(1)} %get-tuple-element.36.left, bf16[7168,256]{1,0:T(8,128)(2,1)S(1)} %copy-done.1, bf16[2,2,16,2688]{3,2,1,0:T(8,128)(2,1)S(1)} %collective-permute-done.53.refs_0_, ...), custom_call_target="tpu_custom_call", output_to_operand_aliasing={{0}: (3, {})} | custom-call | flops 939524096 | bytes 7340032 | tf_op jit(solution)/shard_map/pallas_call | solution.py:319
  240.8 1.7 collective-permute-done.62
  242.6 2.3 collective-permute-start.63
  244.9 1.4 collective-permute-start.55
  246.3 2.0 collective-permute-done.63
  248.5 2.8 %collective-permute-done.55 = bf16[16,2688]{1,0:T(8,128)(2,1)S(1)} collective-permute-done((bf16[16,2688]{1,0:T(8,128)(2,1)S(1)}, bf16[16,2688]{1,0:T(8,128)(2,1)S(1)}, u32[]{:S(2)}, u32[]{:S(2)}) %collective-permute-start.55) | collective-permute-done | bytes 86048 | tf_op jit(solution)/shard_map/ppermute | solution.py:21
  251.5 2.5 psum.15
  (322 shorter events, 55.8 us)
Async XLA Ops:
  7.1 8.7 %collective-permute-start.4 = (bf16[16,1792]{1,0:T(8,128)(2,1)S(1)}, bf16[16,1792]{1,0:T(8,128)(2,1)S(1)}, u32[]{:S(2)}, u32[]{:S(2)}) collective-permute-start(bf16[16,1792]{1,0:T(8,128)(2,1)S(1)} %pad_maximum_fusion.22), channel_id=1, source_target_pairs={{0,2},{2,0},{4,6},{6,4},{8,10},{10,8},{12,14},{14,12},{16,18},{18,... | collective-permute-start | bytes 172040 | tf_op jit(solution)/shard_map/ppermute | solution.py:21
  10.0 7.4 %collective-permute-start.8 = (bf16[16,2688]{1,0:T(8,128)(2,1)S(1)}, bf16[16,2688]{1,0:T(8,128)(2,1)S(1)}, u32[]{:S(2)}, u32[]{:S(2)}) collective-permute-start(bf16[16,2688]{1,0:T(8,128)(2,1)S(1)} %slice.595), channel_id=1, source_target_pairs={{0,16},{2,18},{4,20},{6,22},{8,24},{10,26},{12,28},{14,30},{16,0},... | collective-permute-start | bytes 258056 | tf_op jit(solution)/shard_map/ppermute | solution.py:21
  15.1 7.2 %collective-permute-start = (bf16[16,2816]{1,0:T(8,128)(2,1)S(1)}, bf16[16,2816]{1,0:T(8,128)(2,1)S(1)}, u32[]{:S(2)}, u32[]{:S(2)}) collective-permute-start(bf16[16,2816]{1,0:T(8,128)(2,1)S(1)} %get-tuple-element.106), channel_id=1, source_target_pairs={{0,16},{2,18},{4,20},{6,22},{8,24},{10,26},{12,28},{14,30},{16,0},... | collective-permute-start | bytes 270344 | tf_op jit(solution)/shard_map/ppermute | solution.py:21
  15.8 6.5 %collective-permute-start.5 = (bf16[2,16,1792]{2,1,0:T(8,128)(2,1)S(1)}, bf16[2,16,1792]{2,1,0:T(8,128)(2,1)S(1)}, u32[]{:S(2)}, u32[]{:S(2)}) collective-permute-start(bf16[2,16,1792]{2,1,0:T(8,128)(2,1)S(1)} %get-tuple-element.102), channel_id=1, source_target_pairs={{0,4},{2,6},{4,0},{6,2},{8,12},{10,14},{12,8},{14,10},{16,20},{18,... | collective-permute-start | bytes 344072 | tf_op jit(solution)/shard_map/ppermute | solution.py:21
  17.4 8.3 %collective-permute-start.9 = (bf16[2,16,2688]{2,1,0:T(8,128)(2,1)S(1)}, bf16[2,16,2688]{2,1,0:T(8,128)(2,1)S(1)}, u32[]{:S(2)}, u32[]{:S(2)}) collective-permute-start(bf16[2,16,2688]{2,1,0:T(8,128)(2,1)S(1)} %get-tuple-element.88), channel_id=1, source_target_pairs={{0,8},{2,10},{4,12},{6,14},{8,0},{10,2},{12,4},{14,6},{16,24},{18,... | collective-permute-start | bytes 516104 | tf_op jit(solution)/shard_map/ppermute | solution.py:21
  22.3 11.4 %collective-permute-start.1 = (bf16[2,16,2816]{2,1,0:T(8,128)(2,1)S(1)}, bf16[2,16,2816]{2,1,0:T(8,128)(2,1)S(1)}, u32[]{:S(2)}, u32[]{:S(2)}) collective-permute-start(bf16[2,16,2816]{2,1,0:T(8,128)(2,1)S(1)} %get-tuple-element.86), channel_id=1, source_target_pairs={{0,8},{2,10},{4,12},{6,14},{8,0},{10,2},{12,4},{14,6},{16,24},{18,... | collective-permute-start | bytes 540680 | tf_op jit(solution)/shard_map/ppermute | solution.py:21
  22.4 12.9 %collective-permute-start.6 = (bf16[2,2,16,1792]{3,2,1,0:T(8,128)(2,1)S(1)}, bf16[2,2,16,1792]{3,2,1,0:T(8,128)(2,1)S(1)}, u32[]{:S(2)}, u32[]{:S(2)}) collective-permute-start(bf16[2,2,16,1792]{3,2,1,0:T(8,128)(2,1)S(1)} %get-tuple-element.82), channel_id=1, source_target_pairs={{0,16},{2,18},{4,20},{6,22},{8,24},{10,26},{12,28},{14,30},{16,0},... | collective-permute-start | bytes 688136 | tf_op jit(solution)/shard_map/ppermute | solution.py:21
  25.8 10.8 %collective-permute-start.10 = (bf16[2,2,16,2688]{3,2,1,0:T(8,128)(2,1)S(1)}, bf16[2,2,16,2688]{3,2,1,0:T(8,128)(2,1)S(1)}, u32[]{:S(2)}, u32[]{:S(2)}) collective-permute-start(bf16[2,2,16,2688]{3,2,1,0:T(8,128)(2,1)S(1)} %get-tuple-element.76), channel_id=1, source_target_pairs={{0,2},{2,0},{4,6},{6,4},{8,10},{10,8},{12,14},{14,12},{16,18},{18,... | collective-permute-start | bytes 1032200 | tf_op jit(solution)/shard_map/ppermute | solution.py:21
  33.7 11.4 %collective-permute-start.2 = (bf16[2,2,16,2816]{3,2,1,0:T(8,128)(2,1)S(1)}, bf16[2,2,16,2816]{3,2,1,0:T(8,128)(2,1)S(1)}, u32[]{:S(2)}, u32[]{:S(2)}) collective-permute-start(bf16[2,2,16,2816]{3,2,1,0:T(8,128)(2,1)S(1)} %get-tuple-element.74), channel_id=1, source_target_pairs={{0,4},{2,6},{4,0},{6,2},{8,12},{10,14},{12,8},{14,10},{16,20},{18,... | collective-permute-start | bytes 1081352 | tf_op jit(solution)/shard_map/ppermute | solution.py:21
  35.3 11.3 %collective-permute-start.7 = (bf16[2,2,2,16,1792]{4,3,2,1,0:T(8,128)(2,1)S(1)}, bf16[2,2,2,16,1792]{4,3,2,1,0:T(8,128)(2,1)S(1)}, u32[]{:S(2)}, u32[]{:S(2)}) collective-permute-start(bf16[2,2,2,16,1792]{4,3,2,1,0:T(8,128)(2,1)S(1)} %get-tuple-element.70), channel_id=1, source_target_pairs={{0,8},{2,10},{4,12},{6,14},{8,0},{10,2},{12,4},{14,6},{16,24},{18,... | collective-permute-start | bytes 1376264 | tf_op jit(solution)/shard_map/ppermute | solution.py:21
  36.6 21.3 %collective-permute-start.11 = (bf16[2,2,2,16,2688]{4,3,2,1,0:T(8,128)(2,1)S(1)}, bf16[2,2,2,16,2688]{4,3,2,1,0:T(8,128)(2,1)S(1)}, u32[]{:S(2)}, u32[]{:S(2)}) collective-permute-start(bf16[2,2,2,16,2688]{4,3,2,1,0:T(8,128)(2,1)S(1)} %get-tuple-element.68), channel_id=1, source_target_pairs={{0,4},{2,6},{4,0},{6,2},{8,12},{10,14},{12,8},{14,10},{16,20},{18,... | collective-permute-start | bytes 2064392 | tf_op jit(solution)/shard_map/ppermute | solution.py:21
  45.2 14.3 %collective-permute-start.3 = (bf16[2,2,2,16,2816]{4,3,2,1,0:T(8,128)(2,1)S(1)}, bf16[2,2,2,16,2816]{4,3,2,1,0:T(8,128)(2,1)S(1)}, u32[]{:S(2)}, u32[]{:S(2)}) collective-permute-start(bf16[2,2,2,16,2816]{4,3,2,1,0:T(8,128)(2,1)S(1)} %get-tuple-element.66), channel_id=1, source_target_pairs={{0,2},{2,0},{4,6},{6,4},{8,10},{10,8},{12,14},{14,12},{16,18},{18,... | collective-permute-start | bytes 2162696 | tf_op jit(solution)/shard_map/ppermute | solution.py:21
  63.6 1.6 collective-permute-start.12
  65.3 5.4 %collective-permute-start.14 = (bf16[160,128]{1,0:T(8,128)(2,1)S(1)}, bf16[160,128]{1,0:T(8,128)(2,1)S(1)}, u32[]{:S(2)}, u32[]{:S(2)}) collective-permute-start(bf16[160,128]{1,0:T(8,128)(2,1)S(1)} %get-tuple-element.100), channel_id=1, source_target_pairs={{0,16},{2,18},{4,20},{6,22},{8,24},{10,26},{12,28},{14,30},{16,0},... | collective-permute-start | bytes 122888 | tf_op jit(solution)/shard_map/ppermute | solution.py:21
  65.6 6.2 %collective-permute-start.13 = (bf16[176,128]{1,0:T(8,128)(2,1)S(1)}, bf16[176,128]{1,0:T(8,128)(2,1)S(1)}, u32[]{:S(2)}, u32[]{:S(2)}) collective-permute-start(bf16[176,128]{1,0:T(8,128)(2,1)S(1)} %get-tuple-element.98), channel_id=1, source_target_pairs={{0,16},{2,18},{4,20},{6,22},{8,24},{10,26},{12,28},{14,30},{16,0},... | collective-permute-start | bytes 135176 | tf_op jit(solution)/shard_map/ppermute | solution.py:21
  70.7 6.7 %collective-permute-start.18 = (bf16[2,160,128]{2,1,0:T(8,128)(2,1)S(1)}, bf16[2,160,128]{2,1,0:T(8,128)(2,1)S(1)}, u32[]{:S(2)}, u32[]{:S(2)}) collective-permute-start(bf16[2,160,128]{2,1,0:T(8,128)(2,1)S(1)} %get-tuple-element.108), channel_id=1, source_target_pairs={{0,8},{2,10},{4,12},{6,14},{8,0},{10,2},{12,4},{14,6},{16,24},{18,... | collective-permute-start | bytes 245768 | tf_op jit(solution)/shard_map/ppermute | solution.py:21
  71.7 4.0 %collective-permute-start.15 = (bf16[128,128]{1,0:T(8,128)(2,1)S(1)}, bf16[128,128]{1,0:T(8,128)(2,1)S(1)}, u32[]{:S(2)}, u32[]{:S(2)}) collective-permute-start(bf16[128,128]{1,0:T(8,128)(2,1)S(1)} %fusion.98), channel_id=1, source_target_pairs={{0,2},{2,0},{4,6},{6,4},{8,10},{10,8},{12,14},{14,12},{16,18},{18,... | collective-permute-start | bytes 98312 | tf_op jit(solution)/shard_map/ppermute | solution.py:21
  72.5 5.5 %collective-permute-start.17 = (bf16[2,176,128]{2,1,0:T(8,128)(2,1)S(1)}, bf16[2,176,128]{2,1,0:T(8,128)(2,1)S(1)}, u32[]{:S(2)}, u32[]{:S(2)}) collective-permute-start(bf16[2,176,128]{2,1,0:T(8,128)(2,1)S(1)} %get-tuple-element.104), channel_id=1, source_target_pairs={{0,8},{2,10},{4,12},{6,14},{8,0},{10,2},{12,4},{14,6},{16,24},{18,... | collective-permute-start | bytes 270344 | tf_op jit(solution)/shard_map/ppermute | solution.py:21
  75.7 5.0 %collective-permute-start.16 = (bf16[2,128,128]{2,1,0:T(8,128)(2,1)S(1)}, bf16[2,128,128]{2,1,0:T(8,128)(2,1)S(1)}, u32[]{:S(2)}, u32[]{:S(2)}) collective-permute-start(bf16[2,128,128]{2,1,0:T(8,128)(2,1)S(1)} %get-tuple-element.111), channel_id=1, source_target_pairs={{0,4},{2,6},{4,0},{6,2},{8,12},{10,14},{12,8},{14,10},{16,20},{18,... | collective-permute-start | bytes 196616 | tf_op jit(solution)/shard_map/ppermute | solution.py:21
  77.4 8.7 %collective-permute-start.25 = (bf16[2,2,160,128]{3,2,1,0:T(8,128)(2,1)S(1)}, bf16[2,2,160,128]{3,2,1,0:T(8,128)(2,1)S(1)}, u32[]{:S(2)}, u32[]{:S(2)}) collective-permute-start(bf16[2,2,160,128]{3,2,1,0:T(8,128)(2,1)S(1)} %get-tuple-element.90), channel_id=1, source_target_pairs={{0,2},{2,0},{4,6},{6,4},{8,10},{10,8},{12,14},{14,12},{16,18},{18,... | collective-permute-start | bytes 491528 | tf_op jit(solution)/shard_map/ppermute | solution.py:21
  78.0 7.2 %collective-permute-start.23 = (bf16[2,2,176,128]{3,2,1,0:T(8,128)(2,1)S(1)}, bf16[2,2,176,128]{3,2,1,0:T(8,128)(2,1)S(1)}, u32[]{:S(2)}, u32[]{:S(2)}) collective-permute-start(bf16[2,2,176,128]{3,2,1,0:T(8,128)(2,1)S(1)} %get-tuple-element.84), channel_id=1, source_target_pairs={{0,4},{2,6},{4,0},{6,2},{8,12},{10,14},{12,8},{14,10},{16,20},{18,... | collective-permute-start | bytes 540680 | tf_op jit(solution)/shard_map/ppermute | solution.py:21
  80.7 7.0 %collective-permute-start.21 = (bf16[2,2,128,128]{3,2,1,0:T(8,128)(2,1)S(1)}, bf16[2,2,128,128]{3,2,1,0:T(8,128)(2,1)S(1)}, u32[]{:S(2)}, u32[]{:S(2)}) collective-permute-start(bf16[2,2,128,128]{3,2,1,0:T(8,128)(2,1)S(1)} %fusion.76), channel_id=1, source_target_pairs={{0,24},{2,26},{4,28},{6,30},{8,16},{10,18},{12,20},{14,22},{16,8},... | collective-permute-start | bytes 393224 | tf_op jit(solution)/shard_map/ppermute | solution.py:21
  82.8 9.0 %collective-permute-start.20 = (bf16[2,2,128,128]{3,2,1,0:T(8,128)(2,1)S(1)}, bf16[2,2,128,128]{3,2,1,0:T(8,128)(2,1)S(1)}, u32[]{:S(2)}, u32[]{:S(2)}) collective-permute-start(bf16[2,2,128,128]{3,2,1,0:T(8,128)(2,1)S(1)} %fusion.76), channel_id=1, source_target_pairs={{0,16},{2,18},{4,20},{6,22},{8,24},{10,26},{12,28},{14,30},{16,0},... | collective-permute-start | bytes 393224 | tf_op jit(solution)/shard_map/ppermute | solution.py:21
  83.6 8.3 %collective-permute-start.19 = (bf16[2,2,128,128]{3,2,1,0:T(8,128)(2,1)S(1)}, bf16[2,2,128,128]{3,2,1,0:T(8,128)(2,1)S(1)}, u32[]{:S(2)}, u32[]{:S(2)}) collective-permute-start(bf16[2,2,128,128]{3,2,1,0:T(8,128)(2,1)S(1)} %fusion.76), channel_id=1, source_target_pairs={{0,8},{2,10},{4,12},{6,14},{8,0},{10,2},{12,4},{14,6},{16,24},{18,... | collective-permute-start | bytes 393224 | tf_op jit(solution)/shard_map/ppermute | solution.py:21
  85.3 7.5 %collective-permute-start.24 = (bf16[2,2,2,176,128]{4,3,2,1,0:T(8,128)(2,1)S(1)}, bf16[2,2,2,176,128]{4,3,2,1,0:T(8,128)(2,1)S(1)}, u32[]{:S(2)}, u32[]{:S(2)}) collective-permute-start(bf16[2,2,2,176,128]{4,3,2,1,0:T(8,128)(2,1)S(1)} %get-tuple-element.72), channel_id=1, source_target_pairs={{0,2},{2,0},{4,6},{6,4},{8,10},{10,8},{12,14},{14,12},{16,18},{18,... | collective-permute-start | bytes 1081352 | tf_op jit(solution)/shard_map/ppermute | solution.py:21
  86.1 7.1 %collective-permute-start.26 = (bf16[2,2,2,160,128]{4,3,2,1,0:T(8,128)(2,1)S(1)}, bf16[2,2,2,160,128]{4,3,2,1,0:T(8,128)(2,1)S(1)}, u32[]{:S(2)}, u32[]{:S(2)}) collective-permute-start(bf16[2,2,2,160,128]{4,3,2,1,0:T(8,128)(2,1)S(1)} %get-tuple-element.78), channel_id=1, source_target_pairs={{0,4},{2,6},{4,0},{6,2},{8,12},{10,14},{12,8},{14,10},{16,20},{18,... | collective-permute-start | bytes 983048 | tf_op jit(solution)/shard_map/ppermute | solution.py:21
  91.9 2.1 collective-permute-start.22
  92.9 3.2 %collective-permute-start.27 = (bf16[16,176,128]{2,1,0:T(8,128)(2,1)S(1)}, bf16[16,176,128]{2,1,0:T(8,128)(2,1)S(1)}, u32[]{:S(2)}, u32[]{:S(2)}) collective-permute-start(bf16[16,176,128]{2,1,0:T(8,128)(2,1)S(1)} %bitcast.315), channel_id=1, source_target_pairs={{0,1},{1,0},{2,3},{3,2},{4,5},{5,4},{6,7},{7,6},{8,9},{9,8},{10,11... | collective-permute-start | bytes 2162696 | tf_op jit(solution)/shard_map/ppermute | solution.py:21
  93.3 2.7 %collective-permute-start.28 = (bf16[16,160,128]{2,1,0:T(8,128)(2,1)S(1)}, bf16[16,160,128]{2,1,0:T(8,128)(2,1)S(1)}, u32[]{:S(2)}, u32[]{:S(2)}) collective-permute-start(bf16[16,160,128]{2,1,0:T(8,128)(2,1)S(1)} %bitcast.317), channel_id=1, source_target_pairs={{0,1},{1,0},{2,3},{3,2},{4,5},{5,4},{6,7},{7,6},{8,9},{9,8},{10,11... | collective-permute-start | bytes 1966088 | tf_op jit(solution)/shard_map/ppermute | solution.py:21
  115.5 4.5 %collective-permute-start.31 = (f32[4,256]{1,0:T(4,128)S(1)}, f32[4,256]{1,0:T(4,128)S(1)}, u32[]{:S(2)}, u32[]{:S(2)}) collective-permute-start(f32[4,256]{1,0:T(4,128)S(1)} %slice.492), channel_id=1, source_target_pairs={{0,6},{2,4},{4,2},{6,0},{8,14},{10,12},{12,10},{14,8},{16,22},{18,... | collective-permute-start | bytes 12296 | tf_op jit(solution)/shard_map/ppermute | solution.py:21
  117.3 3.6 %collective-permute-start.30 = (f32[4,256]{1,0:T(4,128)S(1)}, f32[4,256]{1,0:T(4,128)S(1)}, u32[]{:S(2)}, u32[]{:S(2)}) collective-permute-start(f32[4,256]{1,0:T(4,128)S(1)} %slice.492), channel_id=1, source_target_pairs={{0,4},{2,6},{4,0},{6,2},{8,12},{10,14},{12,8},{14,10},{16,20},{18,... | collective-permute-start | bytes 12296 | tf_op jit(solution)/shard_map/ppermute | solution.py:21
  117.8 3.6 %collective-permute-start.29 = (f32[4,256]{1,0:T(4,128)S(1)}, f32[4,256]{1,0:T(4,128)S(1)}, u32[]{:S(2)}, u32[]{:S(2)}) collective-permute-start(f32[4,256]{1,0:T(4,128)S(1)} %slice.492), channel_id=1, source_target_pairs={{0,2},{2,0},{4,6},{6,4},{8,10},{10,8},{12,14},{14,12},{16,18},{18,... | collective-permute-start | bytes 12296 | tf_op jit(solution)/shard_map/ppermute | solution.py:21
  122.6 6.3 %collective-permute-start.34 = (f32[4,256]{1,0:T(4,128)}, f32[4,256]{1,0:T(4,128)}, u32[]{:S(2)}, u32[]{:S(2)}) collective-permute-start(f32[4,256]{1,0:T(4,128)} %fusion.114), channel_id=1, source_target_pairs={{0,24},{2,26},{4,28},{6,30},{8,16},{10,18},{12,20},{14,22},{16,8},... | collective-permute-start | bytes 12296 | tf_op jit(solution)/shard_map/ppermute | solution.py:21
  125.0 4.8 %collective-permute-start.33 = (f32[4,256]{1,0:T(4,128)}, f32[4,256]{1,0:T(4,128)}, u32[]{:S(2)}, u32[]{:S(2)}) collective-permute-start(f32[4,256]{1,0:T(4,128)} %fusion.114), channel_id=1, source_target_pairs={{0,16},{2,18},{4,20},{6,22},{8,24},{10,26},{12,28},{14,30},{16,0},... | collective-permute-start | bytes 12296 | tf_op jit(solution)/shard_map/ppermute | solution.py:21
  125.0 4.8 %collective-permute-start.32 = (f32[4,256]{1,0:T(4,128)}, f32[4,256]{1,0:T(4,128)}, u32[]{:S(2)}, u32[]{:S(2)}) collective-permute-start(f32[4,256]{1,0:T(4,128)} %fusion.114), channel_id=1, source_target_pairs={{0,8},{2,10},{4,12},{6,14},{8,0},{10,2},{12,4},{14,6},{16,24},{18,... | collective-permute-start | bytes 12296 | tf_op jit(solution)/shard_map/ppermute | solution.py:21
  131.5 1.2 collective-permute-start.35
  149.5 3.9 %collective-permute-start.36 = (bf16[8,2,448,128]{3,2,1,0:T(8,128)(2,1)S(1)}, bf16[8,2,448,128]{3,2,1,0:T(8,128)(2,1)S(1)}, u32[]{:S(2)}, u32[]{:S(2)}) collective-permute-start(bf16[8,2,448,128]{3,2,1,0:T(8,128)(2,1)S(1)} %get-tuple-element.35), channel_id=1, source_target_pairs={{0,1},{1,0},{2,3},{3,2},{4,5},{5,4},{6,7},{7,6},{8,9},{9,8},{10,11... | collective-permute-start | bytes 5505032 | tf_op jit(solution)/shard_map/ppermute | solution.py:21
  154.5 21.7 %collective-permute-start.47 = (bf16[2,2,112,128]{3,2,1,0:T(8,128)(2,1)S(1)}, bf16[2,2,112,128]{3,2,1,0:T(8,128)(2,1)S(1)}, u32[]{:S(2)}, u32[]{:S(2)}) collective-permute-start(bf16[2,2,112,128]{3,2,1,0:T(8,128)(2,1)S(1)} %bitcast.377), channel_id=1, source_target_pairs={{0,24},{2,26},{4,28},{6,30},{8,16},{10,18},{12,20},{14,22},{16,8},... | collective-permute-start | bytes 344072 | tf_op jit(solution)/shard_map/ppermute | solution.py:21
  156.1 20.2 %collective-permute-start.46 = (bf16[2,2,112,128]{3,2,1,0:T(8,128)(2,1)S(1)}, bf16[2,2,112,128]{3,2,1,0:T(8,128)(2,1)S(1)}, u32[]{:S(2)}, u32[]{:S(2)}) collective-permute-start(bf16[2,2,112,128]{3,2,1,0:T(8,128)(2,1)S(1)} %bitcast.376), channel_id=1, source_target_pairs={{0,16},{2,18},{4,20},{6,22},{8,24},{10,26},{12,28},{14,30},{16,0},... | collective-permute-start | bytes 344072 | tf_op jit(solution)/shard_map/ppermute | solution.py:21
  157.1 19.1 %collective-permute-start.45 = (bf16[2,2,112,128]{3,2,1,0:T(8,128)(2,1)S(1)}, bf16[2,2,112,128]{3,2,1,0:T(8,128)(2,1)S(1)}, u32[]{:S(2)}, u32[]{:S(2)}) collective-permute-start(bf16[2,2,112,128]{3,2,1,0:T(8,128)(2,1)S(1)} %bitcast.375), channel_id=1, source_target_pairs={{0,8},{2,10},{4,12},{6,14},{8,0},{10,2},{12,4},{14,6},{16,24},{18,... | collective-permute-start | bytes 344072 | tf_op jit(solution)/shard_map/ppermute | solution.py:21
  159.0 9.0 %collective-permute-start.41 = (bf16[2,2,2,160,128]{4,3,1,0,2:T(8,128)(2,1)S(1)}, bf16[2,2,2,160,128]{4,3,1,0,2:T(8,128)(2,1)S(1)}, u32[]{:S(2)}, u32[]{:S(2)}) collective-permute-start(bf16[2,2,2,160,128]{4,3,1,0,2:T(8,128)(2,1)S(1)} %fusion.47), channel_id=1, source_target_pairs={{0,4},{2,6},{4,0},{6,2},{8,12},{10,14},{12,8},{14,10},{16,20},{18,... | collective-permute-start | bytes 983048 | tf_op jit(solution)/shard_map/ppermute | solution.py:21
  160.3 9.9 %collective-permute-start.37 = (bf16[2,2,2,176,128]{4,3,2,1,0:T(8,128)(2,1)S(1)}, bf16[2,2,2,176,128]{4,3,2,1,0:T(8,128)(2,1)S(1)}, u32[]{:S(2)}, u32[]{:S(2)}) collective-permute-start(bf16[2,2,2,176,128]{4,3,2,1,0:T(8,128)(2,1)S(1)} %fusion.39), channel_id=1, source_target_pairs={{0,2},{2,0},{4,6},{6,4},{8,10},{10,8},{12,14},{14,12},{16,18},{18,... | collective-permute-start | bytes 1081352 | tf_op jit(solution)/shard_map/ppermute | solution.py:21
  168.1 5.9 %collective-permute-start.42 = (bf16[2,2,160,128]{3,2,1,0:T(8,128)(2,1)S(1)}, bf16[2,2,160,128]{3,2,1,0:T(8,128)(2,1)S(1)}, u32[]{:S(2)}, u32[]{:S(2)}) collective-permute-start(bf16[2,2,160,128]{3,2,1,0:T(8,128)(2,1)S(1)} %fusion.72), channel_id=1, source_target_pairs={{0,2},{2,0},{4,6},{6,4},{8,10},{10,8},{12,14},{14,12},{16,18},{18,... | collective-permute-start | bytes 491528 | tf_op jit(solution)/shard_map/ppermute | solution.py:21
  170.3 5.9 %collective-permute-start.38 = (bf16[2,2,176,128]{3,2,1,0:T(8,128)(2,1)S(1)}, bf16[2,2,176,128]{3,2,1,0:T(8,128)(2,1)S(1)}, u32[]{:S(2)}, u32[]{:S(2)}) collective-permute-start(bf16[2,2,176,128]{3,2,1,0:T(8,128)(2,1)S(1)} %fusion.66), channel_id=1, source_target_pairs={{0,4},{2,6},{4,0},{6,2},{8,12},{10,14},{12,8},{14,10},{16,20},{18,... | collective-permute-start | bytes 540680 | tf_op jit(solution)/shard_map/ppermute | solution.py:21
  174.1 4.5 %collective-permute-start.43 = (bf16[2,160,128]{2,1,0:T(8,128)(2,1)S(1)}, bf16[2,160,128]{2,1,0:T(8,128)(2,1)S(1)}, u32[]{:S(2)}, u32[]{:S(2)}) collective-permute-start(bf16[2,160,128]{2,1,0:T(8,128)(2,1)S(1)} %fusion.86), channel_id=1, source_target_pairs={{0,8},{2,10},{4,12},{6,14},{8,0},{10,2},{12,4},{14,6},{16,24},{18,... | collective-permute-start | bytes 245768 | tf_op jit(solution)/shard_map/ppermute | solution.py:21
  176.4 4.2 %collective-permute-start.48 = (bf16[2,112,128]{2,1,0:T(8,128)(2,1)S(1)}, bf16[2,112,128]{2,1,0:T(8,128)(2,1)S(1)}, u32[]{:S(2)}, u32[]{:S(2)}) collective-permute-start(bf16[2,112,128]{2,1,0:T(8,128)(2,1)S(1)} %fusion.89), channel_id=1, source_target_pairs={{0,4},{2,6},{4,0},{6,2},{8,12},{10,14},{12,8},{14,10},{16,20},{18,... | collective-permute-start | bytes 172040 | tf_op jit(solution)/shard_map/ppermute | solution.py:21
  176.7 8.2 %collective-permute-start.39 = (bf16[2,176,128]{2,1,0:T(8,128)(2,1)S(1)}, bf16[2,176,128]{2,1,0:T(8,128)(2,1)S(1)}, u32[]{:S(2)}, u32[]{:S(2)}) collective-permute-start(bf16[2,176,128]{2,1,0:T(8,128)(2,1)S(1)} %fusion.82), channel_id=1, source_target_pairs={{0,8},{2,10},{4,12},{6,14},{8,0},{10,2},{12,4},{14,6},{16,24},{18,... | collective-permute-start | bytes 270344 | tf_op jit(solution)/shard_map/ppermute | solution.py:21
  178.6 6.3 %collective-permute-start.44 = (bf16[160,128]{1,0:T(8,128)(2,1)S(1)}, bf16[160,128]{1,0:T(8,128)(2,1)S(1)}, u32[]{:S(2)}, u32[]{:S(2)}) collective-permute-start(bf16[160,128]{1,0:T(8,128)(2,1)S(1)} %fusion.95), channel_id=1, source_target_pairs={{0,16},{2,18},{4,20},{6,22},{8,24},{10,26},{12,28},{14,30},{16,0},... | collective-permute-start | bytes 122888 | tf_op jit(solution)/shard_map/ppermute | solution.py:21
  180.6 4.8 %collective-permute-start.49 = (bf16[112,128]{1,0:T(8,128)(2,1)S(1)}, bf16[112,128]{1,0:T(8,128)(2,1)S(1)}, u32[]{:S(2)}, u32[]{:S(2)}) collective-permute-start(bf16[112,128]{1,0:T(8,128)(2,1)S(1)} %fusion.103), channel_id=1, source_target_pairs={{0,2},{2,0},{4,6},{6,4},{8,10},{10,8},{12,14},{14,12},{16,18},{18,... | collective-permute-start | bytes 86024 | tf_op jit(solution)/shard_map/ppermute | solution.py:21
  185.0 5.0 %collective-permute-start.40 = (bf16[176,128]{1,0:T(8,128)(2,1)S(1)}, bf16[176,128]{1,0:T(8,128)(2,1)S(1)}, u32[]{:S(2)}, u32[]{:S(2)}) collective-permute-start(bf16[176,128]{1,0:T(8,128)(2,1)S(1)} %fusion.94), channel_id=1, source_target_pairs={{0,16},{2,18},{4,20},{6,22},{8,24},{10,26},{12,28},{14,30},{16,0},... | collective-permute-start | bytes 135176 | tf_op jit(solution)/shard_map/ppermute | solution.py:21
  190.2 1.4 collective-permute-start.50
  197.0 34.4 %collective-permute-start.57 = (bf16[2,2,16,1792]{3,2,1,0:T(8,128)(2,1)S(1)}, bf16[2,2,16,1792]{3,2,1,0:T(8,128)(2,1)S(1)}, u32[]{:S(2)}, u32[]{:S(2)}) collective-permute-start(bf16[2,2,16,1792]{3,2,1,0:T(8,128)(2,1)S(1)} %bitcast.360), channel_id=1, source_target_pairs={{0,24},{2,26},{4,28},{6,30},{8,16},{10,18},{12,20},{14,22},{16,8},... | collective-permute-start | bytes 688136 | tf_op jit(solution)/shard_map/ppermute | solution.py:21
  198.8 32.7 %collective-permute-start.56 = (bf16[2,2,16,1792]{3,2,1,0:T(8,128)(2,1)S(1)}, bf16[2,2,16,1792]{3,2,1,0:T(8,128)(2,1)S(1)}, u32[]{:S(2)}, u32[]{:S(2)}) collective-permute-start(bf16[2,2,16,1792]{3,2,1,0:T(8,128)(2,1)S(1)} %bitcast.359), channel_id=1, source_target_pairs={{0,16},{2,18},{4,20},{6,22},{8,24},{10,26},{12,28},{14,30},{16,0},... | collective-permute-start | bytes 688136 | tf_op jit(solution)/shard_map/ppermute | solution.py:21
  198.8 15.4 %collective-permute-start.52 = (bf16[2,2,16,1792]{3,2,1,0:T(8,128)(2,1)S(1)}, bf16[2,2,16,1792]{3,2,1,0:T(8,128)(2,1)S(1)}, u32[]{:S(2)}, u32[]{:S(2)}) collective-permute-start(bf16[2,2,16,1792]{3,2,1,0:T(8,128)(2,1)S(1)} %bitcast.361), channel_id=1, source_target_pairs={{0,8},{2,10},{4,12},{6,14},{8,0},{10,2},{12,4},{14,6},{16,24},{18,... | collective-permute-start | bytes 688136 | tf_op jit(solution)/shard_map/ppermute | solution.py:21
  201.6 18.6 %collective-permute-start.58 = (bf16[2,2,2,16,2688]{4,3,1,0,2:T(8,128)(2,1)S(1)}, bf16[2,2,2,16,2688]{4,3,1,0,2:T(8,128)(2,1)S(1)}, u32[]{:S(2)}, u32[]{:S(2)}) collective-permute-start(bf16[2,2,2,16,2688]{4,3,1,0,2:T(8,128)(2,1)S(1)} %fusion.30), channel_id=1, source_target_pairs={{0,4},{2,6},{4,0},{6,2},{8,12},{10,14},{12,8},{14,10},{16,20},{18,... | collective-permute-start | bytes 2064392 | tf_op jit(solution)/shard_map/ppermute | solution.py:21
  203.0 18.7 %collective-permute-start.51 = (bf16[2,2,2,16,2688]{4,3,0,1,2:T(8,128)(2,1)S(1)}, bf16[2,2,2,16,2688]{4,3,0,1,2:T(8,128)(2,1)S(1)}, u32[]{:S(2)}, u32[]{:S(2)}) collective-permute-start(bf16[2,2,2,16,2688]{4,3,0,1,2:T(8,128)(2,1)S(1)} %fusion.29), channel_id=1, source_target_pairs={{0,2},{2,0},{4,6},{6,4},{8,10},{10,8},{12,14},{14,12},{16,18},{18,... | collective-permute-start | bytes 2064392 | tf_op jit(solution)/shard_map/ppermute | solution.py:21
  220.4 9.7 %collective-permute-start.59 = (bf16[2,2,16,2688]{3,2,1,0:T(8,128)(2,1)S(1)}, bf16[2,2,16,2688]{3,2,1,0:T(8,128)(2,1)S(1)}, u32[]{:S(2)}, u32[]{:S(2)}) collective-permute-start(bf16[2,2,16,2688]{3,2,1,0:T(8,128)(2,1)S(1)} %fusion.43), channel_id=1, source_target_pairs={{0,2},{2,0},{4,6},{6,4},{8,10},{10,8},{12,14},{14,12},{16,18},{18,... | collective-permute-start | bytes 1032200 | tf_op jit(solution)/shard_map/ppermute | solution.py:21
  222.0 9.5 %collective-permute-start.53 = (bf16[2,2,16,2688]{3,2,1,0:T(8,128)(2,1)S(1)}, bf16[2,2,16,2688]{3,2,1,0:T(8,128)(2,1)S(1)}, u32[]{:S(2)}, u32[]{:S(2)}) collective-permute-start(bf16[2,2,16,2688]{3,2,1,0:T(8,128)(2,1)S(1)} %copy.72), channel_id=1, source_target_pairs={{0,4},{2,6},{4,0},{6,2},{8,12},{10,14},{12,8},{14,10},{16,20},{18,... | collective-permute-start | bytes 1032200 | tf_op jit(solution)/shard_map/ppermute | solution.py:21
  231.7 7.8 %collective-permute-start.60 = (bf16[2,16,1792]{2,1,0:T(8,128)(2,1)S(1)}, bf16[2,16,1792]{2,1,0:T(8,128)(2,1)S(1)}, u32[]{:S(2)}, u32[]{:S(2)}) collective-permute-start(bf16[2,16,1792]{2,1,0:T(8,128)(2,1)S(1)} %fusion.79), channel_id=1, source_target_pairs={{0,4},{2,6},{4,0},{6,2},{8,12},{10,14},{12,8},{14,10},{16,20},{18,... | collective-permute-start | bytes 344072 | tf_op jit(solution)/shard_map/ppermute | solution.py:21
  233.5 7.1 %collective-permute-start.54 = (bf16[2,16,2688]{2,1,0:T(8,128)(2,1)S(1)}, bf16[2,16,2688]{2,1,0:T(8,128)(2,1)S(1)}, u32[]{:S(2)}, u32[]{:S(2)}) collective-permute-start(bf16[2,16,2688]{2,1,0:T(8,128)(2,1)S(1)} %fusion.68), channel_id=1, source_target_pairs={{0,8},{2,10},{4,12},{6,14},{8,0},{10,2},{12,4},{14,6},{16,24},{18,... | collective-permute-start | bytes 516104 | tf_op jit(solution)/shard_map/ppermute | solution.py:21
  236.2 6.3 %collective-permute-start.62 = (bf16[2,16,2688]{2,1,0:T(8,128)(2,1)S(1)}, bf16[2,16,2688]{2,1,0:T(8,128)(2,1)S(1)}, u32[]{:S(2)}, u32[]{:S(2)}) collective-permute-start(bf16[2,16,2688]{2,1,0:T(8,128)(2,1)S(1)} %fusion.69), channel_id=1, source_target_pairs={{0,8},{2,10},{4,12},{6,14},{8,0},{10,2},{12,4},{14,6},{16,24},{18,... | collective-permute-start | bytes 516104 | tf_op jit(solution)/shard_map/ppermute | solution.py:21
  239.5 5.3 %collective-permute-start.61 = (bf16[16,1792]{1,0:T(8,128)(2,1)S(1)}, bf16[16,1792]{1,0:T(8,128)(2,1)S(1)}, u32[]{:S(2)}, u32[]{:S(2)}) collective-permute-start(bf16[16,1792]{1,0:T(8,128)(2,1)S(1)} %fusion.90), channel_id=1, source_target_pairs={{0,2},{2,0},{4,6},{6,4},{8,10},{10,8},{12,14},{14,12},{16,18},{18,... | collective-permute-start | bytes 172040 | tf_op jit(solution)/shard_map/ppermute | solution.py:21
  242.6 5.7 %collective-permute-start.63 = (bf16[16,2688]{1,0:T(8,128)(2,1)S(1)}, bf16[16,2688]{1,0:T(8,128)(2,1)S(1)}, u32[]{:S(2)}, u32[]{:S(2)}) collective-permute-start(bf16[16,2688]{1,0:T(8,128)(2,1)S(1)} %fusion.85), channel_id=1, source_target_pairs={{0,16},{2,18},{4,20},{6,22},{8,24},{10,26},{12,28},{14,30},{16,0},... | collective-permute-start | bytes 258056 | tf_op jit(solution)/shard_map/ppermute | solution.py:21
  244.9 6.4 %collective-permute-start.55 = (bf16[16,2688]{1,0:T(8,128)(2,1)S(1)}, bf16[16,2688]{1,0:T(8,128)(2,1)S(1)}, u32[]{:S(2)}, u32[]{:S(2)}) collective-permute-start(bf16[16,2688]{1,0:T(8,128)(2,1)S(1)} %fusion.84), channel_id=1, source_target_pairs={{0,16},{2,18},{4,20},{6,22},{8,24},{10,26},{12,28},{14,30},{16,0},... | collective-permute-start | bytes 258056 | tf_op jit(solution)/shard_map/ppermute | solution.py:21
  (33 other events, 255.8 us)
